TPU v7x, 32 devices: a whole 2x2x4 slice. The times are simulated.
32 devices in a mesh: batch: 8 (over z, x), ch: 4 (over y, core).
Axes of the slice: x: 2, y: 2, z: 4, core: 2. Of those that a mesh axis runs over, the one named last changes fastest.
Arguments:
- clip_features: bfloat16 [528, 36864], P('ch', 'batch'), may hold values from -6 to 6
- visible: int32 [64, 4, 12, 12], P('batch'), may hold values from 0 to 1, as said below
- direct_early: bfloat16 [528, 256], P(None, 'ch'), may hold values from -0.25 to 0.25
- narrow_early: bfloat16 [528, 160], P(None, 'ch'), may hold values from -0.25 to 0.25
- squeeze_early: bfloat16 [528, 32], P(None, 'ch'), may hold values from -0.25 to 0.25
- project_early: bfloat16 [528, 128], P(None, 'ch'), may hold values from -0.25 to 0.25
- direct_late: bfloat16 [832, 256], P(None, 'ch'), may hold values from -0.21875 to 0.21875
- narrow_late: bfloat16 [832, 160], P(None, 'ch'), may hold values from -0.21875 to 0.21875
- squeeze_late: bfloat16 [832, 32], P(None, 'ch'), may hold values from -0.21875 to 0.21875
- project_late: bfloat16 [832, 128], P(None, 'ch'), may hold values from -0.21875 to 0.21875
- wide_kernels: bfloat16 [2, 1382400], P(None, 'ch'), may hold values from -0.09375 to 0.09375
- spread_kernels: bfloat16 [2, 27, 32, 128], P(None, None, None, 'ch'), may hold values from -0.21875 to 0.21875
- direct_norm: bfloat16 [2, 2, 256], P(None, None, 'ch'), may hold values from -1 to 2, as said below
- narrow_norm: bfloat16 [2, 2, 160], P(None, None, 'ch'), may hold values from -1 to 2, as said below
- wide_norm: bfloat16 [2, 2, 320], P(None, None, 'ch'), may hold values from -1 to 2, as said below
- squeeze_norm: bfloat16 [2, 2, 32], P(None, None, 'ch'), may hold values from -1 to 2, as said below
- spread_norm: bfloat16 [2, 2, 128], P(None, None, 'ch'), may hold values from -1 to 2, as said below
- project_norm: bfloat16 [2, 2, 128], P(None, None, 'ch'), may hold values from -1 to 2, as said below
- upstream_direct: bfloat16 [64, 2, 6, 6, 256], P('batch', None, None, None, 'ch'), may hold values from -6 to 6
- upstream_wide: bfloat16 [64, 2, 6, 6, 320], P('batch', None, None, None, 'ch'), may hold values from -6 to 6
- upstream_spread: bfloat16 [64, 2, 6, 6, 128], P('batch', None, None, None, 'ch'), may hold values from -6 to 6
- upstream_project: bfloat16 [64, 2, 6, 6, 128], P('batch', None, None, None, 'ch'), may hold values from -6 to 6
Outputs:
- output_direct: bfloat16 [64, 2, 6, 6, 256], P('batch', None, None, None, 'ch')
- output_wide: bfloat16 [64, 2, 6, 6, 320], P('batch', None, None, None, 'ch')
- output_spread: bfloat16 [64, 2, 6, 6, 128], P('batch', None, None, None, 'ch')
- output_project: bfloat16 [64, 2, 6, 6, 128], P('batch', None, None, None, 'ch')
- feature_grad: float32 [528, 36864], P('ch', 'batch')
- direct_early_grad: float32 [528, 256], P(None, 'ch')
- narrow_early_grad: float32 [528, 160], P(None, 'ch')
- squeeze_early_grad: float32 [528, 32], P(None, 'ch')
- project_early_grad: float32 [528, 128], P(None, 'ch')
- direct_late_grad: float32 [832, 256], P(None, 'ch')
- narrow_late_grad: float32 [832, 160], P(None, 'ch')
- squeeze_late_grad: float32 [832, 32], P(None, 'ch')
- project_late_grad: float32 [832, 128], P(None, 'ch')
- wide_kernels_grad: float32 [2, 1382400], P(None, 'ch')
- spread_kernels_grad: float32 [2, 27, 32, 128], P(None, None, None, 'ch')
- direct_norm_grad: float32 [2, 2, 256], P(None, None, 'ch')
- narrow_norm_grad: float32 [2, 2, 160], P(None, None, 'ch')
- wide_norm_grad: float32 [2, 2, 320], P(None, None, 'ch')
- squeeze_norm_grad: float32 [2, 2, 32], P(None, None, 'ch')
- spread_norm_grad: float32 [2, 2, 128], P(None, None, 'ch')
- project_norm_grad: float32 [2, 2, 128], P(None, None, 'ch')
Inputs may be any that keep to these rules, and one draw needn't show every extreme that they name: `visible`: each clip has one or two occluded tubes, boxes in frames, rows and columns with each side at most half of the clip's; every clip keeps at least three quarters of its voxels. `direct_norm`: row 0 of each block holds positive scales, row 1 shifts. `narrow_norm`: row 0 of each block holds positive scales, row 1 shifts. `wide_norm`: row 0 of each block holds positive scales, row 1 shifts. `squeeze_norm`: row 0 of each block holds positive scales, row 1 shifts. `spread_norm`: row 0 of each block holds positive scales, row 1 shifts. `project_norm`: row 0 of each block holds positive scales, row 1 shifts.
All inputs are finite; a program needn't handle non-finite values.
Results may differ from a plain program's by a relative error of at most 0.025.
Values may be sent and summed in bfloat16 or wider, within the bound.
No kernel may reach another device: no remote copies, remote signals or barrier semaphores. Data moves between devices by JAX's collectives and lax.ppermute only.
A program may use at most 640 MiB of HBM per device.

v0:
```python
import jax
import jax.numpy as jnp
from jax import lax
from jax.sharding import PartitionSpec as P

NARROW = 160


EPSILON = 0.001
CUBE_OFFSETS = [(a, b, c) for a in range(3) for b in range(3) for c in range(3)]


def pad_cells(field):
    return jnp.pad(field, ((0, 0), (1, 1), (1, 1), (1, 1), (0, 0)))


def take_cells(padded, corner, full_shape):
    a, b, c = corner
    return padded[:, a : a + full_shape[1], b : b + full_shape[2], c : c + full_shape[3]]


def point_apply(activation, weight):
    return jnp.einsum("cfhwi,io->cfhwo", activation, weight, preferred_element_type=jnp.float32)


def point_back(gradient, weight):
    return jnp.einsum("cfhwo,io->cfhwi", gradient, weight, preferred_element_type=jnp.float32)


def point_weight(activation, gradient):
    return jnp.einsum("cfhwi,cfhwo->io", activation, gradient, preferred_element_type=jnp.float32)


def cube_apply(activation, kernel):
    padded = pad_cells(activation)
    running = None
    for offset_index, corner in enumerate(CUBE_OFFSETS):
        piece_term = point_apply(take_cells(padded, corner, activation.shape), kernel[offset_index])
        running = piece_term if running is None else running + piece_term
    return running


def cube_back(gradient, kernel):
    padded = pad_cells(gradient)
    running = None
    for offset_index, (a, b, c) in enumerate(CUBE_OFFSETS):
        piece_term = point_back(
            take_cells(padded, (2 - a, 2 - b, 2 - c), gradient.shape), kernel[offset_index]
        )
        running = piece_term if running is None else running + piece_term
    return running


def cube_weight(activation, gradient):
    padded = pad_cells(activation)
    return jnp.stack(
        [
            point_weight(take_cells(padded, corner, activation.shape), gradient)
            for corner in CUBE_OFFSETS
        ]
    )


def mean_cube(field):
    padded = pad_cells(field)
    running = jnp.zeros_like(field)
    for corner in CUBE_OFFSETS:
        running = running + take_cells(padded, corner, field.shape)
    return running / 27.0


def mean_pairs(field):
    clip_count, frame_count, row_count, column_count, channels = field.shape
    grouped = field.reshape(
        clip_count, frame_count // 2, 2, row_count // 2, 2, column_count // 2, 2, channels
    )
    return jnp.mean(grouped, axis=(2, 4, 6))


def spread_pairs(gradient):
    widened = jnp.repeat(jnp.repeat(jnp.repeat(gradient, 2, axis=1), 2, axis=2), 2, axis=3)
    return widened / 8.0


def pair_mask(visible):
    clip_count, frame_count, row_count, column_count = visible.shape
    grouped = visible.reshape(
        clip_count, frame_count // 2, 2, row_count // 2, 2, column_count // 2, 2
    )
    return jnp.max(grouped, axis=(2, 4, 6))


def voxels_last(flat, clip_count, frame_count, row_count, column_count):
    shaped = flat.reshape(flat.shape[0], clip_count, frame_count, row_count, column_count)
    return jnp.transpose(shaped, (1, 2, 3, 4, 0))


def voxels_first(field):
    moved = jnp.transpose(field, (4, 0, 1, 2, 3))
    return moved.reshape(moved.shape[0], -1)


def kernel_unpack(flat, inner_count):
    shaped = flat.reshape(flat.shape[0], -1, 27, inner_count)
    return jnp.transpose(shaped, (0, 2, 3, 1))


def kernel_pack(kernel):
    moved = jnp.transpose(kernel, (0, 3, 1, 2))
    return moved.reshape(moved.shape[0], -1)


def split_vector(vector, widths):
    pieces_out = []
    offset = 0
    for piece_width in widths:
        pieces_out.append(vector[offset : offset + piece_width])
        offset = offset + piece_width
    return pieces_out


def normalize(output, average, inverse_std, affine, masking):
    centred = (output - average) * inverse_std
    shifted = affine[0] * centred + affine[1]
    return (shifted * jax.nn.sigmoid(shifted) * masking, (centred, shifted))


def norm_local(gradient, unit_state, masking):
    centred, shifted = unit_state
    sigmoid_gate = jax.nn.sigmoid(shifted)
    inner_grad = gradient * masking * sigmoid_gate * (1.0 + shifted * (1.0 - sigmoid_gate))
    return (
        inner_grad,
        jnp.sum(inner_grad * centred, axis=(0, 1, 2, 3)),
        jnp.sum(inner_grad, axis=(0, 1, 2, 3)),
    )


def norm_finish(
    inner_grad, unit_state, scale_sum, shift_sum, inverse_std, affine, voxel_count, masking
):
    centred = unit_state[0]
    return (
        affine[0]
        * inverse_std
        * (inner_grad - (shift_sum + centred * scale_sum) / voxel_count)
        * masking
    )


def norm_totals(operations, records):
    widths = [record[1].shape[0] for record in records]
    vector = jnp.concatenate([record[1] for record in records] + [record[2] for record in records])
    pieces_out = split_vector(operations[5](vector), widths + widths)
    return (pieces_out[: len(records)], pieces_out[len(records) :])


def channel_inputs(pieces):
    groups = lax.axis_size("ch")
    local_part = jnp.concatenate(pieces, axis=4)
    gathered = lax.all_gather(local_part, "ch", axis=4, tiled=True)
    leading = gathered.shape[:4]
    grouped = gathered.reshape(leading + (groups, local_part.shape[4]))
    ordered = []
    offset = 0
    for segment in pieces:
        piece_width = segment.shape[4]
        ordered.append(
            grouped[..., offset : offset + piece_width].reshape(leading + (groups * piece_width,))
        )
        offset = offset + piece_width
    return (jnp.concatenate(ordered, axis=4), [groups * segment.shape[4] for segment in pieces])


def channel_returns(partial_sum, widths):
    groups = lax.axis_size("ch")
    leading = partial_sum.shape[:4]
    grouped = []
    offset = 0
    for piece_width in widths:
        grouped.append(
            partial_sum[..., offset : offset + piece_width].reshape(
                leading + (groups, piece_width // groups)
            )
        )
        offset = offset + piece_width
    ordered = jnp.concatenate(grouped, axis=5).reshape(leading + (partial_sum.shape[4],))
    local_part = lax.psum_scatter(
        ordered.astype(jnp.bfloat16), "ch", scatter_dimension=4, tiled=True
    ).astype(jnp.float32)
    pieces_out = []
    offset = 0
    for piece_width in widths:
        pieces_out.append(local_part[..., offset : offset + piece_width // groups])
        offset = offset + piece_width // groups
    return pieces_out


def channel_reduced(first_part, second_part):
    return (
        lax.all_gather(first_part, "ch", axis=4, tiled=True),
        lax.all_gather(second_part, "ch", axis=4, tiled=True),
    )


def channel_reduced_back(first_part, second_part):
    return (
        lax.psum_scatter(
            first_part.astype(jnp.bfloat16), "ch", scatter_dimension=4, tiled=True
        ).astype(jnp.float32),
        lax.psum_scatter(
            second_part.astype(jnp.bfloat16), "ch", scatter_dimension=4, tiled=True
        ).astype(jnp.float32),
    )


def channel_moments(outputs, masking):
    widths = [o.shape[4] for o in outputs]
    first_sums = jnp.concatenate([jnp.sum(o * masking, axis=(0, 1, 2, 3)) for o in outputs])
    totals, voxel_count = lax.psum((first_sums, jnp.sum(masking)), "batch")
    averages = totals / voxel_count
    average_parts = split_vector(averages, widths)
    deviations = []
    for o, m in zip(outputs, average_parts):
        centred = o - m
        deviations.append(jnp.sum(masking * centred * centred, axis=(0, 1, 2, 3)))
    variance = lax.psum(jnp.concatenate(deviations), "batch") / voxel_count
    return (
        split_vector(averages, widths),
        split_vector(lax.rsqrt(variance + EPSILON), widths),
        voxel_count,
    )


def channel_norm_sums(vector):
    return lax.psum(vector, "batch")


def block_forward(operations, activation, masking, weights, affines):
    direct, narrow, squeeze, project, wide_kernel, spread_kernel = weights
    first_level = [
        point_apply(activation, direct),
        point_apply(activation, narrow),
        point_apply(activation, squeeze),
        mean_cube(point_apply(activation, project)),
    ]
    first_index = [0, 1, 3, 5]
    averages, first_inverse, voxel_count = operations[4](first_level, masking)
    values = [None] * 6
    unit_kept = [None] * 6
    inverse_std = [None] * 6
    for k, i in enumerate(first_index):
        values[i], unit_kept[i] = normalize(
            first_level[k], averages[k], first_inverse[k], affines[i], masking
        )
        inverse_std[i] = first_inverse[k]
    gathered_narrow, gathered_squeeze = operations[2](
        values[1].astype(jnp.bfloat16), values[3].astype(jnp.bfloat16)
    )
    second = [cube_apply(gathered_narrow, wide_kernel), cube_apply(gathered_squeeze, spread_kernel)]
    second_averages, second_inverse, voxel_count = operations[4](second, masking)
    for k, i in enumerate([2, 4]):
        values[i], unit_kept[i] = normalize(
            second[k], second_averages[k], second_inverse[k], affines[i], masking
        )
        inverse_std[i] = second_inverse[k]
    outputs = (values[0], values[2], values[4], values[5])
    return (outputs, (unit_kept, inverse_std, voxel_count, gathered_narrow, gathered_squeeze))


def block_backward(operations, gradients, activation, masking, weights, affines, saved_state):
    direct, narrow, squeeze, project, wide_kernel, spread_kernel = weights
    unit_kept, inverse_std, voxel_count, gathered_narrow, gathered_squeeze = saved_state
    outer_index = [0, 2, 4, 5]
    outer_items = [norm_local(g, unit_kept[i], masking) for g, i in zip(gradients, outer_index)]
    scale_sums, shift_sums = norm_totals(operations, outer_items)
    pre_grads = [None] * 6
    affine_grads = [None] * 6
    for k, i in enumerate(outer_index):
        affine_grads[i] = (scale_sums[k], shift_sums[k])
        pre_grads[i] = norm_finish(
            outer_items[k][0],
            unit_kept[i],
            scale_sums[k],
            shift_sums[k],
            inverse_std[i],
            affines[i],
            voxel_count,
            masking,
        )
    wide_grad = pre_grads[2].astype(jnp.bfloat16)
    spread_grad = pre_grads[4].astype(jnp.bfloat16)
    wide_weight = cube_weight(gathered_narrow, wide_grad)
    spread_weight = cube_weight(gathered_squeeze, spread_grad)
    narrow_back, squeeze_back = operations[3](
        cube_back(wide_grad, wide_kernel), cube_back(spread_grad, spread_kernel)
    )
    inner_items = [
        norm_local(narrow_back, unit_kept[1], masking),
        norm_local(squeeze_back, unit_kept[3], masking),
    ]
    scale_inner, shift_inner = norm_totals(operations, inner_items)
    for k, i in enumerate([1, 3]):
        affine_grads[i] = (scale_inner[k], shift_inner[k])
        pre_grads[i] = norm_finish(
            inner_items[k][0],
            unit_kept[i],
            scale_inner[k],
            shift_inner[k],
            inverse_std[i],
            affines[i],
            voxel_count,
            masking,
        )
    direct_grad = pre_grads[0].astype(jnp.bfloat16)
    narrow_grad = pre_grads[1].astype(jnp.bfloat16)
    squeeze_grad = pre_grads[3].astype(jnp.bfloat16)
    project_grad = mean_cube(pre_grads[5]).astype(jnp.bfloat16)
    partial_input = (
        point_back(direct_grad, direct)
        + point_back(narrow_grad, narrow)
        + point_back(squeeze_grad, squeeze)
        + point_back(project_grad, project)
    )
    weight_grads = (
        point_weight(activation, direct_grad),
        point_weight(activation, narrow_grad),
        point_weight(activation, squeeze_grad),
        point_weight(activation, project_grad),
        wide_weight,
        spread_weight,
    )
    return (partial_input, weight_grads, affine_grads)


def run_layers(
    operations, features, visible, points, wide_kernels, spread_kernels, affine_args, upstream
):
    mask_fine = visible.astype(jnp.float32)[..., None]
    mask_coarse = pair_mask(visible).astype(jnp.float32)[..., None]
    local_input = features * visible.astype(jnp.bfloat16)[..., None]
    early_act, early_widths = operations[0]([local_input])
    affine_values = [affine.astype(jnp.float32) for affine in affine_args]
    early_weights = (points[0], points[1], points[2], points[3], wide_kernels[0], spread_kernels[0])
    late_weights = (points[4], points[5], points[6], points[7], wide_kernels[1], spread_kernels[1])
    early_affines = [affine[0] for affine in affine_values]
    late_affines = [affine[1] for affine in affine_values]
    early_out, early_state = block_forward(
        operations, early_act, mask_fine, early_weights, early_affines
    )
    pooled = [mean_pairs(field).astype(jnp.bfloat16) for field in early_out]
    late_act, late_widths = operations[0](pooled)
    late_out, late_state = block_forward(
        operations, late_act, mask_coarse, late_weights, late_affines
    )
    late_grads = [field.astype(jnp.float32) for field in upstream]
    late_partial, late_wgrads, late_agrads = block_backward(
        operations, late_grads, late_act, mask_coarse, late_weights, late_affines, late_state
    )
    early_grads = [spread_pairs(field) for field in operations[1](late_partial, late_widths)]
    early_partial, early_wgrads, early_agrads = block_backward(
        operations, early_grads, early_act, mask_fine, early_weights, early_affines, early_state
    )
    feature_grad = operations[1](early_partial, early_widths)[0] * mask_fine
    weight_grads = (
        early_wgrads[0],
        early_wgrads[1],
        early_wgrads[2],
        early_wgrads[3],
        late_wgrads[0],
        late_wgrads[1],
        late_wgrads[2],
        late_wgrads[3],
        kernel_pack(jnp.stack([early_wgrads[4], late_wgrads[4]])),
        jnp.stack([early_wgrads[5], late_wgrads[5]]),
    )
    affine_grads = tuple(
        (jnp.stack([jnp.stack(early_agrads[i]), jnp.stack(late_agrads[i])]) for i in range(6))
    )
    return (late_out, feature_grad, weight_grads, affine_grads)


def shards(
    clip_features,
    visible,
    direct_early,
    narrow_early,
    squeeze_early,
    project_early,
    direct_late,
    narrow_late,
    squeeze_late,
    project_late,
    wide_kernels,
    spread_kernels,
    direct_norm,
    narrow_norm,
    wide_norm,
    squeeze_norm,
    spread_norm,
    project_norm,
    upstream_direct,
    upstream_wide,
    upstream_spread,
    upstream_project,
):
    features_last = voxels_last(
        clip_features, visible.shape[0], visible.shape[1], visible.shape[2], visible.shape[3]
    )
    operations = (
        channel_inputs,
        channel_returns,
        channel_reduced,
        channel_reduced_back,
        channel_moments,
        channel_norm_sums,
    )
    points = (
        direct_early,
        narrow_early,
        squeeze_early,
        project_early,
        direct_late,
        narrow_late,
        squeeze_late,
        project_late,
    )
    affine_args = (direct_norm, narrow_norm, wide_norm, squeeze_norm, spread_norm, project_norm)
    upstream = (upstream_direct, upstream_wide, upstream_spread, upstream_project)
    late_out, feature_last, weight_local, affine_grads = run_layers(
        operations,
        features_last,
        visible,
        points,
        kernel_unpack(wide_kernels, NARROW),
        spread_kernels,
        affine_args,
        upstream,
    )
    weight_grads = (
        lax.psum(weight_local[0].astype(jnp.bfloat16), "batch").astype(jnp.float32),
        lax.psum(weight_local[1].astype(jnp.bfloat16), "batch").astype(jnp.float32),
        lax.psum(weight_local[2].astype(jnp.bfloat16), "batch").astype(jnp.float32),
        lax.psum(weight_local[3].astype(jnp.bfloat16), "batch").astype(jnp.float32),
        lax.psum(weight_local[4].astype(jnp.bfloat16), "batch").astype(jnp.float32),
        lax.psum(weight_local[5].astype(jnp.bfloat16), "batch").astype(jnp.float32),
        lax.psum(weight_local[6].astype(jnp.bfloat16), "batch").astype(jnp.float32),
        lax.psum(weight_local[7].astype(jnp.bfloat16), "batch").astype(jnp.float32),
        lax.psum(weight_local[8].astype(jnp.bfloat16), "batch").astype(jnp.float32),
        lax.psum(weight_local[9].astype(jnp.bfloat16), "batch").astype(jnp.float32),
    )
    outputs = tuple((field.astype(jnp.bfloat16) for field in late_out))
    feature_grad = voxels_first(feature_last)
    return (
        outputs[0],
        outputs[1],
        outputs[2],
        outputs[3],
        feature_grad,
        weight_grads[0],
        weight_grads[1],
        weight_grads[2],
        weight_grads[3],
        weight_grads[4],
        weight_grads[5],
        weight_grads[6],
        weight_grads[7],
        weight_grads[8],
        weight_grads[9],
        affine_grads[0],
        affine_grads[1],
        affine_grads[2],
        affine_grads[3],
        affine_grads[4],
        affine_grads[5],
    )


def solution(mesh):
    placed = (
        P("ch", "batch"),
        P("batch", None, None, None),
        P(None, "ch"),
        P(None, "ch"),
        P(None, "ch"),
        P(None, "ch"),
        P(None, "ch"),
        P(None, "ch"),
        P(None, "ch"),
        P(None, "ch"),
        P(None, "ch"),
        P(None, None, None, "ch"),
        P(None, None, "ch"),
        P(None, None, "ch"),
        P(None, None, "ch"),
        P(None, None, "ch"),
        P(None, None, "ch"),
        P(None, None, "ch"),
        P("batch", None, None, None, "ch"),
        P("batch", None, None, None, "ch"),
        P("batch", None, None, None, "ch"),
        P("batch", None, None, None, "ch"),
    )
    return jax.shard_map(
        shards,
        mesh=mesh,
        in_specs=placed,
        out_specs=(
            P("batch", None, None, None, "ch"),
            P("batch", None, None, None, "ch"),
            P("batch", None, None, None, "ch"),
            P("batch", None, None, None, "ch"),
            P("ch", "batch"),
            P(None, "ch"),
            P(None, "ch"),
            P(None, "ch"),
            P(None, "ch"),
            P(None, "ch"),
            P(None, "ch"),
            P(None, "ch"),
            P(None, "ch"),
            P(None, "ch"),
            P(None, None, None, "ch"),
            P(None, None, "ch"),
            P(None, None, "ch"),
            P(None, None, "ch"),
            P(None, None, "ch"),
            P(None, None, "ch"),
            P(None, None, "ch"),
        ),
        check_vma=False,
    )
```

profile of v0, /device:TPU:0, one launch (start us, length us, event | category | flops | bytes accessed | tf_op | source)
XLA Modules:
  0.0 2619.7 jit_solution(15389316833034932745)
XLA Ops:
  18.8 24.4 copy.326
  63.9 290.5 %all-gather.3.cloned.1.call-done = bf16[8,4,12,12,528]{3,0,2,1,4:T(8,128)(2,1)} async-done(((bf16[8,4,12,12,132]{3,0,2,1,4:T(8,128)(2,1)}), bf16[8,4,12,12,528]{3,0,2,1,4:T(8,128)(2,1)}) %all-gather.3.cloned.1.call-update) | async-done | bytes 4866064 | tf_op jit(solution)/shard_map/all_gather | solution.py:161
  354.4 56.1 %copy.327 = bf16[8,4,12,12,528]{4,3,2,1,0:T(8,128)(2,1)} copy(bf16[8,4,12,12,528]{3,0,2,1,4:T(8,128)(2,1)} %all-gather.3.cloned.1.call-done) | data formatting | bytes 9732096 | tf_op jit(solution)/shard_map/all_gather | solution.py:161
  410.5 7.2 fusion.694
  417.7 12.4 multiply_reduce_fusion.11
  436.1 35.0 %multiply_reduce_fusion.7 = (f32[32]{0:T(128)S(1)}, f32[8,4,12,12,32]{4,3,2,1,0:T(8,128)}) fusion(f32[8,4,12,12]{3,2,1,0:T(8,128)} %copy.334, f32[8,4,12,12,32]{4,3,2,1,0:T(8,128)} %fusion.694), kind=kLoop, calls=%fused_computation.320 | loop fusion | flops 4128736 | bytes 1198208 | tf_op jit(solution)/shard_map/reduce_sum | solution.py:219
  471.8 21.9 all-reduce.16
  498.5 17.1 psum.176
  517.7 20.9 all_gather.20
  637.0 8.4 copy.337
  656.9 31.4 %multiply_reduce_fusion.5 = (f32[32]{0:T(128)S(1)}, f32[8,4,12,12,32]{4,3,2,1,0:T(8,128)}) fusion(f32[8,4,12,12]{3,2,1,0:T(8,128)S(1)} %copy.328, bf16[2,27,32,32]{3,2,1,0:T(8,128)(2,1)} %param.33, bf16[8,4,12,12,32]{3,4,2,1,0:T(8,128)(2,1)S(1)} %all_gather.20, f32[8,4,12,12,32]{4,3,2,1,0:T(8,128)} %fusion.169, f32[8,4,12,12,32]{4,3,2,1,0:T(8,128)} %fusion.167, ...), kind=kOutput, calls=%fused_computation.309 | convolution fusion | flops 13565920 | bytes 82700416 | tf_op jit(solution)/shard_map/cfhwi,io->cfhwo/dot_general | solution.py:23
  688.3 56.0 %all-gather.5.cloned.1.call-done = bf16[8,4,12,12,160]{3,0,2,1,4:T(8,128)(2,1)} async-done(((bf16[8,4,12,12,40]{3,0,2,1,4:T(8,128)(2,1)}), bf16[8,4,12,12,160]{3,0,2,1,4:T(8,128)(2,1)}) %all-gather.5.cloned.1.call-update) | async-done | bytes 1474576 | tf_op jit(solution)/shard_map/all_gather | solution.py:201
  744.3 30.2 %copy.338 = bf16[8,4,12,12,160]{4,3,2,1,0:T(8,128)(2,1)S(1)} copy(bf16[8,4,12,12,160]{3,0,2,1,4:T(8,128)(2,1)} %all-gather.5.cloned.1.call-done) | data formatting | bytes 2949120 | tf_op jit(solution)/shard_map/all_gather | solution.py:201
  864.0 28.7 %multiply_reduce_fusion.6 = (f32[80]{0:T(128)S(1)}, f32[8,4,12,12,80]{4,3,2,1,0:T(8,128)}) fusion(f32[8,4,12,12]{3,2,1,0:T(8,128)S(1)} %copy.328, bf16[2,27,160,80]{3,2,1,0:T(8,128)(2,1)} %bitcast.3117, bf16[8,4,12,12,160]{4,3,2,1,0:T(8,128)(2,1)S(1)} %copy.338, f32[8,4,12,12,80]{4,3,2,1,0:T(8,128)} %fusion.117, f32[8,4,12,12,80]{4,3,2,1,0:T(8,128)} %fusion.115, ...), kind=kOutput, calls=%fused_computation.311 | convolution fusion | flops 128286640 | bytes 84797760 | tf_op jit(solution)/shard_map/cfhwi,io->cfhwo/dot_general | solution.py:23
  892.8 21.6 psum.177
  918.6 17.1 psum.178
  968.3 110.0 %all_gather.21 = bf16[8,2,6,6,832]{0,1,3,2,4:T(2,128)(2,1)} all-gather(bf16[8,2,6,6,208]{0,1,3,2,4:T(2,128)(2,1)} %copy.371), channel_id=1, replica_groups=mesh['batch'=8,'ch'=4] {'ch'}, dimensions={4}, use_global_device_ids=true | all-gather | bytes 1198080 | tf_op jit(solution)/shard_map/all_gather | solution.py:161
  1078.3 7.8 slice.2592
  1086.1 7.0 fusion.1115
  1099.7 10.2 copy.743
  1110.0 11.1 copy.744
  1134.3 19.7 all-reduce.15
  1155.6 17.1 psum.181
  1176.2 7.5 all_gather.23
  1189.8 20.9 all_gather.22
  1266.7 19.7 psum.182
  1289.2 17.8 psum.183
  1315.2 19.3 psum.184
  1375.1 13.3 all-reduce.13
  1445.7 21.5 psum.185
  1487.1 22.4 copy.738
  1509.5 21.5 reshape.767
  1541.2 11.4 reduce-scatter.13.cloned.1.call-done
  1552.5 7.0 reshape.768
  1584.1 21.3 psum.186
  1606.7 8.0 multiply_multiply_fusion.5
  1629.8 6.9 fusion.201
  1636.7 6.9 fusion.202
  1643.6 7.0 fusion.203
  1670.3 7.0 fusion.207
  1677.3 7.0 fusion.208
  1684.2 6.9 fusion.209
  1691.2 8.0 fusion.210
  1699.2 7.8 fusion.211
  1707.0 7.6 fusion.212
  1714.7 7.7 fusion.213
  1722.3 7.6 fusion.214
  1749.0 6.9 fusion.218
  1755.9 6.9 fusion.219
  1762.8 6.9 fusion.220
  1783.4 7.9 fusion.734
  1916.1 34.9 %fusion.58 = bf16[8,4,12,12,32]{4,3,2,1,0:T(8,128)(2,1)} fusion(f32[8,4,12,12,32]{4,3,2,1,0:T(8,128)} %get-tuple-element.167), kind=kLoop, calls=%fused_computation.276 | loop fusion | flops 4128768 | bytes 884736 | tf_op jit(solution)/shard_map/convert_element_type | solution.py:318
  2058.9 52.2 %add_convert_fusion.1 = bf16[8,4,12,12,32]{3,4,2,1,0:T(8,128)(2,1)} fusion(f32[8,4,12,12,32]{3,4,2,1,0:T(8,128)} %fusion.222, f32[8,4,12,12,32]{3,4,2,1,0:T(8,128)} %fusion.221, f32[8,4,12,12,32]{3,4,2,1,0:T(8,128)} %fusion.220, f32[8,4,12,12,32]{3,4,2,1,0:T(8,128)} %fusion.219, f32[8,4,12,12,32]{3,4,2,1,0:T(8,128)} %fusion.218, ...), kind=kOutput, calls=%fused_computation.210 | convolution fusion | flops 13418496 | bytes 164175872 | tf_op jit(solution)/shard_map/cfhwo,io->cfhwi/dot_general | solution.py:27
  2122.2 52.1 %add_convert_fusion.2 = bf16[8,4,12,12,160]{4,3,2,1,0:T(8,128)(2,1)} fusion(f32[8,4,12,12,160]{4,3,2,1,0:T(8,128)} %fusion.197, f32[8,4,12,12,160]{4,3,2,1,0:T(8,128)} %fusion.196, f32[8,4,12,12,160]{4,3,2,1,0:T(8,128)} %fusion.195, f32[8,4,12,12,160]{4,3,2,1,0:T(8,128)} %fusion.194, f32[8,4,12,12,160]{4,3,2,1,0:T(8,128)} %fusion.193, ...), kind=kOutput, calls=%fused_computation.211 | convolution fusion | flops 137871360 | bytes 166666240 | tf_op jit(solution)/shard_map/cfhwo,io->cfhwi/dot_general | solution.py:27
  2178.4 33.4 %copy.732 = bf16[8,4,12,12,160]{3,2,1,0,4:T(8,128)(2,1)} copy(bf16[8,4,12,12,160]{4,3,2,1,0:T(8,128)(2,1)} %add_convert_fusion.2) | data formatting | bytes 2949120
  2211.8 23.5 reshape.769
  2279.4 7.6 reshape.770
  2287.0 8.2 copy.733
  2299.6 17.3 psum.187
  2323.7 7.9 fusion.704
  2331.6 8.0 fusion.689
  2343.6 20.0 add_convert_fusion
  2384.9 63.8 %all-reduce.28.cloned.1.call-done = (bf16[528,40]{0,1:T(8,128)(2,1)}, bf16[528,8]{0,1:T(8,128)(2,1)}, bf16[528,32]{0,1:T(8,128)(2,1)}, bf16[832,8]{0,1:T(8,128)(2,1)}, bf16[832,32]{0,1:T(8,128)(2,1)}) async-done(((bf16[528,40]{0,1:T(8,128)(2,1)}, bf16[528,8]{0,1:T(8,128)(2,1)}, bf16[528,32]{0,1:T(8,128)(2,1)}, bf16[832,8]{0,1:T(8,128)(2,1)}, bf16[832,32]{0,1:T(8,128)(2,1)}), (bf16[528,40]{0,1:T(8,128)(2,1)}, ...) | async-done | bytes 151056 | tf_op jit(solution)/shard_map/psum | solution.py:442
  2455.7 139.9 %all-reduce.26.cloned.1.call-done = bf16[8,4,12,12,528]{4,3,2,1,0:T(8,128)(2,1)} async-done(((bf16[8,4,12,12,528]{4,3,2,1,0:T(8,128)(2,1)}), bf16[8,4,12,12,528]{4,3,2,1,0:T(8,128)(2,1)}) %all-reduce.26.cloned.1.call-update) | async-done | bytes 4866064
  (1013 shorter events, 948.6 us)
Async XLA Ops:
  7.2 1126.3 %copy-start = (bf16[832,64]{0,1:T(8,128)(2,1)S(1)}, bf16[832,64]{0,1:T(8,128)(2,1)}, u32[]{:S(2)}) copy-start(bf16[832,64]{0,1:T(8,128)(2,1)} %param.28) | copy-start | bytes 319492
  7.2 347.2 %all-gather.3.cloned.1.call-start = ((), (), s32[]{:S(2)}) async-start(), calls=%async_computation.3 | async-start | bytes 64880640 | tf_op jit(solution)/shard_map/all_gather | solution.py:161
  43.3 701.0 %all-gather.5.cloned.1.call-start = ((), (), s32[]{:S(2)}) async-start(), calls=%async_computation.4 | async-start | bytes 19660800 | tf_op jit(solution)/shard_map/all_gather | solution.py:201
  46.6 16.2 copy-start.92
  46.6 15.6 copy-start.90
  46.6 14.9 copy-start.86
  46.7 14.3 copy-start.88
  46.7 16.6 copy-start.94
  46.7 16.6 copy-start.96
  49.0 1748.7 %copy-start.15 = (f32[8,4,12,12]{3,2,1,0:T(8,128)}, f32[8,4,12,12]{3,2,1,0:T(8,128)S(1)}, u32[]{:S(2)}) copy-start(f32[8,4,12,12]{3,2,1,0:T(8,128)S(1)} %copy.328) | copy-start | bytes 55300
  61.5 455.5 %copy-start.147 = (f32[8]{0:T(128)}, f32[8]{0:T(128)S(1)}, u32[]{:S(2)}) copy-start(f32[8]{0:T(128)S(1)} %get-tuple-element.239) | copy-start | bytes 100
  61.5 455.5 %copy-start.149 = (f32[8]{0:T(128)}, f32[8]{0:T(128)S(1)}, u32[]{:S(2)}) copy-start(f32[8]{0:T(128)S(1)} %get-tuple-element.240) | copy-start | bytes 100
  62.7 571.8 %copy-start.143 = (f32[40]{0:T(128)}, f32[40]{0:T(128)S(1)}, u32[]{:S(2)}) copy-start(f32[40]{0:T(128)S(1)} %get-tuple-element.243) | copy-start | bytes 484
  62.7 571.8 %copy-start.145 = (f32[40]{0:T(128)}, f32[40]{0:T(128)S(1)}, u32[]{:S(2)}) copy-start(f32[40]{0:T(128)S(1)} %get-tuple-element.244) | copy-start | bytes 484
  63.9 346.6 %copy-start.70 = (bf16[528,32]{0,1:T(8,128)(2,1)S(1)}, bf16[528,32]{0,1:T(8,128)(2,1)}, u32[]{:S(2)}) copy-start(bf16[528,32]{0,1:T(8,128)(2,1)} %param.27) | copy-start | bytes 101380
  436.1 58.6 %copy-start.22 = (f32[8,4,12,12,64]{4,3,2,1,0:T(8,128)}, f32[8,4,12,12,64]{4,3,2,1,0:T(8,128)S(1)}, u32[]{:S(2)}) copy-start(f32[8,4,12,12,64]{4,3,2,1,0:T(8,128)S(1)} %get-tuple-element.276) | copy-start | bytes 3538948
  494.6 22.5 copy-start.84
  494.6 139.9 %copy-start.141 = (f32[40]{0:T(128)}, f32[40]{0:T(128)S(1)}, u32[]{:S(2)}) copy-start(f32[40]{0:T(128)S(1)} %slice.2077) | copy-start | bytes 484
  494.7 150.8 %copy-start.117 = (f32[64]{0:T(128)}, f32[64]{0:T(128)S(1)}, u32[]{:S(2)}) copy-start(f32[64]{0:T(128)S(1)} %slice.2076) | copy-start | bytes 772
  516.4 118.2 %copy-start.178 = (f32[40]{0:T(128)}, f32[40]{0:T(128)S(1)}, u32[]{:S(2)}) copy-start(f32[40]{0:T(128)S(1)} %slice.2084) | copy-start | bytes 484
  517.1 128.4 %copy-start.166 = (f32[64]{0:T(128)}, f32[64]{0:T(128)S(1)}, u32[]{:S(2)}) copy-start(f32[64]{0:T(128)S(1)} %slice.2080) | copy-start | bytes 772
  538.6 118.2 %copy-start.2 = (bf16[8,4,12,12,32]{3,4,2,1,0:T(8,128)(2,1)}, bf16[8,4,12,12,32]{3,4,2,1,0:T(8,128)(2,1)S(1)}, u32[]{:S(2)}) copy-start(bf16[8,4,12,12,32]{3,4,2,1,0:T(8,128)(2,1)S(1)} %all_gather.20) | copy-start | bytes 884740
  645.4 798.9 %all-reduce.24.cloned.1.call-start = ((), (), s32[]{:S(2)}) async-start(), calls=%async_computation.8 | async-start | bytes 589824
  774.5 89.5 %copy-start.5 = (bf16[8,4,12,12,160]{4,3,2,1,0:T(8,128)(2,1)}, bf16[8,4,12,12,160]{4,3,2,1,0:T(8,128)(2,1)S(1)}, u32[]{:S(2)}) copy-start(bf16[8,4,12,12,160]{4,3,2,1,0:T(8,128)(2,1)S(1)} %copy.338) | copy-start | bytes 4423684
  892.7 24.8 copy-start.17
  915.0 21.4 copy-start.120
  915.1 29.6 %copy-start.104 = (f32[32]{0:T(128)}, f32[32]{0:T(128)S(1)}, u32[]{:S(2)}) copy-start(f32[32]{0:T(128)S(1)} %slice.2196) | copy-start | bytes 388
  915.1 21.3 copy-start.169
  915.1 21.3 copy-start.171
  1132.6 40.9 %copy-start.93 = (f32[2,2,64]{2,1,0:T(2,128)S(1)}, f32[2,2,64]{2,1,0:T(2,128)}, u32[]{:S(2)}) copy-start(f32[2,2,64]{2,1,0:T(2,128)} %copy-done.92) | copy-start | bytes 3076
  1132.6 40.9 %copy-start.99 = (f32[144]{0:T(256)S(1)}, f32[144]{0:T(256)}, u32[]{:S(2)}) copy-start(f32[144]{0:T(256)} %copy-done.98) | copy-start | bytes 1732
  1132.6 41.4 %copy-start.91 = (f32[2,2,40]{2,1,0:T(2,128)S(1)}, f32[2,2,40]{2,1,0:T(2,128)}, u32[]{:S(2)}) copy-start(f32[2,2,40]{2,1,0:T(2,128)} %copy-done.90) | copy-start | bytes 1924
  1132.6 42.0 %copy-start.89 = (f32[2,2,8]{2,1,0:T(2,128)S(1)}, f32[2,2,8]{2,1,0:T(2,128)}, u32[]{:S(2)}) copy-start(f32[2,2,8]{2,1,0:T(2,128)} %copy-done.88) | copy-start | bytes 388
  1132.6 42.6 %copy-start.97 = (f32[2,2,32]{2,1,0:T(2,128)S(1)}, f32[2,2,32]{2,1,0:T(2,128)}, u32[]{:S(2)}) copy-start(f32[2,2,32]{2,1,0:T(2,128)} %copy-done.96) | copy-start | bytes 1540
  1132.6 43.3 %copy-start.111 = (f32[8]{0:T(128)S(1)}, f32[8]{0:T(128)}, u32[]{:S(2)}) copy-start(f32[8]{0:T(128)} %get-tuple-element.237) | copy-start | bytes 100
  1132.6 43.3 %copy-start.114 = (f32[8]{0:T(128)S(1)}, f32[8]{0:T(128)}, u32[]{:S(2)}) copy-start(f32[8]{0:T(128)} %get-tuple-element.238) | copy-start | bytes 100
  1133.5 54.1 %copy-start.40 = (f32[8,2,6,6,40]{4,0,3,2,1:T(8,128)}, f32[8,2,6,6,40]{4,0,3,2,1:T(8,128)S(1)}, u32[]{:S(2)}) copy-start(f32[8,2,6,6,40]{4,0,3,2,1:T(8,128)S(1)} %get-tuple-element.284) | copy-start | bytes 276484
  1133.5 54.1 %copy-start.160 = (f32[40]{0:T(128)S(1)}, f32[40]{0:T(128)}, u32[]{:S(2)}) copy-start(f32[40]{0:T(128)} %get-tuple-element.241) | copy-start | bytes 484
  1133.5 54.1 %copy-start.163 = (f32[40]{0:T(128)S(1)}, f32[40]{0:T(128)}, u32[]{:S(2)}) copy-start(f32[40]{0:T(128)} %get-tuple-element.242) | copy-start | bytes 484
  1134.0 175.5 %copy-start.43 = (f32[8,2,6,6,64]{4,0,3,2,1:T(8,128)}, f32[8,2,6,6,64]{4,0,3,2,1:T(8,128)S(1)}, u32[]{:S(2)}) copy-start(f32[8,2,6,6,64]{4,0,3,2,1:T(8,128)S(1)} %get-tuple-element.286) | copy-start | bytes 442372
  1154.7 21.2 copy-start.106
  1154.8 32.8 %copy-start.151 = (f32[40]{0:T(128)}, f32[40]{0:T(128)S(1)}, u32[]{:S(2)}) copy-start(f32[40]{0:T(128)S(1)} %slice.2236) | copy-start | bytes 484
  1259.9 48.4 %copy-start.87 = (f32[2,2,80]{2,1,0:T(2,128)S(1)}, f32[2,2,80]{2,1,0:T(2,128)}, u32[]{:S(2)}) copy-start(f32[2,2,80]{2,1,0:T(2,128)} %copy-done.86) | copy-start | bytes 3844
  1259.9 48.9 %copy-start.95 = (f32[2,2,32]{2,1,0:T(2,128)S(1)}, f32[2,2,32]{2,1,0:T(2,128)}, u32[]{:S(2)}) copy-start(f32[2,2,32]{2,1,0:T(2,128)} %copy-done.94) | copy-start | bytes 1540
  1261.0 52.1 %copy-start.54 = (bf16[8,2,6,6,32]{4,1,3,2,0:T(2,128)(2,1)S(1)}, bf16[8,2,6,6,32]{4,1,3,2,0:T(2,128)(2,1)}, u32[]{:S(2)}) copy-start(bf16[8,2,6,6,32]{4,1,3,2,0:T(2,128)(2,1)} %param.43) | copy-start | bytes 110596
  1347.1 90.0 %copy-start.47 = (bf16[8,2,6,6,32]{4,0,3,2,1:T(8,128)(2,1)}, bf16[8,2,6,6,32]{4,0,3,2,1:T(8,128)(2,1)S(1)}, u32[]{:S(2)}) copy-start(bf16[8,2,6,6,32]{4,0,3,2,1:T(8,128)(2,1)S(1)} %fusion.671) | copy-start | bytes 110596
  1416.1 136.4 %reduce-scatter.13.cloned.1.call-start = ((), (), s32[]{:S(2)}) async-start(), calls=%async_computation.5 | async-start | bytes 1331200
  1437.2 31.2 %copy-start.76 = (bf16[832,40]{0,1:T(8,128)(2,1)S(1)}, bf16[832,40]{0,1:T(8,128)(2,1)}, u32[]{:S(2)}) copy-start(bf16[832,40]{0,1:T(8,128)(2,1)} %param.29) | copy-start | bytes 199684
  1438.9 29.5 %copy-start.157 = (f32[40]{0:T(128)S(1)}, f32[40]{0:T(128)}, u32[]{:S(2)}) copy-start(f32[40]{0:T(128)} %copy-done.155) | copy-start | bytes 484
  1438.9 29.5 %copy-start.219 = (f32[40]{0:T(128)S(1)}, f32[40]{0:T(128)}, u32[]{:S(2)}) copy-start(f32[40]{0:T(128)} %get-tuple-element.216) | copy-start | bytes 484
  1441.7 28.9 %copy-start.188 = (f32[8]{0:T(128)S(1)}, f32[8]{0:T(128)}, u32[]{:S(2)}) copy-start(f32[8]{0:T(128)} %get-tuple-element.220) | copy-start | bytes 100
  1531.1 741.3 %reduce-scatter.17.cloned.1.call-start = ((), (), s32[]{:S(2)}) async-start(), calls=%async_computation.7 | async-start | bytes 368640
  1578.2 28.5 %copy-start.184 = (f32[32]{0:T(128)S(1)}, f32[32]{0:T(128)}, u32[]{:S(2)}) copy-start(f32[32]{0:T(128)} %get-tuple-element.213) | copy-start | bytes 388
  1578.2 28.4 %copy-start.189 = (f32[32]{0:T(128)S(1)}, f32[32]{0:T(128)}, u32[]{:S(2)}) copy-start(f32[32]{0:T(128)} %get-tuple-element.223) | copy-start | bytes 388
  1614.7 176.6 %copy-start.9 = (bf16[8,4,12,12,32]{4,3,2,1,0:T(8,128)(2,1)}, bf16[8,4,12,12,32]{4,3,2,1,0:T(8,128)(2,1)S(1)}, u32[]{:S(2)}) copy-start(bf16[8,4,12,12,32]{4,3,2,1,0:T(8,128)(2,1)S(1)} %get-tuple-element.168) | copy-start | bytes 884740
  1799.6 112.1 %copy-start.12 = (bf16[8,4,12,12,80]{4,3,2,1,0:T(8,128)(2,1)}, bf16[8,4,12,12,80]{4,3,2,1,0:T(8,128)(2,1)S(1)}, u32[]{:S(2)}) copy-start(bf16[8,4,12,12,80]{4,3,2,1,0:T(8,128)(2,1)S(1)} %multiply_convert_fusion.2) | copy-start | bytes 2211844
  2122.2 52.1 %copy-start.4 = (bf16[8,4,12,12,32]{3,4,2,1,0:T(8,128)(2,1)S(1)}, bf16[8,4,12,12,32]{3,4,2,1,0:T(8,128)(2,1)}, u32[]{:S(2)}) copy-start(bf16[8,4,12,12,32]{3,4,2,1,0:T(8,128)(2,1)} %copy-done.2) | copy-start | bytes 884740
  2122.2 157.2 %reduce-scatter.15.cloned.1.call-start = ((), (), s32[]{:S(2)}) async-start(), calls=%async_computation.6 | async-start | bytes 1843200
  2211.8 23.5 copy-start.8
  2238.4 134.7 %all-reduce.30.cloned.1.call-start = ((), (), s32[]{:S(2)}) async-start(), calls=%async_computation.11 | async-start | bytes 4186112 | tf_op jit(solution)/shard_map/psum | solution.py:441
  2272.2 176.4 %all-reduce.28.cloned.1.call-start = ((), (), s32[]{:S(2)}) async-start(), calls=%async_computation.10 | async-start | bytes 348160 | tf_op jit(solution)/shard_map/psum | solution.py:442
  2295.2 21.9 copy-start.122
  2323.7 15.9 slice-start
  2343.6 252.0 %all-reduce.26.cloned.1.call-start = ((), (), s32[]{:S(2)}) async-start(), calls=%async_computation.9 | async-start | bytes 15728640
  (175 other events, 771.3 us)
Sparse Core Ops, SparseCore 0:
  43.4 311.0 all-gather.2
  645.5 98.6 all-gather.4
  1416.2 28.0 all-reduce.23
  1531.2 21.3 reduce-scatter.12
  2122.3 16.5 reduce-scatter.16
  2238.5 23.8 reduce-scatter.14
  2272.4 100.6 all-reduce.29
  2378.6 70.0 all-reduce.27
  2451.1 144.4 all-reduce.25
where the time goes:
time: 2640 us; the launch traced here: 2620 us
  matrix products  1010 us (38%)
  waiting for transfers between devices  567 us (21%)
  local copies, waits for them, and re-layouts  415 us (16%)
  blocking collectives  404 us (15%)
  other arithmetic  207 us (8%)
    dot_general x116, matrix products, point_back(): jnp.einsum('cfhwo,io->cfhwi', gradient, weight, preferred_element_type=jn...  504 us
    dot_general x116, matrix products, point_apply(): jnp.einsum('cfhwi,io->cfhwo', activation, weight, preferred_element_type=...  325 us
    all_gather x1, waiting for transfers between devices, channel_inputs(): gathered = lax.all_gather(local_part, 'ch', axis=4, tiled=True)  290 us
    dot_general x116, matrix products, point_weight(): jnp.einsum('cfhwi,cfhwo->io', activation, gradient, preferred_element_typ...  176 us
    unnamed x481, local copies, waits for them, and re-layouts  170 us
    unnamed x14, waiting for transfers between devices  154 us
    all_gather x1, blocking collectives, channel_inputs(): gathered = lax.all_gather(local_part, 'ch', axis=4, tiled=True)  110 us
    psum x4, blocking collectives, channel_moments(): totals, voxel_count = lax.psum((first_sums, jnp.sum(masking)), 'batch')  83 us
  transfers between devices with their start and end apart: 9, of which 7 were waited for; matrix products, arithmetic and copies ran while one was open for 13% of the time, Pallas kernels for 0%

commit v1 on v0

v1 whole, which is shorter than its diff:
```python
import jax
import jax.numpy as jnp
import numpy as np
from jax import lax
from jax.experimental import pallas as pl
from jax.experimental.pallas import tpu as pltpu
from jax.sharding import PartitionSpec as P

F32 = jnp.float32
BF16 = jnp.bfloat16
EPSILON = 0.001
BOTH = ("batch", "ch")
DIRECT, NARROW, WIDE, SQUEEZE, SPREAD, PROJECT = 256, 160, 320, 32, 128, 128
REDUCED = NARROW + SQUEEZE
POINT = DIRECT + REDUCED + PROJECT
CONCAT = DIRECT + WIDE + SPREAD + PROJECT
WIDE_COLUMNS = 27 * NARROW
SPREAD_COLUMNS = 27 * SQUEEZE
POINT_WIDTHS = (DIRECT, NARROW, SQUEEZE, PROJECT)
SLOT = {"d": (0, DIRECT), "r": (256, REDUCED), "w": (512, WIDE), "s": (896, SPREAD), "p": (1024, PROJECT)}
SLOTS = 1152
TILE_ROW = {"d": (0, DIRECT), "w": (2, WIDE), "s": (5, SPREAD), "p": (6, PROJECT)}
OUTER = ("d", "w", "s", "p")
CHUNK = 48


class Geometry:
    def __init__(self, frames, height, width, pitch, block):
        self.frames, self.height, self.width, self.pitch = frames, height, width, pitch
        self.block = block
        self.frame_rows = height * pitch
        self.clip_rows = frames * self.frame_rows
        self.padded_rows = (frames + 2) * self.frame_rows
        self.dense = pitch == width


EARLY = Geometry(4, 12, 12, 12, 0)
LATE = Geometry(2, 6, 6, 8, 1)


def nt(a, b):
    return lax.dot_general(a, b, (((1,), (1,)), ((), ())), preferred_element_type=F32)


def nn(a, b):
    return lax.dot_general(a, b, (((1,), (0,)), ((), ())), preferred_element_type=F32)


def tn(a, b):
    return lax.dot_general(a, b, (((0,), (0,)), ((), ())), preferred_element_type=F32)


def call(kernel, outs, ins, scratch=(), flops=0):
    moved = sum(int(np.prod(s)) * jnp.dtype(d).itemsize for s, d in outs)
    moved += sum(int(np.prod(x.shape)) * x.dtype.itemsize for x in ins)
    return pl.pallas_call(
        kernel,
        out_shape=[jax.ShapeDtypeStruct(s, d) for s, d in outs],
        scratch_shapes=[pltpu.VMEM(s, d) for s, d in scratch],
        compiler_params=pltpu.CompilerParams(vmem_limit_bytes=56 * 2**20),
        cost_estimate=pl.CostEstimate(
            flops=int(flops) or 10 * moved, bytes_accessed=moved, transcendentals=0
        ),
    )(*ins)


def each_chunk(rows, body, init=0, chunk=CHUNK):
    return lax.fori_loop(
        0, rows // chunk, lambda i, carry: body(pl.multiple_of(i * chunk, chunk), carry), init
    )


def row(tile, first, width):
    pieces = [
        tile[first + i : first + i + 1, : min(128, width - 128 * i)] for i in range(-(-width // 128))
    ]
    return pieces[0] if len(pieces) == 1 else jnp.concatenate(pieces, axis=1)


def put_row(ref, first, vector):
    width = vector.shape[1]
    for i in range(-(-width // 128)):
        part = vector[:, 128 * i : min(128 * (i + 1), width)]
        ref[first + i : first + i + 1, : part.shape[1]] = part


def affine_of(aff_ref, block, unit):
    start, width = SLOT[unit]
    return (
        aff_ref[2 * block : 2 * block + 1, start : start + width],
        aff_ref[2 * block + 1 : 2 * block + 2, start : start + width],
    )


def fold8(value):
    total = value[0:8]
    for i in range(1, value.shape[0] // 8):
        total = total + value[8 * i : 8 * i + 8]
    return total


def local_moments(y_ref, m_ref, rows, count):
    width = y_ref.shape[1]

    def first(r, acc):
        return acc + fold8(y_ref[pl.ds(r, CHUNK), :] * m_ref[pl.ds(r, CHUNK), 0:1])

    total = each_chunk(rows, first, jnp.zeros((8, width), F32))
    mean = jnp.sum(total, axis=0, keepdims=True) / count

    def second(r, acc):
        centred = (y_ref[pl.ds(r, CHUNK), :] - mean) * m_ref[pl.ds(r, CHUNK), 0:1]
        return acc + fold8(centred * centred)

    spread = each_chunk(rows, second, jnp.zeros((8, width), F32))
    return mean, jnp.sum(spread, axis=0, keepdims=True)


def combine_moments(payload, counts, first, second, size):
    means = payload[:, first : first + size, :]
    total = jnp.sum(counts, axis=0)
    mean = jnp.sum(means * counts, axis=0) / total
    offset = means - mean[None]
    spread = jnp.sum(payload[:, second : second + size, :] + counts * offset * offset, axis=0)
    return mean, lax.rsqrt(spread / total + EPSILON)


def send_tile(pay_ref, tile_ref):
    pay_ref[...] = jnp.broadcast_to(tile_ref[...][None], pay_ref.shape)


def shifted(value, offset):
    if offset == 0:
        return value
    return pltpu.roll(value, (-offset) % value.shape[0], 0)


def cell_index(geo, shape):
    r = lax.broadcasted_iota(jnp.int32, shape, 0).astype(F32)
    line = jnp.floor((r + 0.5) * (1.0 / geo.pitch))
    column = r - geo.pitch * line
    frame = jnp.floor((line + 0.5) * (1.0 / geo.height))
    return line - geo.height * frame, column


def edge_masks(geo, width):
    line, column = cell_index(geo, (geo.clip_rows, width))
    return (
        {e: (line + e > -0.5) & (line + e < geo.height - 0.5) for e in (-1, 1)},
        {e: (column + e > -0.5) & (column + e < geo.width - 0.5) for e in (-1, 1)},
    )


def gather_cells(geo, value, masks, sign, store):
    lines, columns = masks
    for b, dw in enumerate((-1, 0, 1)):
        moved = shifted(value, sign * dw)
        if dw and geo.dense:
            moved = jnp.where(columns[sign * dw], moved, 0.0)
        for a, dh in enumerate((-1, 0, 1)):
            placed = shifted(moved, sign * dh * geo.pitch)
            if dh:
                placed = jnp.where(lines[sign * dh], placed, 0.0)
            store(3 * a + b, placed)


def frame_shift(geo, value, offset):
    if offset == 0:
        return value
    size = geo.frame_rows
    blank = jnp.zeros((size, value.shape[1]), value.dtype)
    if offset > 0:
        return jnp.concatenate([value[size:], blank], axis=0)
    return jnp.concatenate([blank, value[:-size]], axis=0)


def mean_cells(geo, value, masks):
    lines, columns = masks
    total = value
    for e in (-1, 1):
        moved = shifted(value, e)
        total = total + (jnp.where(columns[e], moved, 0.0) if geo.dense else moved)
    again = total
    for e in (-1, 1):
        again = again + jnp.where(lines[e], shifted(total, e * geo.pitch), 0.0)
    return (again + frame_shift(geo, again, 1) + frame_shift(geo, again, -1)) / 27.0


def clear_edges(geo, ref, clip):
    base = clip * geo.padded_rows
    size = geo.frame_rows
    blank = jnp.zeros((size, ref.shape[1]), ref.dtype)
    ref[base : base + size, :] = blank
    ref[base + geo.padded_rows - size : base + geo.padded_rows, :] = blank


def assemble_points(w_ref, scratch, groups):
    for s in range(groups):
        part = w_ref[s].astype(F32)
        at = start = 0
        for width in POINT_WIDTHS:
            own = width // groups
            scratch[start + s * own : start + (s + 1) * own, :] = part[at : at + own, :]
            at += own
            start += width


def split_points(value, scratch, groups):
    size = POINT // groups
    for s in range(groups):
        at = start = 0
        for width in POINT_WIDTHS:
            own = width // groups
            scratch[s * size + at : s * size + at + own, :] = value[
                start + s * own : start + (s + 1) * own, :
            ]
            at += own
            start += width


def prepare_kernel(groups, x_ref, o_ref):
    width = o_ref.shape[2]
    for s in range(groups):
        o_ref[s] = x_ref[:, s * width : (s + 1) * width]


def early_first_kernel(
    groups, x_ref, w_ref, m_ref, mc_ref, a_ref, wt_ref, y_ref, pay_ref, xs, ws, tile
):
    depth, rows = x_ref.shape[1], x_ref.shape[2]
    for s in range(groups):
        xs[s * depth : (s + 1) * depth, :] = x_ref[s].astype(F32)
    for j in range(0, rows, 128):
        size = min(128, rows - j)
        turned = jnp.transpose(xs[:, j : j + size])
        a_ref[j : j + size, :] = (turned * m_ref[j : j + size, 0:1]).astype(BF16)
    assemble_points(w_ref, ws, groups)
    wt_ref[...] = ws[...].astype(BF16)
    y_ref[...] = nt(a_ref[...], wt_ref[DIRECT : DIRECT + REDUCED, :])
    tile[...] = jnp.zeros_like(tile)
    count = jnp.sum(m_ref[...], axis=0, keepdims=True)
    coarse = jnp.sum(mc_ref[...], axis=0, keepdims=True)
    mean, spread = local_moments(y_ref, m_ref, rows, count[:, 0:1])
    put_row(tile, 0, mean)
    put_row(tile, 2, count)
    put_row(tile, 3, coarse)
    put_row(tile, 4, spread)
    send_tile(pay_ref, tile)


def other_points_kernel(geo, clips, a_ref, wt_ref, m_ref, yd_ref, yp_ref, tile):
    yd_ref[...] = nt(a_ref[...], wt_ref[:DIRECT, :])
    projected = nt(a_ref[...], wt_ref[DIRECT + REDUCED :, :])
    masks = edge_masks(geo, PROJECT)
    for c in range(clips):
        rows = slice(c * geo.clip_rows, (c + 1) * geo.clip_rows)
        yp_ref[rows, :] = mean_cells(geo, projected[rows], masks)
    tile[...] = jnp.zeros_like(tile)
    count = jnp.sum(m_ref[...], axis=0, keepdims=True)[:, 0:1]
    for unit, ref in (("d", yd_ref), ("p", yp_ref)):
        mean, spread = local_moments(ref, m_ref, clips * geo.clip_rows, count)
        put_row(tile, TILE_ROW[unit][0], mean)
        put_row(tile, 8 + TILE_ROW[unit][0], spread)


def second_kernel(
    geo, clips, count_row, g_ref, counts_ref, aff_ref, y_ref, m_ref, kw_ref, ks_ref, pd_ref,
    bn_ref, bs_ref, yw_ref, ys_ref, pay_ref, st_ref, us, tile
):
    rows = clips * geo.clip_rows
    counts = counts_ref[:, count_row : count_row + 1, :]
    means, rstds = combine_moments(g_ref[...], counts, 0, 4, 2)
    st_ref[...] = jnp.zeros_like(st_ref)
    st_ref[0:2, :] = means
    st_ref[2:3, :] = jnp.sum(counts, axis=0)
    st_ref[4:6, :] = rstds
    mean, rstd = row(means, 0, REDUCED), row(rstds, 0, REDUCED)
    scale, shift = affine_of(aff_ref, geo.block, "r")

    def activate(r, carry):
        at = pl.ds(r, CHUNK)
        h = scale * ((y_ref[at, :] - mean) * rstd) + shift
        us[at, :] = h * jax.nn.sigmoid(h) * m_ref[at, 0:1]
        return carry

    each_chunk(rows, activate)
    masks = edge_masks(geo, REDUCED)
    size = geo.frame_rows
    for c in range(clips):
        base = c * geo.padded_rows
        clear_edges(geo, bn_ref, c)
        clear_edges(geo, bs_ref, c)

        def store(j, placed):
            at = slice(base + size, base + size + geo.clip_rows)
            bn_ref[at, NARROW * j : NARROW * (j + 1)] = placed[:, :NARROW].astype(BF16)
            bs_ref[at, SQUEEZE * j : SQUEEZE * (j + 1)] = placed[:, NARROW:].astype(BF16)

        gather_cells(geo, us[c * geo.clip_rows : (c + 1) * geo.clip_rows, :], masks, 1, store)
    for c in range(clips):
        base = c * geo.padded_rows
        out = slice(c * geo.clip_rows, (c + 1) * geo.clip_rows)
        for b_ref, k_ref, o_ref in ((bn_ref, kw_ref, yw_ref), (bs_ref, ks_ref, ys_ref)):
            width = b_ref.shape[1]
            total = None
            for t in range(3):
                term = nt(
                    b_ref[base + size * t : base + size * t + geo.clip_rows, :],
                    k_ref[:, width * t : width * (t + 1)],
                )
                total = term if total is None else total + term
            o_ref[out, :] = total
    tile[...] = pd_ref[...]
    own = jnp.sum(m_ref[...], axis=0, keepdims=True)[:, 0:1]
    for unit, ref in (("w", yw_ref), ("s", ys_ref)):
        mean, spread = local_moments(ref, m_ref, rows, own)
        put_row(tile, TILE_ROW[unit][0], mean)
        put_row(tile, 8 + TILE_ROW[unit][0], spread)
    send_tile(pay_ref, tile)


def outer_stats(st, unit):
    first, width = TILE_ROW[unit]
    return row(st, first, width), row(st, 8 + first, width)


def pool_kernel(
    groups, clips, g_ref, counts_ref, aff_ref, yd_ref, yw_ref, ys_ref, yp_ref, m_ref, pool_ref,
    w_ref, mc_ref, a_ref, wt_ref, y_ref, pay_ref, st_ref, high, low, ws, tile
):
    means, rstds = combine_moments(g_ref[...], counts_ref[:, 2:3, :], 0, 8, 8)
    st_ref[0:8, :] = means
    st_ref[8:16, :] = rstds
    st = st_ref[...]
    at_column = 0
    for unit, ref in zip(OUTER, (yd_ref, yw_ref, ys_ref, yp_ref)):
        width = TILE_ROW[unit][1]
        mean, rstd = outer_stats(st, unit)
        scale, shift = affine_of(aff_ref, 0, unit)

        def activate(r, carry):
            at = pl.ds(r, CHUNK)
            h = scale * ((ref[at, :] - mean) * rstd) + shift
            u = h * jax.nn.sigmoid(h) * m_ref[at, 0:1]
            top = u.astype(BF16)
            high[at, :width] = top
            low[at, :width] = (u - top.astype(F32)).astype(BF16)
            return carry

        each_chunk(clips * EARLY.clip_rows, activate)
        for c in range(clips):
            rows = slice(c * EARLY.clip_rows, (c + 1) * EARLY.clip_rows)
            pooled = nn(pool_ref[...], high[rows, :width]) + nn(pool_ref[...], low[rows, :width])
            out = slice(c * LATE.clip_rows, (c + 1) * LATE.clip_rows)
            a_ref[out, at_column : at_column + width] = pooled.astype(BF16)
        at_column += width
    assemble_points(w_ref, ws, groups)
    wt_ref[...] = ws[...].astype(BF16)
    y_ref[...] = nt(a_ref[...], wt_ref[DIRECT : DIRECT + REDUCED, :])
    tile[...] = jnp.zeros_like(tile)
    own = jnp.sum(mc_ref[...], axis=0, keepdims=True)
    mean, spread = local_moments(y_ref, mc_ref, clips * LATE.clip_rows, own[:, 0:1])
    put_row(tile, 0, mean)
    put_row(tile, 4, spread)
    send_tile(pay_ref, tile)


def local_backward(y_ref, dz_of, m_ref, mean, rstd, scale, shift, dh_ref, out_ref, rows):
    width = y_ref.shape[1]

    def body(r, carry):
        at = pl.ds(r, CHUNK)
        masking = m_ref[at, 0:1]
        xhat = (y_ref[at, :] - mean) * rstd
        h = scale * xhat + shift
        gate = jax.nn.sigmoid(h)
        if out_ref is not None:
            out_ref[at, :] = (h * gate * masking).astype(out_ref.dtype)
        dh = dz_of(at) * masking * gate * (1.0 + h * (1.0 - gate))
        dh_ref[at, :] = dh
        return carry[0] + fold8(dh * xhat), carry[1] + fold8(dh)

    blank = jnp.zeros((8, width), F32)
    first, second = each_chunk(rows, body, (blank, blank))
    return jnp.sum(first, axis=0, keepdims=True), jnp.sum(second, axis=0, keepdims=True)


def late_outputs_kernel(
    clips, g_ref, counts_ref, aff_ref, yd_ref, yw_ref, ys_ref, yp_ref, mc_ref,
    ud_ref, uw_ref, us_ref, up_ref,
    od_ref, ow_ref, os_ref, op_ref, dd_ref, dw_ref, ds_ref, dp_ref, pay_ref, st_ref, tile
):
    means, rstds = combine_moments(g_ref[...], counts_ref[:, 3:4, :], 0, 8, 8)
    st_ref[0:8, :] = means
    st_ref[8:16, :] = rstds
    st = st_ref[...]
    tile[...] = jnp.zeros_like(tile)
    for unit, y_ref, up, o_ref, dh_ref in zip(
        OUTER,
        (yd_ref, yw_ref, ys_ref, yp_ref),
        (ud_ref, uw_ref, us_ref, up_ref),
        (od_ref, ow_ref, os_ref, op_ref),
        (dd_ref, dw_ref, ds_ref, dp_ref),
    ):
        mean, rstd = outer_stats(st, unit)
        scale, shift = affine_of(aff_ref, 1, unit)
        sums = local_backward(
            y_ref, lambda at: up[at, :].astype(F32), m_ref=mc_ref, mean=mean, rstd=rstd,
            scale=scale, shift=shift, dh_ref=dh_ref, out_ref=o_ref, rows=clips * LATE.clip_rows,
        )
        put_row(tile, TILE_ROW[unit][0], sums[0])
        put_row(tile, 8 + TILE_ROW[unit][0], sums[1])
    send_tile(pay_ref, tile)


def finish_rows(dh, y, masking, mean, rstd, scale, scale_sum, shift_sum, count):
    xhat = (y - mean) * rstd
    return scale * rstd * (dh - (shift_sum + xhat * scale_sum) / count) * masking


def inner_backward_kernel(
    geo, clips, g_ref, st_ref, str_ref, aff_ref, dw_ref, ds_ref, yw_ref, ys_ref, yr_ref, kw_ref,
    ks_ref, m_ref, gw_ref, gs_ref, dh_ref, pay_ref, sums_ref, pad_w, pad_s, kt_w, kt_s, dz, tile
):
    rows = clips * geo.clip_rows
    size = geo.frame_rows
    sums_ref[...] = jnp.sum(g_ref[...], axis=0)
    sums, st, st_r = sums_ref[...], st_ref[...], str_ref[...]
    count = st_r[2:3, 0:1]
    for unit, d_ref, y_ref, o_ref, pad in (
        ("w", dw_ref, yw_ref, gw_ref, pad_w),
        ("s", ds_ref, ys_ref, gs_ref, pad_s),
    ):
        first, width = TILE_ROW[unit]
        mean, rstd = outer_stats(st, unit)
        scale, _ = affine_of(aff_ref, geo.block, unit)
        scale_sum, shift_sum = row(sums, first, width), row(sums, 8 + first, width)

        def finish(r, carry):
            at = pl.ds(r, CHUNK)
            dy = finish_rows(
                d_ref[at, :], y_ref[at, :], m_ref[at, 0:1], mean, rstd, scale, scale_sum,
                shift_sum, count,
            )
            o_ref[at, :] = dy.astype(BF16)
            return carry

        each_chunk(rows, finish)
        masks = edge_masks(geo, width)
        for c in range(clips):
            base = c * geo.padded_rows
            clear_edges(geo, pad, c)

            def store(j, placed):
                at = slice(base + size, base + size + geo.clip_rows)
                pad[at, width * j : width * (j + 1)] = placed.astype(BF16)

            value = o_ref[c * geo.clip_rows : (c + 1) * geo.clip_rows, :].astype(F32)
            gather_cells(geo, value, masks, -1, store)
    for k_ref, kt, width, depth in ((kw_ref, kt_w, WIDE, NARROW), (ks_ref, kt_s, SPREAD, SQUEEZE)):
        for t in range(3):
            for j in range(9):
                at = (9 * t + j) * depth
                kt[t, width * j : width * (j + 1), :] = k_ref[:, at : at + depth]
    for pad, kt, depth, start in ((pad_w, kt_w, NARROW, 0), (pad_s, kt_s, SQUEEZE, NARROW)):
        for c in range(clips):
            base = c * geo.padded_rows
            total = None
            for t in range(3):
                at = base + size * (2 - t)
                term = nn(pad[at : at + geo.clip_rows, :], kt[t])
                total = term if total is None else total + term
            dz[c * geo.clip_rows : (c + 1) * geo.clip_rows, start : start + depth] = total
    scale, shift = affine_of(aff_ref, geo.block, "r")
    first, second = local_backward(
        yr_ref, lambda at: dz[at, :], m_ref=m_ref, mean=row(st_r, 0, REDUCED),
        rstd=row(st_r, 4, REDUCED), scale=scale, shift=shift, dh_ref=dh_ref, out_ref=None, rows=rows,
    )
    tile[...] = jnp.zeros_like(tile)
    put_row(tile, 0, first)
    put_row(tile, 4, second)
    send_tile(pay_ref, tile)


def kernel_grad_kernel(geo, clips, gw_ref, gs_ref, bn_ref, bs_ref, ow_ref, os_ref):
    size = geo.frame_rows
    for g_ref, b_ref, o_ref in ((gw_ref, bn_ref, ow_ref), (gs_ref, bs_ref, os_ref)):
        width = b_ref.shape[1]
        for t in range(3):
            total = None
            for c in range(clips):
                at = c * geo.padded_rows + size * t
                term = tn(
                    g_ref[c * geo.clip_rows : (c + 1) * geo.clip_rows, :],
                    b_ref[at : at + geo.clip_rows, :],
                )
                total = term if total is None else total + term
            o_ref[:, width * t : width * (t + 1)] = total.astype(BF16)


def point_gradients(
    geo, clips, g_ref, sums_ref, st_ref, str_ref, aff_ref, dr_ref, dd_ref, dp_ref, yr_ref, yd_ref,
    yp_ref, m_ref, gy_ref, sumr_ref, held
):
    rows = clips * geo.clip_rows
    sumr_ref[...] = jnp.sum(g_ref[...], axis=0)
    sums, sums_r, st, st_r = sums_ref[...], sumr_ref[...], st_ref[...], str_ref[...]
    count = st_r[2:3, 0:1]
    scale_d, _ = affine_of(aff_ref, geo.block, "d")
    scale_r, _ = affine_of(aff_ref, geo.block, "r")
    scale_p, _ = affine_of(aff_ref, geo.block, "p")
    mean_d, rstd_d = outer_stats(st, "d")
    mean_p, rstd_p = outer_stats(st, "p")
    mean_r, rstd_r = row(st_r, 0, REDUCED), row(st_r, 4, REDUCED)

    def pair(unit):
        first, width = TILE_ROW[unit]
        return row(sums, first, width), row(sums, 8 + first, width)

    pair_d, pair_p = pair("d"), pair("p")
    pair_r = (row(sums_r, 0, REDUCED), row(sums_r, 4, REDUCED))

    def finish(r, carry):
        at = pl.ds(r, CHUNK)
        masking = m_ref[at, 0:1]
        gy_ref[at, :DIRECT] = finish_rows(
            dd_ref[at, :], yd_ref[at, :], masking, mean_d, rstd_d, scale_d, *pair_d, count
        ).astype(BF16)
        gy_ref[at, DIRECT : DIRECT + REDUCED] = finish_rows(
            dr_ref[at, :], yr_ref[at, :], masking, mean_r, rstd_r, scale_r, *pair_r, count
        ).astype(BF16)
        held[at, :] = finish_rows(
            dp_ref[at, :], yp_ref[at, :], masking, mean_p, rstd_p, scale_p, *pair_p, count
        )
        return carry

    each_chunk(rows, finish)
    masks = edge_masks(geo, PROJECT)
    for c in range(clips):
        at = slice(c * geo.clip_rows, (c + 1) * geo.clip_rows)
        gy_ref[at, DIRECT + REDUCED :] = mean_cells(geo, held[at, :], masks).astype(BF16)


def late_input_kernel(
    clips, g_ref, sums_ref, st_ref, str_ref, aff_ref, dr_ref, dd_ref, dp_ref, yr_ref, yd_ref, yp_ref,
    mc_ref, wt_ref, spread_ref, est_ref, ed_ref, ew_ref, es_ref, ep_ref, m_ref,
    gy_ref, hd_ref, hw_ref, hs_ref, hp_ref, pay_ref, sumr_ref, held, grad, wide, tile
):
    point_gradients(
        LATE, clips, g_ref, sums_ref, st_ref, str_ref, aff_ref, dr_ref, dd_ref, dp_ref, yr_ref,
        yd_ref, yp_ref, mc_ref, gy_ref, sumr_ref, held,
    )
    grad[...] = nn(gy_ref[...], wt_ref[...]).astype(BF16)
    st = est_ref[...]
    tile[...] = jnp.zeros_like(tile)
    column = 0
    for unit, y_ref, dh_ref in zip(
        OUTER, (ed_ref, ew_ref, es_ref, ep_ref), (hd_ref, hw_ref, hs_ref, hp_ref)
    ):
        width = TILE_ROW[unit][1]
        for c in range(clips):
            wide[c * EARLY.clip_rows : (c + 1) * EARLY.clip_rows, :width] = nn(
                spread_ref[...],
                grad[c * LATE.clip_rows : (c + 1) * LATE.clip_rows, column : column + width],
            )
        column += width
        mean, rstd = outer_stats(st, unit)
        scale, shift = affine_of(aff_ref, 0, unit)
        sums = local_backward(
            y_ref, lambda at: wide[at, :width], m_ref=m_ref, mean=mean, rstd=rstd, scale=scale,
            shift=shift, dh_ref=dh_ref, out_ref=None, rows=clips * EARLY.clip_rows,
        )
        put_row(tile, TILE_ROW[unit][0], sums[0])
        put_row(tile, 8 + TILE_ROW[unit][0], sums[1])
    send_tile(pay_ref, tile)


def early_input_kernel(
    groups, clips, g_ref, sums_ref, st_ref, str_ref, aff_ref, dr_ref, dd_ref, dp_ref, yr_ref, yd_ref,
    yp_ref, m_ref, wt_ref, gy_ref, x_ref, sumr_ref, held
):
    point_gradients(
        EARLY, clips, g_ref, sums_ref, st_ref, str_ref, aff_ref, dr_ref, dd_ref, dp_ref, yr_ref,
        yd_ref, yp_ref, m_ref, gy_ref, sumr_ref, held,
    )
    depth = x_ref.shape[1]
    rows = clips * EARLY.clip_rows
    for j in range(0, rows, 128):
        size = min(128, rows - j)
        grad = nn(gy_ref[j : j + size, :], wt_ref[...]) * m_ref[j : j + size, 0:1]
        turned = jnp.transpose(grad)
        for s in range(groups):
            x_ref[s, :, j : j + size] = turned[s * depth : (s + 1) * depth, :].astype(BF16)


def point_grad_kernel(groups, gy_ref, a_ref, o_ref, scratch):
    split_points(tn(gy_ref[...], a_ref[...]), scratch, groups)
    o_ref[...] = scratch[...].astype(BF16)


def feature_kernel(groups, x_ref, o_ref):
    width = x_ref.shape[2]
    for s in range(groups):
        o_ref[:, s * width : (s + 1) * width] = x_ref[s].astype(F32)


def pool_matrix():
    matrix = np.zeros((LATE.clip_rows, EARLY.clip_rows), np.float32)
    for f in range(EARLY.frames):
        for h in range(EARLY.height):
            for w in range(EARLY.width):
                cell = (f // 2) * LATE.frame_rows + (h // 2) * LATE.pitch + w // 2
                matrix[cell, (f * EARLY.height + h) * EARLY.width + w] = 0.125
    return matrix


def pad_late(field):
    padded = jnp.pad(field, ((0, 0), (0, 0), (0, 0), (0, LATE.pitch - LATE.width), (0, 0)))
    return padded.reshape(-1, field.shape[4])


def shards(
    clip_features, visible, direct_early, narrow_early, squeeze_early, project_early, direct_late,
    narrow_late, squeeze_late, project_late, wide_kernels, spread_kernels, direct_norm, narrow_norm,
    wide_norm, squeeze_norm, spread_norm, project_norm, upstream_direct, upstream_wide,
    upstream_spread, upstream_project,
):
    groups = lax.axis_size("ch")
    devices = groups * lax.axis_size("batch")
    me = lax.axis_index("ch")
    held_clips = visible.shape[0]
    clips = held_clips // groups
    rows = clips * EARLY.clip_rows
    late_rows = clips * LATE.clip_rows
    depth = clip_features.shape[0]
    features = depth * groups

    def exchange(payload):
        return lax.all_to_all(payload, BOTH, 0, 0)

    (pieces,) = call(
        lambda *refs: prepare_kernel(groups, *refs), [((groups, depth, rows), BF16)], [clip_features]
    )
    arrived = lax.all_to_all(pieces, "ch", 0, 0)
    own_visible = lax.dynamic_slice_in_dim(visible, me * clips, clips, 0)
    fine = own_visible.astype(F32).reshape(rows, 1)
    mask = jnp.broadcast_to(fine, (rows, 128))
    cells = own_visible.reshape(clips, 2, 2, 6, 2, 6, 2).max(axis=(2, 4, 6)).astype(F32)
    coarse = jnp.broadcast_to(pad_late(cells[..., None]), (late_rows, 128))

    def gathered(value):
        return lax.all_gather(value, "ch", axis=0, tiled=True)

    def stacked_points(parts):
        local = jnp.concatenate([part.T for part in parts], axis=0)
        return lax.all_gather(local, "ch", axis=0)

    early_points = stacked_points((direct_early, narrow_early, squeeze_early, project_early))
    norms = (direct_norm, narrow_norm, squeeze_norm, wide_norm, spread_norm, project_norm)
    joined = lax.all_gather(jnp.concatenate(norms, axis=2), "ch", axis=0).astype(F32)
    units, at = [], 0
    for norm in norms:
        width = norm.shape[2]
        piece = jnp.moveaxis(joined[..., at : at + width], 0, 2)
        units.append(piece.reshape(4, groups * width))
        at += width
    affine = jnp.concatenate(
        [
            units[0], units[1], units[2], jnp.zeros((4, 64), F32), units[3], jnp.zeros((4, 64), F32),
            units[4], units[5],
        ],
        axis=1,
    )
    wide_rows = wide_kernels.reshape(2, -1, WIDE_COLUMNS)
    spread_rows = jnp.transpose(
        spread_kernels.reshape(2, SPREAD_COLUMNS, spread_kernels.shape[3]), (0, 2, 1)
    )
    kw_early = gathered(wide_rows[0])
    ks_early = gathered(spread_rows[0])
    late_points = stacked_points((direct_late, narrow_late, squeeze_late, project_late))
    kw_late = gathered(wide_rows[1])
    ks_late = gathered(spread_rows[1])

    upstream = (upstream_direct, upstream_wide, upstream_spread, upstream_project)
    up_joined = jnp.concatenate(upstream, axis=4)
    up_parts = up_joined.reshape((groups, clips) + up_joined.shape[1:])
    up_arrived = lax.all_to_all(up_parts, "ch", 0, 0)
    ups, at = [], 0
    for part in upstream:
        width = part.shape[4]
        piece = jnp.moveaxis(up_arrived[..., at : at + width], 0, 4)
        ups.append(pad_late(piece.reshape(piece.shape[:4] + (groups * width,))))
        at += width

    pool = jnp.asarray(pool_matrix(), BF16)
    spread_back = jnp.asarray(pool_matrix().T, BF16)

    act, wt, yr, pay = call(
        lambda *refs: early_first_kernel(groups, *refs),
        [
            ((rows, features), BF16), ((POINT, features), BF16), ((rows, REDUCED), F32),
            ((devices, 8, 128), F32),
        ],
        [arrived, early_points, mask, coarse],
        [((features, rows), F32), ((POINT, features), F32), ((8, 128), F32)],
    )
    counts = exchange(pay)
    yd, yp, tile = call(
        lambda *refs: other_points_kernel(EARLY, clips, *refs),
        [((rows, DIRECT), F32), ((rows, PROJECT), F32), ((16, 128), F32)],
        [act, wt, mask],
    )

    def second(geo, count_row, g, y, masking, kw, ks, other):
        own = clips * geo.clip_rows
        padded = clips * geo.padded_rows
        return call(
            lambda *refs: second_kernel(geo, clips, count_row, *refs),
            [
                ((padded, 9 * NARROW), BF16), ((padded, 9 * SQUEEZE), BF16), ((own, WIDE), F32),
                ((own, SPREAD), F32), ((devices, 16, 128), F32), ((8, 128), F32),
            ],
            [g, counts, affine, y, masking, kw, ks, other],
            [((own, REDUCED), F32), ((16, 128), F32)],
        )

    bn, bs, yw, ys, pay, st_r = second(EARLY, 2, counts, yr, mask, kw_early, ks_early, tile)
    g = exchange(pay)
    late_act, late_wt, lyr, pay, st = call(
        lambda *refs: pool_kernel(groups, clips, *refs),
        [
            ((late_rows, CONCAT), BF16), ((POINT, CONCAT), BF16), ((late_rows, REDUCED), F32),
            ((devices, 8, 128), F32), ((16, 128), F32),
        ],
        [g, counts, affine, yd, yw, ys, yp, mask, pool, late_points, coarse],
        [((rows, 384), BF16), ((rows, 384), BF16), ((POINT, CONCAT), F32), ((8, 128), F32)],
    )
    g = exchange(pay)
    lyd, lyp, tile = call(
        lambda *refs: other_points_kernel(LATE, clips, *refs),
        [((late_rows, DIRECT), F32), ((late_rows, PROJECT), F32), ((16, 128), F32)],
        [late_act, late_wt, coarse],
    )
    lbn, lbs, lyw, lys, pay, lst_r = second(LATE, 3, g, lyr, coarse, kw_late, ks_late, tile)
    g = exchange(pay)
    widths = [TILE_ROW[unit][1] for unit in OUTER]
    res = call(
        lambda *refs: late_outputs_kernel(clips, *refs),
        [((late_rows, w), BF16) for w in widths]
        + [((late_rows, w), F32) for w in widths]
        + [((devices, 16, 128), F32), ((16, 128), F32)],
        [g, counts, affine, lyd, lyw, lys, lyp, coarse] + ups,
        [((16, 128), F32)],
    )
    outs, (hd, hw, hs, hp), (pay, lst) = res[:4], res[4:8], res[8:]
    g = exchange(pay)

    def inner(geo, g, st, st_r, hw, hs, yw, ys, yr, kw, ks, masking):
        own = clips * geo.clip_rows
        padded = clips * geo.padded_rows
        return call(
            lambda *refs: inner_backward_kernel(geo, clips, *refs),
            [
                ((own, WIDE), BF16), ((own, SPREAD), BF16), ((own, REDUCED), F32),
                ((devices, 8, 128), F32), ((16, 128), F32),
            ],
            [g, st, st_r, affine, hw, hs, yw, ys, yr, kw, ks, masking],
            [
                ((padded, 9 * WIDE), BF16), ((padded, 9 * SPREAD), BF16),
                ((3, 9 * WIDE, NARROW), BF16), ((3, 9 * SPREAD, SQUEEZE), BF16),
                ((own, REDUCED), F32), ((8, 128), F32),
            ],
        )

    def kernel_grads(geo, gw, gs, bn, bs):
        return call(
            lambda *refs: kernel_grad_kernel(geo, clips, *refs),
            [((WIDE, WIDE_COLUMNS), BF16), ((SPREAD, SPREAD_COLUMNS), BF16)],
            [gw, gs, bn, bs],
        )

    def point_grads(gy, act):
        return call(
            lambda *refs: point_grad_kernel(groups, *refs),
            [((POINT, act.shape[1]), BF16)],
            [gy, act],
            [((POINT, act.shape[1]), F32)],
        )[0]

    def reduced(value):
        part = lax.psum_scatter(value, "ch", scatter_dimension=0, tiled=True)
        return lax.psum(part, "batch")

    gw, gs, hr, pay, late_sums = inner(
        LATE, g, lst, lst_r, hw, hs, lyw, lys, lyr, kw_late, ks_late, coarse
    )
    g = exchange(pay)
    late_kw_grad, late_ks_grad = kernel_grads(LATE, gw, gs, lbn, lbs)
    gy, ed, ew, es, ep, pay, late_sums_r = call(
        lambda *refs: late_input_kernel(clips, *refs),
        [((late_rows, POINT), BF16)]
        + [((rows, w), F32) for w in widths]
        + [((devices, 16, 128), F32), ((8, 128), F32)],
        [g, late_sums, lst, lst_r, affine, hr, hd, hp, lyr, lyd, lyp, coarse, late_wt, spread_back,
         st, yd, yw, ys, yp, mask],
        [((late_rows, PROJECT), F32), ((late_rows, CONCAT), BF16), ((rows, WIDE), F32), ((16, 128), F32)],
    )
    g = exchange(pay)
    late_point_grad = point_grads(gy, late_act)
    gw, gs, hr, pay, sums = inner(EARLY, g, st, st_r, ew, es, yw, ys, yr, kw_early, ks_early, mask)
    g = exchange(pay)
    kw_grad, ks_grad = kernel_grads(EARLY, gw, gs, bn, bs)
    gy, x_grad, sums_r = call(
        lambda *refs: early_input_kernel(groups, clips, *refs),
        [((rows, POINT), BF16), ((groups, depth, rows), BF16), ((8, 128), F32)],
        [g, sums, st, st_r, affine, hr, ed, ep, yr, yd, yp, mask, wt],
        [((rows, PROJECT), F32)],
    )
    x_arrived = lax.all_to_all(x_grad, "ch", 0, 0)
    point_grad = point_grads(gy, act)
    (feature_grad,) = call(
        lambda *refs: feature_kernel(groups, *refs),
        [((depth, groups * rows), F32)],
        [x_arrived],
    )

    out_parts = []
    for o in outs:
        cells = o.reshape(clips, LATE.frames, LATE.height, LATE.pitch, -1)[:, :, :, : LATE.width]
        out_parts.append(cells.reshape(cells.shape[:4] + (groups, -1)))
    out_joined = jnp.moveaxis(jnp.concatenate(out_parts, axis=5), 4, 0)
    out_arrived = lax.all_to_all(out_joined, "ch", 0, 0)
    out_arrived = out_arrived.reshape((held_clips,) + out_arrived.shape[2:])
    outputs, at = [], 0
    for part in upstream:
        outputs.append(out_arrived[..., at : at + part.shape[4]])
        at += part.shape[4]

    def point_outputs(value, parts):
        value = reduced(value).astype(F32)
        result, at = [], 0
        for part in parts:
            width = part.shape[1]
            result.append(value[at : at + width].T)
            at += width
        return result

    early_grads = point_outputs(
        point_grad, (direct_early, narrow_early, squeeze_early, project_early)
    )
    late_grads = point_outputs(late_point_grad, (direct_late, narrow_late, squeeze_late, project_late))
    wide_grad = jnp.stack([reduced(kw_grad), reduced(late_kw_grad)]).astype(F32)
    wide_grad = wide_grad.reshape(wide_kernels.shape)
    spread_grad = jnp.stack([reduced(ks_grad), reduced(late_ks_grad)]).astype(F32)
    spread_grad = jnp.transpose(spread_grad, (0, 2, 1)).reshape(spread_kernels.shape)

    def outer_pair(tile, unit):
        first, width = TILE_ROW[unit]
        return [
            jnp.stack([tile[k : k + 3].reshape(-1)[:width] for k in (base, base + 8)])
            for base in (first,)
        ][0]

    def inner_pair(tile, low, high):
        return jnp.stack([tile[k : k + 2].reshape(-1)[low:high] for k in (0, 4)])

    def own_part(early_pair, late_pair):
        both = jnp.stack([early_pair, late_pair])
        size = both.shape[2] // groups
        return lax.dynamic_slice_in_dim(both, me * size, size, 2)

    norm_grads = [
        own_part(outer_pair(sums, "d"), outer_pair(late_sums, "d")),
        own_part(inner_pair(sums_r, 0, NARROW), inner_pair(late_sums_r, 0, NARROW)),
        own_part(outer_pair(sums, "w"), outer_pair(late_sums, "w")),
        own_part(inner_pair(sums_r, NARROW, REDUCED), inner_pair(late_sums_r, NARROW, REDUCED)),
        own_part(outer_pair(sums, "s"), outer_pair(late_sums, "s")),
        own_part(outer_pair(sums, "p"), outer_pair(late_sums, "p")),
    ]
    return tuple(outputs) + (feature_grad,) + tuple(early_grads) + tuple(late_grads) + (
        wide_grad, spread_grad,
    ) + tuple(norm_grads)


def solution(mesh):
    columns = P(None, "ch")
    norm = P(None, None, "ch")
    clips = P("batch", None, None, None, "ch")
    kernels = P(None, None, None, "ch")
    return jax.shard_map(
        shards,
        mesh=mesh,
        in_specs=(P("ch", "batch"), P("batch", None, None, None)) + (columns,) * 9 + (kernels,)
        + (norm,) * 6 + (clips,) * 4,
        out_specs=(clips,) * 4 + (P("ch", "batch"),) + (columns,) * 9 + (kernels,) + (norm,) * 6,
        check_vma=False,
    )
```

time: 2640 us -> 702 us (0.27)
  matrix products: 1010 us -> 0 us
  local copies, waits for them, and re-layouts: 415 us -> 50.9 us
  blocking collectives: 404 us -> 94 us
  waiting for transfers between devices: 567 us -> 327 us
  other arithmetic: 207 us -> 14 us
  Pallas kernels: 0 us -> 153 us
  starting transfers between devices: 1.05 us -> 38.6 us
    dot_general x348 -> x0, matrix products: 1010 us -> none  [the longest x116 504 us: point_back(): jnp.einsum('cfhwo,io->cfhwi', gradient, weight, preferred_element_type=jn...]
    all_gather x2, waiting for transfers between devices: 346 us -> 0.02 us  [gathered(): return lax.all_gather(value, 'ch', axis=0, tiled=True)]
    psum x12 -> x0, blocking collectives: 232 us -> none  [the longest x4 83 us: channel_moments(): totals, voxel_count = lax.psum((first_sums, jnp.sum(masking)), 'batch')]
    unnamed x481 -> x94, local copies, waits for them, and re-layouts: 170 us -> 7.22 us
    pallas_call x0 -> x17, Pallas kernels: none -> 153 us  [call(): pl.pallas_call(kernel, out_shape=[jax.ShapeDtypeStruct(s, d) for s, d in...]
    unnamed x14 -> x10, waiting for transfers between devices: 154 us -> 1.14 us
    psum x2, waiting for transfers between devices: 66.3 us -> 197 us  [reduced(): return lax.psum(part, 'batch')]
    reduce_scatter x0 -> x6, waiting for transfers between devices: none -> 98.5 us  [reduced(): part = lax.psum_scatter(value, 'ch', scatter_dimension=0, tiled=True)]
  transfers between devices with their start and end apart: 9 -> 20, of which waited for: 7 -> 11; matrix products, arithmetic and copies ran while one was open for 13% -> 5% of each run, Pallas kernels for 0% -> 18%
where the time goes in v1:
time: 702 us; the launch traced here: 693 us
  waiting for transfers between devices  327 us (47%)
  Pallas kernels  153 us (22%)
  blocking collectives  94 us (13%)
  local copies, waits for them, and re-layouts  50.9 us (7%)
  starting transfers between devices  38.6 us (5%)
  between operations  15.4 us (2%)
  other arithmetic  14 us (2%)
    psum x2, waiting for transfers between devices, reduced(): return lax.psum(part, 'batch')  197 us
    pallas_call x17, Pallas kernels, call(): pl.pallas_call(kernel, out_shape=[jax.ShapeDtypeStruct(s, d) for s, d in...  153 us
    reduce_scatter x6, waiting for transfers between devices, reduced(): part = lax.psum_scatter(value, 'ch', scatter_dimension=0, tiled=True)  98.5 us
    all_gather x1, blocking collectives, shards(): lax.all_gather(jnp.concatenate(norms, axis=2), 'ch', axis=0).astype(F32)  30.8 us
    all_to_all x6, waiting for transfers between devices, exchange(): return lax.all_to_all(payload, BOTH, 0, 0)  26.3 us
    all_to_all x2, blocking collectives, exchange(): return lax.all_to_all(payload, BOTH, 0, 0)  25.4 us
    all_to_all x6, starting transfers between devices, exchange(): return lax.all_to_all(payload, BOTH, 0, 0)  23 us
    all_gather x2, blocking collectives, stacked_points(): return lax.all_gather(local, 'ch', axis=0)  22 us
  transfers between devices with their start and end apart: 20, of which 11 were waited for; matrix products, arithmetic and copies ran while one was open for 5% of the time, Pallas kernels for 18%

profile of v1, /device:TPU:0, one launch (start us, length us, event | category | flops | bytes accessed | tf_op | source)
XLA Modules:
  0.0 692.9 jit_solution(10165442990774339252)
XLA Ops:
  7.2 15.9 %slice_reduce_fusion = (bf16[345600]{0:T(1024)(128)(2,1)S(1)}, bf16[345600]{0:T(1024)(128)(2,1)S(1)}) fusion(bf16[2,345600]{1,0:T(2,128)(2,1)} %param.34), kind=kLoop, calls=%fused_computation.1 | loop fusion | bytes 2764800 | tf_op jit(solution)/shard_map/slice | solution.py:681
  23.2 1.9 squeeze.12
  25.1 1.9 squeeze.14
  27.0 2.4 shard_map.391
  29.5 4.4 all-to-all-start
  34.1 30.8 %all-gather.1 = bf16[8,2,256]{2,1,0:T(2,128)(2,1)S(1)} all-gather(bf16[2,2,256]{2,1,0:T(2,128)(2,1)S(1)} %concatenate.20), channel_id=3, replica_groups=mesh['batch'=8,'ch'=4] {'ch'}, dimensions={0}, use_global_device_ids=true | all-gather | bytes 10240 | tf_op jit(solution)/shard_map/all_gather | solution.py:660
  65.1 0.8 fusion.6
  68.4 8.9 %all-gather = bf16[576,528]{1,0:T(8,128)(2,1)} all-gather(bf16[144,528]{1,0:T(8,128)(2,1)S(1)} %pad_maximum_fusion.2), channel_id=2, replica_groups=mesh['batch'=8,'ch'=4] {'ch'}, dimensions={0}, use_global_device_ids=true | all-gather | bytes 760320 | tf_op jit(solution)/shard_map/all_gather | solution.py:656
  77.3 1.2 broadcast_in_dim.16.refs_2_.refs_4_.refs_7_.refs_19_.refs_11_
  78.5 0.7 broadcast_in_dim.18.refs_3_.refs_10_.refs_2_.refs_4_.refs_7_.refs_11_
  79.2 8.5 %shard_map.392 = (bf16[1152,528]{1,0:T(8,128)(2,1)}, bf16[576,528]{1,0:T(8,128)(2,1)}, f32[1152,192]{1,0:T(8,128)}, f32[32,8,128]{2,1,0:T(8,128)}) custom-call(bf16[4,132,1152]{2,1,0:T(8,128)(2,1)} %copy-done.1, bf16[4,144,528]{2,1,0:T(8,128)(2,1)} %bitcast.156, f32[1152,128]{1,0:T(8,128)} %broadcast_in_dim.16.refs_2_.refs_4_.refs_7_.refs_19_.refs_11_, ...), custom_call_target="tpu_custom_call" | custom-call | flops 53534720 | bytes 5353472 | tf_op jit(solution)/shard_map/pallas_call | solution.py:56
  87.7 5.6 all-to-all-start.1
  93.4 7.0 %all-gather.2 = bf16[1,128,864]{2,1,0:T(8,128)(2,1)} all-gather(bf16[1,32,864]{2,1,0:T(8,128)(2,1)S(1)} %get-tuple-element.242), channel_id=4, replica_groups=mesh['batch'=8,'ch'=4] {'ch'}, dimensions={1}, use_global_device_ids=true | all-gather | bytes 276480 | tf_op jit(solution)/shard_map/all_gather | solution.py:652
  100.4 12.3 %shard_map.393 = (f32[1152,256]{1,0:T(8,128)}, f32[1152,128]{1,0:T(8,128)}, f32[16,128]{1,0:T(8,128)}) custom-call(bf16[1152,528]{1,0:T(8,128)(2,1)} %get-tuple-element.84.refs_0_.refs_1_, bf16[576,528]{1,0:T(8,128)(2,1)} %get-tuple-element.85.refs_1_.refs_12_, f32[1152,128]{1,0:T(8,128)} %broadcast_in_dim.16.refs_2_.refs_4_.refs_7_.refs_19_.refs_11_), custom_call_target="tpu_custom_call" | custom-call | flops 41922560 | bytes 4192256 | tf_op jit(solution)/shard_map/pallas_call | solution.py:56
  113.4 23.3 %shard_map.394 = (bf16[1728,1440]{1,0:T(8,128)(2,1)}, bf16[1728,288]{1,0:T(8,128)(2,1)}, f32[1152,320]{1,0:T(8,128)}, f32[1152,128]{1,0:T(8,128)}, f32[32,16,128]{2,1,0:T(8,128)}, /*index=5*/f32[8,128]{1,0:T(8,128)}) custom-call(f32[32,8,128]{2,1,0:T(8,128)} %copy-done.2, f32[32,8,128]{2,1,0:T(8,128)} %copy-done.2, ...), custom_call_target="tpu_custom_call" | custom-call | flops 130519040 | bytes 13051904 | tf_op jit(solution)/shard_map/pallas_call | solution.py:56
  136.7 5.2 all-to-all-start.2
  141.9 13.1 %all-gather.3 = bf16[576,832]{1,0:T(8,128)(2,1)} all-gather(bf16[144,832]{1,0:T(8,128)(2,1)S(1)} %pad_maximum_fusion.1), channel_id=5, replica_groups=mesh['batch'=8,'ch'=4] {'ch'}, dimensions={0}, use_global_device_ids=true | all-gather | bytes 1198080 | tf_op jit(solution)/shard_map/all_gather | solution.py:656
  155.7 14.4 %shard_map.395 = (bf16[192,832]{1,0:T(8,128)(2,1)}, bf16[576,832]{1,0:T(8,128)(2,1)}, f32[192,192]{1,0:T(8,128)}, f32[32,8,128]{2,1,0:T(8,128)}, f32[16,128]{1,0:T(8,128)}) custom-call(f32[32,16,128]{2,1,0:T(8,128)} %copy-done.6, f32[32,8,128]{2,1,0:T(8,128)} %copy-done.2, f32[4,1152]{1,0:T(4,128)} %concatenate.21.refs_2_.refs_3_.refs_4_, ...), custom_call_target="tpu_custom_call" | custom-call | flops 75673600 | bytes 7567360 | tf_op jit(solution)/shard_map/pallas_call | solution.py:56
  170.1 4.5 all-to-all-start.3
  174.6 1.8 pad_maximum_fusion
  176.4 6.4 all-to-all-done.3.refs_0_
  182.8 3.5 all-to-all-start.5
  186.2 8.9 %all-gather.4 = bf16[1,128,864]{2,1,0:T(8,128)(2,1)} all-gather(bf16[1,32,864]{2,1,0:T(8,128)(2,1)S(1)} %get-tuple-element.241), channel_id=6, replica_groups=mesh['batch'=8,'ch'=4] {'ch'}, dimensions={1}, use_global_device_ids=true | all-gather | bytes 276480 | tf_op jit(solution)/shard_map/all_gather | solution.py:652
  195.1 3.7 shard_map.396
  198.8 7.4 %shard_map.397 = (bf16[384,1440]{1,0:T(8,128)(2,1)}, bf16[384,288]{1,0:T(8,128)(2,1)}, f32[192,320]{1,0:T(8,128)}, f32[192,128]{1,0:T(8,128)}, f32[32,16,128]{2,1,0:T(8,128)}, /*index=5*/f32[8,128]{1,0:T(8,128)}) custom-call(f32[32,8,128]{2,1,0:T(8,128)} %copy-done.9, f32[32,8,128]{2,1,0:T(8,128)} %copy-done.2, ...), custom_call_target="tpu_custom_call" | custom-call | flops 54579200 | bytes 5457920 | tf_op jit(solution)/shard_map/pallas_call | solution.py:56
  206.2 2.6 all-to-all-start.4
  213.0 6.4 all-to-all-done.4.refs_0_
  220.1 3.9 shard_map.398
  224.0 13.9 %all_to_all.60.refs_0_ = f32[32,16,128]{2,1,0:T(8,128)} all-to-all(f32[32,16,128]{2,1,0:T(8,128)} %get-tuple-element.106), channel_id=1, replica_groups=mesh['batch'=8,'ch'=4] {'batch','ch'}, dimensions={0} | all-to-all | bytes 524288 | tf_op jit(solution)/shard_map/all_to_all | solution.py:639
  237.9 6.5 shard_map.399
  244.4 11.5 %all_to_all.61.refs_0_ = f32[32,8,128]{2,1,0:T(8,128)} all-to-all(f32[32,8,128]{2,1,0:T(8,128)} %get-tuple-element.111), channel_id=1, replica_groups=mesh['batch'=8,'ch'=4] {'batch','ch'}, dimensions={0} | all-to-all | bytes 262144 | tf_op jit(solution)/shard_map/all_to_all | solution.py:639
  255.9 15.4 %shard_map.400 = (bf16[192,576]{1,0:T(8,128)(2,1)}, f32[1152,256]{1,0:T(8,128)}, f32[1152,320]{1,0:T(8,128)}, f32[1152,128]{1,0:T(8,128)}, f32[1152,128]{1,0:T(8...) custom-call(f32[32,8,128]{2,1,0:T(8,128)} %all_to_all.61.refs_0_, f32[16,128]{1,0:T(8,128)} %get-tuple-element.112.refs_1_, ...), custom_call_target="tpu_custom_call" | custom-call | flops 109752320 | bytes 10975232 | tf_op jit(solution)/shard_map/pallas_call | solution.py:56
  271.3 2.6 all-to-all-start.9
  274.1 4.8 shard_map.407
  279.0 5.5 all-to-all-done.9.refs_0_
  284.5 0.7 copy-done.5
  285.2 22.2 %shard_map.401 = (bf16[1152,320]{1,0:T(8,128)(2,1)}, bf16[1152,128]{1,0:T(8,128)(2,1)}, f32[1152,192]{1,0:T(8,128)}, f32[32,8,128]{2,1,0:T(8,128)}, f32[16,128]{1,0:T(8,128)}) custom-call(f32[32,16,128]{2,1,0:T(8,128)} %copy-done.5, f32[16,128]{1,0:T(8,128)} %get-tuple-element.116.refs_14_.refs_1_.refs_2_, f32[8,128]{1,0:T(8,128)} %get-tuple-element.118.refs_2_.refs_3_, ...), custom_call_target="tpu_custom_call" | custom-call | flops 109383680 | bytes 10938368 | tf_op jit(solution)/shard_map/pallas_call | solution.py:56
  307.4 9.7 %shard_map.406 = (bf16[320,4320]{1,0:T(8,128)(2,1)}, bf16[128,864]{1,0:T(8,128)(2,1)}) custom-call(bf16[1152,320]{1,0:T(8,128)(2,1)} %get-tuple-element.129.refs_0_, bf16[1152,128]{1,0:T(8,128)(2,1)} %get-tuple-element.130.refs_1_, bf16[1728,1440]{1,0:T(8,128)(2,1)} %get-tuple-element.131.refs_2_, bf16[1728,288]{1,0:T(8,128)(2,1)} %get-tuple-element.132.refs_3_), custom_call_target="tpu_custom_call" | custom-call | flops 99901440 | bytes 9990144 | tf_op jit(solution)/shard_map/pallas_call | solution.py:56
  320.0 0.9 copy.119
  321.0 3.5 all-to-all-start.6
  324.5 2.6 shard_map.405
  327.1 3.6 all-to-all-done.6
  330.8 0.8 slice.306
  331.5 0.9 slice.307
  332.4 1.1 fusion.7
  333.6 2.6 all-to-all-start.10
  336.4 8.1 %all-to-all-done.10.refs_0_ = f32[32,8,128]{2,1,0:T(8,128)S(1)} async-done(((f32[32,8,128]{2,1,0:T(8,128)}), f32[32,8,128]{2,1,0:T(8,128)S(1)}, u32[]{:S(2)}, u32[]{:S(2)}) %all-to-all-start.10) | async-done | bytes 131104 | tf_op jit(solution)/shard_map/all_to_all | solution.py:639
  345.1 8.8 %shard_map.402 = (bf16[1152,576]{1,0:T(8,128)(2,1)}, bf16[4,132,1152]{2,1,0:T(8,128)(2,1)}, f32[8,128]{1,0:T(8,128)}) custom-call(f32[32,8,128]{2,1,0:T(8,128)} %copy-done.8, f32[16,128]{1,0:T(8,128)} %get-tuple-element.122.refs_1_, f32[16,128]{1,0:T(8,128)} %get-tuple-element.116.refs_14_.refs_1_.refs_2_, f32[8,128]{1,0:T(8,128)} %get-tuple-element.118.refs_2_.refs_3_, ...), custom_call_target="tpu_custom_call" | custom-call | flops 92241920 | bytes 9224192 | tf_op jit(solution)/shard_map/pallas_call | solution.py:56
  353.9 4.5 shard_map.404
  359.6 13.3 %reduce-scatter.13.cloned.1.call-done = bf16[80,4320]{1,0:T(8,128)(2,1)} async-done(((bf16[320,4320]{1,0:T(8,128)(2,1)}), bf16[80,4320]{1,0:T(8,128)(2,1)}) %reduce-scatter.13.cloned.1.call-update) | async-done | bytes 691216 | tf_op jit(solution)/shard_map/reduce_scatter | solution.py:791
  372.9 3.4 stack.165
  376.3 35.0 %reduce-scatter.11.cloned.1.call-done = bf16[80,4320]{1,0:T(8,128)(2,1)} async-done(((bf16[320,4320]{1,0:T(8,128)(2,1)}), bf16[80,4320]{1,0:T(8,128)(2,1)}) %reduce-scatter.11.cloned.1.call-update) | async-done | bytes 691216 | tf_op jit(solution)/shard_map/reduce_scatter | solution.py:791
  411.3 3.4 stack.164
  414.7 24.0 %reduce-scatter.9.cloned.1.call-done = bf16[144,832]{1,0:T(8,128)(2,1)} async-done(((bf16[576,832]{1,0:T(8,128)(2,1)}), bf16[144,832]{1,0:T(8,128)(2,1)}) %reduce-scatter.9.cloned.1.call-update) | async-done | bytes 239632 | tf_op jit(solution)/shard_map/reduce_scatter | solution.py:791
  438.7 26.2 %reduce-scatter.7.cloned.1.call-done = bf16[144,528]{1,0:T(8,128)(2,1)} async-done(((bf16[576,528]{1,0:T(8,128)(2,1)}), bf16[144,528]{1,0:T(8,128)(2,1)}) %reduce-scatter.7.cloned.1.call-update) | async-done | bytes 152080 | tf_op jit(solution)/shard_map/reduce_scatter | solution.py:791
  466.9 3.5 all-to-all-start.11
  472.0 65.7 %all-reduce.10.cloned.1.call-done = (bf16[1,32,864]{2,1,0:T(8,128)(2,1)}, bf16[1,32,864]{2,1,0:T(8,128)(2,1)}) async-done(((bf16[1,32,864]{2,1,0:T(8,128)(2,1)}, bf16[1,32,864]{2,1,0:T(8,128)(2,1)}), (bf16[1,32,864]{2,1,0:T(8,128)(2,1)}, bf16[1,32,864]{2,1,0:T(8,128)(2,1)})) %all-reduce.10.cloned.1.call-update) | async-done | bytes 110608 | tf_op jit(solution)/shard_map/psum | solution.py:792
  537.7 0.9 convert_bitcast_fusion
  538.5 1.2 copy.122
  539.7 1.1 copy-done
  540.8 2.9 shard_map.403
  543.7 131.3 %all-reduce.12.cloned.1.call-done = (bf16[144,528]{1,0:T(8,128)(2,1)}, bf16[144,832]{1,0:T(8,128)(2,1)}, bf16[1,345600]{1,0:T(2,128)(2,1)}, bf16[1,345600]{1,0:T(2,128)(2,1)}) async-done(((bf16[144,528]{1,0:T(8,128)(2,1)}, bf16[144,832]{1,0:T(8,128)(2,1)}, bf16[1,345600]{1,0:T(2,128)(2,1)}, bf16[1,345600]{1,0:T(2,128)(2,1)}), (bf16[144,528]{1,0:T(8,128)(2,1)}, bf16[144,832]{1,0:T(8,128)(2,1)}, ...) | async-done | bytes 1774096 | tf_op jit(solution)/shard_map/psum | solution.py:792
  675.0 1.1 convert_element_type.44
  681.4 4.2 maximum_convert_fusion
  (201 shorter events, 23.0 us)
Async XLA Ops:
  7.2 105.5 %all-gather.8.cloned.1.call-start = ((), (), s32[]{:S(2)}) async-start(), calls=%async_computation.18 | async-start | bytes 3481600 | tf_op jit(solution)/shard_map/all_gather | solution.py:652
  25.1 173.7 %all-gather.10.cloned.1.call-start = ((), (), s32[]{:S(2)}) async-start(), calls=%async_computation.19 | async-start | bytes 3481600 | tf_op jit(solution)/shard_map/all_gather | solution.py:652
  29.5 4.5 copy-start.32
  29.5 4.5 copy-start.33
  29.5 4.5 copy-start.34
  29.5 4.5 copy-start.35
  29.5 4.5 copy-start.36
  29.5 4.5 copy-start.37
  29.5 47.8 %all-to-all-start = ((bf16[4,132,1152]{2,1,0:T(8,128)(2,1)}), bf16[4,132,1152]{2,1,0:T(8,128)(2,1)S(1)}, u32[]{:S(2)}, u32[]{:S(2)}) async-start(bf16[4,132,1152]{2,1,0:T(8,128)(2,1)} %shard_map.391), calls=%async_computation | async-start | bytes 2506752 | tf_op jit(solution)/shard_map/all_to_all | solution.py:644
  33.9 33.6 %copy-start.10 = (bf16[2,27,32,32]{3,2,1,0:T(8,128)(2,1)S(1)}, bf16[2,27,32,32]{3,2,1,0:T(8,128)(2,1)}, u32[]{:S(2)}) copy-start(bf16[2,27,32,32]{3,2,1,0:T(8,128)(2,1)} %param.35) | copy-start | bytes 331780
  33.9 34.5 %copy-start.19 = (bf16[528,64]{0,1:T(8,128)(2,1)S(1)}, bf16[528,64]{0,1:T(8,128)(2,1)}, u32[]{:S(2)}) copy-start(bf16[528,64]{0,1:T(8,128)(2,1)} %param.26) | copy-start | bytes 202756
  33.9 34.5 %copy-start.22 = (bf16[528,40]{0,1:T(8,128)(2,1)S(1)}, bf16[528,40]{0,1:T(8,128)(2,1)}, u32[]{:S(2)}) copy-start(bf16[528,40]{0,1:T(8,128)(2,1)} %param.27) | copy-start | bytes 126724
  33.9 34.5 %copy-start.25 = (bf16[528,32]{0,1:T(8,128)(2,1)S(1)}, bf16[528,32]{0,1:T(8,128)(2,1)}, u32[]{:S(2)}) copy-start(bf16[528,32]{0,1:T(8,128)(2,1)} %param.29) | copy-start | bytes 101380
  33.9 34.5 %copy-start.29 = (bf16[528,8]{0,1:T(8,128)(2,1)S(1)}, bf16[528,8]{0,1:T(8,128)(2,1)}, u32[]{:S(2)}) copy-start(bf16[528,8]{0,1:T(8,128)(2,1)} %param.28) | copy-start | bytes 25348
  77.3 1.9 copy-start.1
  87.7 25.0 %all-to-all-start.1 = ((f32[32,8,128]{2,1,0:T(8,128)}), f32[32,8,128]{2,1,0:T(8,128)S(1)}, u32[]{:S(2)}, u32[]{:S(2)}) async-start(f32[32,8,128]{2,1,0:T(8,128)} %get-tuple-element.82), calls=%async_computation.1 | async-start | bytes 262144 | tf_op jit(solution)/shard_map/all_to_all | solution.py:639
  112.7 0.7 copy-start.2
  113.4 28.5 %copy-start.17 = (bf16[832,64]{0,1:T(8,128)(2,1)S(1)}, bf16[832,64]{0,1:T(8,128)(2,1)}, u32[]{:S(2)}) copy-start(bf16[832,64]{0,1:T(8,128)(2,1)} %param.30) | copy-start | bytes 319492
  113.4 28.5 %copy-start.20 = (bf16[832,40]{0,1:T(8,128)(2,1)S(1)}, bf16[832,40]{0,1:T(8,128)(2,1)}, u32[]{:S(2)}) copy-start(bf16[832,40]{0,1:T(8,128)(2,1)} %param.31) | copy-start | bytes 199684
  113.4 28.5 %copy-start.21 = (bf16[832,32]{0,1:T(8,128)(2,1)S(1)}, bf16[832,32]{0,1:T(8,128)(2,1)}, u32[]{:S(2)}) copy-start(bf16[832,32]{0,1:T(8,128)(2,1)} %param.33) | copy-start | bytes 159748
  113.4 28.5 %copy-start.28 = (bf16[832,8]{0,1:T(8,128)(2,1)S(1)}, bf16[832,8]{0,1:T(8,128)(2,1)}, u32[]{:S(2)}) copy-start(bf16[832,8]{0,1:T(8,128)(2,1)} %param.32) | copy-start | bytes 39940
  136.7 18.4 %all-to-all-start.2 = ((f32[32,16,128]{2,1,0:T(8,128)}), f32[32,16,128]{2,1,0:T(8,128)S(1)}, u32[]{:S(2)}, u32[]{:S(2)}) async-start(f32[32,16,128]{2,1,0:T(8,128)} %get-tuple-element.87), calls=%async_computation.2 | async-start | bytes 524288 | tf_op jit(solution)/shard_map/all_to_all | solution.py:639
  155.0 0.7 copy-start.6
  155.7 18.8 %copy-start.12 = (bf16[8,2,6,6,32]{4,1,3,2,0:T(2,128)(2,1)S(1)}, bf16[8,2,6,6,32]{4,1,3,2,0:T(2,128)(2,1)}, u32[]{:S(2)}) copy-start(bf16[8,2,6,6,32]{4,1,3,2,0:T(2,128)(2,1)} %param.45) | copy-start | bytes 110596
  155.7 18.8 %copy-start.13 = (bf16[8,2,6,6,32]{4,1,3,2,0:T(2,128)(2,1)S(1)}, bf16[8,2,6,6,32]{4,1,3,2,0:T(2,128)(2,1)}, u32[]{:S(2)}) copy-start(bf16[8,2,6,6,32]{4,1,3,2,0:T(2,128)(2,1)} %param.44) | copy-start | bytes 110596
  155.7 18.9 %copy-start.14 = (bf16[8,2,6,6,80]{4,1,3,2,0:T(2,128)(2,1)S(1)}, bf16[8,2,6,6,80]{4,1,3,2,0:T(2,128)(2,1)}, u32[]{:S(2)}) copy-start(bf16[8,2,6,6,80]{4,1,3,2,0:T(2,128)(2,1)} %param.43) | copy-start | bytes 276484
  155.7 18.9 %copy-start.15 = (bf16[8,2,6,6,64]{4,1,3,2,0:T(2,128)(2,1)S(1)}, bf16[8,2,6,6,64]{4,1,3,2,0:T(2,128)(2,1)}, u32[]{:S(2)}) copy-start(bf16[8,2,6,6,64]{4,1,3,2,0:T(2,128)(2,1)} %param.42) | copy-start | bytes 221188
  170.1 12.7 %all-to-all-start.3 = ((f32[32,8,128]{2,1,0:T(8,128)}), f32[32,8,128]{2,1,0:T(8,128)S(1)}, u32[]{:S(2)}, u32[]{:S(2)}) async-start(f32[32,8,128]{2,1,0:T(8,128)} %get-tuple-element.92), calls=%async_computation.3 | async-start | bytes 262144 | tf_op jit(solution)/shard_map/all_to_all | solution.py:639
  182.8 16.0 %copy-start.9 = (f32[32,8,128]{2,1,0:T(8,128)}, f32[32,8,128]{2,1,0:T(8,128)S(1)}, u32[]{:S(2)}) copy-start(f32[32,8,128]{2,1,0:T(8,128)S(1)} %all-to-all-done.3.refs_0_) | copy-start | bytes 393220
  182.8 23.4 %all-to-all-start.5 = ((bf16[4,2,2,6,6,208]{5,2,4,3,1,0:T(2,128)(2,1)}), bf16[4,2,2,6,6,208]{5,2,4,3,1,0:T(2,128)(2,1)S(1)}, u32[]{:S(2)}, u32[]{:S(2)}) async-start(bf16[4,2,2,6,6,208]{5,2,4,3,1,0:T(2,128)(2,1)} %bitcast.22), calls=%async_computation.5 | async-start | bytes 589824 | tf_op jit(solution)/shard_map/all_to_all | solution.py:687
  206.2 13.2 %all-to-all-start.4 = ((f32[32,16,128]{2,1,0:T(8,128)}), f32[32,16,128]{2,1,0:T(8,128)S(1)}, u32[]{:S(2)}, u32[]{:S(2)}) async-start(f32[32,16,128]{2,1,0:T(8,128)} %get-tuple-element.97), calls=%async_computation.4 | async-start | bytes 524288 | tf_op jit(solution)/shard_map/all_to_all | solution.py:639
  219.4 0.7 copy-start.7
  271.3 13.2 %all-to-all-start.9 = ((f32[32,16,128]{2,1,0:T(8,128)}), f32[32,16,128]{2,1,0:T(8,128)S(1)}, u32[]{:S(2)}, u32[]{:S(2)}) async-start(f32[32,16,128]{2,1,0:T(8,128)} %get-tuple-element.117), calls=%async_computation.9 | async-start | bytes 524288 | tf_op jit(solution)/shard_map/all_to_all | solution.py:639
  273.9 85.4 %reduce-scatter.17.cloned.1.call-start = ((), (), s32[]{:S(2)}) async-start(), calls=%async_computation.25 | async-start | bytes 286720 | tf_op jit(solution)/shard_map/reduce_scatter | solution.py:791
  279.0 80.3 %reduce-scatter.15.cloned.1.call-start = ((), (), s32[]{:S(2)}) async-start(), calls=%async_computation.24 | async-start | bytes 286720 | tf_op jit(solution)/shard_map/reduce_scatter | solution.py:791
  284.5 0.7 copy-start.5
  317.1 55.8 %reduce-scatter.13.cloned.1.call-start = ((), (), s32[]{:S(2)}) async-start(), calls=%async_computation.23 | async-start | bytes 3481600 | tf_op jit(solution)/shard_map/reduce_scatter | solution.py:791
  317.7 93.6 %reduce-scatter.11.cloned.1.call-start = ((), (), s32[]{:S(2)}) async-start(), calls=%async_computation.22 | async-start | bytes 3481600 | tf_op jit(solution)/shard_map/reduce_scatter | solution.py:791
  317.7 0.9 copy-start.16
  317.8 1.1 copy-start.18
  317.8 1.4 copy-start.24
  317.8 1.5 copy-start.23
  321.0 9.8 %all-to-all-start.6 = ((bf16[4,2,2,6,6,208]{5,2,4,3,1,0:T(2,128)(2,1)}), bf16[4,2,2,6,6,208]{5,2,4,3,1,0:T(2,128)(2,1)S(1)}, u32[]{:S(2)}, u32[]{:S(2)}) async-start(bf16[4,2,2,6,6,208]{5,2,4,3,1,0:T(2,128)(2,1)} %copy.119), calls=%async_computation.6 | async-start | bytes 589824 | tf_op jit(solution)/shard_map/all_to_all | solution.py:832
  324.4 114.2 %reduce-scatter.9.cloned.1.call-start = ((), (), s32[]{:S(2)}) async-start(), calls=%async_computation.21 | async-start | bytes 1290240 | tf_op jit(solution)/shard_map/reduce_scatter | solution.py:791
  327.1 6.4 copy-start.27
  327.1 9.2 %copy-start.30 = (f32[8,128]{1,0:T(8,128)S(1)}, f32[8,128]{1,0:T(8,128)}, u32[]{:S(2)}) copy-start(f32[8,128]{1,0:T(8,128)} %get-tuple-element.142) | copy-start | bytes 12292
  333.6 10.8 %all-to-all-start.10 = ((f32[32,8,128]{2,1,0:T(8,128)}), f32[32,8,128]{2,1,0:T(8,128)S(1)}, u32[]{:S(2)}, u32[]{:S(2)}) async-start(f32[32,8,128]{2,1,0:T(8,128)} %get-tuple-element.121), calls=%async_computation.10 | async-start | bytes 262144 | tf_op jit(solution)/shard_map/all_to_all | solution.py:639
  336.2 128.7 %reduce-scatter.7.cloned.1.call-start = ((), (), s32[]{:S(2)}) async-start(), calls=%async_computation.20 | async-start | bytes 921600 | tf_op jit(solution)/shard_map/reduce_scatter | solution.py:791
  344.5 0.7 copy-start.8
  353.9 4.7 copy-start.26
  358.4 179.3 %all-reduce.10.cloned.1.call-start = ((), (), s32[]{:S(2)}) async-start(), calls=%async_computation.26 | async-start | bytes 229376 | tf_op jit(solution)/shard_map/psum | solution.py:792
  359.3 315.7 %all-reduce.12.cloned.1.call-start = ((), (), s32[]{:S(2)}) async-start(), calls=%async_computation.27 | async-start | bytes 6414336 | tf_op jit(solution)/shard_map/psum | solution.py:792
  464.9 5.5 copy-start.31
  466.9 72.8 %all-to-all-start.11 = ((bf16[4,132,1152]{2,1,0:T(8,128)(2,1)}), bf16[4,132,1152]{2,1,0:T(8,128)(2,1)S(1)}, u32[]{:S(2)}, u32[]{:S(2)}) async-start(bf16[4,132,1152]{2,1,0:T(8,128)(2,1)} %get-tuple-element.126), calls=%async_computation.11 | async-start | bytes 2506752 | tf_op jit(solution)/shard_map/all_to_all | solution.py:819
  539.7 1.1 copy-start
  675.0 3.8 copy-start.11
  675.0 6.4 copy-start.3
  675.0 6.4 copy-start.4
Sparse Core Ops, SparseCore 0:
  25.2 41.8 all-gather.7
  69.3 27.2 all-gather.9
  279.1 21.1 reduce-scatter.16
  317.2 17.5 reduce-scatter.14
  337.2 35.7 reduce-scatter.12
  375.5 35.6 reduce-scatter.10
  413.8 24.8 reduce-scatter.8
  441.9 22.9 reduce-scatter.6
  468.4 69.2 all-reduce.9
  542.6 132.3 all-reduce.11

commit v2 on v1

--- a/solution.py
+++ b/solution.py
@@ -9,6 +9,7 @@
 F32 = jnp.float32
 BF16 = jnp.bfloat16
 EPSILON = 0.001
+FLOPS_A_US = 1.1e9
 BOTH = ("batch", "ch")
 DIRECT, NARROW, WIDE, SQUEEZE, SPREAD, PROJECT = 256, 160, 320, 32, 128, 128
 REDUCED = NARROW + SQUEEZE
@@ -19,6 +20,7 @@
 POINT_WIDTHS = (DIRECT, NARROW, SQUEEZE, PROJECT)
 SLOT = {"d": (0, DIRECT), "r": (256, REDUCED), "w": (512, WIDE), "s": (896, SPREAD), "p": (1024, PROJECT)}
 SLOTS = 1152
+NORM_ORDER = ((0, DIRECT), (256, NARROW), (256 + NARROW, SQUEEZE), (512, WIDE), (896, SPREAD), (1024, PROJECT))
 TILE_ROW = {"d": (0, DIRECT), "w": (2, WIDE), "s": (5, SPREAD), "p": (6, PROJECT)}
 OUTER = ("d", "w", "s", "p")
 CHUNK = 48
@@ -50,18 +52,41 @@
     return lax.dot_general(a, b, (((0,), (0,)), ((), ())), preferred_element_type=F32)
 
 
-def call(kernel, outs, ins, scratch=(), flops=0):
+def call(kernel, outs, ins, scratch=(), us=0, idle=0):
     moved = sum(int(np.prod(s)) * jnp.dtype(d).itemsize for s, d in outs)
-    moved += sum(int(np.prod(x.shape)) * x.dtype.itemsize for x in ins)
+    moved += sum(int(np.prod(x.shape)) * x.dtype.itemsize for x in ins[: len(ins) - idle])
+
+    def spec(k, x):
+        if k >= len(ins) - idle:
+            return pl.BlockSpec(memory_space=pl.ANY)
+        return pl.BlockSpec(memory_space=pltpu.SMEM if x.ndim == 1 else pltpu.VMEM)
+
+    def body(*refs):
+        kept = len(ins) - idle
+        kernel(*refs[:kept], *refs[len(ins) :])
+
     return pl.pallas_call(
-        kernel,
+        body,
         out_shape=[jax.ShapeDtypeStruct(s, d) for s, d in outs],
+        in_specs=[spec(k, x) for k, x in enumerate(ins)],
+        out_specs=[pl.BlockSpec(memory_space=pltpu.VMEM)] * len(outs),
         scratch_shapes=[pltpu.VMEM(s, d) for s, d in scratch],
         compiler_params=pltpu.CompilerParams(vmem_limit_bytes=56 * 2**20),
         cost_estimate=pl.CostEstimate(
-            flops=int(flops) or 10 * moved, bytes_accessed=moved, transcendentals=0
+            flops=int(us * FLOPS_A_US) or 10 * moved, bytes_accessed=moved, transcendentals=0
         ),
     )(*ins)
+
+
+def ordered(value, *behind):
+    anywhere = pl.BlockSpec(memory_space=pl.ANY)
+    return pl.pallas_call(
+        lambda *refs: None,
+        out_shape=jax.ShapeDtypeStruct(value.shape, value.dtype),
+        in_specs=[anywhere] * (1 + len(behind)),
+        out_specs=anywhere,
+        input_output_aliases={0: 0},
+    )(value, *behind)
 
 
 def each_chunk(rows, body, init=0, chunk=CHUNK):
@@ -194,39 +219,138 @@
     ref[base + geo.padded_rows - size : base + geo.padded_rows, :] = blank
 
 
-def assemble_points(w_ref, scratch, groups):
-    for s in range(groups):
-        part = w_ref[s].astype(F32)
+def padded16(size):
+    return -(-size // 16) * 16
+
+
+class Packing:
+    def __init__(self, groups, features):
+        self.groups = groups
+        self.wide, self.spread, self.point = WIDE // groups, SPREAD // groups, POINT // groups
+        self.wide_rows = padded16(self.wide)
+        self.spread_rows = padded16(self.spread)
+        self.point_rows = padded16(self.point)
+        self.kernels = 3 * WIDE_TILES * self.wide_rows + 3 * SPREAD_TILES * self.spread_rows
+        self.features = features
+        self.point_tiles = -(-features // 128)
+        self.points = self.point_tiles * self.point_rows
+
+    def kernel_tiles(self):
+        at = 0
+        for own, size, tiles, columns, wide in (
+            (self.wide, self.wide_rows, WIDE_TILES, 9 * NARROW, True),
+            (self.spread, self.spread_rows, SPREAD_TILES, 9 * SQUEEZE, False),
+        ):
+            for t in range(3):
+                for u in range(tiles):
+                    yield at, own, wide, t, u, min(128, columns - 128 * u)
+                    at += size
+
+    def point_blocks(self, start):
+        for u in range(self.point_tiles):
+            yield start + u * self.point_rows, u, min(128, self.features - 128 * u)
+
+    def point_parts(self):
         at = start = 0
         for width in POINT_WIDTHS:
-            own = width // groups
-            scratch[start + s * own : start + (s + 1) * own, :] = part[at : at + own, :]
+            own = width // self.groups
+            yield at, start, own
             at += own
             start += width
 
 
-def split_points(value, scratch, groups):
-    size = POINT // groups
-    for s in range(groups):
-        at = start = 0
-        for width in POINT_WIDTHS:
-            own = width // groups
-            scratch[s * size + at : s * size + at + own, :] = value[
-                start + s * own : start + (s + 1) * own, :
-            ]
-            at += own
-            start += width
-
-
-def prepare_kernel(groups, x_ref, o_ref):
+WIDE_TILES = -(-9 * NARROW // 128)
+SPREAD_TILES = -(-9 * SQUEEZE // 128)
+
+
+def fit_tile(value):
+    width = value.shape[1]
+    if width == 128:
+        return value
+    return jnp.concatenate([value, jnp.zeros((value.shape[0], 128 - width), value.dtype)], axis=1)
+
+
+def pack_points(pack, part_refs, o_ref, start, scratch):
+    for (at, _, own), ref in zip(pack.point_parts(), part_refs):
+        scratch[at : at + own, : pack.features] = ref[...].astype(F32)
+    for at, u, width in pack.point_blocks(start):
+        o_ref[at : at + pack.point, :] = fit_tile(
+            scratch[: pack.point, 128 * u : 128 * u + width].astype(BF16)
+        )
+
+
+def unpack_points(pack, me, piece_refs, start, raw, scratch, wt_ref):
+    for k, ref in enumerate(piece_refs):
+        for at, u, width in pack.point_blocks(start):
+            raw[me ^ k, : pack.point, 128 * u : 128 * u + width] = ref[at : at + pack.point, :width].astype(F32)
+    for s in range(pack.groups):
+        for at, begin, own in pack.point_parts():
+            scratch[begin + s * own : begin + (s + 1) * own, :] = raw[s, at : at + own, : pack.features]
+    wt_ref[...] = scratch[...].astype(BF16)
+
+
+def unpack_kernels(pack, me, piece_refs, kw_ref, ks_ref):
+    for k, ref in enumerate(piece_refs):
+        for at, own, wide, t, u, _ in pack.kernel_tiles():
+            target = kw_ref if wide else ks_ref
+            size = target.shape[2]
+            target[t, me ^ k, :, 128 * u : 128 * u + 128] = ref[at : at + size, :]
+
+
+def whole_kernel(ref, t, own):
+    if own == ref.shape[2]:
+        return ref[t].reshape(ref.shape[1] * own, ref.shape[3])
+    parts = [ref[t, s].astype(F32)[:own] for s in range(ref.shape[1])]
+    return jnp.concatenate(parts, axis=0).astype(BF16)
+
+
+def prepare_kernel(pack, x_ref, norm_ref, p0, p1, p2, p3, o_ref, b_ref, scratch, rows):
     width = o_ref.shape[2]
-    for s in range(groups):
+    for s in range(pack.groups):
         o_ref[s] = x_ref[:, s * width : (s + 1) * width]
+    pack_points(pack, (p0, p1, p2, p3), b_ref, 0, scratch)
+    rows[...] = jnp.zeros_like(rows)
+    for u in range(-(-norm_ref.shape[1] // 128)):
+        part = norm_ref[:, 128 * u : 128 * (u + 1)].astype(F32)
+        rows[4 * u : 4 * u + 4, : part.shape[1]] = part
+    b_ref[pack.points :, :] = rows[...].astype(BF16)
+
+
+def split_kernel(x_ref, a_ref, b_ref):
+    tiles = x_ref.shape[1] // 128
+
+    def move(first, count):
+        value = x_ref[:, pl.ds(128 * first, 128 * count)].astype(F32)
+        for r, ref in ((0, a_ref), (1, b_ref)):
+            parts = [value[r : r + 1, 128 * j : 128 * (j + 1)] for j in range(count)]
+            ref[pl.ds(first, count), :] = jnp.concatenate(parts, axis=0).astype(BF16)
+
+    def step(i, carry):
+        move(pl.multiple_of(16 * i, 16), 16)
+        return carry
+
+    lax.fori_loop(0, tiles // 16, step, 0)
+    if tiles % 16:
+        move(tiles // 16 * 16, tiles % 16)
+
+
+def pack_kernel(pack, w_ref, s_ref, *refs):
+    *part_refs, o_ref, scratch = refs
+    for at, own, wide, t, u, width in pack.kernel_tiles():
+        source, columns = (w_ref, 9 * NARROW) if wide else (s_ref, 9 * SQUEEZE)
+        start = columns * t + 128 * u
+        o_ref[at : at + own, :] = fit_tile(source[:, start : start + width])
+    if part_refs:
+        pack_points(pack, part_refs, o_ref, pack.kernels, scratch)
 
 
 def early_first_kernel(
-    groups, x_ref, w_ref, m_ref, mc_ref, a_ref, wt_ref, y_ref, pay_ref, xs, ws, tile
+    pack, me_ref, x_ref, *refs
 ):
+    groups = pack.groups
+    piece_refs = refs[:groups]
+    m_ref, mc_ref, a_ref, wt_ref, aff_ref, y_ref, pay_ref, xs, raw, ws, norm_raw, tile = refs[groups:]
+    me = me_ref[0]
     depth, rows = x_ref.shape[1], x_ref.shape[2]
     for s in range(groups):
         xs[s * depth : (s + 1) * depth, :] = x_ref[s].astype(F32)
@@ -234,8 +358,20 @@
         size = min(128, rows - j)
         turned = jnp.transpose(xs[:, j : j + size])
         a_ref[j : j + size, :] = (turned * m_ref[j : j + size, 0:1]).astype(BF16)
-    assemble_points(w_ref, ws, groups)
-    wt_ref[...] = ws[...].astype(BF16)
+    unpack_points(pack, me, piece_refs, 0, raw, ws, wt_ref)
+    for k, ref in enumerate(piece_refs):
+        norm_raw[me ^ k] = ref[pack.points :, :].astype(F32)
+    at = 0
+    for slot, whole in NORM_ORDER:
+        own = whole // groups
+        for s in range(groups):
+            left, u = at % 128, at // 128
+            first = min(own, 128 - left)
+            to = slot + s * own
+            aff_ref[:, to : to + first] = norm_raw[s, 4 * u : 4 * u + 4, left : left + first]
+            if first < own:
+                aff_ref[:, to + first : to + own] = norm_raw[s, 4 * u + 4 : 4 * u + 8, : own - first]
+        at += own
     y_ref[...] = nt(a_ref[...], wt_ref[DIRECT : DIRECT + REDUCED, :])
     tile[...] = jnp.zeros_like(tile)
     count = jnp.sum(m_ref[...], axis=0, keepdims=True)
@@ -264,9 +400,11 @@
 
 
 def second_kernel(
-    geo, clips, count_row, g_ref, counts_ref, aff_ref, y_ref, m_ref, kw_ref, ks_ref, pd_ref,
-    bn_ref, bs_ref, yw_ref, ys_ref, pay_ref, st_ref, us, tile
+    geo, clips, pack, count_row, me_ref, g_ref, counts_ref, aff_ref, y_ref, m_ref, pd_ref, *refs
 ):
+    piece_refs = refs[: pack.groups]
+    (bn_ref, bs_ref, yw_ref, ys_ref, kw_ref, ks_ref, pay_ref, st_ref, us, tile) = refs[pack.groups :]
+    unpack_kernels(pack, me_ref[0], piece_refs, kw_ref, ks_ref)
     rows = clips * geo.clip_rows
     counts = counts_ref[:, count_row : count_row + 1, :]
     means, rstds = combine_moments(g_ref[...], counts, 0, 4, 2)
@@ -290,6 +428,9 @@
         base = c * geo.padded_rows
         clear_edges(geo, bn_ref, c)
         clear_edges(geo, bs_ref, c)
+        inside = slice(base + size, base + size + geo.clip_rows)
+        for ref, used in ((bn_ref, 9 * NARROW), (bs_ref, 9 * SQUEEZE)):
+            ref[inside, used:] = jnp.zeros((geo.clip_rows, ref.shape[1] - used), BF16)
 
         def store(j, placed):
             at = slice(base + size, base + size + geo.clip_rows)
@@ -300,13 +441,14 @@
     for c in range(clips):
         base = c * geo.padded_rows
         out = slice(c * geo.clip_rows, (c + 1) * geo.clip_rows)
-        for b_ref, k_ref, o_ref in ((bn_ref, kw_ref, yw_ref), (bs_ref, ks_ref, ys_ref)):
-            width = b_ref.shape[1]
+        for b_ref, k_ref, o_ref, own in (
+            (bn_ref, kw_ref, yw_ref, pack.wide), (bs_ref, ks_ref, ys_ref, pack.spread)
+        ):
             total = None
             for t in range(3):
                 term = nt(
                     b_ref[base + size * t : base + size * t + geo.clip_rows, :],
-                    k_ref[:, width * t : width * (t + 1)],
+                    whole_kernel(k_ref, t, own),
                 )
                 total = term if total is None else total + term
             o_ref[out, :] = total
@@ -325,9 +467,11 @@
 
 
 def pool_kernel(
-    groups, clips, g_ref, counts_ref, aff_ref, yd_ref, yw_ref, ys_ref, yp_ref, m_ref, pool_ref,
-    w_ref, mc_ref, a_ref, wt_ref, y_ref, pay_ref, st_ref, high, low, ws, tile
+    pack, clips, me_ref, g_ref, counts_ref, aff_ref, yd_ref, yw_ref, ys_ref, yp_ref, m_ref, pool_ref,
+    mc_ref, *refs
 ):
+    piece_refs = refs[: pack.groups]
+    a_ref, wt_ref, y_ref, pay_ref, st_ref, high, low, raw, ws, tile = refs[pack.groups :]
     means, rstds = combine_moments(g_ref[...], counts_ref[:, 2:3, :], 0, 8, 8)
     st_ref[0:8, :] = means
     st_ref[8:16, :] = rstds
@@ -354,8 +498,7 @@
             out = slice(c * LATE.clip_rows, (c + 1) * LATE.clip_rows)
             a_ref[out, at_column : at_column + width] = pooled.astype(BF16)
         at_column += width
-    assemble_points(w_ref, ws, groups)
-    wt_ref[...] = ws[...].astype(BF16)
+    unpack_points(pack, me_ref[0], piece_refs, pack.kernels, raw, ws, wt_ref)
     y_ref[...] = nt(a_ref[...], wt_ref[DIRECT : DIRECT + REDUCED, :])
     tile[...] = jnp.zeros_like(tile)
     own = jnp.sum(mc_ref[...], axis=0, keepdims=True)
@@ -418,19 +561,15 @@
     return scale * rstd * (dh - (shift_sum + xhat * scale_sum) / count) * masking
 
 
-def inner_backward_kernel(
-    geo, clips, g_ref, st_ref, str_ref, aff_ref, dw_ref, ds_ref, yw_ref, ys_ref, yr_ref, kw_ref,
-    ks_ref, m_ref, gw_ref, gs_ref, dh_ref, pay_ref, sums_ref, pad_w, pad_s, kt_w, kt_s, dz, tile
+def finish_kernel(
+    geo, clips, g_ref, st_ref, str_ref, aff_ref, dw_ref, ds_ref, yw_ref, ys_ref, m_ref,
+    gw_ref, gs_ref, sums_ref
 ):
     rows = clips * geo.clip_rows
-    size = geo.frame_rows
     sums_ref[...] = jnp.sum(g_ref[...], axis=0)
-    sums, st, st_r = sums_ref[...], st_ref[...], str_ref[...]
-    count = st_r[2:3, 0:1]
-    for unit, d_ref, y_ref, o_ref, pad in (
-        ("w", dw_ref, yw_ref, gw_ref, pad_w),
-        ("s", ds_ref, ys_ref, gs_ref, pad_s),
-    ):
+    sums, st = sums_ref[...], st_ref[...]
+    count = str_ref[2:3, 0:1]
+    for unit, d_ref, y_ref, o_ref in (("w", dw_ref, yw_ref, gw_ref), ("s", ds_ref, ys_ref, gs_ref)):
         first, width = TILE_ROW[unit]
         mean, rstd = outer_stats(st, unit)
         scale, _ = affine_of(aff_ref, geo.block, unit)
@@ -446,6 +585,16 @@
             return carry
 
         each_chunk(rows, finish)
+
+
+def inner_backward_kernel(
+    geo, clips, pack, str_ref, aff_ref, gw_ref, gs_ref, yr_ref, kw_ref, ks_ref, m_ref,
+    dh_ref, pay_ref, pad_w, pad_s, kt_w, kt_s, dz, tile
+):
+    rows = clips * geo.clip_rows
+    size = geo.frame_rows
+    st_r = str_ref[...]
+    for width, g_ref, pad in ((WIDE, gw_ref, pad_w), (SPREAD, gs_ref, pad_s)):
         masks = edge_masks(geo, width)
         for c in range(clips):
             base = c * geo.padded_rows
@@ -455,13 +604,15 @@
                 at = slice(base + size, base + size + geo.clip_rows)
                 pad[at, width * j : width * (j + 1)] = placed.astype(BF16)
 
-            value = o_ref[c * geo.clip_rows : (c + 1) * geo.clip_rows, :].astype(F32)
+            value = g_ref[c * geo.clip_rows : (c + 1) * geo.clip_rows, :].astype(F32)
             gather_cells(geo, value, masks, -1, store)
-    for k_ref, kt, width, depth in ((kw_ref, kt_w, WIDE, NARROW), (ks_ref, kt_s, SPREAD, SQUEEZE)):
+    for k_ref, kt, own, width, depth in (
+        (kw_ref, kt_w, pack.wide, WIDE, NARROW), (ks_ref, kt_s, pack.spread, SPREAD, SQUEEZE)
+    ):
         for t in range(3):
+            whole = whole_kernel(k_ref, t, own)
             for j in range(9):
-                at = (9 * t + j) * depth
-                kt[t, width * j : width * (j + 1), :] = k_ref[:, at : at + depth]
+                kt[t, width * j : width * (j + 1), :] = whole[:, depth * j : depth * (j + 1)]
     for pad, kt, depth, start in ((pad_w, kt_w, NARROW, 0), (pad_s, kt_s, SQUEEZE, NARROW)):
         for c in range(clips):
             base = c * geo.padded_rows
@@ -482,10 +633,11 @@
     send_tile(pay_ref, tile)
 
 
-def kernel_grad_kernel(geo, clips, gw_ref, gs_ref, bn_ref, bs_ref, ow_ref, os_ref):
+def kernel_grad_kernel(
+    geo, clips, pack, me_ref, gw_ref, gs_ref, bn_ref, bs_ref, keep_ref, send_ref, grad_w, grad_s
+):
     size = geo.frame_rows
-    for g_ref, b_ref, o_ref in ((gw_ref, bn_ref, ow_ref), (gs_ref, bs_ref, os_ref)):
-        width = b_ref.shape[1]
+    for g_ref, b_ref, grad in ((gw_ref, bn_ref, grad_w), (gs_ref, bs_ref, grad_s)):
         for t in range(3):
             total = None
             for c in range(clips):
@@ -495,7 +647,118 @@
                     b_ref[at : at + geo.clip_rows, :],
                 )
                 total = term if total is None else total + term
-            o_ref[:, width * t : width * (t + 1)] = total.astype(BF16)
+            grad[t] = total
+    me = me_ref[0]
+    for k in range(pack.groups):
+        target = (keep_ref, send_ref)[k % 2]
+        for at, own, wide, t, u, _ in pack.kernel_tiles():
+            source = grad_w if wide else grad_s
+            first = pl.multiple_of((me ^ k) * own, 8)
+            part = source[t, pl.ds(first, own), 128 * u : 128 * u + 128]
+            target[k // 2, at : at + own, :] = part.astype(BF16)
+
+
+def point_grad_kernel(pack, start, me_ref, gy_ref, a_ref, *refs):
+    keep_ref, send_ref, whole, shares = refs[-4:]
+    for source, target in zip(refs[:-4], (keep_ref, send_ref)):
+        target[:, :start, :] = source[...]
+    whole[...] = tn(gy_ref[...], a_ref[...])
+    for s in range(pack.groups):
+        for at, begin, own in pack.point_parts():
+            shares[s, at : at + own, : pack.features] = whole[begin + s * own : begin + (s + 1) * own, :]
+    me = me_ref[0]
+    for k in range(pack.groups):
+        target = (keep_ref, send_ref)[k % 2]
+        for at, u, width in pack.point_blocks(start):
+            target[k // 2, at : at + pack.point, :] = shares[
+                me ^ k, : pack.point, 128 * u : 128 * u + 128
+            ].astype(BF16)
+
+
+def halve_kernel(keep_ref, got_ref, even_ref, odd_ref):
+    for q in range(keep_ref.shape[0]):
+        target = (even_ref, odd_ref)[q % 2]
+        target[q // 2] = (keep_ref[q].astype(F32) + got_ref[q].astype(F32)).astype(BF16)
+
+
+def add_kernel(keep_ref, got_ref, o_ref):
+    o_ref[...] = (keep_ref[0].astype(F32) + got_ref[0].astype(F32)).astype(BF16)
+
+
+def scatter_kernel(mb_ref, keep_ref, got_ref, *refs):
+    *o_refs, held = refs
+    held[...] = keep_ref[0].astype(F32) + got_ref[0].astype(F32)
+    size = held.shape[0] // len(o_refs)
+    for k, o_ref in enumerate(o_refs):
+        first = pl.multiple_of((mb_ref[0] ^ k) * size, 8)
+        o_ref[...] = held[pl.ds(first, size), :].astype(BF16)
+
+
+def scatter_halves_kernel(mb_ref, keep_ref, got_ref, even_ref, odd_ref, held):
+    held[...] = keep_ref[0].astype(F32) + got_ref[0].astype(F32)
+    size = even_ref.shape[1]
+    for k in range(2 * even_ref.shape[0]):
+        first = pl.multiple_of((mb_ref[0] ^ k) * size, 8)
+        (even_ref, odd_ref)[k % 2][k // 2] = held[pl.ds(first, size), :].astype(BF16)
+
+
+def total_kernel(x_ref, *refs):
+    *p_refs, o_ref = refs
+    total = x_ref[0].astype(F32)
+    for k in range(1, x_ref.shape[0]):
+        total = total + x_ref[k].astype(F32)
+    other = p_refs[0][...].astype(F32)
+    for p_ref in p_refs[1:]:
+        other = other + p_ref[...].astype(F32)
+    size = total.shape[0]
+    o_ref[:, :size, :] = jnp.broadcast_to(total.astype(BF16)[None], (o_ref.shape[0],) + total.shape)
+    o_ref[:, size:, :] = jnp.broadcast_to(other.astype(BF16)[None], (o_ref.shape[0],) + other.shape)
+
+
+def read_kernels(pack, rows, w_ref, s_ref, turned):
+    for at, own, wide, t, u, width in pack.kernel_tiles():
+        target, columns = (w_ref, 9 * NARROW) if wide else (turned, 9 * SQUEEZE)
+        start = columns * t + 128 * u
+        target[:, start : start + width] = rows[at : at + own, :width].astype(F32)
+    s_ref[...] = jnp.transpose(turned[...])
+
+
+def read_points(pack, start, rows, o_refs):
+    for at, u, width in pack.point_blocks(start):
+        block = rows[at : at + pack.point, :].astype(F32)
+        for (first, _, own), o_ref in zip(pack.point_parts(), o_refs):
+            o_ref[:, 128 * u : 128 * u + width] = block[first : first + own, :width]
+
+
+def late_gradients_kernel(pack, batches, mb_ref, *refs):
+    x_refs = refs[:batches]
+    w_ref, s_ref, *o_refs, held, turned = refs[batches:]
+    for k, x_ref in enumerate(x_refs):
+        held[mb_ref[0] ^ k] = x_ref[...]
+    rows = held[...].reshape(-1, 128)
+    read_kernels(pack, rows, w_ref, s_ref, turned)
+    read_points(pack, pack.kernels, rows, o_refs)
+
+
+def early_gradients_kernel(pack, size, x_ref, late_ref, w_ref, s_ref, *refs):
+    *o_refs, held, points, wide, turned = refs
+    rest = x_ref.shape[1] - size
+    for b in range(x_ref.shape[0]):
+        held[b * size : (b + 1) * size, :] = x_ref[b, :size, :]
+        points[b * rest : (b + 1) * rest, :] = x_ref[b, size:, :]
+    read_kernels(pack, held, wide, s_ref, turned)
+    read_points(pack, 0, points, o_refs)
+
+    def join(g, carry):
+        parts = []
+        for r in range(4):
+            at = pl.ds(4 * g + r, 1)
+            parts.append(jnp.concatenate([wide[at, :], late_ref[at, :]], axis=0))
+        first = pl.multiple_of(4 * WIDE_COLUMNS * g, 128)
+        w_ref[:, pl.ds(first, 4 * WIDE_COLUMNS)] = jnp.concatenate(parts, axis=1)
+        return carry
+
+    lax.fori_loop(0, pack.wide // 4, join, 0)
 
 
 def point_gradients(
@@ -576,32 +839,33 @@
 
 
 def early_input_kernel(
-    groups, clips, g_ref, sums_ref, st_ref, str_ref, aff_ref, dr_ref, dd_ref, dp_ref, yr_ref, yd_ref,
-    yp_ref, m_ref, wt_ref, gy_ref, x_ref, sumr_ref, held
+    pack, clips, me_ref, g_ref, sums_ref, st_ref, str_ref, aff_ref, dr_ref, dd_ref, dp_ref, yr_ref,
+    yd_ref, yp_ref, m_ref, wt_ref, gy_ref, *refs
 ):
+    x_refs = refs[: pack.groups]
+    sumr_ref, held, turned = refs[pack.groups :]
     point_gradients(
         EARLY, clips, g_ref, sums_ref, st_ref, str_ref, aff_ref, dr_ref, dd_ref, dp_ref, yr_ref,
         yd_ref, yp_ref, m_ref, gy_ref, sumr_ref, held,
     )
-    depth = x_ref.shape[1]
+    depth = turned.shape[1]
     rows = clips * EARLY.clip_rows
     for j in range(0, rows, 128):
         size = min(128, rows - j)
-        grad = nn(gy_ref[j : j + size, :], wt_ref[...]) * m_ref[j : j + size, 0:1]
-        turned = jnp.transpose(grad)
-        for s in range(groups):
-            x_ref[s, :, j : j + size] = turned[s * depth : (s + 1) * depth, :].astype(BF16)
-
-
-def point_grad_kernel(groups, gy_ref, a_ref, o_ref, scratch):
-    split_points(tn(gy_ref[...], a_ref[...]), scratch, groups)
-    o_ref[...] = scratch[...].astype(BF16)
-
-
-def feature_kernel(groups, x_ref, o_ref):
-    width = x_ref.shape[2]
-    for s in range(groups):
-        o_ref[:, s * width : (s + 1) * width] = x_ref[s].astype(F32)
+        grad = jnp.transpose(nn(gy_ref[j : j + size, :], wt_ref[...]) * m_ref[j : j + size, 0:1])
+        for s in range(pack.groups):
+            turned[s, :, j : j + size] = grad[s * depth : (s + 1) * depth, :].astype(BF16)
+    for k, x_ref in enumerate(x_refs):
+        x_ref[...] = turned[me_ref[0] ^ k]
+
+
+def feature_kernel(pack, me_ref, *refs):
+    *x_refs, o_ref, held = refs
+    for k, x_ref in enumerate(x_refs):
+        held[me_ref[0] ^ k] = x_ref[...]
+    width = held.shape[2]
+    for s in range(pack.groups):
+        o_ref[:, s * width : (s + 1) * width] = held[s].astype(F32)
 
 
 def pool_matrix():
@@ -626,60 +890,81 @@
     upstream_spread, upstream_project,
 ):
     groups = lax.axis_size("ch")
-    devices = groups * lax.axis_size("batch")
+    batches = lax.axis_size("batch")
+    devices = groups * batches
     me = lax.axis_index("ch")
+    me_ref = jnp.reshape(me, (1,)).astype(jnp.int32)
     held_clips = visible.shape[0]
     clips = held_clips // groups
     rows = clips * EARLY.clip_rows
     late_rows = clips * LATE.clip_rows
     depth = clip_features.shape[0]
     features = depth * groups
+    pack = Packing(groups, features)
+    late_pack = Packing(groups, CONCAT)
 
     def exchange(payload):
         return lax.all_to_all(payload, BOTH, 0, 0)
 
-    (pieces,) = call(
-        lambda *refs: prepare_kernel(groups, *refs), [((groups, depth, rows), BF16)], [clip_features]
+    def swap(value, bit):
+        return lax.ppermute(value, "ch", [(i, i ^ bit) for i in range(groups)])
+
+    class Shares:
+        def __init__(self, own):
+            self.pieces, self.bit = {0: own}, groups // 2
+            self.step()
+
+        def step(self):
+            for k in list(self.pieces):
+                self.pieces[k | self.bit] = swap(self.pieces[k], self.bit)
+            self.bit //= 2
+
+        def all(self, *behind):
+            if behind:
+                last = max(self.pieces)
+                self.pieces[last] = ordered(self.pieces[last], *behind)
+            while self.bit:
+                self.step()
+            return [self.pieces[k] for k in range(groups)]
+
+    early_parts = (direct_early, narrow_early, squeeze_early, project_early)
+    late_parts = (direct_late, narrow_late, squeeze_late, project_late)
+    norms = (direct_norm, narrow_norm, squeeze_norm, wide_norm, spread_norm, project_norm)
+    norm_rows = jnp.concatenate(norms, axis=2).reshape(4, -1)
+    norm_space = padded16(4 * -(-norm_rows.shape[1] // 128))
+    pieces, early_points = call(
+        lambda *refs: prepare_kernel(pack, *refs),
+        [((groups, depth, rows), BF16), ((pack.points + norm_space, 128), BF16)],
+        [clip_features, norm_rows] + [part.T for part in early_parts],
+        [((pack.point_rows, pack.point_tiles * 128), F32), ((norm_space, 128), F32)],
+        us=2.5,
     )
     arrived = lax.all_to_all(pieces, "ch", 0, 0)
+    point_shares = Shares(early_points).all()
+    flat_rows = wide_kernels.shape[1] // 128
+    halves = call(split_kernel, [((flat_rows, 128), BF16)] * 2, [wide_kernels, pieces], us=4.8, idle=1)
+    spread_rows = jnp.transpose(
+        spread_kernels.reshape(2, SPREAD_COLUMNS, spread_kernels.shape[3]), (0, 2, 1)
+    )
+
+    def packed(use, block, parts, behind):
+        size = use.kernels + (use.points if parts else 0)
+        return call(
+            lambda *refs: pack_kernel(use, *refs),
+            [((size, 128), BF16)],
+            [halves[block].reshape(-1, WIDE_COLUMNS), spread_rows[block]]
+            + [part.T for part in parts] + list(behind),
+            [((use.point_rows, use.point_tiles * 128), F32)],
+            idle=len(behind),
+            us=2.5,
+        )[0]
+
+    early_shares = Shares(ordered(packed(pack, 0, (), ()), point_shares[-1], arrived)).all()
     own_visible = lax.dynamic_slice_in_dim(visible, me * clips, clips, 0)
     fine = own_visible.astype(F32).reshape(rows, 1)
     mask = jnp.broadcast_to(fine, (rows, 128))
     cells = own_visible.reshape(clips, 2, 2, 6, 2, 6, 2).max(axis=(2, 4, 6)).astype(F32)
     coarse = jnp.broadcast_to(pad_late(cells[..., None]), (late_rows, 128))
-
-    def gathered(value):
-        return lax.all_gather(value, "ch", axis=0, tiled=True)
-
-    def stacked_points(parts):
-        local = jnp.concatenate([part.T for part in parts], axis=0)
-        return lax.all_gather(local, "ch", axis=0)
-
-    early_points = stacked_points((direct_early, narrow_early, squeeze_early, project_early))
-    norms = (direct_norm, narrow_norm, squeeze_norm, wide_norm, spread_norm, project_norm)
-    joined = lax.all_gather(jnp.concatenate(norms, axis=2), "ch", axis=0).astype(F32)
-    units, at = [], 0
-    for norm in norms:
-        width = norm.shape[2]
-        piece = jnp.moveaxis(joined[..., at : at + width], 0, 2)
-        units.append(piece.reshape(4, groups * width))
-        at += width
-    affine = jnp.concatenate(
-        [
-            units[0], units[1], units[2], jnp.zeros((4, 64), F32), units[3], jnp.zeros((4, 64), F32),
-            units[4], units[5],
-        ],
-        axis=1,
-    )
-    wide_rows = wide_kernels.reshape(2, -1, WIDE_COLUMNS)
-    spread_rows = jnp.transpose(
-        spread_kernels.reshape(2, SPREAD_COLUMNS, spread_kernels.shape[3]), (0, 2, 1)
-    )
-    kw_early = gathered(wide_rows[0])
-    ks_early = gathered(spread_rows[0])
-    late_points = stacked_points((direct_late, narrow_late, squeeze_late, project_late))
-    kw_late = gathered(wide_rows[1])
-    ks_late = gathered(spread_rows[1])
 
     upstream = (upstream_direct, upstream_wide, upstream_spread, upstream_project)
     up_joined = jnp.concatenate(upstream, axis=4)
@@ -695,53 +980,71 @@
     pool = jnp.asarray(pool_matrix(), BF16)
     spread_back = jnp.asarray(pool_matrix().T, BF16)
 
-    act, wt, yr, pay = call(
-        lambda *refs: early_first_kernel(groups, *refs),
+    act, wt, affine, yr, pay = call(
+        lambda *refs: early_first_kernel(pack, *refs),
         [
-            ((rows, features), BF16), ((POINT, features), BF16), ((rows, REDUCED), F32),
-            ((devices, 8, 128), F32),
+            ((rows, features), BF16), ((POINT, features), BF16), ((4, SLOTS), F32),
+            ((rows, REDUCED), F32), ((devices, 8, 128), F32),
         ],
-        [arrived, early_points, mask, coarse],
-        [((features, rows), F32), ((POINT, features), F32), ((8, 128), F32)],
-    )
+        [me_ref, arrived] + point_shares + [mask, coarse],
+        [
+            ((features, rows), F32), ((groups, pack.point_rows, pack.point_tiles * 128), F32),
+            ((POINT, features), F32), ((groups, norm_space, 128), F32), ((8, 128), F32),
+        ],
+        us=8.6,
+    )
+    late_share = packed(late_pack, 1, late_parts, (act,))
     counts = exchange(pay)
+    late_shares = Shares(ordered(late_share, counts))
     yd, yp, tile = call(
         lambda *refs: other_points_kernel(EARLY, clips, *refs),
         [((rows, DIRECT), F32), ((rows, PROJECT), F32), ((16, 128), F32)],
         [act, wt, mask],
-    )
-
-    def second(geo, count_row, g, y, masking, kw, ks, other):
+        us=12,
+    )
+
+    def second(geo, count_row, g, y, masking, pieces, other):
         own = clips * geo.clip_rows
         padded = clips * geo.padded_rows
         return call(
-            lambda *refs: second_kernel(geo, clips, count_row, *refs),
+            lambda *refs: second_kernel(geo, clips, pack, count_row, *refs),
             [
-                ((padded, 9 * NARROW), BF16), ((padded, 9 * SQUEEZE), BF16), ((own, WIDE), F32),
-                ((own, SPREAD), F32), ((devices, 16, 128), F32), ((8, 128), F32),
+                ((padded, 128 * WIDE_TILES), BF16), ((padded, 128 * SPREAD_TILES), BF16),
+                ((own, WIDE), F32), ((own, SPREAD), F32),
+                ((3, groups, pack.wide_rows, 128 * WIDE_TILES), BF16),
+                ((3, groups, pack.spread_rows, 128 * SPREAD_TILES), BF16),
+                ((devices, 16, 128), F32), ((8, 128), F32),
             ],
-            [g, counts, affine, y, masking, kw, ks, other],
+            [me_ref, g, counts, affine, y, masking, other] + pieces,
             [((own, REDUCED), F32), ((16, 128), F32)],
+            us=25 if geo is EARLY else 9,
         )
 
-    bn, bs, yw, ys, pay, st_r = second(EARLY, 2, counts, yr, mask, kw_early, ks_early, tile)
+    bn, bs, yw, ys, kw, ks, pay, st_r = second(EARLY, 2, counts, yr, mask, early_shares, tile)
     g = exchange(pay)
+    late_shares = late_shares.all(st_r)
     late_act, late_wt, lyr, pay, st = call(
-        lambda *refs: pool_kernel(groups, clips, *refs),
+        lambda *refs: pool_kernel(late_pack, clips, *refs),
         [
             ((late_rows, CONCAT), BF16), ((POINT, CONCAT), BF16), ((late_rows, REDUCED), F32),
             ((devices, 8, 128), F32), ((16, 128), F32),
         ],
-        [g, counts, affine, yd, yw, ys, yp, mask, pool, late_points, coarse],
-        [((rows, 384), BF16), ((rows, 384), BF16), ((POINT, CONCAT), F32), ((8, 128), F32)],
+        [me_ref, g, counts, affine, yd, yw, ys, yp, mask, pool, coarse] + late_shares,
+        [
+            ((rows, 384), BF16), ((rows, 384), BF16),
+            ((groups, late_pack.point_rows, late_pack.point_tiles * 128), F32),
+            ((POINT, CONCAT), F32), ((8, 128), F32),
+        ],
+        us=15,
     )
     g = exchange(pay)
     lyd, lyp, tile = call(
         lambda *refs: other_points_kernel(LATE, clips, *refs),
         [((late_rows, DIRECT), F32), ((late_rows, PROJECT), F32), ((16, 128), F32)],
         [late_act, late_wt, coarse],
-    )
-    lbn, lbs, lyw, lys, pay, lst_r = second(LATE, 3, g, lyr, coarse, kw_late, ks_late, tile)
+        us=3.7,
+    )
+    lbn, lbs, lyw, lys, lkw, lks, pay, lst_r = second(LATE, 3, g, lyr, coarse, late_shares, tile)
     g = exchange(pay)
     widths = [TILE_ROW[unit][1] for unit in OUTER]
     res = call(
@@ -751,115 +1054,232 @@
         + [((devices, 16, 128), F32), ((16, 128), F32)],
         [g, counts, affine, lyd, lyw, lys, lyp, coarse] + ups,
         [((16, 128), F32)],
+        us=4,
     )
     outs, (hd, hw, hs, hp), (pay, lst) = res[:4], res[4:8], res[8:]
     g = exchange(pay)
 
-    def inner(geo, g, st, st_r, hw, hs, yw, ys, yr, kw, ks, masking):
+    out_parts = []
+    for o in outs:
+        cells = o.reshape(clips, LATE.frames, LATE.height, LATE.pitch, -1)[:, :, :, : LATE.width]
+        out_parts.append(cells.reshape(cells.shape[:4] + (groups, -1)))
+    out_joined = jnp.moveaxis(jnp.concatenate(out_parts, axis=5), 4, 0)
+    def finish(geo, g, st, st_r, hw, hs, yw, ys, masking, behind=()):
+        own = clips * geo.clip_rows
+        return call(
+            lambda *refs: finish_kernel(geo, clips, *refs),
+            [((own, WIDE), BF16), ((own, SPREAD), BF16), ((16, 128), F32)],
+            [g, st, st_r, affine, hw, hs, yw, ys, masking] + list(behind),
+            idle=len(behind),
+            us=7 if geo is EARLY else 2.5,
+        )
+
+    def inner(geo, st_r, gw, gs, yr, kw, ks, masking, behind=()):
         own = clips * geo.clip_rows
         padded = clips * geo.padded_rows
         return call(
-            lambda *refs: inner_backward_kernel(geo, clips, *refs),
-            [
-                ((own, WIDE), BF16), ((own, SPREAD), BF16), ((own, REDUCED), F32),
-                ((devices, 8, 128), F32), ((16, 128), F32),
-            ],
-            [g, st, st_r, affine, hw, hs, yw, ys, yr, kw, ks, masking],
+            lambda *refs: inner_backward_kernel(geo, clips, pack, *refs),
+            [((own, REDUCED), F32), ((devices, 8, 128), F32)],
+            [st_r, affine, gw, gs, yr, kw, ks, masking] + list(behind),
             [
                 ((padded, 9 * WIDE), BF16), ((padded, 9 * SPREAD), BF16),
                 ((3, 9 * WIDE, NARROW), BF16), ((3, 9 * SPREAD, SQUEEZE), BF16),
                 ((own, REDUCED), F32), ((8, 128), F32),
             ],
+            idle=len(behind),
+            us=16 if geo is EARLY else 5.6,
         )
 
-    def kernel_grads(geo, gw, gs, bn, bs):
+    unit = 16 * batches
+
+    def kernel_grads(geo, size, gw, gs, bn, bs):
         return call(
-            lambda *refs: kernel_grad_kernel(geo, clips, *refs),
-            [((WIDE, WIDE_COLUMNS), BF16), ((SPREAD, SPREAD_COLUMNS), BF16)],
-            [gw, gs, bn, bs],
+            lambda *refs: kernel_grad_kernel(geo, clips, pack, *refs),
+            [((groups // 2, size, 128), BF16)] * 2,
+            [me_ref, gw, gs, bn, bs],
+            [((3, WIDE, 128 * WIDE_TILES), F32), ((3, SPREAD, 128 * SPREAD_TILES), F32)],
+            us=10 if geo is EARLY else 5,
         )
 
-    def point_grads(gy, act):
+    def point_grads(use, start, size, gy, act, others=()):
         return call(
-            lambda *refs: point_grad_kernel(groups, *refs),
-            [((POINT, act.shape[1]), BF16)],
-            [gy, act],
-            [((POINT, act.shape[1]), F32)],
-        )[0]
-
-    def reduced(value):
-        part = lax.psum_scatter(value, "ch", scatter_dimension=0, tiled=True)
-        return lax.psum(part, "batch")
-
-    gw, gs, hr, pay, late_sums = inner(
-        LATE, g, lst, lst_r, hw, hs, lyw, lys, lyr, kw_late, ks_late, coarse
-    )
+            lambda *refs: point_grad_kernel(use, start, *refs),
+            [((groups // 2, size, 128), BF16)] * 2,
+            [me_ref, gy, act] + list(others),
+            [((POINT, use.features), F32), ((groups, use.point_rows, use.point_tiles * 128), F32)],
+            us=4.5,
+        )
+
+    class Reduction:
+        def __init__(self, keep, send):
+            self.keep, self.bit = keep, 1
+            self.got = swap(send, 1)
+
+        def halve(self, *behind):
+            while 2 * self.bit < groups:
+                shape = (self.keep.shape[0] // 2,) + self.keep.shape[1:]
+                self.keep, send = call(
+                    halve_kernel, [(shape, BF16)] * 2, [self.keep, self.got] + list(behind),
+                    idle=len(behind),
+                    us=2.5,
+                )
+                self.bit *= 2
+                self.got = swap(send, self.bit)
+            return self.keep
+
+        def add(self, *behind):
+            return call(
+                add_kernel, [(self.keep.shape[1:], BF16)], [self.keep, self.got] + list(behind),
+                idle=len(behind),
+                us=2,
+            )[0]
+
+    mb_ref = jnp.reshape(lax.axis_index("batch"), (1,)).astype(jnp.int32)
+
+    def batch_swap(value, bit):
+        return lax.ppermute(value, "batch", [(i, i ^ bit) for i in range(batches)])
+
+    def whole_units(size):
+        return -(-size // unit) * unit
+
+    gw, gs, late_sums = finish(LATE, g, lst, lst_r, hw, hs, lyw, lys, coarse)
+    hr, pay = inner(LATE, lst_r, gw, gs, lyr, lkw, lks, coarse)
     g = exchange(pay)
-    late_kw_grad, late_ks_grad = kernel_grads(LATE, gw, gs, lbn, lbs)
+    late_halves = kernel_grads(LATE, pack.kernels, gw, gs, lbn, lbs)
+    out_arrived = ordered(lax.all_to_all(out_joined, "ch", 0, 0))
     gy, ed, ew, es, ep, pay, late_sums_r = call(
         lambda *refs: late_input_kernel(clips, *refs),
         [((late_rows, POINT), BF16)]
         + [((rows, w), F32) for w in widths]
         + [((devices, 16, 128), F32), ((8, 128), F32)],
         [g, late_sums, lst, lst_r, affine, hr, hd, hp, lyr, lyd, lyp, coarse, late_wt, spread_back,
-         st, yd, yw, ys, yp, mask],
+         st, yd, yw, ys, yp, mask, late_halves[1], out_arrived],
         [((late_rows, PROJECT), F32), ((late_rows, CONCAT), BF16), ((rows, WIDE), F32), ((16, 128), F32)],
+        idle=2,
+        us=15,
     )
     g = exchange(pay)
-    late_point_grad = point_grads(gy, late_act)
-    gw, gs, hr, pay, sums = inner(EARLY, g, st, st_r, ew, es, yw, ys, yr, kw_early, ks_early, mask)
+    late_size = whole_units(late_pack.kernels + late_pack.points)
+    late_halves = point_grads(late_pack, late_pack.kernels, late_size, gy, late_act, late_halves)
+    late_sum = Reduction(*late_halves)
+    gw, gs, sums = finish(EARLY, g, st, st_r, ew, es, yw, ys, mask, late_halves[1:])
+    halves = kernel_grads(EARLY, whole_units(pack.kernels), gw, gs, bn, bs)
+    early_sum = Reduction(*halves)
+    kept = late_sum.halve(halves[1])
+    hr, pay = inner(EARLY, st_r, gw, gs, yr, kw, ks, mask, behind=(halves[1], kept))
     g = exchange(pay)
-    kw_grad, ks_grad = kernel_grads(EARLY, gw, gs, bn, bs)
-    gy, x_grad, sums_r = call(
-        lambda *refs: early_input_kernel(groups, clips, *refs),
-        [((rows, POINT), BF16), ((groups, depth, rows), BF16), ((8, 128), F32)],
-        [g, sums, st, st_r, affine, hr, ed, ep, yr, yd, yp, mask, wt],
-        [((rows, PROJECT), F32)],
-    )
-    x_arrived = lax.all_to_all(x_grad, "ch", 0, 0)
-    point_grad = point_grads(gy, act)
+    kept = early_sum.halve(hr)
+    late_piece = late_sum.keep.shape[1] // batches
+    late_keep, late_send = call(
+        scatter_halves_kernel,
+        [((batches // 2, late_piece, 128), BF16)] * 2,
+        [mb_ref, late_sum.keep, late_sum.got, hr],
+        [(late_sum.keep.shape[1:], F32)],
+        us=3,
+        idle=1,
+    )
+
+    class BatchHalves(Reduction):
+        def __init__(self, keep, send):
+            self.keep, self.bit = keep, 1
+            self.got = batch_swap(send, 1)
+
+        def step(self, *behind):
+            shape = (self.keep.shape[0] // 2,) + self.keep.shape[1:]
+            self.keep, send = call(
+                halve_kernel, [(shape, BF16)] * 2, [self.keep, self.got] + list(behind),
+                idle=len(behind), us=1.5,
+            )
+            self.bit *= 2
+            self.got = batch_swap(send, self.bit)
+            return self.keep
+
+    late_sum = BatchHalves(late_keep, late_send)
+    gy, *x_parts, sums_r = call(
+        lambda *refs: early_input_kernel(pack, clips, *refs),
+        [((rows, POINT), BF16)] + [((depth, rows), BF16)] * groups + [((8, 128), F32)],
+        [me_ref, g, sums, st, st_r, affine, hr, ed, ep, yr, yd, yp, mask, wt, kept, late_keep],
+        [((rows, PROJECT), F32), ((groups, depth, rows), BF16)],
+        idle=2,
+        us=8.5,
+    )
+    x_parts = [x_parts[0]] + [swap(x_parts[k], k) for k in range(1, groups)]
+    point_halves = point_grads(pack, 0, whole_units(pack.points), gy, act)
+    point_sum = Reduction(*point_halves)
+    kept = late_sum.step(point_halves[1])
+    own = early_sum.add(point_halves[1], kept)
+    parts = lax.all_to_all(own.reshape(batches, -1, 128), "batch", 0, 0)
+    kept = point_sum.halve(own)
+    late_kept = late_sum.step(kept)
+    while 2 * late_sum.bit < batches:
+        late_kept = late_sum.step()
     (feature_grad,) = call(
-        lambda *refs: feature_kernel(groups, *refs),
+        lambda *refs: feature_kernel(pack, *refs),
         [((depth, groups * rows), F32)],
-        [x_arrived],
-    )
-
-    out_parts = []
-    for o in outs:
-        cells = o.reshape(clips, LATE.frames, LATE.height, LATE.pitch, -1)[:, :, :, : LATE.width]
-        out_parts.append(cells.reshape(cells.shape[:4] + (groups, -1)))
-    out_joined = jnp.moveaxis(jnp.concatenate(out_parts, axis=5), 4, 0)
-    out_arrived = lax.all_to_all(out_joined, "ch", 0, 0)
+        [me_ref] + x_parts + [own, late_kept],
+        [((groups, depth, rows), BF16)],
+        idle=2,
+        us=2,
+    )
+    points_size = kept.shape[1] // batches
+    pieces = call(
+        scatter_kernel,
+        [((points_size, 128), BF16)] * batches,
+        [mb_ref, point_sum.keep, point_sum.got],
+        [(kept.shape[1:], F32)],
+        us=1.5,
+    )
+    pieces = [pieces[0]] + [batch_swap(pieces[k], k) for k in range(1, batches)]
+    late_own = late_sum.add(pieces[0])
+    late_pieces, bit = {0: late_own}, batches // 2
+    while bit:
+        for k in list(late_pieces):
+            late_pieces[k | bit] = batch_swap(late_pieces[k], bit)
+        bit //= 2
+    late_pieces = [late_pieces[k] for k in range(batches)]
+    kernels_size = parts.shape[1]
+    (parts,) = call(
+        total_kernel,
+        [((batches, kernels_size + points_size, 128), BF16)],
+        [parts] + list(pieces) + [feature_grad],
+        us=2,
+        idle=1,
+    )
+    early_total = lax.all_to_all(parts, "batch", 0, 0)
     out_arrived = out_arrived.reshape((held_clips,) + out_arrived.shape[2:])
     outputs, at = [], 0
     for part in upstream:
         outputs.append(out_arrived[..., at : at + part.shape[4]])
         at += part.shape[4]
 
-    def point_outputs(value, parts):
-        value = reduced(value).astype(F32)
-        result, at = [], 0
-        for part in parts:
-            width = part.shape[1]
-            result.append(value[at : at + width].T)
-            at += width
-        return result
-
-    early_grads = point_outputs(
-        point_grad, (direct_early, narrow_early, squeeze_early, project_early)
-    )
-    late_grads = point_outputs(late_point_grad, (direct_late, narrow_late, squeeze_late, project_late))
-    wide_grad = jnp.stack([reduced(kw_grad), reduced(late_kw_grad)]).astype(F32)
-    wide_grad = wide_grad.reshape(wide_kernels.shape)
-    spread_grad = jnp.stack([reduced(ks_grad), reduced(late_ks_grad)]).astype(F32)
-    spread_grad = jnp.transpose(spread_grad, (0, 2, 1)).reshape(spread_kernels.shape)
+    late_wide, late_spread, *late_grads = call(
+        lambda *refs: late_gradients_kernel(late_pack, batches, *refs),
+        [((pack.wide, WIDE_COLUMNS), F32), ((SPREAD_COLUMNS, pack.spread), F32)]
+        + [(part.shape[::-1], F32) for part in late_parts],
+        [mb_ref] + late_pieces,
+        [((batches, late_piece, 128), BF16), ((pack.spread, SPREAD_COLUMNS), F32)],
+        us=4,
+    )
+    wide_grad, early_spread, *early_grads = call(
+        lambda *refs: early_gradients_kernel(pack, kernels_size, *refs),
+        [(wide_kernels.shape, F32), ((SPREAD_COLUMNS, pack.spread), F32)]
+        + [(part.shape[::-1], F32) for part in early_parts],
+        [early_total, late_wide],
+        [
+            ((batches * kernels_size, 128), BF16), ((batches * points_size, 128), BF16),
+            ((pack.wide, WIDE_COLUMNS), F32), ((pack.spread, SPREAD_COLUMNS), F32),
+        ],
+        us=8,
+    )
+    early_grads = [part.T for part in early_grads]
+    late_grads = [part.T for part in late_grads]
+    spread_grad = jnp.stack(
+        [part.reshape(spread_kernels.shape[1:]) for part in (early_spread, late_spread)]
+    )
 
     def outer_pair(tile, unit):
         first, width = TILE_ROW[unit]
-        return [
-            jnp.stack([tile[k : k + 3].reshape(-1)[:width] for k in (base, base + 8)])
-            for base in (first,)
-        ][0]
+        return jnp.stack([tile[k : k + 3].reshape(-1)[:width] for k in (first, first + 8)])
 
     def inner_pair(tile, low, high):
         return jnp.stack([tile[k : k + 2].reshape(-1)[low:high] for k in (0, 4)])

time: 702 us -> 446 us (0.64)
  waiting for transfers between devices: 327 us -> 86 us
  blocking collectives: 94 us -> 8.75 us
  Pallas kernels: 153 us -> 209 us
  starting transfers between devices: 38.6 us -> 81.8 us
  between operations: 15.4 us -> 1.72 us
  local copies, waits for them, and re-layouts: 50.9 us -> 42.8 us
    psum x2 -> x0, waiting for transfers between devices: 197 us -> none  [reduced(): return lax.psum(part, 'batch')]
    reduce_scatter x6 -> x0, waiting for transfers between devices: 98.5 us -> none  [reduced(): part = lax.psum_scatter(value, 'ch', scatter_dimension=0, tiled=True)]
    all_gather x5 -> x0, blocking collectives: 68.7 us -> none  [the longest x1 30.8 us: shards(): lax.all_gather(jnp.concatenate(norms, axis=2), 'ch', axis=0).astype(F32)]
    pallas_call x17 -> x38, Pallas kernels: 153 us -> 209 us  [the longest x34 209 us: call(): pl.pallas_call(body, out_shape=[jax.ShapeDtypeStruct(s, d) for s, d in ou...]
    ppermute x0 -> x35, waiting for transfers between devices: none -> 53.6 us  [the longest x17 44.4 us: batch_swap(): return lax.ppermute(value, 'batch', [(i, i ^ bit) for i in range(batches)])]
    ppermute x0 -> x35, starting transfers between devices: none -> 38.2 us  [the longest x17 26.5 us: batch_swap(): return lax.ppermute(value, 'batch', [(i, i ^ bit) for i in range(batches)])]
    all_to_all x2 -> x1, blocking collectives: 25.4 us -> 8.75 us  [shards(): out_arrived = ordered(lax.all_to_all(out_joined, 'ch', 0, 0))]
    slice x7 -> x0, local copies, waits for them, and re-layouts: 16.3 us -> none  [the longest x1 15.9 us: shards(): kw_late = gathered(wide_rows[1])]
  transfers between devices with their start and end apart: 20 -> 47, of which waited for: 11 -> 17; matrix products, arithmetic and copies ran while one was open for 5% -> 6% of each run, Pallas kernels for 18% -> 35%
where the time goes in v2:
time: 446 us; the launch traced here: 439 us
  Pallas kernels  209 us (47%)
  waiting for transfers between devices  86 us (19%)
  starting transfers between devices  81.8 us (18%)
  local copies, waits for them, and re-layouts  42.8 us (10%)
  other arithmetic  9.06 us (2%)
  blocking collectives  8.75 us (2%)
    pallas_call x34, Pallas kernels, call(): pl.pallas_call(body, out_shape=[jax.ShapeDtypeStruct(s, d) for s, d in ou...  209 us
    ppermute x17, waiting for transfers between devices, batch_swap(): return lax.ppermute(value, 'batch', [(i, i ^ bit) for i in range(batches)])  44.4 us
    all_to_all x8, waiting for transfers between devices, exchange(): return lax.all_to_all(payload, BOTH, 0, 0)  30.9 us
    all_to_all x8, starting transfers between devices, exchange(): return lax.all_to_all(payload, BOTH, 0, 0)  29.3 us
    ppermute x17, starting transfers between devices, batch_swap(): return lax.ppermute(value, 'batch', [(i, i ^ bit) for i in range(batches)])  26.5 us
    unnamed x141, local copies, waits for them, and re-layouts  23.1 us
    ppermute x18, starting transfers between devices, swap(): return lax.ppermute(value, 'ch', [(i, i ^ bit) for i in range(groups)])  11.7 us
    ppermute x18, waiting for transfers between devices, swap(): return lax.ppermute(value, 'ch', [(i, i ^ bit) for i in range(groups)])  9.18 us
  transfers between devices with their start and end apart: 47, of which 17 were waited for; matrix products, arithmetic and copies ran while one was open for 6% of the time, Pallas kernels for 35%

profile of v2, /device:TPU:0, one launch (start us, length us, event | category | flops | bytes accessed | tf_op | source)
XLA Modules:
  0.0 439.0 jit_solution(16228184679839049559)
XLA Ops:
  2.1 2.5 shard_map.391
  4.6 3.0 collective-permute-start.1
  7.6 3.5 all-to-all-start
  12.9 4.8 %shard_map.394 = (bf16[2700,128]{1,0:T(8,128)(2,1)}, bf16[2700,128]{1,0:T(8,128)(2,1)}) custom-call(bf16[2,345600]{1,0:T(2,128)(2,1)} %refs_0_.3, bf16[4,132,1152]{2,1,0:T(8,128)(2,1)} %get-tuple-element.130.refs_1_), custom_call_target="tpu_custom_call" | custom-call | flops 5280000000 | bytes 2764800 | tf_op jit(solution)/shard_map/pallas_call | solution.py:68
  17.7 2.9 reshape.199.refs_0_
  23.9 2.3 shard_map.395.refs_0_
  31.4 8.7 %shard_map.392 = (bf16[1152,528]{1,0:T(8,128)(2,1)}, bf16[576,528]{1,0:T(8,128)(2,1)}, f32[4,1152]{1,0:T(4,128)}, f32[1152,192]{1,0:T(8,128)}, f32[32,8,128]{2,1,0:T(8,128)}) custom-call(s32[1]{0:T(128)} %bitcast.refs_0_, bf16[4,132,1152]{2,1,0:T(8,128)(2,1)} %copy-done, bf16[736,128]{1,0:T(8,128)(2,1)} %get-tuple-element.131.refs_2_, ...), custom_call_target="tpu_custom_call" | custom-call | flops 9459999744 | bytes 5517316 | tf_op jit(solution)/shard_map/pallas_call | solution.py:68
  40.1 5.8 %all-to-all-start.1 = ((f32[32,8,128]{2,1,0:T(8,128)}), f32[32,8,128]{2,1,0:T(8,128)S(1)}, u32[]{:S(2)}, u32[]{:S(2)}) async-start(f32[32,8,128]{2,1,0:T(8,128)} %get-tuple-element.132), calls=%async_computation.1 | async-start | bytes 262144 | tf_op jit(solution)/shard_map/all_to_all | solution.py:907
  45.9 2.7 collective-permute-done.4.refs_9_
  48.6 12.7 %shard_map.393 = (f32[1152,256]{1,0:T(8,128)}, f32[1152,128]{1,0:T(8,128)}, f32[16,128]{1,0:T(8,128)}) custom-call(bf16[1152,528]{1,0:T(8,128)(2,1)} %get-tuple-element.135.refs_0_.refs_6_.refs_2_, bf16[576,528]{1,0:T(8,128)(2,1)} %get-tuple-element.136.refs_1_.refs_13_, f32[1152,128]{1,0:T(8,128)} %broadcast_in_dim.16.refs_6_.refs_2_.refs_5_.refs_8_.refs_19_.refs_7_.refs_12_), custom_call_target="tpu_custom_call" | custom-call | flops 13200000000 | bytes 4192256 | tf_op jit(solution)/shard_map/pallas_call | solution.py:68
  61.3 2.5 shard_map.398.refs_0_
  66.0 24.9 %shard_map.397 = (bf16[1728,1536]{1,0:T(8,128)(2,1)}, bf16[1728,384]{1,0:T(8,128)(2,1)}, f32[1152,320]{1,0:T(8,128)}, f32[1152,128]{1,0:T(8,128)}, bf16[3,4,80,1...) custom-call(s32[1]{0:T(128)} %bitcast.refs_0_, ...), custom_call_target="tpu_custom_call" | custom-call | flops 27499999232 | bytes 17217540 | tf_op jit(solution)/shard_map/pallas_call | solution.py:68
  92.5 6.2 %all-to-all-start.2 = ((f32[32,16,128]{2,1,0:T(8,128)}), f32[32,16,128]{2,1,0:T(8,128)S(1)}, u32[]{:S(2)}, u32[]{:S(2)}) async-start(f32[32,16,128]{2,1,0:T(8,128)} %get-tuple-element.139), calls=%async_computation.2 | async-start | bytes 524288 | tf_op jit(solution)/shard_map/all_to_all | solution.py:907
  100.6 8.7 %all-to-all-done.2.refs_1_ = f32[32,16,128]{2,1,0:T(8,128)S(1)} async-done(((f32[32,16,128]{2,1,0:T(8,128)}), f32[32,16,128]{2,1,0:T(8,128)S(1)}, u32[]{:S(2)}, u32[]{:S(2)}) %all-to-all-start.2) | async-done | bytes 262176 | tf_op jit(solution)/shard_map/all_to_all | solution.py:907
  110.1 15.3 %shard_map.401 = (bf16[192,832]{1,0:T(8,128)(2,1)}, bf16[576,832]{1,0:T(8,128)(2,1)}, f32[192,192]{1,0:T(8,128)}, f32[32,8,128]{2,1,0:T(8,128)}, f32[16,128]{1,0:T(8,128)}) custom-call(s32[1]{0:T(128)} %bitcast.refs_0_, f32[32,16,128]{2,1,0:T(8,128)} %copy-done.11, f32[32,8,128]{2,1,0:T(8,128)} %copy-done.5, ...), custom_call_target="tpu_custom_call" | custom-call | flops 16499999744 | bytes 10885124 | tf_op jit(solution)/shard_map/pallas_call | solution.py:68
  125.3 2.6 all-to-all-start.3
  127.9 3.7 shard_map.402
  131.6 4.5 %all-to-all-done.3.refs_1_ = f32[32,8,128]{2,1,0:T(8,128)S(1)} async-done(((f32[32,8,128]{2,1,0:T(8,128)}), f32[32,8,128]{2,1,0:T(8,128)S(1)}, u32[]{:S(2)}, u32[]{:S(2)}) %all-to-all-start.3) | async-done | bytes 131104 | tf_op jit(solution)/shard_map/all_to_all | solution.py:907
  136.2 3.5 all-to-all-start.5
  139.6 9.4 %shard_map.403 = (bf16[384,1536]{1,0:T(8,128)(2,1)}, bf16[384,384]{1,0:T(8,128)(2,1)}, f32[192,320]{1,0:T(8,128)}, f32[192,128]{1,0:T(8,128)}, bf16[3,4,80,1536]...) custom-call(s32[1]{0:T(128)} %bitcast.refs_0_, ...), custom_call_target="tpu_custom_call" | custom-call | flops 9900000256 | bytes 10139652 | tf_op jit(solution)/shard_map/pallas_call | solution.py:68
  149.1 3.1 all-to-all-start.4
  156.4 6.4 %all-to-all-done.4.refs_0_ = f32[32,16,128]{2,1,0:T(8,128)S(1)} async-done(((f32[32,16,128]{2,1,0:T(8,128)}), f32[32,16,128]{2,1,0:T(8,128)S(1)}, u32[]{:S(2)}, u32[]{:S(2)}) %all-to-all-start.4) | async-done | bytes 262176 | tf_op jit(solution)/shard_map/all_to_all | solution.py:907
  163.5 3.9 shard_map.404
  172.4 8.8 %all_to_all.65 = bf16[4,2,2,6,6,208]{5,2,4,3,1,0:T(2,128)(2,1)S(1)} all-to-all(bf16[4,2,2,6,6,208]{5,2,4,3,1,0:T(2,128)(2,1)S(1)} %copy.92), channel_id=1, replica_groups=mesh['batch'=8,'ch'=4] {'ch'}, dimensions={0} | all-to-all | bytes 479232 | tf_op jit(solution)/shard_map/all_to_all | solution.py:1149
  181.2 3.0 all-to-all-start.7
  191.4 3.4 all-to-all-done.7.refs_0_
  195.5 2.5 shard_map.406
  199.5 5.6 %shard_map.407 = (f32[192,192]{1,0:T(8,128)}, f32[32,8,128]{2,1,0:T(8,128)}) custom-call(f32[8,128]{1,0:T(8,128)} %get-tuple-element.160.refs_2_.refs_0_.refs_3_, f32[4,1152]{1,0:T(4,128)} %get-tuple-element.133.refs_3_.refs_2_.refs_1_.refs_4_.refs_5_, bf16[192,320]{1,0:T(8,128)(2,1)} %get-tuple-element.165.refs_2_.refs_1_, ...), custom_call_target="tpu_custom_call" | custom-call | flops 6160000000 | bytes 3962880 | tf_op jit(solution)/shard_map/pallas_call | solution.py:68
  205.1 2.6 all-to-all-start.8
  207.7 5.0 %shard_map.408 = (bf16[2,3168,128]{2,1,0:T(8,128)(2,1)}, bf16[2,3168,128]{2,1,0:T(8,128)(2,1)}) custom-call(s32[1]{0:T(128)} %bitcast.refs_0_, bf16[192,320]{1,0:T(8,128)(2,1)} %get-tuple-element.165.refs_2_.refs_1_, bf16[192,128]{1,0:T(8,128)(2,1)} %get-tuple-element.166.refs_3_.refs_2_, bf16[384,1536]{1,0:T(8,128)(2,1)} %get-tuple-element.175.refs_3_, ...), custom_call_target="tpu_custom_call" | custom-call | flops 5500000256 | bytes 4890628 | tf_op jit(solution)/shard_map/pallas_call | solution.py:68
  213.4 2.5 all-to-all-done.8.refs_0_
  216.6 15.6 %shard_map.409 = (bf16[192,576]{1,0:T(8,128)(2,1)}, f32[1152,256]{1,0:T(8,128)}, f32[1152,320]{1,0:T(8,128)}, f32[1152,128]{1,0:T(8,128)}, f32[1152,128]{1,0:T(8...) custom-call(f32[32,8,128]{2,1,0:T(8,128)} %copy-done.18, f32[16,128]{1,0:T(8,128)} %get-tuple-element.170.refs_1_, ...), custom_call_target="tpu_custom_call" | custom-call | flops 16499999744 | bytes 10975232 | tf_op jit(solution)/shard_map/pallas_call | solution.py:68
  232.1 3.4 all-to-all-start.9
  235.5 4.9 %shard_map.410 = (bf16[2,4224,128]{2,1,0:T(8,128)(2,1)}, bf16[2,4224,128]{2,1,0:T(8,128)(2,1)}) custom-call(s32[1]{0:T(128)} %bitcast.refs_0_, bf16[192,576]{1,0:T(8,128)(2,1)} %get-tuple-element.181.refs_1_, bf16[192,832]{1,0:T(8,128)(2,1)} %get-tuple-element.148.refs_0_.refs_2_, bf16[2,3168,128]{2,1,0:T(8,128)(2,1)} %get-tuple-element.182.refs_3_, ...), custom_call_target="tpu_custom_call" | custom-call | flops 4950000128 | bytes 8110084 | tf_op jit(solution)/shard_map/pallas_call | solution.py:68
  240.7 5.3 %all-to-all-done.9.refs_0_ = f32[32,16,128]{2,1,0:T(8,128)S(1)} async-done(((f32[32,16,128]{2,1,0:T(8,128)}), f32[32,16,128]{2,1,0:T(8,128)S(1)}, u32[]{:S(2)}, u32[]{:S(2)}) %all-to-all-start.9) | async-done | bytes 262176 | tf_op jit(solution)/shard_map/all_to_all | solution.py:907
  246.8 7.3 %shard_map.411 = (bf16[1152,320]{1,0:T(8,128)(2,1)}, bf16[1152,128]{1,0:T(8,128)(2,1)}, f32[16,128]{1,0:T(8,128)}) custom-call(f32[32,16,128]{2,1,0:T(8,128)} %copy-done.10, f32[16,128]{1,0:T(8,128)} %get-tuple-element.174.refs_14_.refs_1_.refs_3_, f32[8,128]{1,0:T(8,128)} %get-tuple-element.145.refs_1_.refs_2_.refs_0_.refs_4_, ...), custom_call_target="tpu_custom_call" | custom-call | flops 7699999744 | bytes 6051840 | tf_op jit(solution)/shard_map/pallas_call | solution.py:68
  254.1 10.4 %shard_map.412 = (bf16[2,3200,128]{2,1,0:T(8,128)(2,1)}, bf16[2,3200,128]{2,1,0:T(8,128)(2,1)}) custom-call(s32[1]{0:T(128)} %bitcast.refs_0_, bf16[1152,320]{1,0:T(8,128)(2,1)} %get-tuple-element.184.refs_1_.refs_2_, bf16[1152,128]{1,0:T(8,128)(2,1)} %get-tuple-element.185.refs_2_.refs_3_, bf16[1728,1536]{1,0:T(8,128)(2,1)} %get-tuple-element.188.refs_3_, ...), custom_call_target="tpu_custom_call" | custom-call | flops 11000000512 | bytes 10944516 | tf_op jit(solution)/shard_map/pallas_call | solution.py:68
  266.6 3.9 shard_map.413
  271.2 16.5 %shard_map.414 = (f32[1152,192]{1,0:T(8,128)}, f32[32,8,128]{2,1,0:T(8,128)}) custom-call(f32[8,128]{1,0:T(8,128)} %get-tuple-element.145.refs_1_.refs_2_.refs_0_.refs_4_, f32[4,1152]{1,0:T(4,128)} %get-tuple-element.133.refs_3_.refs_2_.refs_1_.refs_4_.refs_5_, bf16[1152,320]{1,0:T(8,128)(2,1)} %get-tuple-element.184.refs_1_.refs_2_, ...), custom_call_target="tpu_custom_call" | custom-call | flops 17600000000 | bytes 6789120 | tf_op jit(solution)/shard_map/pallas_call | solution.py:68
  287.7 2.6 all-to-all-start.10
  290.3 3.3 shard_map.415
  295.3 3.1 collective-permute-done.11.refs_2_
  299.4 3.0 shard_map.416
  304.1 8.4 %shard_map.417 = (bf16[1152,576]{1,0:T(8,128)(2,1)}, bf16[132,1152]{1,0:T(8,128)(2,1)}, bf16[132,1152]{1,0:T(8,128)(2,1)}, bf16[132,1152]{1,0:T(8,128)(2,1)}, bf...) custom-call(s32[1]{0:T(128)} %bitcast.refs_0_, f32[32,8,128]{2,1,0:T(8,128)} %copy-done.17, ...), custom_call_target="tpu_custom_call" | custom-call | flops 9349999616 | bytes 9224196 | tf_op jit(solution)/shard_map/pallas_call | solution.py:68
  312.5 4.2 shard_map.418
  317.4 2.1 shard_map.419
  320.4 2.5 shard_map.420.refs_2_.refs_5_
  322.9 3.7 all-to-all-start.11
  327.4 2.0 shard_map.421
  334.0 3.3 collective-permute-done.19.refs_2_
  341.7 7.1 %collective-permute-done.17.refs_1_ = bf16[2,528,128]{2,1,0:T(8,128)(2,1)S(1)} collective-permute-done((bf16[2,528,128]{2,1,0:T(8,128)(2,1)S(1)}, bf16[2,528,128]{2,1,0:T(8,128)(2,1)S(1)}, u32[]{:S(2)}, u32[]{:S(2)}) %collective-permute-start.17) | collective-permute-done | bytes 270368 | tf_op jit(solution)/shard_map/ppermute | solution.py:1140
  353.6 2.6 collective-permute-start.23
  356.7 2.6 collective-permute-start.25
  359.4 2.2 collective-permute-start.26
  361.6 3.0 shard_map.423.refs_9_
  366.9 2.3 shard_map.425
  369.2 3.7 all-to-all-start.12
  374.2 2.8 collective-permute-start.27
  377.1 24.7 %collective-permute-done.27.refs_1_ = bf16[1,528,128]{2,1,0:T(8,128)(2,1)S(1)} collective-permute-done((bf16[1,528,128]{2,1,0:T(8,128)(2,1)S(1)}, bf16[1,528,128]{2,1,0:T(8,128)(2,1)S(1)}, u32[]{:S(2)}, u32[]{:S(2)}) %collective-permute-start.27) | collective-permute-done | bytes 135200 | tf_op jit(solution)/shard_map/ppermute | solution.py:1140
  406.0 4.8 %collective-permute-done.31.refs_5_ = bf16[528,128]{1,0:T(8,128)(2,1)S(1)} collective-permute-done((bf16[528,128]{1,0:T(8,128)(2,1)}, bf16[528,128]{1,0:T(8,128)(2,1)S(1)}, u32[]{:S(2)}, u32[]{:S(2)}) %collective-permute-start.31) | collective-permute-done | bytes 135200 | tf_op jit(solution)/shard_map/ppermute | solution.py:1140
  410.9 2.0 collective-permute-start.28
  419.1 4.0 collective-permute-done.30.refs_4_
  425.3 3.1 shard_map.427
  429.3 7.5 %shard_map.428 = (f32[2,345600]{1,0:T(2,128)}, f32[864,32]{1,0:T(8,128)}, f32[64,528]{1,0:T(8,128)}, f32[40,528]{1,0:T(8,128)}, f32[8,528]{1,0:T(8,128)}, /*index=5*/f32[32,528]{1,0:T(8,128)}) custom-call(bf16[8,496,128]{2,1,0:T(8,128)(2,1)} %copy-done.2, f32[80,4320]{1,0:T(8,128)} %get-tuple-element.225.refs_1_), custom_call_target="tpu_custom_call" | custom-call | flops 8800000000 | bytes 5577728 | tf_op jit(solution)/shard_map/pallas_call | solution.py:68
  (274 shorter events, 82.5 us)
Async XLA Ops:
  4.6 18.7 %collective-permute-start.1 = (bf16[736,128]{1,0:T(8,128)(2,1)}, bf16[736,128]{1,0:T(8,128)(2,1)S(1)}, u32[]{:S(2)}, u32[]{:S(2)}) collective-permute-start(bf16[736,128]{1,0:T(8,128)(2,1)} %get-tuple-element.131.refs_2_), channel_id=1, source_target_pairs={{0,2},{1,3},{2,0},{3,1},{4,6},{5,7},{6,4},{7,5},{8,10},{9,11},{10,... | collective-permute-start | bytes 565256 | tf_op jit(solution)/shard_map/ppermute | solution.py:910
  7.6 22.0 %collective-permute-start = (bf16[736,128]{1,0:T(8,128)(2,1)}, bf16[736,128]{1,0:T(8,128)(2,1)}, u32[]{:S(2)}, u32[]{:S(2)}) collective-permute-start(bf16[736,128]{1,0:T(8,128)(2,1)} %get-tuple-element.131.refs_2_), channel_id=1, source_target_pairs={{0,1},{1,0},{2,3},{3,2},{4,5},{5,4},{6,7},{7,6},{8,9},{9,8},{10,11... | collective-permute-start | bytes 565256 | tf_op jit(solution)/shard_map/ppermute | solution.py:910
  7.6 20.2 %all-to-all-start = ((bf16[4,132,1152]{2,1,0:T(8,128)(2,1)}), bf16[4,132,1152]{2,1,0:T(8,128)(2,1)S(1)}, u32[]{:S(2)}, u32[]{:S(2)}) async-start(bf16[4,132,1152]{2,1,0:T(8,128)(2,1)} %get-tuple-element.130.refs_1_), calls=%async_computation | async-start | bytes 2506752 | tf_op jit(solution)/shard_map/all_to_all | solution.py:942
  23.4 2.8 collective-permute-start.2
  28.8 19.8 %collective-permute-start.4 = (bf16[3168,128]{1,0:T(8,128)(2,1)}, bf16[3168,128]{1,0:T(8,128)(2,1)S(1)}, u32[]{:S(2)}, u32[]{:S(2)}) collective-permute-start(bf16[3168,128]{1,0:T(8,128)(2,1)} %shard_map.396.refs_7_), channel_id=1, source_target_pairs={{0,2},{1,3},{2,0},{3,1},{4,6},{5,7},{6,4},{7,5},{8,10},{9,11},{10,... | collective-permute-start | bytes 2433032 | tf_op jit(solution)/shard_map/ppermute | solution.py:910
  29.6 36.5 %collective-permute-start.3 = (bf16[3168,128]{1,0:T(8,128)(2,1)}, bf16[3168,128]{1,0:T(8,128)(2,1)}, u32[]{:S(2)}, u32[]{:S(2)}) collective-permute-start(bf16[3168,128]{1,0:T(8,128)(2,1)} %shard_map.396.refs_7_), channel_id=1, source_target_pairs={{0,1},{1,0},{2,3},{3,2},{4,5},{5,4},{6,7},{7,6},{8,9},{9,8},{10,11... | collective-permute-start | bytes 2433032 | tf_op jit(solution)/shard_map/ppermute | solution.py:910
  40.1 23.7 %all-to-all-start.1 = ((f32[32,8,128]{2,1,0:T(8,128)}), f32[32,8,128]{2,1,0:T(8,128)S(1)}, u32[]{:S(2)}, u32[]{:S(2)}) async-start(f32[32,8,128]{2,1,0:T(8,128)} %get-tuple-element.132), calls=%async_computation.1 | async-start | bytes 262144 | tf_op jit(solution)/shard_map/all_to_all | solution.py:907
  48.6 12.7 %copy-start.28 = (bf16[3168,128]{1,0:T(8,128)(2,1)}, bf16[3168,128]{1,0:T(8,128)(2,1)S(1)}, u32[]{:S(2)}) copy-start(bf16[3168,128]{1,0:T(8,128)(2,1)S(1)} %collective-permute-done.4.refs_9_) | copy-start | bytes 2433028
  48.6 17.4 %collective-permute-start.5 = (bf16[3168,128]{1,0:T(8,128)(2,1)S(1)}, bf16[3168,128]{1,0:T(8,128)(2,1)}, u32[]{:S(2)}, u32[]{:S(2)}) collective-permute-start(bf16[3168,128]{1,0:T(8,128)(2,1)S(1)} %collective-permute-done.4.refs_9_), channel_id=1, source_target_pairs={{0,1},{1,0},{2,3},{3,2},{4,5},{5,4},{6,7},{7,6},{8,9},{9,8},{10,11... | collective-permute-start | bytes 2433032 | tf_op jit(solution)/shard_map/ppermute | solution.py:910
  64.5 26.5 %collective-permute-start.7 = (bf16[4176,128]{1,0:T(8,128)(2,1)}, bf16[4176,128]{1,0:T(8,128)(2,1)S(1)}, u32[]{:S(2)}, u32[]{:S(2)}) collective-permute-start(bf16[4176,128]{1,0:T(8,128)(2,1)} %shard_map.399.refs_11_.refs_7_), channel_id=1, source_target_pairs={{0,2},{1,3},{2,0},{3,1},{4,6},{5,7},{6,4},{7,5},{8,10},{9,11},{10,... | collective-permute-start | bytes 3207176 | tf_op jit(solution)/shard_map/ppermute | solution.py:910
  66.0 34.6 %collective-permute-start.6 = (bf16[4176,128]{1,0:T(8,128)(2,1)}, bf16[4176,128]{1,0:T(8,128)(2,1)S(1)}, u32[]{:S(2)}, u32[]{:S(2)}) collective-permute-start(bf16[4176,128]{1,0:T(8,128)(2,1)} %shard_map.399.refs_11_.refs_7_), channel_id=1, source_target_pairs={{0,1},{1,0},{2,3},{3,2},{4,5},{5,4},{6,7},{7,6},{8,9},{9,8},{10,11... | collective-permute-start | bytes 3207176 | tf_op jit(solution)/shard_map/ppermute | solution.py:910
  90.9 7.8 %copy-start.13 = (bf16[8,2,6,6,32]{4,1,3,2,0:T(2,128)(2,1)S(1)}, bf16[8,2,6,6,32]{4,1,3,2,0:T(2,128)(2,1)}, u32[]{:S(2)}) copy-start(bf16[8,2,6,6,32]{4,1,3,2,0:T(2,128)(2,1)} %param.45) | copy-start | bytes 110596
  90.9 7.8 %copy-start.14 = (bf16[8,2,6,6,32]{4,1,3,2,0:T(2,128)(2,1)S(1)}, bf16[8,2,6,6,32]{4,1,3,2,0:T(2,128)(2,1)}, u32[]{:S(2)}) copy-start(bf16[8,2,6,6,32]{4,1,3,2,0:T(2,128)(2,1)} %param.44) | copy-start | bytes 110596
  91.0 7.8 %copy-start.15 = (bf16[8,2,6,6,80]{4,1,3,2,0:T(2,128)(2,1)S(1)}, bf16[8,2,6,6,80]{4,1,3,2,0:T(2,128)(2,1)}, u32[]{:S(2)}) copy-start(bf16[8,2,6,6,80]{4,1,3,2,0:T(2,128)(2,1)} %param.43) | copy-start | bytes 276484
  91.0 7.8 %copy-start.16 = (bf16[8,2,6,6,64]{4,1,3,2,0:T(2,128)(2,1)S(1)}, bf16[8,2,6,6,64]{4,1,3,2,0:T(2,128)(2,1)}, u32[]{:S(2)}) copy-start(bf16[8,2,6,6,64]{4,1,3,2,0:T(2,128)(2,1)} %param.42) | copy-start | bytes 221188
  92.0 17.3 %collective-permute-start.8 = (bf16[4176,128]{1,0:T(8,128)(2,1)}, bf16[4176,128]{1,0:T(8,128)(2,1)}, u32[]{:S(2)}, u32[]{:S(2)}) collective-permute-start(bf16[4176,128]{1,0:T(8,128)(2,1)} %shard_map.400.refs_13_.refs_9_), channel_id=1, source_target_pairs={{0,1},{1,0},{2,3},{3,2},{4,5},{5,4},{6,7},{7,6},{8,9},{9,8},{10,11... | collective-permute-start | bytes 3207176 | tf_op jit(solution)/shard_map/ppermute | solution.py:910
  92.5 16.8 %all-to-all-start.2 = ((f32[32,16,128]{2,1,0:T(8,128)}), f32[32,16,128]{2,1,0:T(8,128)S(1)}, u32[]{:S(2)}, u32[]{:S(2)}) async-start(f32[32,16,128]{2,1,0:T(8,128)} %get-tuple-element.139), calls=%async_computation.2 | async-start | bytes 524288 | tf_op jit(solution)/shard_map/all_to_all | solution.py:907
  100.6 8.8 %copy-start.26 = (bf16[4176,128]{1,0:T(8,128)(2,1)}, bf16[4176,128]{1,0:T(8,128)(2,1)S(1)}, u32[]{:S(2)}) copy-start(bf16[4176,128]{1,0:T(8,128)(2,1)S(1)} %collective-permute-done.6.refs_12_.refs_8_) | copy-start | bytes 3207172
  125.3 10.8 %all-to-all-start.3 = ((f32[32,8,128]{2,1,0:T(8,128)}), f32[32,8,128]{2,1,0:T(8,128)S(1)}, u32[]{:S(2)}, u32[]{:S(2)}) async-start(f32[32,8,128]{2,1,0:T(8,128)} %get-tuple-element.146), calls=%async_computation.3 | async-start | bytes 262144 | tf_op jit(solution)/shard_map/all_to_all | solution.py:907
  136.2 12.9 %all-to-all-start.5 = ((bf16[4,2,2,6,6,208]{5,2,4,3,1,0:T(2,128)(2,1)}), bf16[4,2,2,6,6,208]{5,2,4,3,1,0:T(2,128)(2,1)S(1)}, u32[]{:S(2)}, u32[]{:S(2)}) async-start(bf16[4,2,2,6,6,208]{5,2,4,3,1,0:T(2,128)(2,1)} %bitcast.14), calls=%async_computation.5 | async-start | bytes 589824 | tf_op jit(solution)/shard_map/all_to_all | solution.py:972
  149.1 13.7 %all-to-all-start.4 = ((f32[32,16,128]{2,1,0:T(8,128)}), f32[32,16,128]{2,1,0:T(8,128)S(1)}, u32[]{:S(2)}, u32[]{:S(2)}) async-start(f32[32,16,128]{2,1,0:T(8,128)} %get-tuple-element.151), calls=%async_computation.4 | async-start | bytes 524288 | tf_op jit(solution)/shard_map/all_to_all | solution.py:907
  181.2 13.6 %all-to-all-start.7 = ((f32[32,16,128]{2,1,0:T(8,128)}), f32[32,16,128]{2,1,0:T(8,128)S(1)}, u32[]{:S(2)}, u32[]{:S(2)}) async-start(f32[32,16,128]{2,1,0:T(8,128)} %get-tuple-element.161), calls=%async_computation.7 | async-start | bytes 524288 | tf_op jit(solution)/shard_map/all_to_all | solution.py:907
  205.1 10.8 %all-to-all-start.8 = ((f32[32,8,128]{2,1,0:T(8,128)}), f32[32,8,128]{2,1,0:T(8,128)S(1)}, u32[]{:S(2)}, u32[]{:S(2)}) async-start(f32[32,8,128]{2,1,0:T(8,128)} %get-tuple-element.169), calls=%async_computation.8 | async-start | bytes 262144 | tf_op jit(solution)/shard_map/all_to_all | solution.py:907
  232.1 14.0 %all-to-all-start.9 = ((f32[32,16,128]{2,1,0:T(8,128)}), f32[32,16,128]{2,1,0:T(8,128)S(1)}, u32[]{:S(2)}, u32[]{:S(2)}) async-start(f32[32,16,128]{2,1,0:T(8,128)} %get-tuple-element.178), calls=%async_computation.9 | async-start | bytes 524288 | tf_op jit(solution)/shard_map/all_to_all | solution.py:907
  240.4 24.8 %collective-permute-start.9 = (bf16[2,4224,128]{2,1,0:T(8,128)(2,1)}, bf16[2,4224,128]{2,1,0:T(8,128)(2,1)S(1)}, u32[]{:S(2)}, u32[]{:S(2)}) collective-permute-start(bf16[2,4224,128]{2,1,0:T(8,128)(2,1)} %get-tuple-element.183.refs_9_), channel_id=1, source_target_pairs={{0,1},{1,0},{2,3},{3,2},{4,5},{5,4},{6,7},{7,6},{8,9},{9,8},{10,11... | collective-permute-start | bytes 6488072 | tf_op jit(solution)/shard_map/ppermute | solution.py:910
  254.1 10.4 %copy-start.20 = (f32[16,128]{1,0:T(8,128)S(1)}, f32[16,128]{1,0:T(8,128)}, u32[]{:S(2)}) copy-start(f32[16,128]{1,0:T(8,128)} %get-tuple-element.194.refs_2_) | copy-start | bytes 24580
  264.5 25.8 %collective-permute-start.10 = (bf16[2,3200,128]{2,1,0:T(8,128)(2,1)}, bf16[2,3200,128]{2,1,0:T(8,128)(2,1)}, u32[]{:S(2)}, u32[]{:S(2)}) collective-permute-start(bf16[2,3200,128]{2,1,0:T(8,128)(2,1)} %get-tuple-element.190.refs_2_.refs_8_), channel_id=1, source_target_pairs={{0,1},{1,0},{2,3},{3,2},{4,5},{5,4},{6,7},{7,6},{8,9},{9,8},{10,11... | collective-permute-start | bytes 4915208 | tf_op jit(solution)/shard_map/ppermute | solution.py:910
  270.4 28.0 %collective-permute-start.11 = (bf16[1,4224,128]{2,1,0:T(8,128)(2,1)}, bf16[1,4224,128]{2,1,0:T(8,128)(2,1)S(1)}, u32[]{:S(2)}, u32[]{:S(2)}) collective-permute-start(bf16[1,4224,128]{2,1,0:T(8,128)(2,1)} %get-tuple-element.200), channel_id=1, source_target_pairs={{0,2},{1,3},{2,0},{3,1},{4,6},{5,7},{6,4},{7,5},{8,10},{9,11},{10,... | collective-permute-start | bytes 3244040 | tf_op jit(solution)/shard_map/ppermute | solution.py:910
  287.7 15.7 %all-to-all-start.10 = ((f32[32,8,128]{2,1,0:T(8,128)}), f32[32,8,128]{2,1,0:T(8,128)S(1)}, u32[]{:S(2)}, u32[]{:S(2)}) async-start(f32[32,8,128]{2,1,0:T(8,128)} %get-tuple-element.193), calls=%async_computation.10 | async-start | bytes 262144 | tf_op jit(solution)/shard_map/all_to_all | solution.py:907
  293.6 25.9 %collective-permute-start.15 = (bf16[1,3200,128]{2,1,0:T(8,128)(2,1)}, bf16[1,3200,128]{2,1,0:T(8,128)(2,1)S(1)}, u32[]{:S(2)}, u32[]{:S(2)}) collective-permute-start(bf16[1,3200,128]{2,1,0:T(8,128)(2,1)} %get-tuple-element.206), channel_id=1, source_target_pairs={{0,2},{1,3},{2,0},{3,1},{4,6},{5,7},{6,4},{7,5},{8,10},{9,11},{10,... | collective-permute-start | bytes 2457608 | tf_op jit(solution)/shard_map/ppermute | solution.py:910
  302.4 14.2 %collective-permute-start.16 = (bf16[4,528,128]{2,1,0:T(8,128)(2,1)}, bf16[4,528,128]{2,1,0:T(8,128)(2,1)S(1)}, u32[]{:S(2)}, u32[]{:S(2)}) collective-permute-start(bf16[4,528,128]{2,1,0:T(8,128)(2,1)} %get-tuple-element.209), channel_id=1, source_target_pairs={{0,4},{4,0},{8,12},{12,8},{16,20},{20,16},{24,28},{28,24},{1,5},{5... | collective-permute-start | bytes 1622024 | tf_op jit(solution)/shard_map/ppermute | solution.py:1140
  316.6 10.0 %collective-permute-start.18 = (bf16[2,768,128]{2,1,0:T(8,128)(2,1)}, bf16[2,768,128]{2,1,0:T(8,128)(2,1)S(1)}, u32[]{:S(2)}, u32[]{:S(2)}) collective-permute-start(bf16[2,768,128]{2,1,0:T(8,128)(2,1)} %get-tuple-element.208.refs_2_), channel_id=1, source_target_pairs={{0,1},{1,0},{2,3},{3,2},{4,5},{5,4},{6,7},{7,6},{8,9},{9,8},{10,11... | collective-permute-start | bytes 1179656 | tf_op jit(solution)/shard_map/ppermute | solution.py:910
  322.9 43.1 %all-to-all-start.11 = ((bf16[8,400,128]{2,1,0:T(8,128)(2,1)}), bf16[8,400,128]{2,1,0:T(8,128)(2,1)S(1)}, u32[]{:S(2)}, u32[]{:S(2)}) async-start(bf16[8,400,128]{2,1,0:T(8,128)(2,1)} %bitcast.132), calls=%async_computation.11 | async-start | bytes 1638400 | tf_op jit(solution)/shard_map/all_to_all | solution.py:1211
  329.4 7.9 %collective-permute-start.19 = (bf16[1,768,128]{2,1,0:T(8,128)(2,1)}, bf16[1,768,128]{2,1,0:T(8,128)(2,1)S(1)}, u32[]{:S(2)}, u32[]{:S(2)}) collective-permute-start(bf16[1,768,128]{2,1,0:T(8,128)(2,1)} %get-tuple-element.215), channel_id=1, source_target_pairs={{0,2},{1,3},{2,0},{3,1},{4,6},{5,7},{6,4},{7,5},{8,10},{9,11},{10,... | collective-permute-start | bytes 589832 | tf_op jit(solution)/shard_map/ppermute | solution.py:910
  330.1 18.7 %collective-permute-start.17 = (bf16[2,528,128]{2,1,0:T(8,128)(2,1)S(1)}, bf16[2,528,128]{2,1,0:T(8,128)(2,1)S(1)}, u32[]{:S(2)}, u32[]{:S(2)}) collective-permute-start(bf16[2,528,128]{2,1,0:T(8,128)(2,1)S(1)} %copy-done.37), channel_id=1, source_target_pairs={{0,8},{4,12},{8,0},{12,4},{16,24},{20,28},{24,16},{28,20},{1,9},{5... | collective-permute-start | bytes 811016 | tf_op jit(solution)/shard_map/ppermute | solution.py:1140
  332.0 20.0 %collective-permute-start.12 = (bf16[132,1152]{1,0:T(8,128)(2,1)S(1)}, bf16[132,1152]{1,0:T(8,128)(2,1)S(1)}, u32[]{:S(2)}, u32[]{:S(2)}) collective-permute-start(bf16[132,1152]{1,0:T(8,128)(2,1)S(1)} %copy-done.33), channel_id=1, source_target_pairs={{0,1},{1,0},{2,3},{3,2},{4,5},{5,4},{6,7},{7,6},{8,9},{9,8},{10,11... | collective-permute-start | bytes 912392 | tf_op jit(solution)/shard_map/ppermute | solution.py:910
  332.1 21.5 %collective-permute-start.13 = (bf16[132,1152]{1,0:T(8,128)(2,1)S(1)}, bf16[132,1152]{1,0:T(8,128)(2,1)S(1)}, u32[]{:S(2)}, u32[]{:S(2)}) collective-permute-start(bf16[132,1152]{1,0:T(8,128)(2,1)S(1)} %copy-done.32), channel_id=1, source_target_pairs={{0,2},{1,3},{2,0},{3,1},{4,6},{5,7},{6,4},{7,5},{8,10},{9,11},{10,... | collective-permute-start | bytes 912392 | tf_op jit(solution)/shard_map/ppermute | solution.py:910
  333.5 22.7 %collective-permute-start.14 = (bf16[132,1152]{1,0:T(8,128)(2,1)S(1)}, bf16[132,1152]{1,0:T(8,128)(2,1)S(1)}, u32[]{:S(2)}, u32[]{:S(2)}) collective-permute-start(bf16[132,1152]{1,0:T(8,128)(2,1)S(1)} %copy-done.31), channel_id=1, source_target_pairs={{0,3},{1,2},{2,1},{3,0},{4,7},{5,6},{6,5},{7,4},{8,11},{9,10},{10,... | collective-permute-start | bytes 912392 | tf_op jit(solution)/shard_map/ppermute | solution.py:910
  339.7 17.0 %collective-permute-start.20 = (bf16[96,128]{1,0:T(8,128)(2,1)}, bf16[96,128]{1,0:T(8,128)(2,1)S(1)}, u32[]{:S(2)}, u32[]{:S(2)}) collective-permute-start(bf16[96,128]{1,0:T(8,128)(2,1)} %get-tuple-element.217), channel_id=1, source_target_pairs={{0,4},{4,0},{8,12},{12,8},{16,20},{20,16},{24,28},{28,24},{1,5},{5... | collective-permute-start | bytes 73736 | tf_op jit(solution)/shard_map/ppermute | solution.py:1140
  348.8 7.9 %copy-start.53 = (bf16[96,128]{1,0:T(8,128)(2,1)S(1)}, bf16[96,128]{1,0:T(8,128)(2,1)}, u32[]{:S(2)}) copy-start(bf16[96,128]{1,0:T(8,128)(2,1)} %get-tuple-element.222) | copy-start | bytes 73732
  348.8 10.6 %copy-start.51 = (bf16[96,128]{1,0:T(8,128)(2,1)S(1)}, bf16[96,128]{1,0:T(8,128)(2,1)}, u32[]{:S(2)}) copy-start(bf16[96,128]{1,0:T(8,128)(2,1)} %get-tuple-element.223) | copy-start | bytes 73732
  348.8 10.5 %collective-permute-start.21 = (bf16[96,128]{1,0:T(8,128)(2,1)}, bf16[96,128]{1,0:T(8,128)(2,1)S(1)}, u32[]{:S(2)}, u32[]{:S(2)}) collective-permute-start(bf16[96,128]{1,0:T(8,128)(2,1)} %get-tuple-element.218), channel_id=1, source_target_pairs={{0,8},{4,12},{8,0},{12,4},{16,24},{20,28},{24,16},{28,20},{1,9},{5... | collective-permute-start | bytes 73736 | tf_op jit(solution)/shard_map/ppermute | solution.py:1140
  352.0 9.5 %copy-start.34 = (bf16[132,1152]{1,0:T(8,128)(2,1)}, bf16[132,1152]{1,0:T(8,128)(2,1)S(1)}, u32[]{:S(2)}) copy-start(bf16[132,1152]{1,0:T(8,128)(2,1)S(1)} %collective-permute-done.12.refs_2_) | copy-start | bytes 912388
  352.0 12.5 %collective-permute-start.22 = (bf16[96,128]{1,0:T(8,128)(2,1)S(1)}, bf16[96,128]{1,0:T(8,128)(2,1)S(1)}, u32[]{:S(2)}, u32[]{:S(2)}) collective-permute-start(bf16[96,128]{1,0:T(8,128)(2,1)S(1)} %copy-done.56), channel_id=1, source_target_pairs={{0,12},{4,8},{8,4},{12,0},{16,28},{20,24},{24,20},{28,16},{1,13},{... | collective-permute-start | bytes 73736 | tf_op jit(solution)/shard_map/ppermute | solution.py:1140
  353.6 7.9 %copy-start.35 = (bf16[132,1152]{1,0:T(8,128)(2,1)}, bf16[132,1152]{1,0:T(8,128)(2,1)S(1)}, u32[]{:S(2)}) copy-start(bf16[132,1152]{1,0:T(8,128)(2,1)S(1)} %collective-permute-done.13.refs_3_) | copy-start | bytes 912388
  353.6 10.9 %collective-permute-start.23 = (bf16[96,128]{1,0:T(8,128)(2,1)S(1)}, bf16[96,128]{1,0:T(8,128)(2,1)S(1)}, u32[]{:S(2)}, u32[]{:S(2)}) collective-permute-start(bf16[96,128]{1,0:T(8,128)(2,1)S(1)} %copy-done.55), channel_id=1, source_target_pairs={{0,16},{4,20},{8,24},{12,28},{16,0},{20,4},{24,8},{28,12},{1,17},{... | collective-permute-start | bytes 73736 | tf_op jit(solution)/shard_map/ppermute | solution.py:1140
  356.2 8.3 %collective-permute-start.24 = (bf16[96,128]{1,0:T(8,128)(2,1)S(1)}, bf16[96,128]{1,0:T(8,128)(2,1)S(1)}, u32[]{:S(2)}, u32[]{:S(2)}) collective-permute-start(bf16[96,128]{1,0:T(8,128)(2,1)S(1)} %copy-done.54), channel_id=1, source_target_pairs={{0,20},{4,16},{8,28},{12,24},{16,4},{20,0},{24,12},{28,8},{1,21},{... | collective-permute-start | bytes 73736 | tf_op jit(solution)/shard_map/ppermute | solution.py:1140
  356.7 7.8 %copy-start.50 = (bf16[96,128]{1,0:T(8,128)(2,1)}, bf16[96,128]{1,0:T(8,128)(2,1)S(1)}, u32[]{:S(2)}) copy-start(bf16[96,128]{1,0:T(8,128)(2,1)S(1)} %collective-permute-done.20.refs_2_) | copy-start | bytes 73732
  356.7 7.9 %collective-permute-start.25 = (bf16[96,128]{1,0:T(8,128)(2,1)S(1)}, bf16[96,128]{1,0:T(8,128)(2,1)S(1)}, u32[]{:S(2)}, u32[]{:S(2)}) collective-permute-start(bf16[96,128]{1,0:T(8,128)(2,1)S(1)} %copy-done.53), channel_id=1, source_target_pairs={{0,24},{4,28},{8,16},{12,20},{16,8},{20,12},{24,0},{28,4},{1,25},{... | collective-permute-start | bytes 73736 | tf_op jit(solution)/shard_map/ppermute | solution.py:1140
  359.4 6.6 %collective-permute-start.26 = (bf16[96,128]{1,0:T(8,128)(2,1)S(1)}, bf16[96,128]{1,0:T(8,128)(2,1)S(1)}, u32[]{:S(2)}, u32[]{:S(2)}) collective-permute-start(bf16[96,128]{1,0:T(8,128)(2,1)S(1)} %copy-done.51), channel_id=1, source_target_pairs={{0,28},{4,24},{8,20},{12,16},{16,12},{20,8},{24,4},{28,0},{1,29},{... | collective-permute-start | bytes 73736 | tf_op jit(solution)/shard_map/ppermute | solution.py:1140
  369.2 7.9 %copy-start.22 = (f32[8,128]{1,0:T(8,128)S(1)}, f32[8,128]{1,0:T(8,128)}, u32[]{:S(2)}) copy-start(f32[8,128]{1,0:T(8,128)} %get-tuple-element.237) | copy-start | bytes 12292
  369.2 59.1 %all-to-all-start.12 = ((bf16[8,496,128]{2,1,0:T(8,128)(2,1)}), bf16[8,496,128]{2,1,0:T(8,128)(2,1)S(1)}, u32[]{:S(2)}, u32[]{:S(2)}) async-start(bf16[8,496,128]{2,1,0:T(8,128)(2,1)} %shard_map.425), calls=%async_computation.12 | async-start | bytes 2031616 | tf_op jit(solution)/shard_map/all_to_all | solution.py:1248
  374.2 27.5 %collective-permute-start.27 = (bf16[1,528,128]{2,1,0:T(8,128)(2,1)S(1)}, bf16[1,528,128]{2,1,0:T(8,128)(2,1)S(1)}, u32[]{:S(2)}, u32[]{:S(2)}) collective-permute-start(bf16[1,528,128]{2,1,0:T(8,128)(2,1)S(1)} %copy-done.41), channel_id=1, source_target_pairs={{0,16},{4,20},{8,24},{12,28},{16,0},{20,4},{24,8},{28,12},{1,17},{... | collective-permute-start | bytes 405512 | tf_op jit(solution)/shard_map/ppermute | solution.py:1140
  404.1 6.8 %collective-permute-start.31 = (bf16[528,128]{1,0:T(8,128)(2,1)}, bf16[528,128]{1,0:T(8,128)(2,1)S(1)}, u32[]{:S(2)}, u32[]{:S(2)}) collective-permute-start(bf16[528,128]{1,0:T(8,128)(2,1)} %shard_map.426.refs_1_), channel_id=1, source_target_pairs={{0,16},{4,20},{8,24},{12,28},{16,0},{20,4},{24,8},{28,12},{1,17},{... | collective-permute-start | bytes 405512 | tf_op jit(solution)/shard_map/ppermute | solution.py:1140
  404.1 8.9 %collective-permute-start.29 = (bf16[528,128]{1,0:T(8,128)(2,1)}, bf16[528,128]{1,0:T(8,128)(2,1)S(1)}, u32[]{:S(2)}, u32[]{:S(2)}) collective-permute-start(bf16[528,128]{1,0:T(8,128)(2,1)} %shard_map.426.refs_1_), channel_id=1, source_target_pairs={{0,8},{4,12},{8,0},{12,4},{16,24},{20,28},{24,16},{28,20},{1,9},{5... | collective-permute-start | bytes 405512 | tf_op jit(solution)/shard_map/ppermute | solution.py:1140
  410.9 13.7 %copy-start.42 = (bf16[528,128]{1,0:T(8,128)(2,1)}, bf16[528,128]{1,0:T(8,128)(2,1)S(1)}, u32[]{:S(2)}) copy-start(bf16[528,128]{1,0:T(8,128)(2,1)S(1)} %collective-permute-done.31.refs_5_) | copy-start | bytes 405508
  410.9 5.0 %collective-permute-start.33 = (bf16[528,128]{1,0:T(8,128)(2,1)S(1)}, bf16[528,128]{1,0:T(8,128)(2,1)S(1)}, u32[]{:S(2)}, u32[]{:S(2)}) collective-permute-start(bf16[528,128]{1,0:T(8,128)(2,1)S(1)} %collective-permute-done.31.refs_5_), channel_id=1, source_target_pairs={{0,8},{4,12},{8,0},{12,4},{16,24},{20,28},{24,16},{28,20},{1,9},{5... | collective-permute-start | bytes 405512 | tf_op jit(solution)/shard_map/ppermute | solution.py:1140
  410.9 8.2 %collective-permute-start.28 = (bf16[528,128]{1,0:T(8,128)(2,1)}, bf16[528,128]{1,0:T(8,128)(2,1)S(1)}, u32[]{:S(2)}, u32[]{:S(2)}) collective-permute-start(bf16[528,128]{1,0:T(8,128)(2,1)} %shard_map.426.refs_1_), channel_id=1, source_target_pairs={{0,4},{4,0},{8,12},{12,8},{16,20},{20,16},{24,28},{28,24},{1,5},{5... | collective-permute-start | bytes 405512 | tf_op jit(solution)/shard_map/ppermute | solution.py:1140
  412.9 10.2 %collective-permute-start.32 = (bf16[528,128]{1,0:T(8,128)(2,1)S(1)}, bf16[528,128]{1,0:T(8,128)(2,1)S(1)}, u32[]{:S(2)}, u32[]{:S(2)}) collective-permute-start(bf16[528,128]{1,0:T(8,128)(2,1)S(1)} %collective-permute-done.31.refs_5_), channel_id=1, source_target_pairs={{0,4},{4,0},{8,12},{12,8},{16,20},{20,16},{24,28},{28,24},{1,5},{5... | collective-permute-start | bytes 405512 | tf_op jit(solution)/shard_map/ppermute | solution.py:1140
  413.0 11.5 %copy-start.43 = (bf16[528,128]{1,0:T(8,128)(2,1)}, bf16[528,128]{1,0:T(8,128)(2,1)S(1)}, u32[]{:S(2)}) copy-start(bf16[528,128]{1,0:T(8,128)(2,1)S(1)} %collective-permute-done.29.refs_3_) | copy-start | bytes 405508
  413.0 10.1 %collective-permute-start.30 = (bf16[528,128]{1,0:T(8,128)(2,1)S(1)}, bf16[528,128]{1,0:T(8,128)(2,1)S(1)}, u32[]{:S(2)}, u32[]{:S(2)}) collective-permute-start(bf16[528,128]{1,0:T(8,128)(2,1)S(1)} %collective-permute-done.29.refs_3_), channel_id=1, source_target_pairs={{0,4},{4,0},{8,12},{12,8},{16,20},{20,16},{24,28},{28,24},{1,5},{5... | collective-permute-start | bytes 405512 | tf_op jit(solution)/shard_map/ppermute | solution.py:1140
  415.9 8.7 %copy-start.44 = (bf16[528,128]{1,0:T(8,128)(2,1)}, bf16[528,128]{1,0:T(8,128)(2,1)S(1)}, u32[]{:S(2)}) copy-start(bf16[528,128]{1,0:T(8,128)(2,1)S(1)} %collective-permute-done.33.refs_7_) | copy-start | bytes 405508
  415.9 8.7 %collective-permute-start.34 = (bf16[528,128]{1,0:T(8,128)(2,1)S(1)}, bf16[528,128]{1,0:T(8,128)(2,1)S(1)}, u32[]{:S(2)}, u32[]{:S(2)}) collective-permute-start(bf16[528,128]{1,0:T(8,128)(2,1)S(1)} %collective-permute-done.33.refs_7_), channel_id=1, source_target_pairs={{0,4},{4,0},{8,12},{12,8},{16,20},{20,16},{24,28},{28,24},{1,5},{5... | collective-permute-start | bytes 405512 | tf_op jit(solution)/shard_map/ppermute | solution.py:1140
  429.3 7.5 %copy-start.6 = (f32[864,32]{1,0:T(8,128)S(1)}, f32[864,32]{1,0:T(8,128)}, u32[]{:S(2)}) copy-start(f32[864,32]{1,0:T(8,128)} %get-tuple-element.236) | copy-start | bytes 331780
  (45 other events, 103.5 us)

commit v3 on v2

--- a/solution.py
+++ b/solution.py
@@ -23,7 +23,7 @@
 NORM_ORDER = ((0, DIRECT), (256, NARROW), (256 + NARROW, SQUEEZE), (512, WIDE), (896, SPREAD), (1024, PROJECT))
 TILE_ROW = {"d": (0, DIRECT), "w": (2, WIDE), "s": (5, SPREAD), "p": (6, PROJECT)}
 OUTER = ("d", "w", "s", "p")
-CHUNK = 48
+CHUNK = 96
 
 
 class Geometry:
@@ -95,6 +95,13 @@
     )
 
 
+def wide_mask(m_ref, at, width):
+    part = m_ref[at, :]
+    if width <= 128:
+        return part[:, :width]
+    return jnp.concatenate([part] * -(-width // 128), axis=1)[:, :width]
+
+
 def row(tile, first, width):
     pieces = [
         tile[first + i : first + i + 1, : min(128, width - 128 * i)] for i in range(-(-width // 128))
@@ -128,13 +135,15 @@
     width = y_ref.shape[1]
 
     def first(r, acc):
-        return acc + fold8(y_ref[pl.ds(r, CHUNK), :] * m_ref[pl.ds(r, CHUNK), 0:1])
+        at = pl.ds(r, CHUNK)
+        return acc + fold8(y_ref[at, :] * wide_mask(m_ref, at, width))
 
     total = each_chunk(rows, first, jnp.zeros((8, width), F32))
     mean = jnp.sum(total, axis=0, keepdims=True) / count
 
     def second(r, acc):
-        centred = (y_ref[pl.ds(r, CHUNK), :] - mean) * m_ref[pl.ds(r, CHUNK), 0:1]
+        at = pl.ds(r, CHUNK)
+        centred = (y_ref[at, :] - mean) * wide_mask(m_ref, at, width)
         return acc + fold8(centred * centred)
 
     spread = each_chunk(rows, second, jnp.zeros((8, width), F32))
@@ -357,7 +366,7 @@
     for j in range(0, rows, 128):
         size = min(128, rows - j)
         turned = jnp.transpose(xs[:, j : j + size])
-        a_ref[j : j + size, :] = (turned * m_ref[j : j + size, 0:1]).astype(BF16)
+        a_ref[j : j + size, :] = (turned * wide_mask(m_ref, slice(j, j + size), turned.shape[1])).astype(BF16)
     unpack_points(pack, me, piece_refs, 0, raw, ws, wt_ref)
     for k, ref in enumerate(piece_refs):
         norm_raw[me ^ k] = ref[pack.points :, :].astype(F32)
@@ -418,7 +427,7 @@
     def activate(r, carry):
         at = pl.ds(r, CHUNK)
         h = scale * ((y_ref[at, :] - mean) * rstd) + shift
-        us[at, :] = h * jax.nn.sigmoid(h) * m_ref[at, 0:1]
+        us[at, :] = h * jax.nn.sigmoid(h) * wide_mask(m_ref, at, REDUCED)
         return carry
 
     each_chunk(rows, activate)
@@ -485,7 +494,7 @@
         def activate(r, carry):
             at = pl.ds(r, CHUNK)
             h = scale * ((ref[at, :] - mean) * rstd) + shift
-            u = h * jax.nn.sigmoid(h) * m_ref[at, 0:1]
+            u = h * jax.nn.sigmoid(h) * wide_mask(m_ref, at, width)
             top = u.astype(BF16)
             high[at, :width] = top
             low[at, :width] = (u - top.astype(F32)).astype(BF16)
@@ -513,7 +522,7 @@
 
     def body(r, carry):
         at = pl.ds(r, CHUNK)
-        masking = m_ref[at, 0:1]
+        masking = wide_mask(m_ref, at, width)
         xhat = (y_ref[at, :] - mean) * rstd
         h = scale * xhat + shift
         gate = jax.nn.sigmoid(h)
@@ -578,7 +587,7 @@
         def finish(r, carry):
             at = pl.ds(r, CHUNK)
             dy = finish_rows(
-                d_ref[at, :], y_ref[at, :], m_ref[at, 0:1], mean, rstd, scale, scale_sum,
+                d_ref[at, :], y_ref[at, :], wide_mask(m_ref, at, width), mean, rstd, scale, scale_sum,
                 shift_sum, count,
             )
             o_ref[at, :] = dy.astype(BF16)
@@ -634,8 +643,13 @@
 
 
 def kernel_grad_kernel(
-    geo, clips, pack, me_ref, gw_ref, gs_ref, bn_ref, bs_ref, keep_ref, send_ref, grad_w, grad_s
+    geo, clips, pack, halves, me_ref, gw_ref, gs_ref, bn_ref, bs_ref, *refs
 ):
+    send_ref, grad_w, grad_s = refs[-3:]
+    if halves:
+        keep_ref = refs[-4]
+        for source, target in zip(refs[:-4], (keep_ref, send_ref)):
+            target[:, pack.kernels : pack.kernels + source.shape[1], :] = source[...]
     size = geo.frame_rows
     for g_ref, b_ref, grad in ((gw_ref, bn_ref, grad_w), (gs_ref, bs_ref, grad_s)):
         for t in range(3):
@@ -650,18 +664,15 @@
             grad[t] = total
     me = me_ref[0]
     for k in range(pack.groups):
-        target = (keep_ref, send_ref)[k % 2]
+        target, place = ((keep_ref, send_ref)[k % 2], k // 2) if halves else (send_ref, me ^ k)
         for at, own, wide, t, u, _ in pack.kernel_tiles():
             source = grad_w if wide else grad_s
             first = pl.multiple_of((me ^ k) * own, 8)
             part = source[t, pl.ds(first, own), 128 * u : 128 * u + 128]
-            target[k // 2, at : at + own, :] = part.astype(BF16)
-
-
-def point_grad_kernel(pack, start, me_ref, gy_ref, a_ref, *refs):
-    keep_ref, send_ref, whole, shares = refs[-4:]
-    for source, target in zip(refs[:-4], (keep_ref, send_ref)):
-        target[:, :start, :] = source[...]
+            target[place, at : at + own, :] = part.astype(BF16)
+
+
+def point_grad_kernel(pack, me_ref, gy_ref, a_ref, keep_ref, send_ref, whole, shares):
     whole[...] = tn(gy_ref[...], a_ref[...])
     for s in range(pack.groups):
         for at, begin, own in pack.point_parts():
@@ -669,7 +680,7 @@
     me = me_ref[0]
     for k in range(pack.groups):
         target = (keep_ref, send_ref)[k % 2]
-        for at, u, width in pack.point_blocks(start):
+        for at, u, width in pack.point_blocks(0):
             target[k // 2, at : at + pack.point, :] = shares[
                 me ^ k, : pack.point, 128 * u : 128 * u + 128
             ].astype(BF16)
@@ -685,34 +696,19 @@
     o_ref[...] = (keep_ref[0].astype(F32) + got_ref[0].astype(F32)).astype(BF16)
 
 
-def scatter_kernel(mb_ref, keep_ref, got_ref, *refs):
-    *o_refs, held = refs
-    held[...] = keep_ref[0].astype(F32) + got_ref[0].astype(F32)
-    size = held.shape[0] // len(o_refs)
-    for k, o_ref in enumerate(o_refs):
-        first = pl.multiple_of((mb_ref[0] ^ k) * size, 8)
-        o_ref[...] = held[pl.ds(first, size), :].astype(BF16)
-
-
-def scatter_halves_kernel(mb_ref, keep_ref, got_ref, even_ref, odd_ref, held):
-    held[...] = keep_ref[0].astype(F32) + got_ref[0].astype(F32)
+def scatter_halves_kernel(mb_ref, x_ref, even_ref, odd_ref, held):
+    held[...] = x_ref[...].astype(F32)
     size = even_ref.shape[1]
     for k in range(2 * even_ref.shape[0]):
         first = pl.multiple_of((mb_ref[0] ^ k) * size, 8)
         (even_ref, odd_ref)[k % 2][k // 2] = held[pl.ds(first, size), :].astype(BF16)
 
 
-def total_kernel(x_ref, *refs):
-    *p_refs, o_ref = refs
+def total_kernel(x_ref, o_ref):
     total = x_ref[0].astype(F32)
     for k in range(1, x_ref.shape[0]):
         total = total + x_ref[k].astype(F32)
-    other = p_refs[0][...].astype(F32)
-    for p_ref in p_refs[1:]:
-        other = other + p_ref[...].astype(F32)
-    size = total.shape[0]
-    o_ref[:, :size, :] = jnp.broadcast_to(total.astype(BF16)[None], (o_ref.shape[0],) + total.shape)
-    o_ref[:, size:, :] = jnp.broadcast_to(other.astype(BF16)[None], (o_ref.shape[0],) + other.shape)
+    o_ref[...] = jnp.broadcast_to(total.astype(BF16)[None], o_ref.shape)
 
 
 def read_kernels(pack, rows, w_ref, s_ref, turned):
@@ -732,22 +728,21 @@
 
 def late_gradients_kernel(pack, batches, mb_ref, *refs):
     x_refs = refs[:batches]
-    w_ref, s_ref, *o_refs, held, turned = refs[batches:]
+    w_ref, s_ref, held, turned = refs[batches:]
     for k, x_ref in enumerate(x_refs):
         held[mb_ref[0] ^ k] = x_ref[...]
-    rows = held[...].reshape(-1, 128)
-    read_kernels(pack, rows, w_ref, s_ref, turned)
-    read_points(pack, pack.kernels, rows, o_refs)
-
-
-def early_gradients_kernel(pack, size, x_ref, late_ref, w_ref, s_ref, *refs):
-    *o_refs, held, points, wide, turned = refs
-    rest = x_ref.shape[1] - size
-    for b in range(x_ref.shape[0]):
-        held[b * size : (b + 1) * size, :] = x_ref[b, :size, :]
-        points[b * rest : (b + 1) * rest, :] = x_ref[b, size:, :]
-    read_kernels(pack, held, wide, s_ref, turned)
-    read_points(pack, 0, points, o_refs)
+    read_kernels(pack, held[...].reshape(-1, 128), w_ref, s_ref, turned)
+
+
+def points_out_kernel(pack, x_ref, *o_refs):
+    read_points(pack, 0, x_ref[...].reshape(-1, 128), o_refs)
+
+
+def early_gradients_kernel(pack, late_pack, x_ref, late_ref, w_ref, s_ref, *refs):
+    *o_refs, wide, turned = refs
+    rows = x_ref[...].reshape(-1, 128)
+    read_kernels(pack, rows, wide, s_ref, turned)
+    read_points(late_pack, pack.kernels, rows, o_refs)
 
     def join(g, carry):
         parts = []
@@ -785,15 +780,14 @@
 
     def finish(r, carry):
         at = pl.ds(r, CHUNK)
-        masking = m_ref[at, 0:1]
         gy_ref[at, :DIRECT] = finish_rows(
-            dd_ref[at, :], yd_ref[at, :], masking, mean_d, rstd_d, scale_d, *pair_d, count
+            dd_ref[at, :], yd_ref[at, :], wide_mask(m_ref, at, DIRECT), mean_d, rstd_d, scale_d, *pair_d, count
         ).astype(BF16)
         gy_ref[at, DIRECT : DIRECT + REDUCED] = finish_rows(
-            dr_ref[at, :], yr_ref[at, :], masking, mean_r, rstd_r, scale_r, *pair_r, count
+            dr_ref[at, :], yr_ref[at, :], wide_mask(m_ref, at, REDUCED), mean_r, rstd_r, scale_r, *pair_r, count
         ).astype(BF16)
         held[at, :] = finish_rows(
-            dp_ref[at, :], yp_ref[at, :], masking, mean_p, rstd_p, scale_p, *pair_p, count
+            dp_ref[at, :], yp_ref[at, :], m_ref[at, :], mean_p, rstd_p, scale_p, *pair_p, count
         )
         return carry
 
@@ -852,7 +846,7 @@
     rows = clips * EARLY.clip_rows
     for j in range(0, rows, 128):
         size = min(128, rows - j)
-        grad = jnp.transpose(nn(gy_ref[j : j + size, :], wt_ref[...]) * m_ref[j : j + size, 0:1])
+        grad = jnp.transpose(nn(gy_ref[j : j + size, :], wt_ref[...]) * wide_mask(m_ref, slice(j, j + size), wt_ref.shape[1]))
         for s in range(pack.groups):
             turned[s, :, j : j + size] = grad[s * depth : (s + 1) * depth, :].astype(BF16)
     for k, x_ref in enumerate(x_refs):
@@ -1092,22 +1086,24 @@
 
     unit = 16 * batches
 
-    def kernel_grads(geo, size, gw, gs, bn, bs):
+    def kernel_grads(geo, size, gw, gs, bn, bs, halves, others=()):
+        outs = [(groups // 2, size, 128)] * 2 if halves else [(groups, size, 128)]
         return call(
-            lambda *refs: kernel_grad_kernel(geo, clips, pack, *refs),
-            [((groups // 2, size, 128), BF16)] * 2,
-            [me_ref, gw, gs, bn, bs],
+            lambda *refs: kernel_grad_kernel(geo, clips, pack, halves, *refs),
+            [(shape, BF16) for shape in outs],
+            [me_ref, gw, gs, bn, bs] + list(others),
             [((3, WIDE, 128 * WIDE_TILES), F32), ((3, SPREAD, 128 * SPREAD_TILES), F32)],
             us=10 if geo is EARLY else 5,
         )
 
-    def point_grads(use, start, size, gy, act, others=()):
+    def point_grads(use, size, gy, act, behind=()):
         return call(
-            lambda *refs: point_grad_kernel(use, start, *refs),
+            lambda *refs: point_grad_kernel(use, *refs),
             [((groups // 2, size, 128), BF16)] * 2,
-            [me_ref, gy, act] + list(others),
+            [me_ref, gy, act] + list(behind),
             [((POINT, use.features), F32), ((groups, use.point_rows, use.point_tiles * 128), F32)],
             us=4.5,
+            idle=len(behind),
         )
 
     class Reduction:
@@ -1145,7 +1141,8 @@
     gw, gs, late_sums = finish(LATE, g, lst, lst_r, hw, hs, lyw, lys, coarse)
     hr, pay = inner(LATE, lst_r, gw, gs, lyr, lkw, lks, coarse)
     g = exchange(pay)
-    late_halves = kernel_grads(LATE, pack.kernels, gw, gs, lbn, lbs)
+    (late_kernels,) = kernel_grads(LATE, whole_units(pack.kernels), gw, gs, lbn, lbs, False)
+    late_share = lax.psum_scatter(late_kernels, "ch", scatter_dimension=0)
     out_arrived = ordered(lax.all_to_all(out_joined, "ch", 0, 0))
     gy, ed, ew, es, ep, pay, late_sums_r = call(
         lambda *refs: late_input_kernel(clips, *refs),
@@ -1153,31 +1150,18 @@
         + [((rows, w), F32) for w in widths]
         + [((devices, 16, 128), F32), ((8, 128), F32)],
         [g, late_sums, lst, lst_r, affine, hr, hd, hp, lyr, lyd, lyp, coarse, late_wt, spread_back,
-         st, yd, yw, ys, yp, mask, late_halves[1], out_arrived],
+         st, yd, yw, ys, yp, mask, late_kernels, out_arrived],
         [((late_rows, PROJECT), F32), ((late_rows, CONCAT), BF16), ((rows, WIDE), F32), ((16, 128), F32)],
         idle=2,
         us=15,
     )
     g = exchange(pay)
-    late_size = whole_units(late_pack.kernels + late_pack.points)
-    late_halves = point_grads(late_pack, late_pack.kernels, late_size, gy, late_act, late_halves)
-    late_sum = Reduction(*late_halves)
-    gw, gs, sums = finish(EARLY, g, st, st_r, ew, es, yw, ys, mask, late_halves[1:])
-    halves = kernel_grads(EARLY, whole_units(pack.kernels), gw, gs, bn, bs)
+    late_points = point_grads(late_pack, late_pack.points, gy, late_act)
+    gw, gs, sums = finish(EARLY, g, st, st_r, ew, es, yw, ys, mask, late_points[1:])
+    halves = kernel_grads(
+        EARLY, whole_units(pack.kernels + late_pack.points), gw, gs, bn, bs, True, late_points
+    )
     early_sum = Reduction(*halves)
-    kept = late_sum.halve(halves[1])
-    hr, pay = inner(EARLY, st_r, gw, gs, yr, kw, ks, mask, behind=(halves[1], kept))
-    g = exchange(pay)
-    kept = early_sum.halve(hr)
-    late_piece = late_sum.keep.shape[1] // batches
-    late_keep, late_send = call(
-        scatter_halves_kernel,
-        [((batches // 2, late_piece, 128), BF16)] * 2,
-        [mb_ref, late_sum.keep, late_sum.got, hr],
-        [(late_sum.keep.shape[1:], F32)],
-        us=3,
-        idle=1,
-    )
 
     class BatchHalves(Reduction):
         def __init__(self, keep, send):
@@ -1194,82 +1178,101 @@
             self.got = batch_swap(send, self.bit)
             return self.keep
 
-    late_sum = BatchHalves(late_keep, late_send)
+        def spread(self, *behind):
+            own = self.add(*behind)
+            self.pieces, self.bit = {0: own}, batches // 2
+            return own
+
+        def double(self):
+            got = {k | self.bit: batch_swap(self.pieces[k], self.bit) for k in self.pieces}
+            self.pieces.update(got)
+            self.bit //= 2
+            return list(got.values())
+
+    late_piece = late_share.shape[0] // batches
+    late_halves = call(
+        scatter_halves_kernel,
+        [((batches // 2, late_piece, 128), BF16)] * 2,
+        [mb_ref, late_share, halves[1]],
+        [(late_share.shape, F32)],
+        us=3,
+        idle=1,
+    )
+    late_sum = BatchHalves(*late_halves)
+    kept = early_sum.halve(late_halves[1])
+    hr, pay = inner(EARLY, st_r, gw, gs, yr, kw, ks, mask, behind=(kept,))
+    g = exchange(pay)
+    late_kept = late_sum.step(hr)
+    own = early_sum.add(late_kept)
+    parts = lax.all_to_all(own.reshape(batches, -1, 128), "batch", 0, 0)
+    late_kept = own
+    while 2 * late_sum.bit < batches:
+        late_kept = late_sum.step(own)
     gy, *x_parts, sums_r = call(
         lambda *refs: early_input_kernel(pack, clips, *refs),
         [((rows, POINT), BF16)] + [((depth, rows), BF16)] * groups + [((8, 128), F32)],
-        [me_ref, g, sums, st, st_r, affine, hr, ed, ep, yr, yd, yp, mask, wt, kept, late_keep],
+        [me_ref, g, sums, st, st_r, affine, hr, ed, ep, yr, yd, yp, mask, wt, late_kept],
         [((rows, PROJECT), F32), ((groups, depth, rows), BF16)],
-        idle=2,
+        idle=1,
         us=8.5,
     )
     x_parts = [x_parts[0]] + [swap(x_parts[k], k) for k in range(1, groups)]
-    point_halves = point_grads(pack, 0, whole_units(pack.points), gy, act)
+    late_own = late_sum.spread(gy)
+    point_halves = point_grads(pack, whole_units(pack.points), gy, act, (late_own,))
     point_sum = Reduction(*point_halves)
-    kept = late_sum.step(point_halves[1])
-    own = early_sum.add(point_halves[1], kept)
-    parts = lax.all_to_all(own.reshape(batches, -1, 128), "batch", 0, 0)
-    kept = point_sum.halve(own)
-    late_kept = late_sum.step(kept)
-    while 2 * late_sum.bit < batches:
-        late_kept = late_sum.step()
+    kept = point_sum.halve()
     (feature_grad,) = call(
         lambda *refs: feature_kernel(pack, *refs),
         [((depth, groups * rows), F32)],
-        [me_ref] + x_parts + [own, late_kept],
+        [me_ref] + x_parts + [kept],
         [((groups, depth, rows), BF16)],
-        idle=2,
+        idle=1,
         us=2,
     )
-    points_size = kept.shape[1] // batches
-    pieces = call(
-        scatter_kernel,
-        [((points_size, 128), BF16)] * batches,
-        [mb_ref, point_sum.keep, point_sum.got],
-        [(kept.shape[1:], F32)],
-        us=1.5,
-    )
-    pieces = [pieces[0]] + [batch_swap(pieces[k], k) for k in range(1, batches)]
-    late_own = late_sum.add(pieces[0])
-    late_pieces, bit = {0: late_own}, batches // 2
-    while bit:
-        for k in list(late_pieces):
-            late_pieces[k | bit] = batch_swap(late_pieces[k], bit)
-        bit //= 2
-    late_pieces = [late_pieces[k] for k in range(batches)]
-    kernels_size = parts.shape[1]
+    got = late_sum.double()
     (parts,) = call(
         total_kernel,
-        [((batches, kernels_size + points_size, 128), BF16)],
-        [parts] + list(pieces) + [feature_grad],
+        [(parts.shape, BF16)],
+        [parts, feature_grad] + got,
         us=2,
-        idle=1,
+        idle=1 + len(got),
     )
     early_total = lax.all_to_all(parts, "batch", 0, 0)
+    while late_sum.bit:
+        late_sum.double()
+    late_pieces = [late_sum.pieces[k] for k in range(batches)]
+    late_wide, late_spread = call(
+        lambda *refs: late_gradients_kernel(pack, batches, *refs),
+        [((pack.wide, WIDE_COLUMNS), F32), ((SPREAD_COLUMNS, pack.spread), F32)],
+        [mb_ref] + late_pieces,
+        [((batches, late_piece, 128), BF16), ((pack.spread, SPREAD_COLUMNS), F32)],
+        us=3,
+    )
+    point_own = point_sum.add(early_total)
+    point_parts = lax.all_to_all(point_own.reshape(batches, -1, 128), "batch", 0, 0)
+    (point_parts,) = call(
+        total_kernel, [(point_parts.shape, BF16)], [point_parts, late_wide], us=1, idle=1
+    )
+    point_total = lax.all_to_all(point_parts, "batch", 0, 0)
     out_arrived = out_arrived.reshape((held_clips,) + out_arrived.shape[2:])
     outputs, at = [], 0
     for part in upstream:
         outputs.append(out_arrived[..., at : at + part.shape[4]])
         at += part.shape[4]
 
-    late_wide, late_spread, *late_grads = call(
-        lambda *refs: late_gradients_kernel(late_pack, batches, *refs),
-        [((pack.wide, WIDE_COLUMNS), F32), ((SPREAD_COLUMNS, pack.spread), F32)]
+    wide_grad, early_spread, *late_grads = call(
+        lambda *refs: early_gradients_kernel(pack, late_pack, *refs),
+        [(wide_kernels.shape, F32), ((SPREAD_COLUMNS, pack.spread), F32)]
         + [(part.shape[::-1], F32) for part in late_parts],
-        [mb_ref] + late_pieces,
-        [((batches, late_piece, 128), BF16), ((pack.spread, SPREAD_COLUMNS), F32)],
-        us=4,
-    )
-    wide_grad, early_spread, *early_grads = call(
-        lambda *refs: early_gradients_kernel(pack, kernels_size, *refs),
-        [(wide_kernels.shape, F32), ((SPREAD_COLUMNS, pack.spread), F32)]
-        + [(part.shape[::-1], F32) for part in early_parts],
         [early_total, late_wide],
-        [
-            ((batches * kernels_size, 128), BF16), ((batches * points_size, 128), BF16),
-            ((pack.wide, WIDE_COLUMNS), F32), ((pack.spread, SPREAD_COLUMNS), F32),
-        ],
+        [((pack.wide, WIDE_COLUMNS), F32), ((pack.spread, SPREAD_COLUMNS), F32)],
         us=8,
+    )
+    early_grads = call(
+        lambda *refs: points_out_kernel(pack, *refs),
+        [(part.shape[::-1], F32) for part in early_parts],
+        [point_total],
+        us=1.5,
     )
     early_grads = [part.T for part in early_grads]
     late_grads = [part.T for part in late_grads]

time: 446 us -> 411 us (0.922)
  Pallas kernels: 209 us -> 169 us
  between operations: 1.72 us -> 15 us
  blocking collectives: 8.75 us -> 0 us
  waiting for transfers between devices: 86 us -> 94.3 us
  local copies, waits for them, and re-layouts: 42.8 us -> 38 us
    pallas_call x34 -> x35, Pallas kernels: 209 us -> 169 us  [call(): pl.pallas_call(body, out_shape=[jax.ShapeDtypeStruct(s, d) for s, d in ou...]
    ppermute x17 -> x10, waiting for transfers between devices: 44.4 us -> 15.5 us  [batch_swap(): return lax.ppermute(value, 'batch', [(i, i ^ bit) for i in range(batches)])]
    ppermute x18 -> x16, waiting for transfers between devices: 9.18 us -> 27.5 us  [swap(): return lax.ppermute(value, 'ch', [(i, i ^ bit) for i in range(groups)])]
    ppermute x17 -> x10, starting transfers between devices: 26.5 us -> 12 us  [batch_swap(): return lax.ppermute(value, 'batch', [(i, i ^ bit) for i in range(batches)])]
    all_to_all x8, waiting for transfers between devices: 30.9 us -> 43.7 us  [exchange(): return lax.all_to_all(payload, BOTH, 0, 0)]
    all_to_all x0 -> x3, starting transfers between devices: none -> 10.5 us  [the longest x1 3.62 us: shards(): lax.all_to_all(point_own.reshape(batches, -1, 128), 'batch', 0, 0)]
    all_to_all x1 -> x0, blocking collectives: 8.75 us -> none  [shards(): out_arrived = ordered(lax.all_to_all(out_joined, 'ch', 0, 0))]
    ppermute x18 -> x16, starting transfers between devices: 11.7 us -> 9.25 us  [swap(): return lax.ppermute(value, 'ch', [(i, i ^ bit) for i in range(groups)])]
  transfers between devices with their start and end apart: 47 -> 42, of which waited for: 17 -> 17; matrix products, arithmetic and copies ran while one was open for 6% -> 7% of each run, Pallas kernels for 35% -> 35%
where the time goes in v3:
time: 411 us; the launch traced here: 404 us
  Pallas kernels  169 us (41%)
  waiting for transfers between devices  94.3 us (23%)
  starting transfers between devices  79 us (19%)
  local copies, waits for them, and re-layouts  38 us (9%)
  between operations  15 us (4%)
  other arithmetic  9.07 us (2%)
    pallas_call x35, Pallas kernels, call(): pl.pallas_call(body, out_shape=[jax.ShapeDtypeStruct(s, d) for s, d in ou...  169 us
    all_to_all x8, waiting for transfers between devices, exchange(): return lax.all_to_all(payload, BOTH, 0, 0)  43.7 us
    all_to_all x8, starting transfers between devices, exchange(): return lax.all_to_all(payload, BOTH, 0, 0)  28.7 us
    ppermute x16, waiting for transfers between devices, swap(): return lax.ppermute(value, 'ch', [(i, i ^ bit) for i in range(groups)])  27.5 us
    unnamed x125, local copies, waits for them, and re-layouts  22.6 us
    ppermute x10, waiting for transfers between devices, batch_swap(): return lax.ppermute(value, 'batch', [(i, i ^ bit) for i in range(batches)])  15.5 us
    ppermute x10, starting transfers between devices, batch_swap(): return lax.ppermute(value, 'batch', [(i, i ^ bit) for i in range(batches)])  12 us
    ppermute x16, starting transfers between devices, swap(): return lax.ppermute(value, 'ch', [(i, i ^ bit) for i in range(groups)])  9.25 us
  transfers between devices with their start and end apart: 42, of which 17 were waited for; matrix products, arithmetic and copies ran while one was open for 7% of the time, Pallas kernels for 35%

profile of v3, /device:TPU:0, one launch (start us, length us, event | category | flops | bytes accessed | tf_op | source)
XLA Modules:
  0.0 404.3 jit_solution(5594985629824279059)
XLA Ops:
  8.6 2.5 shard_map.391
  11.2 3.0 collective-permute-start.1
  14.1 3.5 all-to-all-start
  19.4 4.8 %shard_map.394 = (bf16[2700,128]{1,0:T(8,128)(2,1)}, bf16[2700,128]{1,0:T(8,128)(2,1)}) custom-call(bf16[2,345600]{1,0:T(2,128)(2,1)} %refs_0_.3, bf16[4,132,1152]{2,1,0:T(8,128)(2,1)} %get-tuple-element.118.refs_1_), custom_call_target="tpu_custom_call" | custom-call | flops 5280000000 | bytes 2764800 | tf_op jit(solution)/shard_map/pallas_call | solution.py:68
  24.2 2.9 reshape.202.refs_0_
  30.4 2.3 shard_map.395.refs_0_
  38.0 5.3 %shard_map.392 = (bf16[1152,528]{1,0:T(8,128)(2,1)}, bf16[576,528]{1,0:T(8,128)(2,1)}, f32[4,1152]{1,0:T(4,128)}, f32[1152,192]{1,0:T(8,128)}, f32[32,8,128]{2,1,0:T(8,128)}) custom-call(s32[1]{0:T(128)} %bitcast.refs_0_, bf16[4,132,1152]{2,1,0:T(8,128)(2,1)} %copy-done.1, bf16[736,128]{1,0:T(8,128)(2,1)} %get-tuple-element.119.refs_2_, ...), custom_call_target="tpu_custom_call" | custom-call | flops 9459999744 | bytes 5517316 | tf_op jit(solution)/shard_map/pallas_call | solution.py:68
  43.3 5.8 %all-to-all-start.1 = ((f32[32,8,128]{2,1,0:T(8,128)}), f32[32,8,128]{2,1,0:T(8,128)S(1)}, u32[]{:S(2)}, u32[]{:S(2)}) async-start(f32[32,8,128]{2,1,0:T(8,128)} %get-tuple-element.120), calls=%async_computation.1 | async-start | bytes 262144 | tf_op jit(solution)/shard_map/all_to_all | solution.py:901
  49.1 7.2 %collective-permute-done.4.refs_9_ = bf16[3168,128]{1,0:T(8,128)(2,1)S(1)} collective-permute-done((bf16[3168,128]{1,0:T(8,128)(2,1)}, bf16[3168,128]{1,0:T(8,128)(2,1)S(1)}, u32[]{:S(2)}, u32[]{:S(2)}) %collective-permute-start.4) | collective-permute-done | bytes 811040 | tf_op jit(solution)/shard_map/ppermute | solution.py:904
  56.3 6.0 %shard_map.393 = (f32[1152,256]{1,0:T(8,128)}, f32[1152,128]{1,0:T(8,128)}, f32[16,128]{1,0:T(8,128)}) custom-call(bf16[1152,528]{1,0:T(8,128)(2,1)} %get-tuple-element.123.refs_0_.refs_6_.refs_2_, bf16[576,528]{1,0:T(8,128)(2,1)} %get-tuple-element.124.refs_1_.refs_13_, f32[1152,128]{1,0:T(8,128)} %broadcast_in_dim.16.refs_6_.refs_2_.refs_5_.refs_8_.refs_19_.refs_7_.refs_12_), custom_call_target="tpu_custom_call" | custom-call | flops 13200000000 | bytes 4192256 | tf_op jit(solution)/shard_map/pallas_call | solution.py:68
  62.3 2.5 shard_map.398.refs_0_
  67.1 17.1 %shard_map.397 = (bf16[1728,1536]{1,0:T(8,128)(2,1)}, bf16[1728,384]{1,0:T(8,128)(2,1)}, f32[1152,320]{1,0:T(8,128)}, f32[1152,128]{1,0:T(8,128)}, bf16[3,4,80,1...) custom-call(s32[1]{0:T(128)} %bitcast.refs_0_, ...), custom_call_target="tpu_custom_call" | custom-call | flops 27499999232 | bytes 17217540 | tf_op jit(solution)/shard_map/pallas_call | solution.py:68
  84.2 7.2 %collective-permute-done.7.refs_0_ = bf16[4176,128]{1,0:T(8,128)(2,1)S(1)} collective-permute-done((bf16[4176,128]{1,0:T(8,128)(2,1)}, bf16[4176,128]{1,0:T(8,128)(2,1)S(1)}, u32[]{:S(2)}, u32[]{:S(2)}) %collective-permute-start.7) | collective-permute-done | bytes 1069088 | tf_op jit(solution)/shard_map/ppermute | solution.py:904
  92.6 6.2 %all-to-all-start.2 = ((f32[32,16,128]{2,1,0:T(8,128)}), f32[32,16,128]{2,1,0:T(8,128)S(1)}, u32[]{:S(2)}, u32[]{:S(2)}) async-start(f32[32,16,128]{2,1,0:T(8,128)} %get-tuple-element.127), calls=%async_computation.2 | async-start | bytes 524288 | tf_op jit(solution)/shard_map/all_to_all | solution.py:901
  100.7 8.7 %all-to-all-done.2.refs_1_ = f32[32,16,128]{2,1,0:T(8,128)S(1)} async-done(((f32[32,16,128]{2,1,0:T(8,128)}), f32[32,16,128]{2,1,0:T(8,128)S(1)}, u32[]{:S(2)}, u32[]{:S(2)}) %all-to-all-start.2) | async-done | bytes 262176 | tf_op jit(solution)/shard_map/all_to_all | solution.py:901
  110.1 9.1 %shard_map.401 = (bf16[192,832]{1,0:T(8,128)(2,1)}, bf16[576,832]{1,0:T(8,128)(2,1)}, f32[192,192]{1,0:T(8,128)}, f32[32,8,128]{2,1,0:T(8,128)}, f32[16,128]{1,0:T(8,128)}) custom-call(s32[1]{0:T(128)} %bitcast.refs_0_, f32[32,16,128]{2,1,0:T(8,128)} %copy-done.11, f32[32,8,128]{2,1,0:T(8,128)} %copy-done.6, ...), custom_call_target="tpu_custom_call" | custom-call | flops 16499999744 | bytes 10885124 | tf_op jit(solution)/shard_map/pallas_call | solution.py:68
  119.2 2.6 all-to-all-start.3
  121.7 2.6 shard_map.402
  124.4 5.6 %all-to-all-done.3.refs_1_ = f32[32,8,128]{2,1,0:T(8,128)S(1)} async-done(((f32[32,8,128]{2,1,0:T(8,128)}), f32[32,8,128]{2,1,0:T(8,128)S(1)}, u32[]{:S(2)}, u32[]{:S(2)}) %all-to-all-start.3) | async-done | bytes 131104 | tf_op jit(solution)/shard_map/all_to_all | solution.py:901
  130.0 3.5 all-to-all-start.5
  133.4 8.1 %shard_map.403 = (bf16[384,1536]{1,0:T(8,128)(2,1)}, bf16[384,384]{1,0:T(8,128)(2,1)}, f32[192,320]{1,0:T(8,128)}, f32[192,128]{1,0:T(8,128)}, bf16[3,4,80,1536]...) custom-call(s32[1]{0:T(128)} %bitcast.refs_0_, ...), custom_call_target="tpu_custom_call" | custom-call | flops 9900000256 | bytes 10139652 | tf_op jit(solution)/shard_map/pallas_call | solution.py:68
  141.6 3.1 all-to-all-start.4
  148.9 6.4 %all-to-all-done.4.refs_0_ = f32[32,16,128]{2,1,0:T(8,128)S(1)} async-done(((f32[32,16,128]{2,1,0:T(8,128)}), f32[32,16,128]{2,1,0:T(8,128)S(1)}, u32[]{:S(2)}, u32[]{:S(2)}) %all-to-all-start.4) | async-done | bytes 262176 | tf_op jit(solution)/shard_map/all_to_all | solution.py:901
  156.0 3.1 shard_map.404
  159.1 2.7 all-to-all-start.7
  164.9 7.5 %all-to-all-done.7.refs_0_ = f32[32,16,128]{2,1,0:T(8,128)S(1)} async-done(((f32[32,16,128]{2,1,0:T(8,128)}), f32[32,16,128]{2,1,0:T(8,128)S(1)}, u32[]{:S(2)}, u32[]{:S(2)}) %all-to-all-start.7) | async-done | bytes 262176 | tf_op jit(solution)/shard_map/all_to_all | solution.py:901
  173.1 2.1 shard_map.406
  175.2 5.3 %shard_map.408.refs_20_ = bf16[4,3200,128]{2,1,0:T(8,128)(2,1)} custom-call(s32[1]{0:T(128)} %bitcast.refs_0_, bf16[192,320]{1,0:T(8,128)(2,1)} %get-tuple-element.153.refs_2_.refs_1_, bf16[192,128]{1,0:T(8,128)(2,1)} %get-tuple-element.154.refs_3_.refs_2_, bf16[384,1536]{1,0:T(8,128)(2,1)} %get-tuple-element.163.refs_3_, ...), custom_call_target="tpu_custom_call" | custom-call | flops 5500000256 | bytes 4923396 | tf_op jit(solution)/shard_map/pallas_call | solution.py:68
  182.1 3.5 all-to-all-start.6
  185.6 6.1 %shard_map.407 = (f32[192,192]{1,0:T(8,128)}, f32[32,8,128]{2,1,0:T(8,128)}) custom-call(f32[8,128]{1,0:T(8,128)} %get-tuple-element.148.refs_2_.refs_0_.refs_3_, f32[4,1152]{1,0:T(4,128)} %get-tuple-element.121.refs_3_.refs_2_.refs_1_.refs_4_.refs_5_, bf16[192,320]{1,0:T(8,128)(2,1)} %get-tuple-element.153.refs_2_.refs_1_, ...), custom_call_target="tpu_custom_call" | custom-call | flops 6160000000 | bytes 3962880 | tf_op jit(solution)/shard_map/pallas_call | solution.py:68
  191.9 2.8 all-to-all-start.8
  195.5 7.5 %all-to-all-done.8.refs_0_ = f32[32,8,128]{2,1,0:T(8,128)S(1)} async-done(((f32[32,8,128]{2,1,0:T(8,128)}), f32[32,8,128]{2,1,0:T(8,128)S(1)}, u32[]{:S(2)}, u32[]{:S(2)}) %all-to-all-start.8) | async-done | bytes 131104 | tf_op jit(solution)/shard_map/all_to_all | solution.py:901
  203.7 9.9 %shard_map.409 = (bf16[192,576]{1,0:T(8,128)(2,1)}, f32[1152,256]{1,0:T(8,128)}, f32[1152,320]{1,0:T(8,128)}, f32[1152,128]{1,0:T(8,128)}, f32[1152,128]{1,0:T(8...) custom-call(f32[32,8,128]{2,1,0:T(8,128)} %copy-done.21, f32[16,128]{1,0:T(8,128)} %get-tuple-element.158.refs_1_, ...), custom_call_target="tpu_custom_call" | custom-call | flops 16499999744 | bytes 10975232 | tf_op jit(solution)/shard_map/pallas_call | solution.py:68
  213.7 2.6 all-to-all-start.9
  216.2 2.7 shard_map.410
  219.0 7.9 %all-to-all-done.9.refs_0_ = f32[32,16,128]{2,1,0:T(8,128)S(1)} async-done(((f32[32,16,128]{2,1,0:T(8,128)}), f32[32,16,128]{2,1,0:T(8,128)S(1)}, u32[]{:S(2)}, u32[]{:S(2)}) %all-to-all-start.9) | async-done | bytes 262176 | tf_op jit(solution)/shard_map/all_to_all | solution.py:901
  227.6 4.7 %shard_map.411 = (bf16[1152,320]{1,0:T(8,128)(2,1)}, bf16[1152,128]{1,0:T(8,128)(2,1)}, f32[16,128]{1,0:T(8,128)}) custom-call(f32[32,16,128]{2,1,0:T(8,128)} %copy-done.12, f32[16,128]{1,0:T(8,128)} %get-tuple-element.162.refs_14_.refs_1_.refs_3_, f32[8,128]{1,0:T(8,128)} %get-tuple-element.133.refs_1_.refs_2_.refs_0_.refs_4_, ...), custom_call_target="tpu_custom_call" | custom-call | flops 7699999744 | bytes 6051840 | tf_op jit(solution)/shard_map/pallas_call | solution.py:68
  232.2 11.0 %shard_map.412 = (bf16[2,4224,128]{2,1,0:T(8,128)(2,1)}, bf16[2,4224,128]{2,1,0:T(8,128)(2,1)}) custom-call(s32[1]{0:T(128)} %bitcast.refs_0_, bf16[1152,320]{1,0:T(8,128)(2,1)} %get-tuple-element.170.refs_1_.refs_2_, bf16[1152,128]{1,0:T(8,128)(2,1)} %get-tuple-element.171.refs_2_.refs_3_, bf16[1728,1536]{1,0:T(8,128)(2,1)} %get-tuple-element.174.refs_3_, ...), custom_call_target="tpu_custom_call" | custom-call | flops 11000000512 | bytes 13025284 | tf_op jit(solution)/shard_map/pallas_call | solution.py:68
  246.9 2.2 shard_map.413
  251.3 3.8 shard_map.414
  256.0 15.2 %shard_map.415 = (f32[1152,192]{1,0:T(8,128)}, f32[32,8,128]{2,1,0:T(8,128)}) custom-call(f32[8,128]{1,0:T(8,128)} %get-tuple-element.133.refs_1_.refs_2_.refs_0_.refs_4_, f32[4,1152]{1,0:T(4,128)} %get-tuple-element.121.refs_3_.refs_2_.refs_1_.refs_4_.refs_5_, bf16[1152,320]{1,0:T(8,128)(2,1)} %get-tuple-element.170.refs_1_.refs_2_, ...), custom_call_target="tpu_custom_call" | custom-call | flops 17600000000 | bytes 6789120 | tf_op jit(solution)/shard_map/pallas_call | solution.py:68
  271.2 2.8 all-to-all-start.10
  274.0 1.9 shard_map.416
  277.7 4.9 %collective-permute-done.12.refs_1_ = bf16[1,4224,128]{2,1,0:T(8,128)(2,1)S(1)} collective-permute-done((bf16[1,4224,128]{2,1,0:T(8,128)(2,1)}, bf16[1,4224,128]{2,1,0:T(8,128)(2,1)S(1)}, u32[]{:S(2)}, u32[]{:S(2)}) %collective-permute-start.12) | collective-permute-done | bytes 1081376 | tf_op jit(solution)/shard_map/ppermute | solution.py:904
  283.7 2.8 shard_map.417.refs_2_
  288.9 5.1 %all-to-all-start.11 = ((bf16[8,528,128]{2,1,0:T(8,128)(2,1)}), bf16[8,528,128]{2,1,0:T(8,128)(2,1)S(1)}, u32[]{:S(2)}, u32[]{:S(2)}) async-start(bf16[8,528,128]{2,1,0:T(8,128)(2,1)} %bitcast.31), calls=%async_computation.12 | async-start | bytes 2162688 | tf_op jit(solution)/shard_map/all_to_all | solution.py:1207
  294.0 7.5 %shard_map.419 = (bf16[1152,576]{1,0:T(8,128)(2,1)}, bf16[132,1152]{1,0:T(8,128)(2,1)}, bf16[132,1152]{1,0:T(8,128)(2,1)}, bf16[132,1152]{1,0:T(8,128)(2,1)}, bf...) custom-call(s32[1]{0:T(128)} %bitcast.refs_0_, f32[32,8,128]{2,1,0:T(8,128)} %copy-done.20, ...), custom_call_target="tpu_custom_call" | custom-call | flops 9349999616 | bytes 9224196 | tf_op jit(solution)/shard_map/pallas_call | solution.py:68
  303.8 4.2 %shard_map.421 = (bf16[2,768,128]{2,1,0:T(8,128)(2,1)}, bf16[2,768,128]{2,1,0:T(8,128)(2,1)}) custom-call(s32[1]{0:T(128)} %bitcast.refs_0_, bf16[1152,576]{1,0:T(8,128)(2,1)} %get-tuple-element.195.refs_2_.refs_1_, bf16[1152,528]{1,0:T(8,128)(2,1)} %get-tuple-element.123.refs_0_.refs_6_.refs_2_, bf16[400,128]{1,0:T(8,128)(2,1)} %shard_map.420.refs_3_.refs_1_), custom_call_target="tpu_custom_call" | custom-call | flops 4950000128 | bytes 3330052 | tf_op jit(solution)/shard_map/pallas_call | solution.py:68
  310.1 3.0 collective-permute-start.19
  315.7 3.2 collective-permute-done.14.refs_3_
  318.9 5.0 %collective-permute-done.15.refs_4_ = bf16[132,1152]{1,0:T(8,128)(2,1)S(1)} collective-permute-done((bf16[132,1152]{1,0:T(8,128)(2,1)S(1)}, bf16[132,1152]{1,0:T(8,128)(2,1)S(1)}, u32[]{:S(2)}, u32[]{:S(2)}) %collective-permute-start.15) | collective-permute-done | bytes 304160 | tf_op jit(solution)/shard_map/ppermute | solution.py:904
  324.6 3.0 shard_map.423.refs_1_
  329.2 2.4 shard_map.424
  331.6 6.1 %all-to-all-start.12 = ((bf16[8,528,128]{2,1,0:T(8,128)(2,1)}), bf16[8,528,128]{2,1,0:T(8,128)(2,1)S(1)}, u32[]{:S(2)}, u32[]{:S(2)}) async-start(bf16[8,528,128]{2,1,0:T(8,128)(2,1)} %shard_map.424), calls=%async_computation.13 | async-start | bytes 2162688 | tf_op jit(solution)/shard_map/all_to_all | solution.py:1240
  340.3 2.0 collective-permute-start.21
  343.0 1.9 collective-permute-start.20
  345.1 14.8 %collective-permute-done.21.refs_3_ = bf16[400,128]{1,0:T(8,128)(2,1)S(1)} collective-permute-done((bf16[400,128]{1,0:T(8,128)(2,1)S(1)}, bf16[400,128]{1,0:T(8,128)(2,1)S(1)}, u32[]{:S(2)}, u32[]{:S(2)}) %collective-permute-start.21) | collective-permute-done | bytes 102432 | tf_op jit(solution)/shard_map/ppermute | solution.py:1136
  362.8 2.3 all-to-all-done.12.refs_2_.refs_0_
  367.8 3.6 all-to-all-start.13
  373.5 2.8 shard_map.426
  376.3 3.4 all-to-all-done.13.refs_0_
  381.9 3.4 all-to-all-start.14
  385.4 7.5 %shard_map.429 = (f32[2,345600]{1,0:T(2,128)}, f32[864,32]{1,0:T(8,128)}, f32[64,832]{1,0:T(8,128)}, f32[40,832]{1,0:T(8,128)}, f32[8,832]{1,0:T(8,128)}, /*index=5*/f32[32,832]{1,0:T(8,128)}) custom-call(bf16[8,528,128]{2,1,0:T(8,128)(2,1)} %copy-done.2, f32[80,4320]{1,0:T(8,128)} %get-tuple-element.201.refs_1_), custom_call_target="tpu_custom_call" | custom-call | flops 8800000000 | bytes 5818368 | tf_op jit(solution)/shard_map/pallas_call | solution.py:68
  392.9 2.0 pad_maximum_fusion
  (249 shorter events, 66.9 us)
Async XLA Ops:
  11.2 18.7 %collective-permute-start.1 = (bf16[736,128]{1,0:T(8,128)(2,1)}, bf16[736,128]{1,0:T(8,128)(2,1)S(1)}, u32[]{:S(2)}, u32[]{:S(2)}) collective-permute-start(bf16[736,128]{1,0:T(8,128)(2,1)} %get-tuple-element.119.refs_2_), channel_id=1, source_target_pairs={{0,2},{1,3},{2,0},{3,1},{4,6},{5,7},{6,4},{7,5},{8,10},{9,11},{10,... | collective-permute-start | bytes 565256 | tf_op jit(solution)/shard_map/ppermute | solution.py:904
  14.1 22.0 %collective-permute-start = (bf16[736,128]{1,0:T(8,128)(2,1)}, bf16[736,128]{1,0:T(8,128)(2,1)}, u32[]{:S(2)}, u32[]{:S(2)}) collective-permute-start(bf16[736,128]{1,0:T(8,128)(2,1)} %get-tuple-element.119.refs_2_), channel_id=1, source_target_pairs={{0,1},{1,0},{2,3},{3,2},{4,5},{5,4},{6,7},{7,6},{8,9},{9,8},{10,11... | collective-permute-start | bytes 565256 | tf_op jit(solution)/shard_map/ppermute | solution.py:904
  14.1 20.2 %all-to-all-start = ((bf16[4,132,1152]{2,1,0:T(8,128)(2,1)}), bf16[4,132,1152]{2,1,0:T(8,128)(2,1)S(1)}, u32[]{:S(2)}, u32[]{:S(2)}) async-start(bf16[4,132,1152]{2,1,0:T(8,128)(2,1)} %get-tuple-element.118.refs_1_), calls=%async_computation | async-start | bytes 2506752 | tf_op jit(solution)/shard_map/all_to_all | solution.py:936
  29.9 2.8 collective-permute-start.2
  35.4 21.0 %collective-permute-start.4 = (bf16[3168,128]{1,0:T(8,128)(2,1)}, bf16[3168,128]{1,0:T(8,128)(2,1)S(1)}, u32[]{:S(2)}, u32[]{:S(2)}) collective-permute-start(bf16[3168,128]{1,0:T(8,128)(2,1)} %shard_map.396.refs_7_), channel_id=1, source_target_pairs={{0,2},{1,3},{2,0},{3,1},{4,6},{5,7},{6,4},{7,5},{8,10},{9,11},{10,... | collective-permute-start | bytes 2433032 | tf_op jit(solution)/shard_map/ppermute | solution.py:904
  36.1 31.0 %collective-permute-start.3 = (bf16[3168,128]{1,0:T(8,128)(2,1)}, bf16[3168,128]{1,0:T(8,128)(2,1)}, u32[]{:S(2)}, u32[]{:S(2)}) collective-permute-start(bf16[3168,128]{1,0:T(8,128)(2,1)} %shard_map.396.refs_7_), channel_id=1, source_target_pairs={{0,1},{1,0},{2,3},{3,2},{4,5},{5,4},{6,7},{7,6},{8,9},{9,8},{10,11... | collective-permute-start | bytes 2433032 | tf_op jit(solution)/shard_map/ppermute | solution.py:904
  43.3 21.6 %all-to-all-start.1 = ((f32[32,8,128]{2,1,0:T(8,128)}), f32[32,8,128]{2,1,0:T(8,128)S(1)}, u32[]{:S(2)}, u32[]{:S(2)}) async-start(f32[32,8,128]{2,1,0:T(8,128)} %get-tuple-element.120), calls=%async_computation.1 | async-start | bytes 262144 | tf_op jit(solution)/shard_map/all_to_all | solution.py:901
  56.3 6.0 %copy-start.32 = (bf16[3168,128]{1,0:T(8,128)(2,1)}, bf16[3168,128]{1,0:T(8,128)(2,1)S(1)}, u32[]{:S(2)}) copy-start(bf16[3168,128]{1,0:T(8,128)(2,1)S(1)} %collective-permute-done.4.refs_9_) | copy-start | bytes 2433028
  56.3 10.8 %collective-permute-start.5 = (bf16[3168,128]{1,0:T(8,128)(2,1)S(1)}, bf16[3168,128]{1,0:T(8,128)(2,1)}, u32[]{:S(2)}, u32[]{:S(2)}) collective-permute-start(bf16[3168,128]{1,0:T(8,128)(2,1)S(1)} %collective-permute-done.4.refs_9_), channel_id=1, source_target_pairs={{0,1},{1,0},{2,3},{3,2},{4,5},{5,4},{6,7},{7,6},{8,9},{9,8},{10,11... | collective-permute-start | bytes 2433032 | tf_op jit(solution)/shard_map/ppermute | solution.py:904
  65.5 25.9 %collective-permute-start.7 = (bf16[4176,128]{1,0:T(8,128)(2,1)}, bf16[4176,128]{1,0:T(8,128)(2,1)S(1)}, u32[]{:S(2)}, u32[]{:S(2)}) collective-permute-start(bf16[4176,128]{1,0:T(8,128)(2,1)} %shard_map.399.refs_11_.refs_7_), channel_id=1, source_target_pairs={{0,2},{1,3},{2,0},{3,1},{4,6},{5,7},{6,4},{7,5},{8,10},{9,11},{10,... | collective-permute-start | bytes 3207176 | tf_op jit(solution)/shard_map/ppermute | solution.py:904
  67.1 33.5 %collective-permute-start.6 = (bf16[4176,128]{1,0:T(8,128)(2,1)}, bf16[4176,128]{1,0:T(8,128)(2,1)S(1)}, u32[]{:S(2)}, u32[]{:S(2)}) collective-permute-start(bf16[4176,128]{1,0:T(8,128)(2,1)} %shard_map.399.refs_11_.refs_7_), channel_id=1, source_target_pairs={{0,1},{1,0},{2,3},{3,2},{4,5},{5,4},{6,7},{7,6},{8,9},{9,8},{10,11... | collective-permute-start | bytes 3207176 | tf_op jit(solution)/shard_map/ppermute | solution.py:904
  92.5 6.4 %copy-start.16 = (bf16[8,2,6,6,32]{4,1,3,2,0:T(2,128)(2,1)S(1)}, bf16[8,2,6,6,32]{4,1,3,2,0:T(2,128)(2,1)}, u32[]{:S(2)}) copy-start(bf16[8,2,6,6,32]{4,1,3,2,0:T(2,128)(2,1)} %param.45) | copy-start | bytes 110596
  92.5 6.4 %copy-start.17 = (bf16[8,2,6,6,32]{4,1,3,2,0:T(2,128)(2,1)S(1)}, bf16[8,2,6,6,32]{4,1,3,2,0:T(2,128)(2,1)}, u32[]{:S(2)}) copy-start(bf16[8,2,6,6,32]{4,1,3,2,0:T(2,128)(2,1)} %param.44) | copy-start | bytes 110596
  92.5 6.4 %copy-start.18 = (bf16[8,2,6,6,80]{4,1,3,2,0:T(2,128)(2,1)S(1)}, bf16[8,2,6,6,80]{4,1,3,2,0:T(2,128)(2,1)}, u32[]{:S(2)}) copy-start(bf16[8,2,6,6,80]{4,1,3,2,0:T(2,128)(2,1)} %param.43) | copy-start | bytes 276484
  92.5 6.4 %copy-start.19 = (bf16[8,2,6,6,64]{4,1,3,2,0:T(2,128)(2,1)S(1)}, bf16[8,2,6,6,64]{4,1,3,2,0:T(2,128)(2,1)}, u32[]{:S(2)}) copy-start(bf16[8,2,6,6,64]{4,1,3,2,0:T(2,128)(2,1)} %param.42) | copy-start | bytes 221188
  92.5 16.9 %collective-permute-start.8 = (bf16[4176,128]{1,0:T(8,128)(2,1)}, bf16[4176,128]{1,0:T(8,128)(2,1)}, u32[]{:S(2)}, u32[]{:S(2)}) collective-permute-start(bf16[4176,128]{1,0:T(8,128)(2,1)} %shard_map.400.refs_13_.refs_9_), channel_id=1, source_target_pairs={{0,1},{1,0},{2,3},{3,2},{4,5},{5,4},{6,7},{7,6},{8,9},{9,8},{10,11... | collective-permute-start | bytes 3207176 | tf_op jit(solution)/shard_map/ppermute | solution.py:904
  92.6 16.8 %all-to-all-start.2 = ((f32[32,16,128]{2,1,0:T(8,128)}), f32[32,16,128]{2,1,0:T(8,128)S(1)}, u32[]{:S(2)}, u32[]{:S(2)}) async-start(f32[32,16,128]{2,1,0:T(8,128)} %get-tuple-element.127), calls=%async_computation.2 | async-start | bytes 524288 | tf_op jit(solution)/shard_map/all_to_all | solution.py:901
  100.7 8.7 %copy-start.31 = (bf16[4176,128]{1,0:T(8,128)(2,1)}, bf16[4176,128]{1,0:T(8,128)(2,1)S(1)}, u32[]{:S(2)}) copy-start(bf16[4176,128]{1,0:T(8,128)(2,1)S(1)} %collective-permute-done.6.refs_12_.refs_8_) | copy-start | bytes 3207172
  119.2 10.8 %all-to-all-start.3 = ((f32[32,8,128]{2,1,0:T(8,128)}), f32[32,8,128]{2,1,0:T(8,128)S(1)}, u32[]{:S(2)}, u32[]{:S(2)}) async-start(f32[32,8,128]{2,1,0:T(8,128)} %get-tuple-element.134), calls=%async_computation.3 | async-start | bytes 262144 | tf_op jit(solution)/shard_map/all_to_all | solution.py:901
  130.0 11.6 %all-to-all-start.5 = ((bf16[4,2,2,6,6,208]{5,2,4,3,1,0:T(2,128)(2,1)}), bf16[4,2,2,6,6,208]{5,2,4,3,1,0:T(2,128)(2,1)S(1)}, u32[]{:S(2)}, u32[]{:S(2)}) async-start(bf16[4,2,2,6,6,208]{5,2,4,3,1,0:T(2,128)(2,1)} %bitcast.14), calls=%async_computation.5 | async-start | bytes 589824 | tf_op jit(solution)/shard_map/all_to_all | solution.py:966
  141.6 13.7 %all-to-all-start.4 = ((f32[32,16,128]{2,1,0:T(8,128)}), f32[32,16,128]{2,1,0:T(8,128)S(1)}, u32[]{:S(2)}, u32[]{:S(2)}) async-start(f32[32,16,128]{2,1,0:T(8,128)} %get-tuple-element.139), calls=%async_computation.4 | async-start | bytes 524288 | tf_op jit(solution)/shard_map/all_to_all | solution.py:901
  159.0 5.5 %copy-start.24 = (bf16[192,128]{1,0:T(8,128)(2,1)S(1)}, bf16[192,128]{1,0:T(8,128)(2,1)}, u32[]{:S(2)}) copy-start(bf16[192,128]{1,0:T(8,128)(2,1)} %get-tuple-element.146) | copy-start | bytes 147460
  159.1 5.6 %copy-start.23 = (bf16[192,128]{1,0:T(8,128)(2,1)S(1)}, bf16[192,128]{1,0:T(8,128)(2,1)}, u32[]{:S(2)}) copy-start(bf16[192,128]{1,0:T(8,128)(2,1)} %get-tuple-element.147) | copy-start | bytes 147460
  159.1 13.3 %all-to-all-start.7 = ((f32[32,16,128]{2,1,0:T(8,128)}), f32[32,16,128]{2,1,0:T(8,128)S(1)}, u32[]{:S(2)}, u32[]{:S(2)}) async-start(f32[32,16,128]{2,1,0:T(8,128)} %get-tuple-element.149), calls=%async_computation.7 | async-start | bytes 524288 | tf_op jit(solution)/shard_map/all_to_all | solution.py:901
  161.8 85.0 %reduce-scatter.2.cloned.1.call-start = ((), (), s32[]{:S(2)}) async-start(), calls=%async_computation.16 | async-start | bytes 4096000 | tf_op jit(solution)/shard_map/reduce_scatter | solution.py:1145
  182.1 9.8 %all-to-all-start.6 = ((bf16[4,2,2,6,6,208]{5,2,4,3,1,0:T(2,128)(2,1)}), bf16[4,2,2,6,6,208]{5,2,4,3,1,0:T(2,128)(2,1)S(1)}, u32[]{:S(2)}, u32[]{:S(2)}) async-start(bf16[4,2,2,6,6,208]{5,2,4,3,1,0:T(2,128)(2,1)} %copy.92), calls=%async_computation.6 | async-start | bytes 589824 | tf_op jit(solution)/shard_map/all_to_all | solution.py:1146
  191.9 11.1 %all-to-all-start.8 = ((f32[32,8,128]{2,1,0:T(8,128)}), f32[32,8,128]{2,1,0:T(8,128)S(1)}, u32[]{:S(2)}, u32[]{:S(2)}) async-start(f32[32,8,128]{2,1,0:T(8,128)} %get-tuple-element.157), calls=%async_computation.8 | async-start | bytes 262144 | tf_op jit(solution)/shard_map/all_to_all | solution.py:901
  213.7 13.2 %all-to-all-start.9 = ((f32[32,16,128]{2,1,0:T(8,128)}), f32[32,16,128]{2,1,0:T(8,128)S(1)}, u32[]{:S(2)}, u32[]{:S(2)}) async-start(f32[32,16,128]{2,1,0:T(8,128)} %get-tuple-element.165), calls=%async_computation.9 | async-start | bytes 524288 | tf_op jit(solution)/shard_map/all_to_all | solution.py:901
  232.2 11.0 %copy-start = (bf16[4,2,2,6,6,208]{5,4,3,2,1,0:T(8,128)(2,1)S(1)}, bf16[4,2,2,6,6,208]{5,4,3,2,1,0:T(8,128)(2,1)}, u32[]{:S(2)}) copy-start(bf16[4,2,2,6,6,208]{5,4,3,2,1,0:T(8,128)(2,1)} %shard_map.405.refs_21_) | copy-start | bytes 718852
  243.2 6.8 %collective-permute-start.9 = (bf16[2,4224,128]{2,1,0:T(8,128)(2,1)}, bf16[2,4224,128]{2,1,0:T(8,128)(2,1)S(1)}, u32[]{:S(2)}, u32[]{:S(2)}) collective-permute-start(bf16[2,4224,128]{2,1,0:T(8,128)(2,1)} %get-tuple-element.178.refs_2_), channel_id=1, source_target_pairs={{0,1},{1,0},{2,3},{3,2},{4,5},{5,4},{6,7},{7,6},{8,9},{9,8},{10,11... | collective-permute-start | bytes 6488072 | tf_op jit(solution)/shard_map/ppermute | solution.py:904
  249.1 24.9 %collective-permute-start.10 = (bf16[4,400,128]{2,1,0:T(8,128)(2,1)}, bf16[4,400,128]{2,1,0:T(8,128)(2,1)}, u32[]{:S(2)}, u32[]{:S(2)}) collective-permute-start(bf16[4,400,128]{2,1,0:T(8,128)(2,1)} %get-tuple-element.179.refs_2_), channel_id=1, source_target_pairs={{0,4},{4,0},{8,12},{12,8},{16,20},{20,16},{24,28},{28,24},{1,5},{5... | collective-permute-start | bytes 1228808 | tf_op jit(solution)/shard_map/ppermute | solution.py:1136
  255.2 27.5 %collective-permute-start.12 = (bf16[1,4224,128]{2,1,0:T(8,128)(2,1)}, bf16[1,4224,128]{2,1,0:T(8,128)(2,1)S(1)}, u32[]{:S(2)}, u32[]{:S(2)}) collective-permute-start(bf16[1,4224,128]{2,1,0:T(8,128)(2,1)} %get-tuple-element.189), channel_id=1, source_target_pairs={{0,2},{1,3},{2,0},{3,1},{4,6},{5,7},{6,4},{7,5},{8,10},{9,11},{10,... | collective-permute-start | bytes 3244040 | tf_op jit(solution)/shard_map/ppermute | solution.py:904
  271.2 17.7 %all-to-all-start.10 = ((f32[32,8,128]{2,1,0:T(8,128)}), f32[32,8,128]{2,1,0:T(8,128)S(1)}, u32[]{:S(2)}, u32[]{:S(2)}) async-start(f32[32,8,128]{2,1,0:T(8,128)} %get-tuple-element.181), calls=%async_computation.11 | async-start | bytes 262144 | tf_op jit(solution)/shard_map/all_to_all | solution.py:901
  276.0 10.5 %collective-permute-start.11 = (bf16[2,400,128]{2,1,0:T(8,128)(2,1)}, bf16[2,400,128]{2,1,0:T(8,128)(2,1)S(1)}, u32[]{:S(2)}, u32[]{:S(2)}) collective-permute-start(bf16[2,400,128]{2,1,0:T(8,128)(2,1)} %get-tuple-element.188), channel_id=1, source_target_pairs={{0,8},{4,12},{8,0},{12,4},{16,24},{20,28},{24,16},{28,20},{1,9},{5... | collective-permute-start | bytes 614408 | tf_op jit(solution)/shard_map/ppermute | solution.py:1136
  288.9 12.7 %collective-permute-start.16 = (bf16[1,400,128]{2,1,0:T(8,128)(2,1)}, bf16[1,400,128]{2,1,0:T(8,128)(2,1)S(1)}, u32[]{:S(2)}, u32[]{:S(2)}) collective-permute-start(bf16[1,400,128]{2,1,0:T(8,128)(2,1)} %get-tuple-element.196), channel_id=1, source_target_pairs={{0,16},{4,20},{8,24},{12,28},{16,0},{20,4},{24,8},{28,12},{1,17},{... | collective-permute-start | bytes 307208 | tf_op jit(solution)/shard_map/ppermute | solution.py:1136
  288.9 5.1 %copy-start.20 = (f32[32,8,128]{2,1,0:T(8,128)}, f32[32,8,128]{2,1,0:T(8,128)S(1)}, u32[]{:S(2)}) copy-start(f32[32,8,128]{2,1,0:T(8,128)S(1)} %all-to-all-done.10.refs_1_) | copy-start | bytes 393220
  288.9 38.6 %all-to-all-start.11 = ((bf16[8,528,128]{2,1,0:T(8,128)(2,1)}), bf16[8,528,128]{2,1,0:T(8,128)(2,1)S(1)}, u32[]{:S(2)}, u32[]{:S(2)}) async-start(bf16[8,528,128]{2,1,0:T(8,128)(2,1)} %bitcast.31), calls=%async_computation.12 | async-start | bytes 2162688 | tf_op jit(solution)/shard_map/all_to_all | solution.py:1207
  303.8 4.8 %copy-start.35 = (bf16[132,1152]{1,0:T(8,128)(2,1)S(1)}, bf16[132,1152]{1,0:T(8,128)(2,1)}, u32[]{:S(2)}) copy-start(bf16[132,1152]{1,0:T(8,128)(2,1)} %get-tuple-element.193) | copy-start | bytes 912388
  303.8 5.1 %copy-start.34 = (bf16[132,1152]{1,0:T(8,128)(2,1)S(1)}, bf16[132,1152]{1,0:T(8,128)(2,1)}, u32[]{:S(2)}) copy-start(bf16[132,1152]{1,0:T(8,128)(2,1)} %get-tuple-element.194) | copy-start | bytes 912388
  303.8 6.2 %copy-start.25 = (f32[16,128]{1,0:T(8,128)S(1)}, f32[16,128]{1,0:T(8,128)}, u32[]{:S(2)}) copy-start(f32[16,128]{1,0:T(8,128)} %get-tuple-element.182.refs_2_) | copy-start | bytes 24580
  303.8 6.2 %copy-start.44 = (bf16[400,128]{1,0:T(8,128)(2,1)S(1)}, bf16[400,128]{1,0:T(8,128)(2,1)}, u32[]{:S(2)}) copy-start(bf16[400,128]{1,0:T(8,128)(2,1)} %shard_map.420.refs_3_.refs_1_) | copy-start | bytes 307204
  308.0 5.0 %collective-permute-start.17 = (bf16[2,768,128]{2,1,0:T(8,128)(2,1)}, bf16[2,768,128]{2,1,0:T(8,128)(2,1)S(1)}, u32[]{:S(2)}, u32[]{:S(2)}) collective-permute-start(bf16[2,768,128]{2,1,0:T(8,128)(2,1)} %get-tuple-element.198), channel_id=1, source_target_pairs={{0,1},{1,0},{2,3},{3,2},{4,5},{5,4},{6,7},{7,6},{8,9},{9,8},{10,11... | collective-permute-start | bytes 1179656 | tf_op jit(solution)/shard_map/ppermute | solution.py:904
  308.1 7.6 %collective-permute-start.13 = (bf16[132,1152]{1,0:T(8,128)(2,1)S(1)}, bf16[132,1152]{1,0:T(8,128)(2,1)S(1)}, u32[]{:S(2)}, u32[]{:S(2)}) collective-permute-start(bf16[132,1152]{1,0:T(8,128)(2,1)S(1)} %copy-done.36), channel_id=1, source_target_pairs={{0,1},{1,0},{2,3},{3,2},{4,5},{5,4},{6,7},{7,6},{8,9},{9,8},{10,11... | collective-permute-start | bytes 912392 | tf_op jit(solution)/shard_map/ppermute | solution.py:904
  308.6 10.3 %collective-permute-start.14 = (bf16[132,1152]{1,0:T(8,128)(2,1)S(1)}, bf16[132,1152]{1,0:T(8,128)(2,1)S(1)}, u32[]{:S(2)}, u32[]{:S(2)}) collective-permute-start(bf16[132,1152]{1,0:T(8,128)(2,1)S(1)} %copy-done.35), channel_id=1, source_target_pairs={{0,2},{1,3},{2,0},{3,1},{4,6},{5,7},{6,4},{7,5},{8,10},{9,11},{10,... | collective-permute-start | bytes 912392 | tf_op jit(solution)/shard_map/ppermute | solution.py:904
  308.9 14.9 %collective-permute-start.15 = (bf16[132,1152]{1,0:T(8,128)(2,1)S(1)}, bf16[132,1152]{1,0:T(8,128)(2,1)S(1)}, u32[]{:S(2)}, u32[]{:S(2)}) collective-permute-start(bf16[132,1152]{1,0:T(8,128)(2,1)S(1)} %copy-done.34), channel_id=1, source_target_pairs={{0,3},{1,2},{2,1},{3,0},{4,7},{5,6},{6,5},{7,4},{8,11},{9,10},{10,... | collective-permute-start | bytes 912392 | tf_op jit(solution)/shard_map/ppermute | solution.py:904
  310.1 17.5 %collective-permute-start.19 = (bf16[400,128]{1,0:T(8,128)(2,1)S(1)}, bf16[400,128]{1,0:T(8,128)(2,1)S(1)}, u32[]{:S(2)}, u32[]{:S(2)}) collective-permute-start(bf16[400,128]{1,0:T(8,128)(2,1)S(1)} %copy-done.44), channel_id=1, source_target_pairs={{0,16},{4,20},{8,24},{12,28},{16,0},{20,4},{24,8},{28,12},{1,17},{... | collective-permute-start | bytes 307208 | tf_op jit(solution)/shard_map/ppermute | solution.py:1136
  315.7 8.2 %copy-start.37 = (bf16[132,1152]{1,0:T(8,128)(2,1)}, bf16[132,1152]{1,0:T(8,128)(2,1)S(1)}, u32[]{:S(2)}) copy-start(bf16[132,1152]{1,0:T(8,128)(2,1)S(1)} %collective-permute-done.13.refs_2_) | copy-start | bytes 912388
  318.9 5.0 %copy-start.38 = (bf16[132,1152]{1,0:T(8,128)(2,1)}, bf16[132,1152]{1,0:T(8,128)(2,1)S(1)}, u32[]{:S(2)}) copy-start(bf16[132,1152]{1,0:T(8,128)(2,1)S(1)} %collective-permute-done.14.refs_3_) | copy-start | bytes 912388
  331.6 8.2 %copy-start.27 = (f32[8,128]{1,0:T(8,128)S(1)}, f32[8,128]{1,0:T(8,128)}, u32[]{:S(2)}) copy-start(f32[8,128]{1,0:T(8,128)} %get-tuple-element.213) | copy-start | bytes 12292
  331.6 8.3 %copy-start.41 = (bf16[1,768,128]{2,1,0:T(8,128)(2,1)S(1)}, bf16[1,768,128]{2,1,0:T(8,128)(2,1)}, u32[]{:S(2)}) copy-start(bf16[1,768,128]{2,1,0:T(8,128)(2,1)} %get-tuple-element.200) | copy-start | bytes 589828
  331.6 10.7 %copy-start.46 = (bf16[400,128]{1,0:T(8,128)(2,1)S(1)}, bf16[400,128]{1,0:T(8,128)(2,1)}, u32[]{:S(2)}) copy-start(bf16[400,128]{1,0:T(8,128)(2,1)} %copy-done.45) | copy-start | bytes 307204
  331.6 33.5 %all-to-all-start.12 = ((bf16[8,528,128]{2,1,0:T(8,128)(2,1)}), bf16[8,528,128]{2,1,0:T(8,128)(2,1)S(1)}, u32[]{:S(2)}, u32[]{:S(2)}) async-start(bf16[8,528,128]{2,1,0:T(8,128)(2,1)} %shard_map.424), calls=%async_computation.13 | async-start | bytes 2162688 | tf_op jit(solution)/shard_map/all_to_all | solution.py:1240
  339.9 23.0 %collective-permute-start.18 = (bf16[1,768,128]{2,1,0:T(8,128)(2,1)S(1)}, bf16[1,768,128]{2,1,0:T(8,128)(2,1)S(1)}, u32[]{:S(2)}, u32[]{:S(2)}) collective-permute-start(bf16[1,768,128]{2,1,0:T(8,128)(2,1)S(1)} %copy-done.41), channel_id=1, source_target_pairs={{0,2},{1,3},{2,0},{3,1},{4,6},{5,7},{6,4},{7,5},{8,10},{9,11},{10,... | collective-permute-start | bytes 589832 | tf_op jit(solution)/shard_map/ppermute | solution.py:904
  340.3 19.6 %collective-permute-start.21 = (bf16[400,128]{1,0:T(8,128)(2,1)S(1)}, bf16[400,128]{1,0:T(8,128)(2,1)S(1)}, u32[]{:S(2)}, u32[]{:S(2)}) collective-permute-start(bf16[400,128]{1,0:T(8,128)(2,1)S(1)} %copy-done.44), channel_id=1, source_target_pairs={{0,8},{4,12},{8,0},{12,4},{16,24},{20,28},{24,16},{28,20},{1,9},{5... | collective-permute-start | bytes 307208 | tf_op jit(solution)/shard_map/ppermute | solution.py:1136
  342.3 19.5 %collective-permute-start.24 = (bf16[400,128]{1,0:T(8,128)(2,1)S(1)}, bf16[400,128]{1,0:T(8,128)(2,1)S(1)}, u32[]{:S(2)}, u32[]{:S(2)}) collective-permute-start(bf16[400,128]{1,0:T(8,128)(2,1)S(1)} %copy-done.46), channel_id=1, source_target_pairs={{0,8},{4,12},{8,0},{12,4},{16,24},{20,28},{24,16},{28,20},{1,9},{5... | collective-permute-start | bytes 307208 | tf_op jit(solution)/shard_map/ppermute | solution.py:1136
  343.0 29.1 %collective-permute-start.20 = (bf16[400,128]{1,0:T(8,128)(2,1)S(1)}, bf16[400,128]{1,0:T(8,128)(2,1)S(1)}, u32[]{:S(2)}, u32[]{:S(2)}) collective-permute-start(bf16[400,128]{1,0:T(8,128)(2,1)S(1)} %copy-done.44), channel_id=1, source_target_pairs={{0,4},{4,0},{8,12},{12,8},{16,20},{20,16},{24,28},{28,24},{1,5},{5... | collective-permute-start | bytes 307208 | tf_op jit(solution)/shard_map/ppermute | solution.py:1136
  345.0 27.2 %collective-permute-start.23 = (bf16[400,128]{1,0:T(8,128)(2,1)S(1)}, bf16[400,128]{1,0:T(8,128)(2,1)S(1)}, u32[]{:S(2)}, u32[]{:S(2)}) collective-permute-start(bf16[400,128]{1,0:T(8,128)(2,1)S(1)} %copy-done.46), channel_id=1, source_target_pairs={{0,4},{4,0},{8,12},{12,8},{16,20},{20,16},{24,28},{28,24},{1,5},{5... | collective-permute-start | bytes 307208 | tf_op jit(solution)/shard_map/ppermute | solution.py:1136
  359.9 8.0 %copy-start.47 = (bf16[400,128]{1,0:T(8,128)(2,1)}, bf16[400,128]{1,0:T(8,128)(2,1)S(1)}, u32[]{:S(2)}) copy-start(bf16[400,128]{1,0:T(8,128)(2,1)S(1)} %collective-permute-done.21.refs_3_) | copy-start | bytes 307204
  359.9 12.2 %collective-permute-start.22 = (bf16[400,128]{1,0:T(8,128)(2,1)S(1)}, bf16[400,128]{1,0:T(8,128)(2,1)S(1)}, u32[]{:S(2)}, u32[]{:S(2)}) collective-permute-start(bf16[400,128]{1,0:T(8,128)(2,1)S(1)} %collective-permute-done.21.refs_3_), channel_id=1, source_target_pairs={{0,4},{4,0},{8,12},{12,8},{16,20},{20,16},{24,28},{28,24},{1,5},{5... | collective-permute-start | bytes 307208 | tf_op jit(solution)/shard_map/ppermute | solution.py:1136
  361.8 6.0 %copy-start.48 = (bf16[400,128]{1,0:T(8,128)(2,1)}, bf16[400,128]{1,0:T(8,128)(2,1)S(1)}, u32[]{:S(2)}) copy-start(bf16[400,128]{1,0:T(8,128)(2,1)S(1)} %collective-permute-done.24.refs_7_) | copy-start | bytes 307204
  361.8 10.4 %collective-permute-start.25 = (bf16[400,128]{1,0:T(8,128)(2,1)S(1)}, bf16[400,128]{1,0:T(8,128)(2,1)S(1)}, u32[]{:S(2)}, u32[]{:S(2)}) collective-permute-start(bf16[400,128]{1,0:T(8,128)(2,1)S(1)} %collective-permute-done.24.refs_7_), channel_id=1, source_target_pairs={{0,4},{4,0},{8,12},{12,8},{16,20},{20,16},{24,28},{28,24},{1,5},{5... | collective-permute-start | bytes 307208 | tf_op jit(solution)/shard_map/ppermute | solution.py:1136
  367.8 11.8 %all-to-all-start.13 = ((bf16[8,96,128]{2,1,0:T(8,128)(2,1)}), bf16[8,96,128]{2,1,0:T(8,128)(2,1)S(1)}, u32[]{:S(2)}, u32[]{:S(2)}) async-start(bf16[8,96,128]{2,1,0:T(8,128)(2,1)} %bitcast.138), calls=%async_computation.14 | async-start | bytes 393216 | tf_op jit(solution)/shard_map/all_to_all | solution.py:1252
  381.9 12.9 %all-to-all-start.14 = ((bf16[8,96,128]{2,1,0:T(8,128)(2,1)}), bf16[8,96,128]{2,1,0:T(8,128)(2,1)S(1)}, u32[]{:S(2)}, u32[]{:S(2)}) async-start(bf16[8,96,128]{2,1,0:T(8,128)(2,1)} %shard_map.427), calls=%async_computation.15 | async-start | bytes 393216 | tf_op jit(solution)/shard_map/all_to_all | solution.py:1256
  385.3 7.5 %copy-start.7 = (f32[864,32]{1,0:T(8,128)S(1)}, f32[864,32]{1,0:T(8,128)}, u32[]{:S(2)}) copy-start(f32[864,32]{1,0:T(8,128)} %get-tuple-element.212) | copy-start | bytes 331780
  (32 other events, 45.3 us)
Sparse Core Ops, SparseCore 0:
  180.7 37.6 reduce-scatter.1

commit v4 on v3

--- a/solution.py
+++ b/solution.py
@@ -343,14 +343,15 @@
         move(tiles // 16 * 16, tiles % 16)
 
 
-def pack_kernel(pack, w_ref, s_ref, *refs):
-    *part_refs, o_ref, scratch = refs
+def pack_kernel(pack, w_ref, s_ref, o_ref):
     for at, own, wide, t, u, width in pack.kernel_tiles():
         source, columns = (w_ref, 9 * NARROW) if wide else (s_ref, 9 * SQUEEZE)
         start = columns * t + 128 * u
         o_ref[at : at + own, :] = fit_tile(source[:, start : start + width])
-    if part_refs:
-        pack_points(pack, part_refs, o_ref, pack.kernels, scratch)
+
+
+def pack_late_kernel(pack, p0, p1, p2, p3, o_ref, scratch):
+    pack_points(pack, (p0, p1, p2, p3), o_ref, 0, scratch)
 
 
 def early_first_kernel(
@@ -507,7 +508,7 @@
             out = slice(c * LATE.clip_rows, (c + 1) * LATE.clip_rows)
             a_ref[out, at_column : at_column + width] = pooled.astype(BF16)
         at_column += width
-    unpack_points(pack, me_ref[0], piece_refs, pack.kernels, raw, ws, wt_ref)
+    unpack_points(pack, me_ref[0], piece_refs, 0, raw, ws, wt_ref)
     y_ref[...] = nt(a_ref[...], wt_ref[DIRECT : DIRECT + REDUCED, :])
     tile[...] = jnp.zeros_like(tile)
     own = jnp.sum(mc_ref[...], axis=0, keepdims=True)
@@ -527,7 +528,7 @@
         h = scale * xhat + shift
         gate = jax.nn.sigmoid(h)
         if out_ref is not None:
-            out_ref[at, :] = (h * gate * masking).astype(out_ref.dtype)
+            out_ref[at, :width] = (h * gate * masking).astype(out_ref.dtype)
         dh = dz_of(at) * masking * gate * (1.0 + h * (1.0 - gate))
         dh_ref[at, :] = dh
         return carry[0] + fold8(dh * xhat), carry[1] + fold8(dh)
@@ -537,31 +538,52 @@
     return jnp.sum(first, axis=0, keepdims=True), jnp.sum(second, axis=0, keepdims=True)
 
 
+def cut_kernel(me_ref, x_ref, *o_refs):
+    size = o_refs[0].shape[0]
+    for k, o_ref in enumerate(o_refs):
+        o_ref[...] = x_ref[pl.ds(pl.multiple_of((me_ref[0] ^ k) * size, 16), size), :]
+
+
+def join_kernel(me_ref, *refs):
+    *x_refs, o_ref = refs
+    for k, x_ref in enumerate(x_refs):
+        o_ref[me_ref[0] ^ k] = x_ref[...]
+
+
 def late_outputs_kernel(
-    clips, g_ref, counts_ref, aff_ref, yd_ref, yw_ref, ys_ref, yp_ref, mc_ref,
-    ud_ref, uw_ref, us_ref, up_ref,
-    od_ref, ow_ref, os_ref, op_ref, dd_ref, dw_ref, ds_ref, dp_ref, pay_ref, st_ref, tile
+    clips, groups, me_ref, g_ref, counts_ref, aff_ref, yd_ref, yw_ref, ys_ref, yp_ref, mc_ref, *refs
 ):
+    up_refs, o_refs = refs[:groups], refs[groups : 2 * groups]
+    dd_ref, dw_ref, ds_ref, dp_ref, pay_ref, st_ref, shares, up, out, tile = refs[2 * groups :]
+    me = me_ref[0]
     means, rstds = combine_moments(g_ref[...], counts_ref[:, 3:4, :], 0, 8, 8)
     st_ref[0:8, :] = means
     st_ref[8:16, :] = rstds
     st = st_ref[...]
     tile[...] = jnp.zeros_like(tile)
-    for unit, y_ref, up, o_ref, dh_ref in zip(
-        OUTER,
-        (yd_ref, yw_ref, ys_ref, yp_ref),
-        (ud_ref, uw_ref, us_ref, up_ref),
-        (od_ref, ow_ref, os_ref, op_ref),
-        (dd_ref, dw_ref, ds_ref, dp_ref),
+    for k, ref in enumerate(up_refs):
+        shares[me ^ k] = ref[...].astype(F32)
+    at = 0
+    for unit, y_ref, dh_ref in zip(
+        OUTER, (yd_ref, yw_ref, ys_ref, yp_ref), (dd_ref, dw_ref, ds_ref, dp_ref)
     ):
         mean, rstd = outer_stats(st, unit)
         scale, shift = affine_of(aff_ref, 1, unit)
-        sums = local_backward(
-            y_ref, lambda at: up[at, :].astype(F32), m_ref=mc_ref, mean=mean, rstd=rstd,
-            scale=scale, shift=shift, dh_ref=dh_ref, out_ref=o_ref, rows=clips * LATE.clip_rows,
+        width = TILE_ROW[unit][1]
+        own = width // groups
+        for s in range(groups):
+            up[:, s * own : (s + 1) * own] = shares[s, :, at : at + own]
+        first, second = local_backward(
+            y_ref, lambda rows: up[rows, :width], m_ref=mc_ref, mean=mean, rstd=rstd, scale=scale,
+            shift=shift, dh_ref=dh_ref, out_ref=out, rows=clips * LATE.clip_rows,
         )
-        put_row(tile, TILE_ROW[unit][0], sums[0])
-        put_row(tile, 8 + TILE_ROW[unit][0], sums[1])
+        for s in range(groups):
+            shares[s, :, at : at + own] = out[:, s * own : (s + 1) * own]
+        at += own
+        put_row(tile, TILE_ROW[unit][0], first)
+        put_row(tile, 8 + TILE_ROW[unit][0], second)
+    for k, ref in enumerate(o_refs):
+        ref[...] = shares[me ^ k].astype(BF16)
     send_tile(pay_ref, tile)
 
 
@@ -646,10 +668,9 @@
     geo, clips, pack, halves, me_ref, gw_ref, gs_ref, bn_ref, bs_ref, *refs
 ):
     send_ref, grad_w, grad_s = refs[-3:]
-    if halves:
-        keep_ref = refs[-4]
-        for source, target in zip(refs[:-4], (keep_ref, send_ref)):
-            target[:, pack.kernels : pack.kernels + source.shape[1], :] = source[...]
+    keep_refs = refs[-4:-3] if halves else ()
+    for source, target in zip(refs[:-4], (*keep_refs, send_ref)):
+        target[:, pack.kernels : pack.kernels + source.shape[1], :] = source[...]
     size = geo.frame_rows
     for g_ref, b_ref, grad in ((gw_ref, bn_ref, grad_w), (gs_ref, bs_ref, grad_s)):
         for t in range(3):
@@ -664,7 +685,7 @@
             grad[t] = total
     me = me_ref[0]
     for k in range(pack.groups):
-        target, place = ((keep_ref, send_ref)[k % 2], k // 2) if halves else (send_ref, me ^ k)
+        target, place = ((*keep_refs, send_ref)[k % 2], k // 2) if halves else (send_ref, me ^ k)
         for at, own, wide, t, u, _ in pack.kernel_tiles():
             source = grad_w if wide else grad_s
             first = pl.multiple_of((me ^ k) * own, 8)
@@ -677,12 +698,11 @@
     for s in range(pack.groups):
         for at, begin, own in pack.point_parts():
             shares[s, at : at + own, : pack.features] = whole[begin + s * own : begin + (s + 1) * own, :]
-    me = me_ref[0]
     for k in range(pack.groups):
         target = (keep_ref, send_ref)[k % 2]
         for at, u, width in pack.point_blocks(0):
             target[k // 2, at : at + pack.point, :] = shares[
-                me ^ k, : pack.point, 128 * u : 128 * u + 128
+                me_ref[0] ^ k, : pack.point, 128 * u : 128 * u + 128
             ].astype(BF16)
 
 
@@ -704,11 +724,18 @@
         (even_ref, odd_ref)[k % 2][k // 2] = held[pl.ds(first, size), :].astype(BF16)
 
 
-def total_kernel(x_ref, o_ref):
-    total = x_ref[0].astype(F32)
-    for k in range(1, x_ref.shape[0]):
-        total = total + x_ref[k].astype(F32)
-    o_ref[...] = jnp.broadcast_to(total.astype(BF16)[None], o_ref.shape)
+def total_kernel(*refs):
+    *x_refs, o_ref = refs
+    at = 0
+    for x_ref in x_refs:
+        total = x_ref[0].astype(F32)
+        for k in range(1, x_ref.shape[0]):
+            total = total + x_ref[k].astype(F32)
+        size = x_ref.shape[1]
+        o_ref[:, at : at + size, :] = jnp.broadcast_to(
+            total.astype(BF16)[None], (o_ref.shape[0],) + total.shape
+        )
+        at += size
 
 
 def read_kernels(pack, rows, w_ref, s_ref, turned):
@@ -734,15 +761,12 @@
     read_kernels(pack, held[...].reshape(-1, 128), w_ref, s_ref, turned)
 
 
-def points_out_kernel(pack, x_ref, *o_refs):
-    read_points(pack, 0, x_ref[...].reshape(-1, 128), o_refs)
-
-
-def early_gradients_kernel(pack, late_pack, x_ref, late_ref, w_ref, s_ref, *refs):
+def early_gradients_kernel(pack, late_pack, size, x_ref, late_ref, w_ref, s_ref, *refs):
     *o_refs, wide, turned = refs
-    rows = x_ref[...].reshape(-1, 128)
+    rows = x_ref[:, :size, :].reshape(-1, 128)
     read_kernels(pack, rows, wide, s_ref, turned)
-    read_points(late_pack, pack.kernels, rows, o_refs)
+    read_points(late_pack, pack.kernels, rows, o_refs[len(o_refs) // 2 :])
+    read_points(pack, 0, x_ref[:, size:, :].reshape(-1, 128), o_refs[: len(o_refs) // 2])
 
     def join(g, carry):
         parts = []
@@ -941,19 +965,16 @@
         spread_kernels.reshape(2, SPREAD_COLUMNS, spread_kernels.shape[3]), (0, 2, 1)
     )
 
-    def packed(use, block, parts, behind):
-        size = use.kernels + (use.points if parts else 0)
+    def packed(use, block, behind):
         return call(
             lambda *refs: pack_kernel(use, *refs),
-            [((size, 128), BF16)],
-            [halves[block].reshape(-1, WIDE_COLUMNS), spread_rows[block]]
-            + [part.T for part in parts] + list(behind),
-            [((use.point_rows, use.point_tiles * 128), F32)],
+            [((use.kernels, 128), BF16)],
+            [halves[block].reshape(-1, WIDE_COLUMNS), spread_rows[block]] + list(behind),
+            us=2.5,
             idle=len(behind),
-            us=2.5,
         )[0]
 
-    early_shares = Shares(ordered(packed(pack, 0, (), ()), point_shares[-1], arrived)).all()
+    early_shares = Shares(ordered(packed(pack, 0, ()), point_shares[-1], arrived)).all()
     own_visible = lax.dynamic_slice_in_dim(visible, me * clips, clips, 0)
     fine = own_visible.astype(F32).reshape(rows, 1)
     mask = jnp.broadcast_to(fine, (rows, 128))
@@ -961,15 +982,11 @@
     coarse = jnp.broadcast_to(pad_late(cells[..., None]), (late_rows, 128))
 
     upstream = (upstream_direct, upstream_wide, upstream_spread, upstream_project)
-    up_joined = jnp.concatenate(upstream, axis=4)
-    up_parts = up_joined.reshape((groups, clips) + up_joined.shape[1:])
-    up_arrived = lax.all_to_all(up_parts, "ch", 0, 0)
-    ups, at = [], 0
-    for part in upstream:
-        width = part.shape[4]
-        piece = jnp.moveaxis(up_arrived[..., at : at + width], 0, 4)
-        ups.append(pad_late(piece.reshape(piece.shape[:4] + (groups * width,))))
-        at += width
+    up_rows = pad_late(jnp.concatenate(upstream, axis=4))
+    up_pieces = call(
+        cut_kernel, [((late_rows, up_rows.shape[1]), BF16)] * groups, [me_ref, up_rows], us=1
+    )
+    up_pieces = [up_pieces[0]] + [swap(up_pieces[k], k) for k in range(1, groups)]
 
     pool = jnp.asarray(pool_matrix(), BF16)
     spread_back = jnp.asarray(pool_matrix().T, BF16)
@@ -987,9 +1004,18 @@
         ],
         us=8.6,
     )
-    late_share = packed(late_pack, 1, late_parts, (act,))
+    (late_points_own,) = call(
+        lambda *refs: pack_late_kernel(late_pack, *refs),
+        [((late_pack.points, 128), BF16)],
+        [part.T for part in late_parts] + [act],
+        [((late_pack.point_rows, late_pack.point_tiles * 128), F32)],
+        us=1.5,
+        idle=1,
+    )
+    late_own = packed(pack, 1, (act,))
     counts = exchange(pay)
-    late_shares = Shares(ordered(late_share, counts))
+    late_point_shares = Shares(ordered(late_points_own, counts)).all()
+    late_shares = Shares(ordered(late_own, late_point_shares[groups // 2]))
     yd, yp, tile = call(
         lambda *refs: other_points_kernel(EARLY, clips, *refs),
         [((rows, DIRECT), F32), ((rows, PROJECT), F32), ((16, 128), F32)],
@@ -997,7 +1023,7 @@
         us=12,
     )
 
-    def second(geo, count_row, g, y, masking, pieces, other):
+    def second(geo, count_row, g, y, masking, pieces, other, behind=()):
         own = clips * geo.clip_rows
         padded = clips * geo.padded_rows
         return call(
@@ -1009,21 +1035,23 @@
                 ((3, groups, pack.spread_rows, 128 * SPREAD_TILES), BF16),
                 ((devices, 16, 128), F32), ((8, 128), F32),
             ],
-            [me_ref, g, counts, affine, y, masking, other] + pieces,
+            [me_ref, g, counts, affine, y, masking, other] + pieces + list(behind),
             [((own, REDUCED), F32), ((16, 128), F32)],
+            idle=len(behind),
             us=25 if geo is EARLY else 9,
         )
 
-    bn, bs, yw, ys, kw, ks, pay, st_r = second(EARLY, 2, counts, yr, mask, early_shares, tile)
+    bn, bs, yw, ys, kw, ks, pay, st_r = second(
+        EARLY, 2, counts, yr, mask, early_shares, tile, (late_own,)
+    )
     g = exchange(pay)
-    late_shares = late_shares.all(st_r)
     late_act, late_wt, lyr, pay, st = call(
         lambda *refs: pool_kernel(late_pack, clips, *refs),
         [
             ((late_rows, CONCAT), BF16), ((POINT, CONCAT), BF16), ((late_rows, REDUCED), F32),
             ((devices, 8, 128), F32), ((16, 128), F32),
         ],
-        [me_ref, g, counts, affine, yd, yw, ys, yp, mask, pool, coarse] + late_shares,
+        [me_ref, g, counts, affine, yd, yw, ys, yp, mask, pool, coarse] + late_point_shares,
         [
             ((rows, 384), BF16), ((rows, 384), BF16),
             ((groups, late_pack.point_rows, late_pack.point_tiles * 128), F32),
@@ -1038,26 +1066,27 @@
         [late_act, late_wt, coarse],
         us=3.7,
     )
+    late_shares = late_shares.all(g)
     lbn, lbs, lyw, lys, lkw, lks, pay, lst_r = second(LATE, 3, g, lyr, coarse, late_shares, tile)
     g = exchange(pay)
     widths = [TILE_ROW[unit][1] for unit in OUTER]
     res = call(
-        lambda *refs: late_outputs_kernel(clips, *refs),
-        [((late_rows, w), BF16) for w in widths]
+        lambda *refs: late_outputs_kernel(clips, groups, *refs),
+        [(up_pieces[0].shape, BF16)] * groups
         + [((late_rows, w), F32) for w in widths]
         + [((devices, 16, 128), F32), ((16, 128), F32)],
-        [g, counts, affine, lyd, lyw, lys, lyp, coarse] + ups,
-        [((16, 128), F32)],
+        [me_ref, g, counts, affine, lyd, lyw, lys, lyp, coarse] + up_pieces,
+        [
+            ((groups,) + up_pieces[0].shape, F32), ((late_rows, WIDE), F32), ((late_rows, WIDE), F32),
+            ((16, 128), F32),
+        ],
         us=4,
     )
-    outs, (hd, hw, hs, hp), (pay, lst) = res[:4], res[4:8], res[8:]
+    outs, (hd, hw, hs, hp), (pay, lst) = res[:groups], res[groups : groups + 4], res[groups + 4 :]
     g = exchange(pay)
 
-    out_parts = []
-    for o in outs:
-        cells = o.reshape(clips, LATE.frames, LATE.height, LATE.pitch, -1)[:, :, :, : LATE.width]
-        out_parts.append(cells.reshape(cells.shape[:4] + (groups, -1)))
-    out_joined = jnp.moveaxis(jnp.concatenate(out_parts, axis=5), 4, 0)
+    outs = [outs[0]] + [swap(outs[k], k) for k in range(1, groups)]
+
     def finish(geo, g, st, st_r, hw, hs, yw, ys, masking, behind=()):
         own = clips * geo.clip_rows
         return call(
@@ -1141,9 +1170,16 @@
     gw, gs, late_sums = finish(LATE, g, lst, lst_r, hw, hs, lyw, lys, coarse)
     hr, pay = inner(LATE, lst_r, gw, gs, lyr, lkw, lks, coarse)
     g = exchange(pay)
-    (late_kernels,) = kernel_grads(LATE, whole_units(pack.kernels), gw, gs, lbn, lbs, False)
+    (late_kernels,) = kernel_grads(
+        LATE, whole_units(pack.kernels), gw, gs, lbn, lbs, False
+    )
     late_share = lax.psum_scatter(late_kernels, "ch", scatter_dimension=0)
-    out_arrived = ordered(lax.all_to_all(out_joined, "ch", 0, 0))
+    (out_arrived,) = call(
+        join_kernel,
+        [((groups,) + outs[0].shape, BF16)],
+        [me_ref] + outs,
+        us=1,
+    )
     gy, ed, ew, es, ep, pay, late_sums_r = call(
         lambda *refs: late_input_kernel(clips, *refs),
         [((late_rows, POINT), BF16)]
@@ -1158,9 +1194,8 @@
     g = exchange(pay)
     late_points = point_grads(late_pack, late_pack.points, gy, late_act)
     gw, gs, sums = finish(EARLY, g, st, st_r, ew, es, yw, ys, mask, late_points[1:])
-    halves = kernel_grads(
-        EARLY, whole_units(pack.kernels + late_pack.points), gw, gs, bn, bs, True, late_points
-    )
+    early_size = whole_units(pack.kernels + late_pack.points)
+    halves = kernel_grads(EARLY, early_size, gw, gs, bn, bs, True, late_points)
     early_sum = Reduction(*halves)
 
     class BatchHalves(Reduction):
@@ -1221,19 +1256,24 @@
     point_halves = point_grads(pack, whole_units(pack.points), gy, act, (late_own,))
     point_sum = Reduction(*point_halves)
     kept = point_sum.halve()
+    got = late_sum.double()
+    point_own = point_sum.add(parts, *got)
+    point_parts = lax.all_to_all(point_own.reshape(batches, -1, 128), "batch", 0, 0)
     (feature_grad,) = call(
         lambda *refs: feature_kernel(pack, *refs),
         [((depth, groups * rows), F32)],
-        [me_ref] + x_parts + [kept],
+        [me_ref] + x_parts + [point_own],
         [((groups, depth, rows), BF16)],
         idle=1,
         us=2,
     )
-    got = late_sum.double()
+    while late_sum.bit > 1:
+        got = late_sum.double()
+    kernels_size, points_size = parts.shape[1], point_parts.shape[1]
     (parts,) = call(
         total_kernel,
-        [(parts.shape, BF16)],
-        [parts, feature_grad] + got,
+        [((batches, kernels_size + points_size, 128), BF16)],
+        [parts, point_parts, feature_grad] + got,
         us=2,
         idle=1 + len(got),
     )
@@ -1246,36 +1286,25 @@
         [((pack.wide, WIDE_COLUMNS), F32), ((SPREAD_COLUMNS, pack.spread), F32)],
         [mb_ref] + late_pieces,
         [((batches, late_piece, 128), BF16), ((pack.spread, SPREAD_COLUMNS), F32)],
-        us=3,
-    )
-    point_own = point_sum.add(early_total)
-    point_parts = lax.all_to_all(point_own.reshape(batches, -1, 128), "batch", 0, 0)
-    (point_parts,) = call(
-        total_kernel, [(point_parts.shape, BF16)], [point_parts, late_wide], us=1, idle=1
-    )
-    point_total = lax.all_to_all(point_parts, "batch", 0, 0)
-    out_arrived = out_arrived.reshape((held_clips,) + out_arrived.shape[2:])
+        us=4,
+    )
+    out_arrived = out_arrived.reshape(
+        held_clips, LATE.frames, LATE.height, LATE.pitch, -1
+    )[:, :, :, : LATE.width]
     outputs, at = [], 0
     for part in upstream:
         outputs.append(out_arrived[..., at : at + part.shape[4]])
         at += part.shape[4]
 
-    wide_grad, early_spread, *late_grads = call(
-        lambda *refs: early_gradients_kernel(pack, late_pack, *refs),
+    wide_grad, early_spread, *point_outs = call(
+        lambda *refs: early_gradients_kernel(pack, late_pack, kernels_size, *refs),
         [(wide_kernels.shape, F32), ((SPREAD_COLUMNS, pack.spread), F32)]
-        + [(part.shape[::-1], F32) for part in late_parts],
+        + [(part.shape[::-1], F32) for part in early_parts + late_parts],
         [early_total, late_wide],
         [((pack.wide, WIDE_COLUMNS), F32), ((pack.spread, SPREAD_COLUMNS), F32)],
         us=8,
     )
-    early_grads = call(
-        lambda *refs: points_out_kernel(pack, *refs),
-        [(part.shape[::-1], F32) for part in early_parts],
-        [point_total],
-        us=1.5,
-    )
-    early_grads = [part.T for part in early_grads]
-    late_grads = [part.T for part in late_grads]
+    point_outs = [part.T for part in point_outs]
     spread_grad = jnp.stack(
         [part.reshape(spread_kernels.shape[1:]) for part in (early_spread, late_spread)]
     )
@@ -1300,7 +1329,7 @@
         own_part(outer_pair(sums, "s"), outer_pair(late_sums, "s")),
         own_part(outer_pair(sums, "p"), outer_pair(late_sums, "p")),
     ]
-    return tuple(outputs) + (feature_grad,) + tuple(early_grads) + tuple(late_grads) + (
+    return tuple(outputs) + (feature_grad,) + tuple(point_outs) + (
         wide_grad, spread_grad,
     ) + tuple(norm_grads)
 

time: 411 us -> 400 us (0.973)
  blocking collectives: 0 us -> 15.6 us
  waiting for transfers between devices: 94.3 us -> 81.6 us
  starting transfers between devices: 79 us -> 70.9 us
  local copies, waits for them, and re-layouts: 38 us -> 32.6 us
    all_to_all x8 -> x7, waiting for transfers between devices: 43.7 us -> 23.7 us  [exchange(): return lax.all_to_all(payload, BOTH, 0, 0)]
    all_to_all x0 -> x1, blocking collectives: none -> 15.6 us  [exchange(): return lax.all_to_all(payload, BOTH, 0, 0)]
    ppermute x10, waiting for transfers between devices: 15.5 us -> 28.4 us  [batch_swap(): return lax.ppermute(value, 'batch', [(i, i ^ bit) for i in range(batches)])]
    all_to_all x3 -> x0, starting transfers between devices: 10.3 us -> none  [the longest x1 3.45 us: shards(): out_arrived = ordered(lax.all_to_all(out_joined, 'ch', 0, 0))]
    ppermute x16 -> x25, starting transfers between devices: 9.25 us -> 15.6 us  [swap(): return lax.ppermute(value, 'ch', [(i, i ^ bit) for i in range(groups)])]
    ppermute x16 -> x25, waiting for transfers between devices: 27.5 us -> 25.5 us  [swap(): return lax.ppermute(value, 'ch', [(i, i ^ bit) for i in range(groups)])]
    all_to_all x8 -> x7, starting transfers between devices: 28.7 us -> 26.7 us  [exchange(): return lax.all_to_all(payload, BOTH, 0, 0)]
    pallas_call x35 -> x36, Pallas kernels: 169 us -> 170 us  [call(): pl.pallas_call(body, out_shape=[jax.ShapeDtypeStruct(s, d) for s, d in ou...]
  transfers between devices with their start and end apart: 42 -> 47, of which waited for: 17 -> 19; matrix products, arithmetic and copies ran while one was open for 7% -> 5% of each run, Pallas kernels for 35% -> 35%
where the time goes in v4:
time: 400 us; the launch traced here: 394 us
  Pallas kernels  170 us (42%)
  waiting for transfers between devices  81.6 us (20%)
  starting transfers between devices  70.9 us (18%)
  local copies, waits for them, and re-layouts  32.6 us (8%)
  blocking collectives  15.6 us (4%)
  between operations  15 us (4%)
  other arithmetic  7.79 us (2%)
    pallas_call x36, Pallas kernels, call(): pl.pallas_call(body, out_shape=[jax.ShapeDtypeStruct(s, d) for s, d in ou...  170 us
    ppermute x10, waiting for transfers between devices, batch_swap(): return lax.ppermute(value, 'batch', [(i, i ^ bit) for i in range(batches)])  28.4 us
    all_to_all x7, starting transfers between devices, exchange(): return lax.all_to_all(payload, BOTH, 0, 0)  26.7 us
    ppermute x25, waiting for transfers between devices, swap(): return lax.ppermute(value, 'ch', [(i, i ^ bit) for i in range(groups)])  25.5 us
    all_to_all x7, waiting for transfers between devices, exchange(): return lax.all_to_all(payload, BOTH, 0, 0)  23.7 us
    unnamed x144, local copies, waits for them, and re-layouts  22 us
    all_to_all x1, blocking collectives, exchange(): return lax.all_to_all(payload, BOTH, 0, 0)  15.6 us
    ppermute x25, starting transfers between devices, swap(): return lax.ppermute(value, 'ch', [(i, i ^ bit) for i in range(groups)])  15.6 us
  transfers between devices with their start and end apart: 47, of which 19 were waited for; matrix products, arithmetic and copies ran while one was open for 5% of the time, Pallas kernels for 35%

profile of v4, /device:TPU:0, one launch (start us, length us, event | category | flops | bytes accessed | tf_op | source)
XLA Modules:
  0.0 393.9 jit_solution(17235344534421346822)
XLA Ops:
  8.6 2.5 shard_map.391
  11.2 3.0 collective-permute-start.1
  14.1 3.5 all-to-all-start
  19.4 4.8 %shard_map.394 = (bf16[2700,128]{1,0:T(8,128)(2,1)}, bf16[2700,128]{1,0:T(8,128)(2,1)}) custom-call(bf16[2,345600]{1,0:T(2,128)(2,1)} %refs_0_.3, bf16[4,132,1152]{2,1,0:T(8,128)(2,1)} %get-tuple-element.122.refs_1_), custom_call_target="tpu_custom_call" | custom-call | flops 5280000000 | bytes 2764800 | tf_op jit(solution)/shard_map/pallas_call | solution.py:68
  24.2 2.9 reshape.156.refs_0_
  27.4 1.9 reshape.154.refs_0_
  30.4 2.3 shard_map.395.refs_0_
  38.0 5.3 %shard_map.392 = (bf16[1152,528]{1,0:T(8,128)(2,1)}, bf16[576,528]{1,0:T(8,128)(2,1)}, f32[4,1152]{1,0:T(4,128)}, f32[1152,192]{1,0:T(8,128)}, f32[32,8,128]{2,1,0:T(8,128)}) custom-call(s32[1]{0:T(128)} %bitcast.refs_0_, bf16[4,132,1152]{2,1,0:T(8,128)(2,1)} %copy-done, bf16[736,128]{1,0:T(8,128)(2,1)} %get-tuple-element.123.refs_2_, ...), custom_call_target="tpu_custom_call" | custom-call | flops 9459999744 | bytes 5517316 | tf_op jit(solution)/shard_map/pallas_call | solution.py:68
  43.3 5.9 %all-to-all-start.1 = ((f32[32,8,128]{2,1,0:T(8,128)}), f32[32,8,128]{2,1,0:T(8,128)S(1)}, u32[]{:S(2)}, u32[]{:S(2)}) async-start(f32[32,8,128]{2,1,0:T(8,128)} %get-tuple-element.124), calls=%async_computation.1 | async-start | bytes 262144 | tf_op jit(solution)/shard_map/all_to_all | solution.py:925
  49.1 7.2 %collective-permute-done.4.refs_9_ = bf16[3168,128]{1,0:T(8,128)(2,1)S(1)} collective-permute-done((bf16[3168,128]{1,0:T(8,128)(2,1)}, bf16[3168,128]{1,0:T(8,128)(2,1)S(1)}, u32[]{:S(2)}, u32[]{:S(2)}) %collective-permute-start.4) | collective-permute-done | bytes 811040 | tf_op jit(solution)/shard_map/ppermute | solution.py:928
  56.3 5.9 %shard_map.393 = (f32[1152,256]{1,0:T(8,128)}, f32[1152,128]{1,0:T(8,128)}, f32[16,128]{1,0:T(8,128)}) custom-call(bf16[1152,528]{1,0:T(8,128)(2,1)} %get-tuple-element.127.refs_0_.refs_2_.refs_4_, bf16[576,528]{1,0:T(8,128)(2,1)} %get-tuple-element.128.refs_1_.refs_13_, f32[1152,128]{1,0:T(8,128)} %broadcast_in_dim.16.refs_6_.refs_2_.refs_5_.refs_8_.refs_19_.refs_7_.refs_12_), custom_call_target="tpu_custom_call" | custom-call | flops 13200000000 | bytes 4192256 | tf_op jit(solution)/shard_map/pallas_call | solution.py:68
  64.0 2.4 shard_map.397.refs_11_.refs_0_
  69.8 17.1 %shard_map.398 = (bf16[1728,1536]{1,0:T(8,128)(2,1)}, bf16[1728,384]{1,0:T(8,128)(2,1)}, f32[1152,320]{1,0:T(8,128)}, f32[1152,128]{1,0:T(8,128)}, bf16[3,4,80,1...) custom-call(s32[1]{0:T(128)} %bitcast.refs_0_, ...), custom_call_target="tpu_custom_call" | custom-call | flops 27499999232 | bytes 17217540 | tf_op jit(solution)/shard_map/pallas_call | solution.py:68
  86.9 4.9 %all-to-all-start.2 = ((f32[32,16,128]{2,1,0:T(8,128)}), f32[32,16,128]{2,1,0:T(8,128)S(1)}, u32[]{:S(2)}, u32[]{:S(2)}) async-start(f32[32,16,128]{2,1,0:T(8,128)} %get-tuple-element.132), calls=%async_computation.2 | async-start | bytes 524288 | tf_op jit(solution)/shard_map/all_to_all | solution.py:925
  94.6 8.0 %all-to-all-done.2.refs_1_ = f32[32,16,128]{2,1,0:T(8,128)S(1)} async-done(((f32[32,16,128]{2,1,0:T(8,128)}), f32[32,16,128]{2,1,0:T(8,128)S(1)}, u32[]{:S(2)}, u32[]{:S(2)}) %all-to-all-start.2) | async-done | bytes 262176 | tf_op jit(solution)/shard_map/all_to_all | solution.py:925
  103.3 8.0 %shard_map.401 = (bf16[192,832]{1,0:T(8,128)(2,1)}, bf16[576,832]{1,0:T(8,128)(2,1)}, f32[192,192]{1,0:T(8,128)}, f32[32,8,128]{2,1,0:T(8,128)}, f32[16,128]{1,0:T(8,128)}) custom-call(s32[1]{0:T(128)} %bitcast.refs_0_, f32[32,16,128]{2,1,0:T(8,128)} %copy-done.12, f32[32,8,128]{2,1,0:T(8,128)} %copy-done.7, ...), custom_call_target="tpu_custom_call" | custom-call | flops 16499999744 | bytes 7641092 | tf_op jit(solution)/shard_map/pallas_call | solution.py:68
  111.3 3.0 all-to-all-start.3
  114.6 7.9 %all-to-all-done.3.refs_1_ = f32[32,8,128]{2,1,0:T(8,128)S(1)} async-done(((f32[32,8,128]{2,1,0:T(8,128)}), f32[32,8,128]{2,1,0:T(8,128)S(1)}, u32[]{:S(2)}, u32[]{:S(2)}) %all-to-all-start.3) | async-done | bytes 131104 | tf_op jit(solution)/shard_map/all_to_all | solution.py:925
  124.3 2.7 shard_map.402
  128.2 7.8 %shard_map.405 = (bf16[384,1536]{1,0:T(8,128)(2,1)}, bf16[384,384]{1,0:T(8,128)(2,1)}, f32[192,320]{1,0:T(8,128)}, f32[192,128]{1,0:T(8,128)}, bf16[3,4,80,1536]...) custom-call(s32[1]{0:T(128)} %bitcast.refs_0_, ...), custom_call_target="tpu_custom_call" | custom-call | flops 9900000256 | bytes 9107460 | tf_op jit(solution)/shard_map/pallas_call | solution.py:68
  136.1 2.6 all-to-all-start.4
  144.4 4.6 %collective-permute-done.13.refs_11_ = bf16[192,208]{1,0:T(8,128)(2,1)S(1)} collective-permute-done((bf16[192,208]{1,0:T(8,128)(2,1)}, bf16[192,208]{1,0:T(8,128)(2,1)S(1)}, u32[]{:S(2)}, u32[]{:S(2)}) %collective-permute-start.13) | collective-permute-done | bytes 79904 | tf_op jit(solution)/shard_map/ppermute | solution.py:928
  151.2 4.2 %shard_map.407 = (bf16[192,208]{1,0:T(8,128)(2,1)}, bf16[192,208]{1,0:T(8,128)(2,1)}, bf16[192,208]{1,0:T(8,128)(2,1)}, bf16[192,208]{1,0:T(8,128)(2,1)}, f32[19...) custom-call(s32[1]{0:T(128)} %bitcast.refs_0_, ...), custom_call_target="tpu_custom_call" | custom-call | flops 4400000000 | bytes 2697220 | tf_op jit(solution)/shard_map/pallas_call | solution.py:68
  155.4 15.6 %all_to_all.60.refs_0_ = f32[32,16,128]{2,1,0:T(8,128)} all-to-all(f32[32,16,128]{2,1,0:T(8,128)} %get-tuple-element.157), channel_id=1, replica_groups=mesh['batch'=8,'ch'=4] {'batch','ch'}, dimensions={0} | all-to-all | bytes 524288 | tf_op jit(solution)/shard_map/all_to_all | solution.py:925
  171.0 2.1 shard_map.409
  173.2 5.3 %shard_map.411.refs_20_ = bf16[4,3200,128]{2,1,0:T(8,128)(2,1)} custom-call(s32[1]{0:T(128)} %bitcast.refs_0_, bf16[192,320]{1,0:T(8,128)(2,1)} %get-tuple-element.161.refs_2_.refs_1_, bf16[192,128]{1,0:T(8,128)(2,1)} %get-tuple-element.162.refs_3_.refs_2_, bf16[384,1536]{1,0:T(8,128)(2,1)} %get-tuple-element.171.refs_3_, ...), custom_call_target="tpu_custom_call" | custom-call | flops 5500000256 | bytes 4923396 | tf_op jit(solution)/shard_map/pallas_call | solution.py:68
  178.6 5.5 %shard_map.410 = (f32[192,192]{1,0:T(8,128)}, f32[32,8,128]{2,1,0:T(8,128)}) custom-call(f32[8,128]{1,0:T(8,128)} %get-tuple-element.156.refs_2_.refs_0_.refs_3_, f32[4,1152]{1,0:T(4,128)} %get-tuple-element.125.refs_3_.refs_1_.refs_4_.refs_5_, bf16[192,320]{1,0:T(8,128)(2,1)} %get-tuple-element.161.refs_2_.refs_1_, ...), custom_call_target="tpu_custom_call" | custom-call | flops 6160000000 | bytes 3962880 | tf_op jit(solution)/shard_map/pallas_call | solution.py:68
  184.0 2.6 all-to-all-start.6
  188.6 4.8 %collective-permute-done.16.refs_3_ = bf16[192,208]{1,0:T(8,128)(2,1)S(1)} collective-permute-done((bf16[192,208]{1,0:T(8,128)(2,1)S(1)}, bf16[192,208]{1,0:T(8,128)(2,1)S(1)}, u32[]{:S(2)}, u32[]{:S(2)}) %collective-permute-start.16) | collective-permute-done | bytes 79904 | tf_op jit(solution)/shard_map/ppermute | solution.py:928
  195.5 1.8 shard_map.408.refs_21_
  198.0 9.9 %shard_map.412 = (bf16[192,576]{1,0:T(8,128)(2,1)}, f32[1152,256]{1,0:T(8,128)}, f32[1152,320]{1,0:T(8,128)}, f32[1152,128]{1,0:T(8,128)}, f32[1152,128]{1,0:T(8...) custom-call(f32[32,8,128]{2,1,0:T(8,128)} %copy-done.23, f32[16,128]{1,0:T(8,128)} %get-tuple-element.166.refs_1_, ...), custom_call_target="tpu_custom_call" | custom-call | flops 16499999744 | bytes 10975232 | tf_op jit(solution)/shard_map/pallas_call | solution.py:68
  207.9 4.9 %all-to-all-start.7 = ((f32[32,16,128]{2,1,0:T(8,128)}), f32[32,16,128]{2,1,0:T(8,128)S(1)}, u32[]{:S(2)}, u32[]{:S(2)}) async-start(f32[32,16,128]{2,1,0:T(8,128)} %get-tuple-element.173), calls=%async_computation.7 | async-start | bytes 524288 | tf_op jit(solution)/shard_map/all_to_all | solution.py:925
  212.8 2.7 shard_map.413
  215.5 7.8 %all-to-all-done.7.refs_0_ = f32[32,16,128]{2,1,0:T(8,128)S(1)} async-done(((f32[32,16,128]{2,1,0:T(8,128)}), f32[32,16,128]{2,1,0:T(8,128)S(1)}, u32[]{:S(2)}, u32[]{:S(2)}) %all-to-all-start.7) | async-done | bytes 262176 | tf_op jit(solution)/shard_map/all_to_all | solution.py:925
  224.1 4.7 %shard_map.414 = (bf16[1152,320]{1,0:T(8,128)(2,1)}, bf16[1152,128]{1,0:T(8,128)(2,1)}, f32[16,128]{1,0:T(8,128)}) custom-call(f32[32,16,128]{2,1,0:T(8,128)} %copy-done.13, f32[16,128]{1,0:T(8,128)} %get-tuple-element.170.refs_14_.refs_1_.refs_3_, f32[8,128]{1,0:T(8,128)} %get-tuple-element.155.refs_2_.refs_0_.refs_4_, ...), custom_call_target="tpu_custom_call" | custom-call | flops 7699999744 | bytes 6051840 | tf_op jit(solution)/shard_map/pallas_call | solution.py:68
  228.8 11.0 %shard_map.415 = (bf16[2,4224,128]{2,1,0:T(8,128)(2,1)}, bf16[2,4224,128]{2,1,0:T(8,128)(2,1)}) custom-call(s32[1]{0:T(128)} %bitcast.refs_0_, bf16[1152,320]{1,0:T(8,128)(2,1)} %get-tuple-element.178.refs_1_.refs_2_, bf16[1152,128]{1,0:T(8,128)(2,1)} %get-tuple-element.179.refs_2_.refs_3_, bf16[1728,1536]{1,0:T(8,128)(2,1)} %get-tuple-element.182.refs_3_, ...), custom_call_target="tpu_custom_call" | custom-call | flops 11000000512 | bytes 13025284 | tf_op jit(solution)/shard_map/pallas_call | solution.py:68
  243.4 2.2 shard_map.416
  247.9 3.9 shard_map.417
  252.6 15.2 %shard_map.418 = (f32[1152,192]{1,0:T(8,128)}, f32[32,8,128]{2,1,0:T(8,128)}) custom-call(f32[8,128]{1,0:T(8,128)} %get-tuple-element.155.refs_2_.refs_0_.refs_4_, f32[4,1152]{1,0:T(4,128)} %get-tuple-element.125.refs_3_.refs_1_.refs_4_.refs_5_, bf16[1152,320]{1,0:T(8,128)(2,1)} %get-tuple-element.178.refs_1_.refs_2_, ...), custom_call_target="tpu_custom_call" | custom-call | flops 17600000000 | bytes 6789120 | tf_op jit(solution)/shard_map/pallas_call | solution.py:68
  267.8 2.9 all-to-all-start.8
  270.7 1.9 shard_map.419
  274.4 4.8 %collective-permute-done.21.refs_1_ = bf16[1,4224,128]{2,1,0:T(8,128)(2,1)S(1)} collective-permute-done((bf16[1,4224,128]{2,1,0:T(8,128)(2,1)}, bf16[1,4224,128]{2,1,0:T(8,128)(2,1)S(1)}, u32[]{:S(2)}, u32[]{:S(2)}) %collective-permute-start.21) | collective-permute-done | bytes 1081376 | tf_op jit(solution)/shard_map/ppermute | solution.py:928
  280.2 2.8 shard_map.420.refs_2_
  285.5 5.0 %all-to-all-start.9 = ((bf16[8,528,128]{2,1,0:T(8,128)(2,1)}), bf16[8,528,128]{2,1,0:T(8,128)(2,1)S(1)}, u32[]{:S(2)}, u32[]{:S(2)}) async-start(bf16[8,528,128]{2,1,0:T(8,128)(2,1)} %bitcast.18), calls=%async_computation.10 | async-start | bytes 2162688 | tf_op jit(solution)/shard_map/all_to_all | solution.py:1242
  290.6 7.5 %shard_map.422 = (bf16[1152,576]{1,0:T(8,128)(2,1)}, bf16[132,1152]{1,0:T(8,128)(2,1)}, bf16[132,1152]{1,0:T(8,128)(2,1)}, bf16[132,1152]{1,0:T(8,128)(2,1)}, bf...) custom-call(s32[1]{0:T(128)} %bitcast.refs_0_, f32[32,8,128]{2,1,0:T(8,128)} %copy-done.22, ...), custom_call_target="tpu_custom_call" | custom-call | flops 9349999616 | bytes 9224196 | tf_op jit(solution)/shard_map/pallas_call | solution.py:68
  300.4 4.1 %shard_map.424 = (bf16[2,768,128]{2,1,0:T(8,128)(2,1)}, bf16[2,768,128]{2,1,0:T(8,128)(2,1)}) custom-call(s32[1]{0:T(128)} %bitcast.refs_0_, bf16[1152,576]{1,0:T(8,128)(2,1)} %get-tuple-element.203.refs_2_.refs_1_, bf16[1152,528]{1,0:T(8,128)(2,1)} %get-tuple-element.127.refs_0_.refs_2_.refs_4_, bf16[400,128]{1,0:T(8,128)(2,1)} %shard_map.423.refs_3_.refs_1_), custom_call_target="tpu_custom_call" | custom-call | flops 4950000128 | bytes 3330052 | tf_op jit(solution)/shard_map/pallas_call | solution.py:68
  304.6 3.0 collective-permute-start.28
  308.3 2.0 shard_map.425
  312.6 8.2 %collective-permute-done.28.refs_3_.refs_5_ = bf16[400,128]{1,0:T(8,128)(2,1)S(1)} collective-permute-done((bf16[400,128]{1,0:T(8,128)(2,1)S(1)}, bf16[400,128]{1,0:T(8,128)(2,1)S(1)}, u32[]{:S(2)}, u32[]{:S(2)}) %collective-permute-start.28) | collective-permute-done | bytes 102432 | tf_op jit(solution)/shard_map/ppermute | solution.py:1165
  323.7 3.4 all-to-all-start.10
  327.1 2.0 collective-permute-start.29
  331.0 3.0 shard_map.427.refs_2_
  334.0 2.0 collective-permute-done.29.refs_3_
  338.4 2.5 shard_map.428
  340.9 4.7 %all-to-all-start.11 = ((bf16[8,624,128]{2,1,0:T(8,128)(2,1)}), bf16[8,624,128]{2,1,0:T(8,128)(2,1)S(1)}, u32[]{:S(2)}, u32[]{:S(2)}) async-start(bf16[8,624,128]{2,1,0:T(8,128)(2,1)} %shard_map.428), calls=%async_computation.12 | async-start | bytes 2555904 | tf_op jit(solution)/shard_map/all_to_all | solution.py:1280
  348.4 2.0 collective-permute-start.31
  350.5 2.0 collective-permute-start.33
  353.2 7.9 %collective-permute-done.31.refs_2_ = bf16[400,128]{1,0:T(8,128)(2,1)S(1)} collective-permute-done((bf16[400,128]{1,0:T(8,128)(2,1)S(1)}, bf16[400,128]{1,0:T(8,128)(2,1)S(1)}, u32[]{:S(2)}, u32[]{:S(2)}) %collective-permute-start.31) | collective-permute-done | bytes 102432 | tf_op jit(solution)/shard_map/ppermute | solution.py:1165
  361.1 4.1 %collective-permute-done.32.refs_4_ = bf16[400,128]{1,0:T(8,128)(2,1)S(1)} collective-permute-done((bf16[400,128]{1,0:T(8,128)(2,1)S(1)}, bf16[400,128]{1,0:T(8,128)(2,1)S(1)}, u32[]{:S(2)}, u32[]{:S(2)}) %collective-permute-start.32) | collective-permute-done | bytes 102432 | tf_op jit(solution)/shard_map/ppermute | solution.py:1165
  365.2 3.8 collective-permute-done.33.refs_6_
  370.9 2.8 shard_map.429
  373.7 2.4 all-to-all-done.11.refs_0_
  377.1 7.7 %shard_map.430 = (f32[2,345600]{1,0:T(2,128)}, f32[864,32]{1,0:T(8,128)}, f32[64,528]{1,0:T(8,128)}, f32[40,528]{1,0:T(8,128)}, f32[8,528]{1,0:T(8,128)}, /*inde...) custom-call(bf16[8,624,128]{2,1,0:T(8,128)(2,1)} %copy-done.2, ...), custom_call_target="tpu_custom_call" | custom-call | flops 8800000000 | bytes 6319104 | tf_op jit(solution)/shard_map/pallas_call | solution.py:68
  384.8 2.0 pad_maximum_fusion
  (267 shorter events, 65.8 us)
Async XLA Ops:
  11.2 18.7 %collective-permute-start.1 = (bf16[736,128]{1,0:T(8,128)(2,1)}, bf16[736,128]{1,0:T(8,128)(2,1)S(1)}, u32[]{:S(2)}, u32[]{:S(2)}) collective-permute-start(bf16[736,128]{1,0:T(8,128)(2,1)} %get-tuple-element.123.refs_2_), channel_id=1, source_target_pairs={{0,2},{1,3},{2,0},{3,1},{4,6},{5,7},{6,4},{7,5},{8,10},{9,11},{10,... | collective-permute-start | bytes 565256 | tf_op jit(solution)/shard_map/ppermute | solution.py:928
  14.1 22.0 %collective-permute-start = (bf16[736,128]{1,0:T(8,128)(2,1)}, bf16[736,128]{1,0:T(8,128)(2,1)S(1)}, u32[]{:S(2)}, u32[]{:S(2)}) collective-permute-start(bf16[736,128]{1,0:T(8,128)(2,1)} %get-tuple-element.123.refs_2_), channel_id=1, source_target_pairs={{0,1},{1,0},{2,3},{3,2},{4,5},{5,4},{6,7},{7,6},{8,9},{9,8},{10,11... | collective-permute-start | bytes 565256 | tf_op jit(solution)/shard_map/ppermute | solution.py:928
  14.1 20.2 %all-to-all-start = ((bf16[4,132,1152]{2,1,0:T(8,128)(2,1)}), bf16[4,132,1152]{2,1,0:T(8,128)(2,1)S(1)}, u32[]{:S(2)}, u32[]{:S(2)}) async-start(bf16[4,132,1152]{2,1,0:T(8,128)(2,1)} %get-tuple-element.122.refs_1_), calls=%async_computation | async-start | bytes 2506752 | tf_op jit(solution)/shard_map/all_to_all | solution.py:960
  29.9 2.8 collective-permute-start.2
  35.4 21.0 %collective-permute-start.4 = (bf16[3168,128]{1,0:T(8,128)(2,1)}, bf16[3168,128]{1,0:T(8,128)(2,1)S(1)}, u32[]{:S(2)}, u32[]{:S(2)}) collective-permute-start(bf16[3168,128]{1,0:T(8,128)(2,1)} %shard_map.396.refs_7_), channel_id=1, source_target_pairs={{0,2},{1,3},{2,0},{3,1},{4,6},{5,7},{6,4},{7,5},{8,10},{9,11},{10,... | collective-permute-start | bytes 2433032 | tf_op jit(solution)/shard_map/ppermute | solution.py:928
  36.1 32.6 %collective-permute-start.3 = (bf16[3168,128]{1,0:T(8,128)(2,1)}, bf16[3168,128]{1,0:T(8,128)(2,1)S(1)}, u32[]{:S(2)}, u32[]{:S(2)}) collective-permute-start(bf16[3168,128]{1,0:T(8,128)(2,1)} %shard_map.396.refs_7_), channel_id=1, source_target_pairs={{0,1},{1,0},{2,3},{3,2},{4,5},{5,4},{6,7},{7,6},{8,9},{9,8},{10,11... | collective-permute-start | bytes 2433032 | tf_op jit(solution)/shard_map/ppermute | solution.py:928
  43.3 23.1 %all-to-all-start.1 = ((f32[32,8,128]{2,1,0:T(8,128)}), f32[32,8,128]{2,1,0:T(8,128)S(1)}, u32[]{:S(2)}, u32[]{:S(2)}) async-start(f32[32,8,128]{2,1,0:T(8,128)} %get-tuple-element.124), calls=%async_computation.1 | async-start | bytes 262144 | tf_op jit(solution)/shard_map/all_to_all | solution.py:925
  56.3 12.3 %collective-permute-start.5 = (bf16[3168,128]{1,0:T(8,128)(2,1)S(1)}, bf16[3168,128]{1,0:T(8,128)(2,1)S(1)}, u32[]{:S(2)}, u32[]{:S(2)}) collective-permute-start(bf16[3168,128]{1,0:T(8,128)(2,1)S(1)} %collective-permute-done.4.refs_9_), channel_id=1, source_target_pairs={{0,1},{1,0},{2,3},{3,2},{4,5},{5,4},{6,7},{7,6},{8,9},{9,8},{10,11... | collective-permute-start | bytes 2433032 | tf_op jit(solution)/shard_map/ppermute | solution.py:928
  67.1 25.1 %collective-permute-start.7 = (bf16[1008,128]{1,0:T(8,128)(2,1)}, bf16[1008,128]{1,0:T(8,128)(2,1)S(1)}, u32[]{:S(2)}, u32[]{:S(2)}) collective-permute-start(bf16[1008,128]{1,0:T(8,128)(2,1)} %shard_map.400.refs_11_), channel_id=1, source_target_pairs={{0,2},{1,3},{2,0},{3,1},{4,6},{5,7},{6,4},{7,5},{8,10},{9,11},{10,... | collective-permute-start | bytes 774152 | tf_op jit(solution)/shard_map/ppermute | solution.py:928
  69.8 22.0 %copy-start.15 = (bf16[1008,128]{1,0:T(8,128)(2,1)S(1)}, bf16[1008,128]{1,0:T(8,128)(2,1)}, u32[]{:S(2)}) copy-start(bf16[1008,128]{1,0:T(8,128)(2,1)} %shard_map.400.refs_11_) | copy-start | bytes 774148
  86.9 15.6 %all-to-all-start.2 = ((f32[32,16,128]{2,1,0:T(8,128)}), f32[32,16,128]{2,1,0:T(8,128)S(1)}, u32[]{:S(2)}, u32[]{:S(2)}) async-start(f32[32,16,128]{2,1,0:T(8,128)} %get-tuple-element.132), calls=%async_computation.2 | async-start | bytes 524288 | tf_op jit(solution)/shard_map/all_to_all | solution.py:925
  91.9 2.7 collective-permute-start.6
  92.2 2.4 collective-permute-start.8
  92.9 29.6 %collective-permute-start.10 = (bf16[3168,128]{1,0:T(8,128)(2,1)}, bf16[3168,128]{1,0:T(8,128)(2,1)S(1)}, u32[]{:S(2)}, u32[]{:S(2)}) collective-permute-start(bf16[3168,128]{1,0:T(8,128)(2,1)} %shard_map.403.refs_7_), channel_id=1, source_target_pairs={{0,2},{1,3},{2,0},{3,1},{4,6},{5,7},{6,4},{7,5},{8,10},{9,11},{10,... | collective-permute-start | bytes 2433032 | tf_op jit(solution)/shard_map/ppermute | solution.py:928
  94.6 8.0 %copy-start.42 = (bf16[1008,128]{1,0:T(8,128)(2,1)}, bf16[1008,128]{1,0:T(8,128)(2,1)S(1)}, u32[]{:S(2)}) copy-start(bf16[1008,128]{1,0:T(8,128)(2,1)S(1)} %collective-permute-done.6.refs_12_) | copy-start | bytes 774148
  94.6 8.0 %copy-start.43 = (bf16[1008,128]{1,0:T(8,128)(2,1)}, bf16[1008,128]{1,0:T(8,128)(2,1)S(1)}, u32[]{:S(2)}) copy-start(bf16[1008,128]{1,0:T(8,128)(2,1)S(1)} %collective-permute-done.8.refs_14_) | copy-start | bytes 774148
  103.3 11.0 %copy-start.4 = (bf16[3168,128]{1,0:T(8,128)(2,1)S(1)}, bf16[3168,128]{1,0:T(8,128)(2,1)}, u32[]{:S(2)}) copy-start(bf16[3168,128]{1,0:T(8,128)(2,1)} %shard_map.403.refs_7_) | copy-start | bytes 2433028
  111.3 11.2 %all-to-all-start.3 = ((f32[32,8,128]{2,1,0:T(8,128)}), f32[32,8,128]{2,1,0:T(8,128)S(1)}, u32[]{:S(2)}, u32[]{:S(2)}) async-start(f32[32,8,128]{2,1,0:T(8,128)} %get-tuple-element.137), calls=%async_computation.3 | async-start | bytes 262144 | tf_op jit(solution)/shard_map/all_to_all | solution.py:925
  114.3 12.6 %collective-permute-start.9 = (bf16[3168,128]{1,0:T(8,128)(2,1)S(1)}, bf16[3168,128]{1,0:T(8,128)(2,1)S(1)}, u32[]{:S(2)}, u32[]{:S(2)}) collective-permute-start(bf16[3168,128]{1,0:T(8,128)(2,1)S(1)} %copy-done.4), channel_id=1, source_target_pairs={{0,1},{1,0},{2,3},{3,2},{4,5},{5,4},{6,7},{7,6},{8,9},{9,8},{10,11... | collective-permute-start | bytes 2433032 | tf_op jit(solution)/shard_map/ppermute | solution.py:928
  124.1 2.9 collective-permute-start.11
  128.2 10.5 %copy-start.18 = (bf16[8,2,6,6,32]{4,1,3,2,0:T(2,128)(2,1)S(1)}, bf16[8,2,6,6,32]{4,1,3,2,0:T(2,128)(2,1)}, u32[]{:S(2)}) copy-start(bf16[8,2,6,6,32]{4,1,3,2,0:T(2,128)(2,1)} %param.45) | copy-start | bytes 110596
  128.2 10.5 %copy-start.19 = (bf16[8,2,6,6,32]{4,1,3,2,0:T(2,128)(2,1)S(1)}, bf16[8,2,6,6,32]{4,1,3,2,0:T(2,128)(2,1)}, u32[]{:S(2)}) copy-start(bf16[8,2,6,6,32]{4,1,3,2,0:T(2,128)(2,1)} %param.44) | copy-start | bytes 110596
  128.2 10.5 %copy-start.20 = (bf16[8,2,6,6,80]{4,1,3,2,0:T(2,128)(2,1)S(1)}, bf16[8,2,6,6,80]{4,1,3,2,0:T(2,128)(2,1)}, u32[]{:S(2)}) copy-start(bf16[8,2,6,6,80]{4,1,3,2,0:T(2,128)(2,1)} %param.43) | copy-start | bytes 276484
  128.2 10.5 %copy-start.21 = (bf16[8,2,6,6,64]{4,1,3,2,0:T(2,128)(2,1)S(1)}, bf16[8,2,6,6,64]{4,1,3,2,0:T(2,128)(2,1)}, u32[]{:S(2)}) copy-start(bf16[8,2,6,6,64]{4,1,3,2,0:T(2,128)(2,1)} %param.42) | copy-start | bytes 221188
  136.1 14.3 %all-to-all-start.4 = ((f32[32,16,128]{2,1,0:T(8,128)}), f32[32,16,128]{2,1,0:T(8,128)S(1)}, u32[]{:S(2)}, u32[]{:S(2)}) async-start(f32[32,16,128]{2,1,0:T(8,128)} %get-tuple-element.142), calls=%async_computation.4 | async-start | bytes 524288 | tf_op jit(solution)/shard_map/all_to_all | solution.py:925
  138.7 104.7 %reduce-scatter.2.cloned.1.call-start = ((), (), s32[]{:S(2)}) async-start(), calls=%async_computation.13 | async-start | bytes 4096000 | tf_op jit(solution)/shard_map/reduce_scatter | solution.py:1176
  142.5 1.9 collective-permute-start.12
  142.6 6.4 %collective-permute-start.13 = (bf16[192,208]{1,0:T(8,128)(2,1)}, bf16[192,208]{1,0:T(8,128)(2,1)S(1)}, u32[]{:S(2)}, u32[]{:S(2)}) collective-permute-start(bf16[192,208]{1,0:T(8,128)(2,1)} %get-tuple-element.149), channel_id=1, source_target_pairs={{0,2},{1,3},{2,0},{3,1},{4,6},{5,7},{6,4},{7,5},{8,10},{9,11},{10,... | collective-permute-start | bytes 239624 | tf_op jit(solution)/shard_map/ppermute | solution.py:928
  144.3 6.1 %collective-permute-start.14 = (bf16[192,208]{1,0:T(8,128)(2,1)}, bf16[192,208]{1,0:T(8,128)(2,1)S(1)}, u32[]{:S(2)}, u32[]{:S(2)}) collective-permute-start(bf16[192,208]{1,0:T(8,128)(2,1)} %get-tuple-element.150), channel_id=1, source_target_pairs={{0,3},{1,2},{2,1},{3,0},{4,7},{5,6},{6,5},{7,4},{8,11},{9,10},{10,... | collective-permute-start | bytes 239624 | tf_op jit(solution)/shard_map/ppermute | solution.py:928
  178.5 8.1 %copy-start.62 = (bf16[192,208]{1,0:T(8,128)(2,1)S(1)}, bf16[192,208]{1,0:T(8,128)(2,1)}, u32[]{:S(2)}) copy-start(bf16[192,208]{1,0:T(8,128)(2,1)} %get-tuple-element.152) | copy-start | bytes 239620
  178.5 8.3 %copy-start.61 = (bf16[192,208]{1,0:T(8,128)(2,1)S(1)}, bf16[192,208]{1,0:T(8,128)(2,1)}, u32[]{:S(2)}) copy-start(bf16[192,208]{1,0:T(8,128)(2,1)} %get-tuple-element.153) | copy-start | bytes 239620
  178.5 10.0 %copy-start.60 = (bf16[192,208]{1,0:T(8,128)(2,1)S(1)}, bf16[192,208]{1,0:T(8,128)(2,1)}, u32[]{:S(2)}) copy-start(bf16[192,208]{1,0:T(8,128)(2,1)} %get-tuple-element.154) | copy-start | bytes 239620
  184.0 13.4 %all-to-all-start.6 = ((f32[32,8,128]{2,1,0:T(8,128)}), f32[32,8,128]{2,1,0:T(8,128)S(1)}, u32[]{:S(2)}, u32[]{:S(2)}) async-start(f32[32,8,128]{2,1,0:T(8,128)} %get-tuple-element.165), calls=%async_computation.6 | async-start | bytes 262144 | tf_op jit(solution)/shard_map/all_to_all | solution.py:925
  186.6 2.0 collective-permute-start.15
  186.8 6.5 %collective-permute-start.16 = (bf16[192,208]{1,0:T(8,128)(2,1)S(1)}, bf16[192,208]{1,0:T(8,128)(2,1)S(1)}, u32[]{:S(2)}, u32[]{:S(2)}) collective-permute-start(bf16[192,208]{1,0:T(8,128)(2,1)S(1)} %copy-done.61), channel_id=1, source_target_pairs={{0,2},{1,3},{2,0},{3,1},{4,6},{5,7},{6,4},{7,5},{8,10},{9,11},{10,... | collective-permute-start | bytes 239624 | tf_op jit(solution)/shard_map/ppermute | solution.py:928
  188.5 6.4 %collective-permute-start.17 = (bf16[192,208]{1,0:T(8,128)(2,1)S(1)}, bf16[192,208]{1,0:T(8,128)(2,1)S(1)}, u32[]{:S(2)}, u32[]{:S(2)}) collective-permute-start(bf16[192,208]{1,0:T(8,128)(2,1)S(1)} %copy-done.60), channel_id=1, source_target_pairs={{0,3},{1,2},{2,1},{3,0},{4,7},{5,6},{6,5},{7,4},{8,11},{9,10},{10,... | collective-permute-start | bytes 239624 | tf_op jit(solution)/shard_map/ppermute | solution.py:928
  207.9 15.5 %all-to-all-start.7 = ((f32[32,16,128]{2,1,0:T(8,128)}), f32[32,16,128]{2,1,0:T(8,128)S(1)}, u32[]{:S(2)}, u32[]{:S(2)}) async-start(f32[32,16,128]{2,1,0:T(8,128)} %get-tuple-element.173), calls=%async_computation.7 | async-start | bytes 524288 | tf_op jit(solution)/shard_map/all_to_all | solution.py:925
  228.8 11.0 %copy-start.1 = (bf16[4,192,208]{2,1,0:T(8,128)(2,1)S(1)}, bf16[4,192,208]{2,1,0:T(8,128)(2,1)}, u32[]{:S(2)}) copy-start(bf16[4,192,208]{2,1,0:T(8,128)(2,1)} %shard_map.408.refs_21_) | copy-start | bytes 958468
  239.8 6.8 %collective-permute-start.18 = (bf16[2,4224,128]{2,1,0:T(8,128)(2,1)}, bf16[2,4224,128]{2,1,0:T(8,128)(2,1)S(1)}, u32[]{:S(2)}, u32[]{:S(2)}) collective-permute-start(bf16[2,4224,128]{2,1,0:T(8,128)(2,1)} %get-tuple-element.186.refs_2_), channel_id=1, source_target_pairs={{0,1},{1,0},{2,3},{3,2},{4,5},{5,4},{6,7},{7,6},{8,9},{9,8},{10,11... | collective-permute-start | bytes 6488072 | tf_op jit(solution)/shard_map/ppermute | solution.py:928
  245.6 25.0 %collective-permute-start.19 = (bf16[4,400,128]{2,1,0:T(8,128)(2,1)}, bf16[4,400,128]{2,1,0:T(8,128)(2,1)}, u32[]{:S(2)}, u32[]{:S(2)}) collective-permute-start(bf16[4,400,128]{2,1,0:T(8,128)(2,1)} %get-tuple-element.187.refs_2_), channel_id=1, source_target_pairs={{0,4},{4,0},{8,12},{12,8},{16,20},{20,16},{24,28},{28,24},{1,5},{5... | collective-permute-start | bytes 1228808 | tf_op jit(solution)/shard_map/ppermute | solution.py:1165
  251.7 27.5 %collective-permute-start.21 = (bf16[1,4224,128]{2,1,0:T(8,128)(2,1)}, bf16[1,4224,128]{2,1,0:T(8,128)(2,1)S(1)}, u32[]{:S(2)}, u32[]{:S(2)}) collective-permute-start(bf16[1,4224,128]{2,1,0:T(8,128)(2,1)} %get-tuple-element.197), channel_id=1, source_target_pairs={{0,2},{1,3},{2,0},{3,1},{4,6},{5,7},{6,4},{7,5},{8,10},{9,11},{10,... | collective-permute-start | bytes 3244040 | tf_op jit(solution)/shard_map/ppermute | solution.py:928
  267.8 17.7 %all-to-all-start.8 = ((f32[32,8,128]{2,1,0:T(8,128)}), f32[32,8,128]{2,1,0:T(8,128)S(1)}, u32[]{:S(2)}, u32[]{:S(2)}) async-start(f32[32,8,128]{2,1,0:T(8,128)} %get-tuple-element.189), calls=%async_computation.9 | async-start | bytes 262144 | tf_op jit(solution)/shard_map/all_to_all | solution.py:925
  272.6 10.4 %collective-permute-start.20 = (bf16[2,400,128]{2,1,0:T(8,128)(2,1)}, bf16[2,400,128]{2,1,0:T(8,128)(2,1)S(1)}, u32[]{:S(2)}, u32[]{:S(2)}) collective-permute-start(bf16[2,400,128]{2,1,0:T(8,128)(2,1)} %get-tuple-element.196), channel_id=1, source_target_pairs={{0,8},{4,12},{8,0},{12,4},{16,24},{20,28},{24,16},{28,20},{1,9},{5... | collective-permute-start | bytes 614408 | tf_op jit(solution)/shard_map/ppermute | solution.py:1165
  285.4 12.7 %collective-permute-start.25 = (bf16[1,400,128]{2,1,0:T(8,128)(2,1)}, bf16[1,400,128]{2,1,0:T(8,128)(2,1)S(1)}, u32[]{:S(2)}, u32[]{:S(2)}) collective-permute-start(bf16[1,400,128]{2,1,0:T(8,128)(2,1)} %get-tuple-element.204), channel_id=1, source_target_pairs={{0,16},{4,20},{8,24},{12,28},{16,0},{20,4},{24,8},{28,12},{1,17},{... | collective-permute-start | bytes 307208 | tf_op jit(solution)/shard_map/ppermute | solution.py:1165
  285.5 35.3 %all-to-all-start.9 = ((bf16[8,528,128]{2,1,0:T(8,128)(2,1)}), bf16[8,528,128]{2,1,0:T(8,128)(2,1)S(1)}, u32[]{:S(2)}, u32[]{:S(2)}) async-start(bf16[8,528,128]{2,1,0:T(8,128)(2,1)} %bitcast.18), calls=%async_computation.10 | async-start | bytes 2162688 | tf_op jit(solution)/shard_map/all_to_all | solution.py:1242
  304.5 3.1 collective-permute-start.26
  304.6 16.2 %collective-permute-start.28 = (bf16[400,128]{1,0:T(8,128)(2,1)S(1)}, bf16[400,128]{1,0:T(8,128)(2,1)S(1)}, u32[]{:S(2)}, u32[]{:S(2)}) collective-permute-start(bf16[400,128]{1,0:T(8,128)(2,1)S(1)} %copy-done.48), channel_id=1, source_target_pairs={{0,16},{4,20},{8,24},{12,28},{16,0},{20,4},{24,8},{28,12},{1,17},{... | collective-permute-start | bytes 307208 | tf_op jit(solution)/shard_map/ppermute | solution.py:1165
  310.3 10.5 %collective-permute-start.27 = (bf16[1,768,128]{2,1,0:T(8,128)(2,1)}, bf16[1,768,128]{2,1,0:T(8,128)(2,1)S(1)}, u32[]{:S(2)}, u32[]{:S(2)}) collective-permute-start(bf16[1,768,128]{2,1,0:T(8,128)(2,1)} %get-tuple-element.208), channel_id=1, source_target_pairs={{0,2},{1,3},{2,0},{3,1},{4,6},{5,7},{6,4},{7,5},{8,10},{9,11},{10,... | collective-permute-start | bytes 589832 | tf_op jit(solution)/shard_map/ppermute | solution.py:928
  310.6 18.6 %collective-permute-start.22 = (bf16[132,1152]{1,0:T(8,128)(2,1)S(1)}, bf16[132,1152]{1,0:T(8,128)(2,1)S(1)}, u32[]{:S(2)}, u32[]{:S(2)}) collective-permute-start(bf16[132,1152]{1,0:T(8,128)(2,1)S(1)} %copy-done.38), channel_id=1, source_target_pairs={{0,1},{1,0},{2,3},{3,2},{4,5},{5,4},{6,7},{7,6},{8,9},{9,8},{10,11... | collective-permute-start | bytes 912392 | tf_op jit(solution)/shard_map/ppermute | solution.py:928
  310.7 18.5 %collective-permute-start.23 = (bf16[132,1152]{1,0:T(8,128)(2,1)S(1)}, bf16[132,1152]{1,0:T(8,128)(2,1)S(1)}, u32[]{:S(2)}, u32[]{:S(2)}) collective-permute-start(bf16[132,1152]{1,0:T(8,128)(2,1)S(1)} %copy-done.37), channel_id=1, source_target_pairs={{0,2},{1,3},{2,0},{3,1},{4,6},{5,7},{6,4},{7,5},{8,10},{9,11},{10,... | collective-permute-start | bytes 912392 | tf_op jit(solution)/shard_map/ppermute | solution.py:928
  312.5 17.8 %collective-permute-start.24 = (bf16[132,1152]{1,0:T(8,128)(2,1)S(1)}, bf16[132,1152]{1,0:T(8,128)(2,1)S(1)}, u32[]{:S(2)}, u32[]{:S(2)}) collective-permute-start(bf16[132,1152]{1,0:T(8,128)(2,1)S(1)} %copy-done.36), channel_id=1, source_target_pairs={{0,3},{1,2},{2,1},{3,0},{4,7},{5,6},{6,5},{7,4},{8,11},{9,10},{10,... | collective-permute-start | bytes 912392 | tf_op jit(solution)/shard_map/ppermute | solution.py:928
  323.7 13.5 %all-to-all-start.10 = ((bf16[8,96,128]{2,1,0:T(8,128)(2,1)}), bf16[8,96,128]{2,1,0:T(8,128)(2,1)S(1)}, u32[]{:S(2)}, u32[]{:S(2)}) async-start(bf16[8,96,128]{2,1,0:T(8,128)(2,1)} %bitcast.109), calls=%async_computation.11 | async-start | bytes 393216 | tf_op jit(solution)/shard_map/all_to_all | solution.py:1261
  327.1 8.9 %collective-permute-start.29 = (bf16[400,128]{1,0:T(8,128)(2,1)S(1)}, bf16[400,128]{1,0:T(8,128)(2,1)S(1)}, u32[]{:S(2)}, u32[]{:S(2)}) collective-permute-start(bf16[400,128]{1,0:T(8,128)(2,1)S(1)} %copy-done.48), channel_id=1, source_target_pairs={{0,8},{4,12},{8,0},{12,4},{16,24},{20,28},{24,16},{28,20},{1,9},{5... | collective-permute-start | bytes 307208 | tf_op jit(solution)/shard_map/ppermute | solution.py:1165
  329.1 8.1 %collective-permute-start.30 = (bf16[400,128]{1,0:T(8,128)(2,1)}, bf16[400,128]{1,0:T(8,128)(2,1)S(1)}, u32[]{:S(2)}, u32[]{:S(2)}) collective-permute-start(bf16[400,128]{1,0:T(8,128)(2,1)} %copy-done.49), channel_id=1, source_target_pairs={{0,8},{4,12},{8,0},{12,4},{16,24},{20,28},{24,16},{28,20},{1,9},{5... | collective-permute-start | bytes 307208 | tf_op jit(solution)/shard_map/ppermute | solution.py:1165
  340.9 9.5 %copy-start.52 = (bf16[400,128]{1,0:T(8,128)(2,1)S(1)}, bf16[400,128]{1,0:T(8,128)(2,1)}, u32[]{:S(2)}) copy-start(bf16[400,128]{1,0:T(8,128)(2,1)} %copy-done.51) | copy-start | bytes 307204
  340.9 9.6 %copy-start.50 = (bf16[400,128]{1,0:T(8,128)(2,1)S(1)}, bf16[400,128]{1,0:T(8,128)(2,1)}, u32[]{:S(2)}) copy-start(bf16[400,128]{1,0:T(8,128)(2,1)} %copy-done.49) | copy-start | bytes 307204
  340.9 11.6 %copy-start.54 = (bf16[400,128]{1,0:T(8,128)(2,1)S(1)}, bf16[400,128]{1,0:T(8,128)(2,1)}, u32[]{:S(2)}) copy-start(bf16[400,128]{1,0:T(8,128)(2,1)} %copy-done.53) | copy-start | bytes 307204
  340.9 35.2 %all-to-all-start.11 = ((bf16[8,624,128]{2,1,0:T(8,128)(2,1)}), bf16[8,624,128]{2,1,0:T(8,128)(2,1)S(1)}, u32[]{:S(2)}, u32[]{:S(2)}) async-start(bf16[8,624,128]{2,1,0:T(8,128)(2,1)} %shard_map.428), calls=%async_computation.12 | async-start | bytes 2555904 | tf_op jit(solution)/shard_map/all_to_all | solution.py:1280
  348.4 12.7 %collective-permute-start.31 = (bf16[400,128]{1,0:T(8,128)(2,1)S(1)}, bf16[400,128]{1,0:T(8,128)(2,1)S(1)}, u32[]{:S(2)}, u32[]{:S(2)}) collective-permute-start(bf16[400,128]{1,0:T(8,128)(2,1)S(1)} %copy-done.48), channel_id=1, source_target_pairs={{0,4},{4,0},{8,12},{12,8},{16,20},{20,16},{24,28},{28,24},{1,5},{5... | collective-permute-start | bytes 307208 | tf_op jit(solution)/shard_map/ppermute | solution.py:1165
  350.4 14.7 %collective-permute-start.32 = (bf16[400,128]{1,0:T(8,128)(2,1)S(1)}, bf16[400,128]{1,0:T(8,128)(2,1)S(1)}, u32[]{:S(2)}, u32[]{:S(2)}) collective-permute-start(bf16[400,128]{1,0:T(8,128)(2,1)S(1)} %copy-done.52), channel_id=1, source_target_pairs={{0,4},{4,0},{8,12},{12,8},{16,20},{20,16},{24,28},{28,24},{1,5},{5... | collective-permute-start | bytes 307208 | tf_op jit(solution)/shard_map/ppermute | solution.py:1165
  350.5 18.5 %collective-permute-start.33 = (bf16[400,128]{1,0:T(8,128)(2,1)S(1)}, bf16[400,128]{1,0:T(8,128)(2,1)S(1)}, u32[]{:S(2)}, u32[]{:S(2)}) collective-permute-start(bf16[400,128]{1,0:T(8,128)(2,1)S(1)} %copy-done.50), channel_id=1, source_target_pairs={{0,4},{4,0},{8,12},{12,8},{16,20},{20,16},{24,28},{28,24},{1,5},{5... | collective-permute-start | bytes 307208 | tf_op jit(solution)/shard_map/ppermute | solution.py:1165
  352.5 17.7 %collective-permute-start.34 = (bf16[400,128]{1,0:T(8,128)(2,1)S(1)}, bf16[400,128]{1,0:T(8,128)(2,1)S(1)}, u32[]{:S(2)}, u32[]{:S(2)}) collective-permute-start(bf16[400,128]{1,0:T(8,128)(2,1)S(1)} %copy-done.54), channel_id=1, source_target_pairs={{0,4},{4,0},{8,12},{12,8},{16,20},{20,16},{24,28},{28,24},{1,5},{5... | collective-permute-start | bytes 307208 | tf_op jit(solution)/shard_map/ppermute | solution.py:1165
  361.1 9.1 %copy-start.56 = (bf16[400,128]{1,0:T(8,128)(2,1)}, bf16[400,128]{1,0:T(8,128)(2,1)S(1)}, u32[]{:S(2)}) copy-start(bf16[400,128]{1,0:T(8,128)(2,1)S(1)} %collective-permute-done.31.refs_2_) | copy-start | bytes 307204
  377.1 7.7 %copy-start.9 = (f32[864,32]{1,0:T(8,128)S(1)}, f32[864,32]{1,0:T(8,128)}, u32[]{:S(2)}) copy-start(f32[864,32]{1,0:T(8,128)} %get-tuple-element.220) | copy-start | bytes 331780
  (52 other events, 100.1 us)
Sparse Core Ops, SparseCore 0:
  178.6 36.5 reduce-scatter.1

commit v5 on v4

--- a/solution.py
+++ b/solution.py
@@ -23,6 +23,10 @@
 NORM_ORDER = ((0, DIRECT), (256, NARROW), (256 + NARROW, SQUEEZE), (512, WIDE), (896, SPREAD), (1024, PROJECT))
 TILE_ROW = {"d": (0, DIRECT), "w": (2, WIDE), "s": (5, SPREAD), "p": (6, PROJECT)}
 OUTER = ("d", "w", "s", "p")
+SUMS = {
+    "w": ((0, 0), (0, 320), WIDE), "s": ((0, 640), (0, 768), SPREAD), "p": ((0, 896), (1, 896), PROJECT),
+    "d": ((1, 384), (1, 640), DIRECT), "r": ((1, 0), (1, 192), REDUCED),
+}
 CHUNK = 96
 
 
@@ -114,6 +118,29 @@
     for i in range(-(-width // 128)):
         part = vector[:, 128 * i : min(128 * (i + 1), width)]
         ref[first + i : first + i + 1, : part.shape[1]] = part
+
+
+def put_sums(tiles, unit, sums):
+    for (which, start), vector in zip(SUMS[unit][:2], sums):
+        at = 0
+        while at < vector.shape[1]:
+            r, lane = divmod(start + at, 128)
+            size = min(128 - lane, vector.shape[1] - at)
+            tiles[which][r : r + 1, lane : lane + size] = vector[:, at : at + size]
+            at += size
+
+
+def get_sums(tiles, unit):
+    sums = []
+    for which, start in SUMS[unit][:2]:
+        pieces, at = [], 0
+        while at < SUMS[unit][2]:
+            r, lane = divmod(start + at, 128)
+            size = min(128 - lane, SUMS[unit][2] - at)
+            pieces.append(tiles[which][r : r + 1, lane : lane + size])
+            at += size
+        sums.append(pieces[0] if len(pieces) == 1 else jnp.concatenate(pieces, axis=1))
+    return sums
 
 
 def affine_of(aff_ref, block, unit):
@@ -554,13 +581,14 @@
     clips, groups, me_ref, g_ref, counts_ref, aff_ref, yd_ref, yw_ref, ys_ref, yp_ref, mc_ref, *refs
 ):
     up_refs, o_refs = refs[:groups], refs[groups : 2 * groups]
-    dd_ref, dw_ref, ds_ref, dp_ref, pay_ref, st_ref, shares, up, out, tile = refs[2 * groups :]
+    dd_ref, dw_ref, ds_ref, dp_ref, pay_ref, rest_ref, st_ref, shares, up, out, tile = refs[2 * groups :]
     me = me_ref[0]
     means, rstds = combine_moments(g_ref[...], counts_ref[:, 3:4, :], 0, 8, 8)
     st_ref[0:8, :] = means
     st_ref[8:16, :] = rstds
     st = st_ref[...]
     tile[...] = jnp.zeros_like(tile)
+    rest_ref[...] = jnp.zeros_like(rest_ref)
     for k, ref in enumerate(up_refs):
         shares[me ^ k] = ref[...].astype(F32)
     at = 0
@@ -573,15 +601,14 @@
         own = width // groups
         for s in range(groups):
             up[:, s * own : (s + 1) * own] = shares[s, :, at : at + own]
-        first, second = local_backward(
+        sums = local_backward(
             y_ref, lambda rows: up[rows, :width], m_ref=mc_ref, mean=mean, rstd=rstd, scale=scale,
             shift=shift, dh_ref=dh_ref, out_ref=out, rows=clips * LATE.clip_rows,
         )
         for s in range(groups):
             shares[s, :, at : at + own] = out[:, s * own : (s + 1) * own]
         at += own
-        put_row(tile, TILE_ROW[unit][0], first)
-        put_row(tile, 8 + TILE_ROW[unit][0], second)
+        put_sums((tile, rest_ref), unit, sums)
     for k, ref in enumerate(o_refs):
         ref[...] = shares[me ^ k].astype(BF16)
     send_tile(pay_ref, tile)
@@ -604,7 +631,7 @@
         first, width = TILE_ROW[unit]
         mean, rstd = outer_stats(st, unit)
         scale, _ = affine_of(aff_ref, geo.block, unit)
-        scale_sum, shift_sum = row(sums, first, width), row(sums, 8 + first, width)
+        scale_sum, shift_sum = get_sums((sums,), unit)
 
         def finish(r, carry):
             at = pl.ds(r, CHUNK)
@@ -619,7 +646,7 @@
 
 
 def inner_backward_kernel(
-    geo, clips, pack, str_ref, aff_ref, gw_ref, gs_ref, yr_ref, kw_ref, ks_ref, m_ref,
+    geo, clips, pack, str_ref, aff_ref, gw_ref, gs_ref, yr_ref, kw_ref, ks_ref, m_ref, rest_ref,
     dh_ref, pay_ref, pad_w, pad_s, kt_w, kt_s, dz, tile
 ):
     rows = clips * geo.clip_rows
@@ -654,13 +681,12 @@
                 total = term if total is None else total + term
             dz[c * geo.clip_rows : (c + 1) * geo.clip_rows, start : start + depth] = total
     scale, shift = affine_of(aff_ref, geo.block, "r")
-    first, second = local_backward(
+    sums = local_backward(
         yr_ref, lambda at: dz[at, :], m_ref=m_ref, mean=row(st_r, 0, REDUCED),
         rstd=row(st_r, 4, REDUCED), scale=scale, shift=shift, dh_ref=dh_ref, out_ref=None, rows=rows,
     )
-    tile[...] = jnp.zeros_like(tile)
-    put_row(tile, 0, first)
-    put_row(tile, 4, second)
+    tile[...] = rest_ref[...]
+    put_sums((None, tile), "r", sums)
     send_tile(pay_ref, tile)
 
 
@@ -795,12 +821,7 @@
     mean_p, rstd_p = outer_stats(st, "p")
     mean_r, rstd_r = row(st_r, 0, REDUCED), row(st_r, 4, REDUCED)
 
-    def pair(unit):
-        first, width = TILE_ROW[unit]
-        return row(sums, first, width), row(sums, 8 + first, width)
-
-    pair_d, pair_p = pair("d"), pair("p")
-    pair_r = (row(sums_r, 0, REDUCED), row(sums_r, 4, REDUCED))
+    pair_d, pair_p, pair_r = (get_sums((sums, sums_r), unit) for unit in "dpr")
 
     def finish(r, carry):
         at = pl.ds(r, CHUNK)
@@ -825,7 +846,7 @@
 def late_input_kernel(
     clips, g_ref, sums_ref, st_ref, str_ref, aff_ref, dr_ref, dd_ref, dp_ref, yr_ref, yd_ref, yp_ref,
     mc_ref, wt_ref, spread_ref, est_ref, ed_ref, ew_ref, es_ref, ep_ref, m_ref,
-    gy_ref, hd_ref, hw_ref, hs_ref, hp_ref, pay_ref, sumr_ref, held, grad, wide, tile
+    gy_ref, hd_ref, hw_ref, hs_ref, hp_ref, pay_ref, rest_ref, sumr_ref, held, grad, wide, tile
 ):
     point_gradients(
         LATE, clips, g_ref, sums_ref, st_ref, str_ref, aff_ref, dr_ref, dd_ref, dp_ref, yr_ref,
@@ -834,6 +855,7 @@
     grad[...] = nn(gy_ref[...], wt_ref[...]).astype(BF16)
     st = est_ref[...]
     tile[...] = jnp.zeros_like(tile)
+    rest_ref[...] = jnp.zeros_like(rest_ref)
     column = 0
     for unit, y_ref, dh_ref in zip(
         OUTER, (ed_ref, ew_ref, es_ref, ep_ref), (hd_ref, hw_ref, hs_ref, hp_ref)
@@ -851,8 +873,7 @@
             y_ref, lambda at: wide[at, :width], m_ref=m_ref, mean=mean, rstd=rstd, scale=scale,
             shift=shift, dh_ref=dh_ref, out_ref=None, rows=clips * EARLY.clip_rows,
         )
-        put_row(tile, TILE_ROW[unit][0], sums[0])
-        put_row(tile, 8 + TILE_ROW[unit][0], sums[1])
+        put_sums((tile, rest_ref), unit, sums)
     send_tile(pay_ref, tile)
 
 
@@ -974,7 +995,7 @@
             idle=len(behind),
         )[0]
 
-    early_shares = Shares(ordered(packed(pack, 0, ()), point_shares[-1], arrived)).all()
+    early_shares = Shares(ordered(packed(pack, 0, ()), point_shares[-1], arrived))
     own_visible = lax.dynamic_slice_in_dim(visible, me * clips, clips, 0)
     fine = own_visible.astype(F32).reshape(rows, 1)
     mask = jnp.broadcast_to(fine, (rows, 128))
@@ -1041,6 +1062,7 @@
             us=25 if geo is EARLY else 9,
         )
 
+    early_shares = early_shares.all(counts)
     bn, bs, yw, ys, kw, ks, pay, st_r = second(
         EARLY, 2, counts, yr, mask, early_shares, tile, (late_own,)
     )
@@ -1074,15 +1096,15 @@
         lambda *refs: late_outputs_kernel(clips, groups, *refs),
         [(up_pieces[0].shape, BF16)] * groups
         + [((late_rows, w), F32) for w in widths]
-        + [((devices, 16, 128), F32), ((16, 128), F32)],
+        + [((devices, 8, 128), F32), ((8, 128), F32), ((16, 128), F32)],
         [me_ref, g, counts, affine, lyd, lyw, lys, lyp, coarse] + up_pieces,
         [
             ((groups,) + up_pieces[0].shape, F32), ((late_rows, WIDE), F32), ((late_rows, WIDE), F32),
-            ((16, 128), F32),
+            ((8, 128), F32),
         ],
         us=4,
     )
-    outs, (hd, hw, hs, hp), (pay, lst) = res[:groups], res[groups : groups + 4], res[groups + 4 :]
+    outs, (hd, hw, hs, hp), (pay, rest, lst) = res[:groups], res[groups : groups + 4], res[groups + 4 :]
     g = exchange(pay)
 
     outs = [outs[0]] + [swap(outs[k], k) for k in range(1, groups)]
@@ -1091,19 +1113,19 @@
         own = clips * geo.clip_rows
         return call(
             lambda *refs: finish_kernel(geo, clips, *refs),
-            [((own, WIDE), BF16), ((own, SPREAD), BF16), ((16, 128), F32)],
+            [((own, WIDE), BF16), ((own, SPREAD), BF16), ((8, 128), F32)],
             [g, st, st_r, affine, hw, hs, yw, ys, masking] + list(behind),
             idle=len(behind),
             us=7 if geo is EARLY else 2.5,
         )
 
-    def inner(geo, st_r, gw, gs, yr, kw, ks, masking, behind=()):
+    def inner(geo, st_r, gw, gs, yr, kw, ks, masking, rest, behind=()):
         own = clips * geo.clip_rows
         padded = clips * geo.padded_rows
         return call(
             lambda *refs: inner_backward_kernel(geo, clips, pack, *refs),
             [((own, REDUCED), F32), ((devices, 8, 128), F32)],
-            [st_r, affine, gw, gs, yr, kw, ks, masking] + list(behind),
+            [st_r, affine, gw, gs, yr, kw, ks, masking, rest] + list(behind),
             [
                 ((padded, 9 * WIDE), BF16), ((padded, 9 * SPREAD), BF16),
                 ((3, 9 * WIDE, NARROW), BF16), ((3, 9 * SPREAD, SQUEEZE), BF16),
@@ -1168,32 +1190,35 @@
         return -(-size // unit) * unit
 
     gw, gs, late_sums = finish(LATE, g, lst, lst_r, hw, hs, lyw, lys, coarse)
-    hr, pay = inner(LATE, lst_r, gw, gs, lyr, lkw, lks, coarse)
+    hr, pay = inner(LATE, lst_r, gw, gs, lyr, lkw, lks, coarse, rest)
     g = exchange(pay)
     (late_kernels,) = kernel_grads(
         LATE, whole_units(pack.kernels), gw, gs, lbn, lbs, False
     )
-    late_share = lax.psum_scatter(late_kernels, "ch", scatter_dimension=0)
+    late_share = lax.psum_scatter(ordered(late_kernels, g), "ch", scatter_dimension=0)
+    gy, ed, ew, es, ep, pay, rest, late_sums_r = call(
+        lambda *refs: late_input_kernel(clips, *refs),
+        [((late_rows, POINT), BF16)]
+        + [((rows, w), F32) for w in widths]
+        + [((devices, 8, 128), F32), ((8, 128), F32), ((8, 128), F32)],
+        [g, late_sums, lst, lst_r, affine, hr, hd, hp, lyr, lyd, lyp, coarse, late_wt, spread_back,
+         st, yd, yw, ys, yp, mask, late_kernels],
+        [((late_rows, PROJECT), F32), ((late_rows, CONCAT), BF16), ((rows, WIDE), F32), ((8, 128), F32)],
+        idle=1,
+        us=15,
+    )
+    g = exchange(pay)
     (out_arrived,) = call(
         join_kernel,
         [((groups,) + outs[0].shape, BF16)],
-        [me_ref] + outs,
+        [me_ref] + outs + [gy],
         us=1,
-    )
-    gy, ed, ew, es, ep, pay, late_sums_r = call(
-        lambda *refs: late_input_kernel(clips, *refs),
-        [((late_rows, POINT), BF16)]
-        + [((rows, w), F32) for w in widths]
-        + [((devices, 16, 128), F32), ((8, 128), F32)],
-        [g, late_sums, lst, lst_r, affine, hr, hd, hp, lyr, lyd, lyp, coarse, late_wt, spread_back,
-         st, yd, yw, ys, yp, mask, late_kernels, out_arrived],
-        [((late_rows, PROJECT), F32), ((late_rows, CONCAT), BF16), ((rows, WIDE), F32), ((16, 128), F32)],
-        idle=2,
-        us=15,
-    )
-    g = exchange(pay)
+        idle=1,
+    )
     late_points = point_grads(late_pack, late_pack.points, gy, late_act)
-    gw, gs, sums = finish(EARLY, g, st, st_r, ew, es, yw, ys, mask, late_points[1:])
+    gw, gs, sums = finish(
+        EARLY, g, st, st_r, ew, es, yw, ys, mask, (late_points[1], out_arrived)
+    )
     early_size = whole_units(pack.kernels + late_pack.points)
     halves = kernel_grads(EARLY, early_size, gw, gs, bn, bs, True, late_points)
     early_sum = Reduction(*halves)
@@ -1235,7 +1260,7 @@
     )
     late_sum = BatchHalves(*late_halves)
     kept = early_sum.halve(late_halves[1])
-    hr, pay = inner(EARLY, st_r, gw, gs, yr, kw, ks, mask, behind=(kept,))
+    hr, pay = inner(EARLY, st_r, gw, gs, yr, kw, ks, mask, rest, behind=(kept,))
     g = exchange(pay)
     late_kept = late_sum.step(hr)
     own = early_sum.add(late_kept)
@@ -1257,7 +1282,7 @@
     point_sum = Reduction(*point_halves)
     kept = point_sum.halve()
     got = late_sum.double()
-    point_own = point_sum.add(parts, *got)
+    point_own = point_sum.add(parts)
     point_parts = lax.all_to_all(point_own.reshape(batches, -1, 128), "batch", 0, 0)
     (feature_grad,) = call(
         lambda *refs: feature_kernel(pack, *refs),
@@ -1309,25 +1334,23 @@
         [part.reshape(spread_kernels.shape[1:]) for part in (early_spread, late_spread)]
     )
 
-    def outer_pair(tile, unit):
-        first, width = TILE_ROW[unit]
-        return jnp.stack([tile[k : k + 3].reshape(-1)[:width] for k in (first, first + 8)])
-
-    def inner_pair(tile, low, high):
-        return jnp.stack([tile[k : k + 2].reshape(-1)[low:high] for k in (0, 4)])
+    def sum_pair(tiles, unit, low=0, high=None):
+        first, second, width = SUMS[unit]
+        flat = [tile.reshape(-1) for tile in tiles]
+        high = width if high is None else high
+        return jnp.stack([flat[t][at + low : at + high] for t, at in (first, second)])
 
     def own_part(early_pair, late_pair):
         both = jnp.stack([early_pair, late_pair])
         size = both.shape[2] // groups
         return lax.dynamic_slice_in_dim(both, me * size, size, 2)
 
+    early_tiles, late_tiles = (sums, sums_r), (late_sums, late_sums_r)
     norm_grads = [
-        own_part(outer_pair(sums, "d"), outer_pair(late_sums, "d")),
-        own_part(inner_pair(sums_r, 0, NARROW), inner_pair(late_sums_r, 0, NARROW)),
-        own_part(outer_pair(sums, "w"), outer_pair(late_sums, "w")),
-        own_part(inner_pair(sums_r, NARROW, REDUCED), inner_pair(late_sums_r, NARROW, REDUCED)),
-        own_part(outer_pair(sums, "s"), outer_pair(late_sums, "s")),
-        own_part(outer_pair(sums, "p"), outer_pair(late_sums, "p")),
+        own_part(*(sum_pair(tiles, *part) for tiles in (early_tiles, late_tiles)))
+        for part in (
+            ("d",), ("r", 0, NARROW), ("w",), ("r", NARROW, REDUCED), ("s",), ("p",),
+        )
     ]
     return tuple(outputs) + (feature_grad,) + tuple(point_outs) + (
         wide_grad, spread_grad,

time: 400 us -> 388 us (0.970)
  waiting for transfers between devices: 81.6 us -> 64.8 us
  local copies, waits for them, and re-layouts: 32.6 us -> 38.1 us
    ppermute x25, waiting for transfers between devices: 25.5 us -> 16.1 us  [swap(): return lax.ppermute(value, 'ch', [(i, i ^ bit) for i in range(groups)])]
    ppermute x10, waiting for transfers between devices: 28.4 us -> 19.1 us  [batch_swap(): return lax.ppermute(value, 'batch', [(i, i ^ bit) for i in range(batches)])]
    unnamed x144 -> x143, local copies, waits for them, and re-layouts: 22 us -> 27.3 us
  transfers between devices with their start and end apart: 47 -> 47, of which waited for: 19 -> 20; matrix products, arithmetic and copies ran while one was open for 5% -> 6% of each run, Pallas kernels for 35% -> 36%
where the time goes in v5:
time: 388 us; the launch traced here: 382 us
  Pallas kernels  170 us (44%)
  starting transfers between devices  72.2 us (19%)
  waiting for transfers between devices  64.8 us (17%)
  local copies, waits for them, and re-layouts  38.1 us (10%)
  between operations  14.9 us (4%)
  blocking collectives  13.3 us (3%)
  other arithmetic  8.41 us (2%)
    pallas_call x36, Pallas kernels, call(): pl.pallas_call(body, out_shape=[jax.ShapeDtypeStruct(s, d) for s, d in ou...  170 us
    all_to_all x7, starting transfers between devices, exchange(): return lax.all_to_all(payload, BOTH, 0, 0)  28.2 us
    unnamed x143, local copies, waits for them, and re-layouts  27.3 us
    all_to_all x7, waiting for transfers between devices, exchange(): return lax.all_to_all(payload, BOTH, 0, 0)  23.2 us
    ppermute x10, waiting for transfers between devices, batch_swap(): return lax.ppermute(value, 'batch', [(i, i ^ bit) for i in range(batches)])  19.1 us
    ppermute x25, waiting for transfers between devices, swap(): return lax.ppermute(value, 'ch', [(i, i ^ bit) for i in range(groups)])  16.1 us
    ppermute x25, starting transfers between devices, swap(): return lax.ppermute(value, 'ch', [(i, i ^ bit) for i in range(groups)])  15.1 us
    all_to_all x1, blocking collectives, exchange(): return lax.all_to_all(payload, BOTH, 0, 0)  13.3 us
  transfers between devices with their start and end apart: 47, of which 20 were waited for; matrix products, arithmetic and copies ran while one was open for 6% of the time, Pallas kernels for 36%

profile of v5, /device:TPU:0, one launch (start us, length us, event | category | flops | bytes accessed | tf_op | source)
XLA Modules:
  0.0 382.0 jit_solution(744827370133921858)
XLA Ops:
  8.6 2.5 shard_map.391
  11.6 2.5 collective-permute-start.1
  14.1 3.5 all-to-all-start
  19.4 4.8 %shard_map.394 = (bf16[2700,128]{1,0:T(8,128)(2,1)}, bf16[2700,128]{1,0:T(8,128)(2,1)}) custom-call(bf16[2,345600]{1,0:T(2,128)(2,1)} %refs_0_.3, bf16[4,132,1152]{2,1,0:T(8,128)(2,1)} %get-tuple-element.124.refs_1_), custom_call_target="tpu_custom_call" | custom-call | flops 5280000000 | bytes 2764800 | tf_op jit(solution)/shard_map/pallas_call | solution.py:72
  24.2 2.9 reshape.136.refs_0_
  27.4 1.9 reshape.138.refs_0_
  30.4 2.3 shard_map.395.refs_0_
  38.2 5.3 %shard_map.392 = (bf16[1152,528]{1,0:T(8,128)(2,1)}, bf16[576,528]{1,0:T(8,128)(2,1)}, f32[4,1152]{1,0:T(4,128)}, f32[1152,192]{1,0:T(8,128)}, f32[32,8,128]{2,1,0:T(8,128)}) custom-call(s32[1]{0:T(128)} %bitcast.refs_0_, bf16[4,132,1152]{2,1,0:T(8,128)(2,1)} %copy-done, bf16[736,128]{1,0:T(8,128)(2,1)} %get-tuple-element.125.refs_2_, ...), custom_call_target="tpu_custom_call" | custom-call | flops 9459999744 | bytes 5517316 | tf_op jit(solution)/shard_map/pallas_call | solution.py:72
  43.5 5.4 %all-to-all-start.1 = ((f32[32,8,128]{2,1,0:T(8,128)}), f32[32,8,128]{2,1,0:T(8,128)S(1)}, u32[]{:S(2)}, u32[]{:S(2)}) async-start(f32[32,8,128]{2,1,0:T(8,128)} %get-tuple-element.126), calls=%async_computation.1 | async-start | bytes 262144 | tf_op jit(solution)/shard_map/all_to_all | solution.py:946
  50.7 2.3 shard_map.398.refs_11_.refs_0_
  53.0 4.3 %all-to-all-done.1.refs_1_.refs_2_ = f32[32,8,128]{2,1,0:T(8,128)S(1)} async-done(((f32[32,8,128]{2,1,0:T(8,128)}), f32[32,8,128]{2,1,0:T(8,128)S(1)}, u32[]{:S(2)}, u32[]{:S(2)}) %all-to-all-start.1) | async-done | bytes 131104 | tf_op jit(solution)/shard_map/all_to_all | solution.py:946
  59.1 5.7 %shard_map.393 = (f32[1152,256]{1,0:T(8,128)}, f32[1152,128]{1,0:T(8,128)}, f32[16,128]{1,0:T(8,128)}) custom-call(bf16[1152,528]{1,0:T(8,128)(2,1)} %get-tuple-element.129.refs_0_.refs_2_.refs_4_, bf16[576,528]{1,0:T(8,128)(2,1)} %get-tuple-element.130.refs_1_.refs_13_, f32[1152,128]{1,0:T(8,128)} %broadcast_in_dim.16.refs_6_.refs_2_.refs_5_.refs_8_.refs_19_.refs_7_.refs_12_), custom_call_target="tpu_custom_call" | custom-call | flops 13200000000 | bytes 4192256 | tf_op jit(solution)/shard_map/pallas_call | solution.py:72
  66.8 17.0 %shard_map.399 = (bf16[1728,1536]{1,0:T(8,128)(2,1)}, bf16[1728,384]{1,0:T(8,128)(2,1)}, f32[1152,320]{1,0:T(8,128)}, f32[1152,128]{1,0:T(8,128)}, bf16[3,4,80,1...) custom-call(s32[1]{0:T(128)} %bitcast.refs_0_, ...), custom_call_target="tpu_custom_call" | custom-call | flops 27499999232 | bytes 17217540 | tf_op jit(solution)/shard_map/pallas_call | solution.py:72
  83.8 5.6 %all-to-all-start.2 = ((f32[32,16,128]{2,1,0:T(8,128)}), f32[32,16,128]{2,1,0:T(8,128)S(1)}, u32[]{:S(2)}, u32[]{:S(2)}) async-start(f32[32,16,128]{2,1,0:T(8,128)} %get-tuple-element.134), calls=%async_computation.2 | async-start | bytes 524288 | tf_op jit(solution)/shard_map/all_to_all | solution.py:946
  92.2 8.0 %all-to-all-done.2.refs_1_ = f32[32,16,128]{2,1,0:T(8,128)S(1)} async-done(((f32[32,16,128]{2,1,0:T(8,128)}), f32[32,16,128]{2,1,0:T(8,128)S(1)}, u32[]{:S(2)}, u32[]{:S(2)}) %all-to-all-start.2) | async-done | bytes 262176 | tf_op jit(solution)/shard_map/all_to_all | solution.py:946
  100.9 8.1 %shard_map.402 = (bf16[192,832]{1,0:T(8,128)(2,1)}, bf16[576,832]{1,0:T(8,128)(2,1)}, f32[192,192]{1,0:T(8,128)}, f32[32,8,128]{2,1,0:T(8,128)}, f32[16,128]{1,0:T(8,128)}) custom-call(s32[1]{0:T(128)} %bitcast.refs_0_, f32[32,16,128]{2,1,0:T(8,128)} %copy-done.14, f32[32,8,128]{2,1,0:T(8,128)} %copy-done.3, ...), custom_call_target="tpu_custom_call" | custom-call | flops 16499999744 | bytes 7641092 | tf_op jit(solution)/shard_map/pallas_call | solution.py:72
  108.9 3.0 all-to-all-start.3
  112.2 7.9 %all-to-all-done.3.refs_1_ = f32[32,8,128]{2,1,0:T(8,128)S(1)} async-done(((f32[32,8,128]{2,1,0:T(8,128)}), f32[32,8,128]{2,1,0:T(8,128)S(1)}, u32[]{:S(2)}, u32[]{:S(2)}) %all-to-all-start.3) | async-done | bytes 131104 | tf_op jit(solution)/shard_map/all_to_all | solution.py:946
  121.9 2.7 shard_map.403
  125.8 7.8 %shard_map.406 = (bf16[384,1536]{1,0:T(8,128)(2,1)}, bf16[384,384]{1,0:T(8,128)(2,1)}, f32[192,320]{1,0:T(8,128)}, f32[192,128]{1,0:T(8,128)}, bf16[3,4,80,1536]...) custom-call(s32[1]{0:T(128)} %bitcast.refs_0_, ...), custom_call_target="tpu_custom_call" | custom-call | flops 9900000256 | bytes 9107460 | tf_op jit(solution)/shard_map/pallas_call | solution.py:72
  133.6 2.6 all-to-all-start.4
  141.9 4.6 %collective-permute-done.13.refs_11_ = bf16[192,208]{1,0:T(8,128)(2,1)S(1)} collective-permute-done((bf16[192,208]{1,0:T(8,128)(2,1)}, bf16[192,208]{1,0:T(8,128)(2,1)S(1)}, u32[]{:S(2)}, u32[]{:S(2)}) %collective-permute-start.13) | collective-permute-done | bytes 79904 | tf_op jit(solution)/shard_map/ppermute | solution.py:949
  148.6 4.1 %shard_map.408 = (bf16[192,208]{1,0:T(8,128)(2,1)}, bf16[192,208]{1,0:T(8,128)(2,1)}, bf16[192,208]{1,0:T(8,128)(2,1)}, bf16[192,208]{1,0:T(8,128)(2,1)}, f32[19...) custom-call(s32[1]{0:T(128)} %bitcast.refs_0_, ...), custom_call_target="tpu_custom_call" | custom-call | flops 4400000000 | bytes 2570244 | tf_op jit(solution)/shard_map/pallas_call | solution.py:72
  152.8 13.3 %all_to_all.60.refs_0_ = f32[32,8,128]{2,1,0:T(8,128)} all-to-all(f32[32,8,128]{2,1,0:T(8,128)} %get-tuple-element.158), channel_id=1, replica_groups=mesh['batch'=8,'ch'=4] {'batch','ch'}, dimensions={0} | all-to-all | bytes 262144 | tf_op jit(solution)/shard_map/all_to_all | solution.py:946
  166.0 2.2 shard_map.409
  168.2 5.5 %shard_map.410 = (f32[192,192]{1,0:T(8,128)}, f32[32,8,128]{2,1,0:T(8,128)}) custom-call(f32[8,128]{1,0:T(8,128)} %get-tuple-element.157.refs_2_.refs_0_.refs_3_, f32[4,1152]{1,0:T(4,128)} %get-tuple-element.127.refs_3_.refs_1_.refs_4_.refs_5_, bf16[192,320]{1,0:T(8,128)(2,1)} %get-tuple-element.162.refs_2_.refs_1_, ...), custom_call_target="tpu_custom_call" | custom-call | flops 6160000000 | bytes 3966976 | tf_op jit(solution)/shard_map/pallas_call | solution.py:72
  173.7 2.6 all-to-all-start.6
  176.3 5.4 %shard_map.411.refs_20_ = bf16[4,3200,128]{2,1,0:T(8,128)(2,1)} custom-call(s32[1]{0:T(128)} %bitcast.refs_0_, bf16[192,320]{1,0:T(8,128)(2,1)} %get-tuple-element.162.refs_2_.refs_1_, bf16[192,128]{1,0:T(8,128)(2,1)} %get-tuple-element.163.refs_3_.refs_2_, bf16[384,1536]{1,0:T(8,128)(2,1)} %get-tuple-element.173.refs_3_, ...), custom_call_target="tpu_custom_call" | custom-call | flops 5500000256 | bytes 4923396 | tf_op jit(solution)/shard_map/pallas_call | solution.py:72
  181.7 3.9 %copy.84.refs_0_ = bf16[4,3200,128]{2,1,0:T(8,128)(2,1)} copy(bf16[4,3200,128]{2,1,0:T(8,128)(2,1)} %shard_map.411.refs_20_) | data formatting | bytes 6553600
  189.1 9.9 %shard_map.412 = (bf16[192,576]{1,0:T(8,128)(2,1)}, f32[1152,256]{1,0:T(8,128)}, f32[1152,320]{1,0:T(8,128)}, f32[1152,128]{1,0:T(8,128)}, f32[1152,128]{1,0:T(8...) custom-call(f32[32,8,128]{2,1,0:T(8,128)} %copy-done.9, f32[8,128]{1,0:T(8,128)} %get-tuple-element.168.refs_1_, ...), custom_call_target="tpu_custom_call" | custom-call | flops 16499999744 | bytes 10844160 | tf_op jit(solution)/shard_map/pallas_call | solution.py:72
  198.9 5.9 %all-to-all-start.7 = ((f32[32,8,128]{2,1,0:T(8,128)}), f32[32,8,128]{2,1,0:T(8,128)S(1)}, u32[]{:S(2)}, u32[]{:S(2)}) async-start(f32[32,8,128]{2,1,0:T(8,128)} %get-tuple-element.177), calls=%async_computation.7 | async-start | bytes 262144 | tf_op jit(solution)/shard_map/all_to_all | solution.py:946
  204.8 2.9 shard_map.414
  210.2 2.9 all-to-all-done.7.refs_0_
  213.8 4.8 %shard_map.415 = (bf16[1152,320]{1,0:T(8,128)(2,1)}, bf16[1152,128]{1,0:T(8,128)(2,1)}, f32[8,128]{1,0:T(8,128)}) custom-call(f32[32,8,128]{2,1,0:T(8,128)} %copy-done.24, f32[16,128]{1,0:T(8,128)} %get-tuple-element.172.refs_14_.refs_1_.refs_3_, f32[8,128]{1,0:T(8,128)} %get-tuple-element.176.refs_2_.refs_0_.refs_4_, ...), custom_call_target="tpu_custom_call" | custom-call | flops 7699999744 | bytes 5916672 | tf_op jit(solution)/shard_map/pallas_call | solution.py:72
  218.6 11.0 %shard_map.416 = (bf16[2,4224,128]{2,1,0:T(8,128)(2,1)}, bf16[2,4224,128]{2,1,0:T(8,128)(2,1)}) custom-call(s32[1]{0:T(128)} %bitcast.refs_0_, bf16[1152,320]{1,0:T(8,128)(2,1)} %get-tuple-element.181.refs_1_.refs_2_, bf16[1152,128]{1,0:T(8,128)(2,1)} %get-tuple-element.182.refs_2_.refs_3_, bf16[1728,1536]{1,0:T(8,128)(2,1)} %get-tuple-element.186.refs_3_, ...), custom_call_target="tpu_custom_call" | custom-call | flops 11000000512 | bytes 13025284 | tf_op jit(solution)/shard_map/pallas_call | solution.py:72
  233.4 2.2 shard_map.418
  237.5 3.9 %shard_map.419 = (bf16[1,4224,128]{2,1,0:T(8,128)(2,1)}, bf16[1,4224,128]{2,1,0:T(8,128)(2,1)}) custom-call(bf16[2,4224,128]{2,1,0:T(8,128)(2,1)} %get-tuple-element.189.refs_0_, bf16[2,4224,128]{2,1,0:T(8,128)(2,1)} %copy-done.29, bf16[4,400,128]{2,1,0:T(8,128)(2,1)} %get-tuple-element.191.refs_2_), custom_call_target="tpu_custom_call" | custom-call | flops 2750000128 | bytes 6488064 | tf_op jit(solution)/shard_map/pallas_call | solution.py:72
  242.1 15.1 %shard_map.420 = (f32[1152,192]{1,0:T(8,128)}, f32[32,8,128]{2,1,0:T(8,128)}) custom-call(f32[8,128]{1,0:T(8,128)} %get-tuple-element.176.refs_2_.refs_0_.refs_4_, f32[4,1152]{1,0:T(4,128)} %get-tuple-element.127.refs_3_.refs_1_.refs_4_.refs_5_, bf16[1152,320]{1,0:T(8,128)(2,1)} %get-tuple-element.181.refs_1_.refs_2_, ...), custom_call_target="tpu_custom_call" | custom-call | flops 17600000000 | bytes 6793216 | tf_op jit(solution)/shard_map/pallas_call | solution.py:72
  257.3 3.1 all-to-all-start.8
  260.4 1.9 shard_map.421
  264.1 4.7 %collective-permute-done.21.refs_1_ = bf16[1,4224,128]{2,1,0:T(8,128)(2,1)S(1)} collective-permute-done((bf16[1,4224,128]{2,1,0:T(8,128)(2,1)}, bf16[1,4224,128]{2,1,0:T(8,128)(2,1)S(1)}, u32[]{:S(2)}, u32[]{:S(2)}) %collective-permute-start.21) | collective-permute-done | bytes 1081376 | tf_op jit(solution)/shard_map/ppermute | solution.py:949
  269.8 2.8 shard_map.422.refs_2_
  275.8 4.5 %all-to-all-start.9 = ((bf16[8,528,128]{2,1,0:T(8,128)(2,1)}), bf16[8,528,128]{2,1,0:T(8,128)(2,1)S(1)}, u32[]{:S(2)}, u32[]{:S(2)}) async-start(bf16[8,528,128]{2,1,0:T(8,128)(2,1)} %bitcast.18), calls=%async_computation.10 | async-start | bytes 2162688 | tf_op jit(solution)/shard_map/all_to_all | solution.py:1267
  280.3 7.7 %shard_map.424 = (bf16[1152,576]{1,0:T(8,128)(2,1)}, bf16[132,1152]{1,0:T(8,128)(2,1)}, bf16[132,1152]{1,0:T(8,128)(2,1)}, bf16[132,1152]{1,0:T(8,128)(2,1)}, bf...) custom-call(s32[1]{0:T(128)} %bitcast.refs_0_, f32[32,8,128]{2,1,0:T(8,128)} %copy-done.23, ...), custom_call_target="tpu_custom_call" | custom-call | flops 9349999616 | bytes 9220100 | tf_op jit(solution)/shard_map/pallas_call | solution.py:72
  290.2 4.1 %shard_map.426 = (bf16[2,768,128]{2,1,0:T(8,128)(2,1)}, bf16[2,768,128]{2,1,0:T(8,128)(2,1)}) custom-call(s32[1]{0:T(128)} %bitcast.refs_0_, bf16[1152,576]{1,0:T(8,128)(2,1)} %get-tuple-element.207.refs_2_.refs_1_, bf16[1152,528]{1,0:T(8,128)(2,1)} %get-tuple-element.129.refs_0_.refs_2_.refs_4_, bf16[400,128]{1,0:T(8,128)(2,1)} %shard_map.425.refs_3_.refs_1_), custom_call_target="tpu_custom_call" | custom-call | flops 4950000128 | bytes 3330052 | tf_op jit(solution)/shard_map/pallas_call | solution.py:72
  294.4 1.8 collective-permute-done.26.refs_1_
  297.0 2.0 shard_map.427
  301.4 2.8 collective-permute-start.29
  304.2 2.7 collective-permute-done.27.refs_1_
  306.9 2.1 all-to-all-done.9.refs_2_.refs_0_
  311.8 4.0 %all-to-all-start.10 = ((bf16[8,96,128]{2,1,0:T(8,128)(2,1)}), bf16[8,96,128]{2,1,0:T(8,128)(2,1)S(1)}, u32[]{:S(2)}, u32[]{:S(2)}) async-start(bf16[8,96,128]{2,1,0:T(8,128)(2,1)} %bitcast.89), calls=%async_computation.11 | async-start | bytes 393216 | tf_op jit(solution)/shard_map/all_to_all | solution.py:1286
  315.8 2.1 collective-permute-start.28
  319.5 3.0 shard_map.429.refs_2_
  325.6 2.5 shard_map.430
  328.1 4.7 %all-to-all-start.11 = ((bf16[8,624,128]{2,1,0:T(8,128)(2,1)}), bf16[8,624,128]{2,1,0:T(8,128)(2,1)S(1)}, u32[]{:S(2)}, u32[]{:S(2)}) async-start(bf16[8,624,128]{2,1,0:T(8,128)(2,1)} %shard_map.430), calls=%async_computation.12 | async-start | bytes 2555904 | tf_op jit(solution)/shard_map/all_to_all | solution.py:1305
  336.3 2.0 collective-permute-start.31
  338.4 2.0 collective-permute-start.33
  341.1 6.4 %collective-permute-done.31.refs_2_ = bf16[400,128]{1,0:T(8,128)(2,1)S(1)} collective-permute-done((bf16[400,128]{1,0:T(8,128)(2,1)S(1)}, bf16[400,128]{1,0:T(8,128)(2,1)S(1)}, u32[]{:S(2)}, u32[]{:S(2)}) %collective-permute-start.31) | collective-permute-done | bytes 102432 | tf_op jit(solution)/shard_map/ppermute | solution.py:1187
  347.5 3.7 collective-permute-done.32.refs_4_
  351.2 5.6 %collective-permute-done.33.refs_6_ = bf16[400,128]{1,0:T(8,128)(2,1)S(1)} collective-permute-done((bf16[400,128]{1,0:T(8,128)(2,1)}, bf16[400,128]{1,0:T(8,128)(2,1)S(1)}, u32[]{:S(2)}, u32[]{:S(2)}) %collective-permute-start.33) | collective-permute-done | bytes 102432 | tf_op jit(solution)/shard_map/ppermute | solution.py:1187
  358.9 2.8 shard_map.431
  361.8 2.4 all-to-all-done.11.refs_0_
  365.2 7.7 %shard_map.432 = (f32[2,345600]{1,0:T(2,128)}, f32[864,32]{1,0:T(8,128)}, f32[64,528]{1,0:T(8,128)}, f32[40,528]{1,0:T(8,128)}, f32[8,528]{1,0:T(8,128)}, /*inde...) custom-call(bf16[8,624,128]{2,1,0:T(8,128)(2,1)} %copy-done.2, ...), custom_call_target="tpu_custom_call" | custom-call | flops 8800000000 | bytes 6319104 | tf_op jit(solution)/shard_map/pallas_call | solution.py:72
  372.9 2.0 pad_maximum_fusion
  (272 shorter events, 69.6 us)
Async XLA Ops:
  11.2 25.3 %collective-permute-start = (bf16[736,128]{1,0:T(8,128)(2,1)}, bf16[736,128]{1,0:T(8,128)(2,1)S(1)}, u32[]{:S(2)}, u32[]{:S(2)}) collective-permute-start(bf16[736,128]{1,0:T(8,128)(2,1)} %get-tuple-element.125.refs_2_), channel_id=1, source_target_pairs={{0,1},{1,0},{2,3},{3,2},{4,5},{5,4},{6,7},{7,6},{8,9},{9,8},{10,11... | collective-permute-start | bytes 565256 | tf_op jit(solution)/shard_map/ppermute | solution.py:949
  11.6 18.3 %collective-permute-start.1 = (bf16[736,128]{1,0:T(8,128)(2,1)}, bf16[736,128]{1,0:T(8,128)(2,1)S(1)}, u32[]{:S(2)}, u32[]{:S(2)}) collective-permute-start(bf16[736,128]{1,0:T(8,128)(2,1)} %get-tuple-element.125.refs_2_), channel_id=1, source_target_pairs={{0,2},{1,3},{2,0},{3,1},{4,6},{5,7},{6,4},{7,5},{8,10},{9,11},{10,... | collective-permute-start | bytes 565256 | tf_op jit(solution)/shard_map/ppermute | solution.py:949
  14.1 20.2 %all-to-all-start = ((bf16[4,132,1152]{2,1,0:T(8,128)(2,1)}), bf16[4,132,1152]{2,1,0:T(8,128)(2,1)S(1)}, u32[]{:S(2)}, u32[]{:S(2)}) async-start(bf16[4,132,1152]{2,1,0:T(8,128)(2,1)} %get-tuple-element.124.refs_1_), calls=%async_computation | async-start | bytes 2506752 | tf_op jit(solution)/shard_map/all_to_all | solution.py:981
  29.9 2.8 collective-permute-start.2
  35.3 30.2 %collective-permute-start.3 = (bf16[3168,128]{1,0:T(8,128)(2,1)}, bf16[3168,128]{1,0:T(8,128)(2,1)S(1)}, u32[]{:S(2)}, u32[]{:S(2)}) collective-permute-start(bf16[3168,128]{1,0:T(8,128)(2,1)} %shard_map.396.refs_7_), channel_id=1, source_target_pairs={{0,1},{1,0},{2,3},{3,2},{4,5},{5,4},{6,7},{7,6},{8,9},{9,8},{10,11... | collective-permute-start | bytes 2433032 | tf_op jit(solution)/shard_map/ppermute | solution.py:949
  35.4 22.0 %collective-permute-start.4 = (bf16[3168,128]{1,0:T(8,128)(2,1)}, bf16[3168,128]{1,0:T(8,128)(2,1)S(1)}, u32[]{:S(2)}, u32[]{:S(2)}) collective-permute-start(bf16[3168,128]{1,0:T(8,128)(2,1)} %shard_map.396.refs_7_), channel_id=1, source_target_pairs={{0,2},{1,3},{2,0},{3,1},{4,6},{5,7},{6,4},{7,5},{8,10},{9,11},{10,... | collective-permute-start | bytes 2433032 | tf_op jit(solution)/shard_map/ppermute | solution.py:949
  43.5 13.8 %all-to-all-start.1 = ((f32[32,8,128]{2,1,0:T(8,128)}), f32[32,8,128]{2,1,0:T(8,128)S(1)}, u32[]{:S(2)}, u32[]{:S(2)}) async-start(f32[32,8,128]{2,1,0:T(8,128)} %get-tuple-element.126), calls=%async_computation.1 | async-start | bytes 262144 | tf_op jit(solution)/shard_map/all_to_all | solution.py:946
  59.0 6.6 %collective-permute-start.5 = (bf16[3168,128]{1,0:T(8,128)(2,1)}, bf16[3168,128]{1,0:T(8,128)(2,1)S(1)}, u32[]{:S(2)}, u32[]{:S(2)}) collective-permute-start(bf16[3168,128]{1,0:T(8,128)(2,1)} %shard_map.397.refs_9_), channel_id=1, source_target_pairs={{0,1},{1,0},{2,3},{3,2},{4,5},{5,4},{6,7},{7,6},{8,9},{9,8},{10,11... | collective-permute-start | bytes 2433032 | tf_op jit(solution)/shard_map/ppermute | solution.py:949
  64.8 25.0 %collective-permute-start.7 = (bf16[1008,128]{1,0:T(8,128)(2,1)}, bf16[1008,128]{1,0:T(8,128)(2,1)S(1)}, u32[]{:S(2)}, u32[]{:S(2)}) collective-permute-start(bf16[1008,128]{1,0:T(8,128)(2,1)} %shard_map.401.refs_11_), channel_id=1, source_target_pairs={{0,2},{1,3},{2,0},{3,1},{4,6},{5,7},{6,4},{7,5},{8,10},{9,11},{10,... | collective-permute-start | bytes 774152 | tf_op jit(solution)/shard_map/ppermute | solution.py:949
  66.8 22.6 %copy-start.16 = (bf16[1008,128]{1,0:T(8,128)(2,1)S(1)}, bf16[1008,128]{1,0:T(8,128)(2,1)}, u32[]{:S(2)}) copy-start(bf16[1008,128]{1,0:T(8,128)(2,1)} %shard_map.401.refs_11_) | copy-start | bytes 774148
  83.8 16.3 %all-to-all-start.2 = ((f32[32,16,128]{2,1,0:T(8,128)}), f32[32,16,128]{2,1,0:T(8,128)S(1)}, u32[]{:S(2)}, u32[]{:S(2)}) async-start(f32[32,16,128]{2,1,0:T(8,128)} %get-tuple-element.134), calls=%async_computation.2 | async-start | bytes 524288 | tf_op jit(solution)/shard_map/all_to_all | solution.py:946
  89.5 2.7 collective-permute-start.6
  89.8 2.4 collective-permute-start.8
  90.5 29.6 %collective-permute-start.10 = (bf16[3168,128]{1,0:T(8,128)(2,1)}, bf16[3168,128]{1,0:T(8,128)(2,1)S(1)}, u32[]{:S(2)}, u32[]{:S(2)}) collective-permute-start(bf16[3168,128]{1,0:T(8,128)(2,1)} %shard_map.404.refs_7_), channel_id=1, source_target_pairs={{0,2},{1,3},{2,0},{3,1},{4,6},{5,7},{6,4},{7,5},{8,10},{9,11},{10,... | collective-permute-start | bytes 2433032 | tf_op jit(solution)/shard_map/ppermute | solution.py:949
  92.2 8.0 %copy-start.42 = (bf16[1008,128]{1,0:T(8,128)(2,1)}, bf16[1008,128]{1,0:T(8,128)(2,1)S(1)}, u32[]{:S(2)}) copy-start(bf16[1008,128]{1,0:T(8,128)(2,1)S(1)} %collective-permute-done.6.refs_12_) | copy-start | bytes 774148
  92.2 8.0 %copy-start.43 = (bf16[1008,128]{1,0:T(8,128)(2,1)}, bf16[1008,128]{1,0:T(8,128)(2,1)S(1)}, u32[]{:S(2)}) copy-start(bf16[1008,128]{1,0:T(8,128)(2,1)S(1)} %collective-permute-done.8.refs_14_) | copy-start | bytes 774148
  100.9 11.1 %copy-start.5 = (bf16[3168,128]{1,0:T(8,128)(2,1)S(1)}, bf16[3168,128]{1,0:T(8,128)(2,1)}, u32[]{:S(2)}) copy-start(bf16[3168,128]{1,0:T(8,128)(2,1)} %shard_map.404.refs_7_) | copy-start | bytes 2433028
  108.9 11.2 %all-to-all-start.3 = ((f32[32,8,128]{2,1,0:T(8,128)}), f32[32,8,128]{2,1,0:T(8,128)S(1)}, u32[]{:S(2)}, u32[]{:S(2)}) async-start(f32[32,8,128]{2,1,0:T(8,128)} %get-tuple-element.139), calls=%async_computation.3 | async-start | bytes 262144 | tf_op jit(solution)/shard_map/all_to_all | solution.py:946
  111.9 12.7 %collective-permute-start.9 = (bf16[3168,128]{1,0:T(8,128)(2,1)S(1)}, bf16[3168,128]{1,0:T(8,128)(2,1)S(1)}, u32[]{:S(2)}, u32[]{:S(2)}) collective-permute-start(bf16[3168,128]{1,0:T(8,128)(2,1)S(1)} %copy-done.5), channel_id=1, source_target_pairs={{0,1},{1,0},{2,3},{3,2},{4,5},{5,4},{6,7},{7,6},{8,9},{9,8},{10,11... | collective-permute-start | bytes 2433032 | tf_op jit(solution)/shard_map/ppermute | solution.py:949
  121.7 2.9 collective-permute-start.11
  125.7 10.4 %copy-start.19 = (bf16[8,2,6,6,32]{4,1,3,2,0:T(2,128)(2,1)S(1)}, bf16[8,2,6,6,32]{4,1,3,2,0:T(2,128)(2,1)}, u32[]{:S(2)}) copy-start(bf16[8,2,6,6,32]{4,1,3,2,0:T(2,128)(2,1)} %param.45) | copy-start | bytes 110596
  125.7 10.5 %copy-start.20 = (bf16[8,2,6,6,32]{4,1,3,2,0:T(2,128)(2,1)S(1)}, bf16[8,2,6,6,32]{4,1,3,2,0:T(2,128)(2,1)}, u32[]{:S(2)}) copy-start(bf16[8,2,6,6,32]{4,1,3,2,0:T(2,128)(2,1)} %param.44) | copy-start | bytes 110596
  125.7 10.5 %copy-start.21 = (bf16[8,2,6,6,80]{4,1,3,2,0:T(2,128)(2,1)S(1)}, bf16[8,2,6,6,80]{4,1,3,2,0:T(2,128)(2,1)}, u32[]{:S(2)}) copy-start(bf16[8,2,6,6,80]{4,1,3,2,0:T(2,128)(2,1)} %param.43) | copy-start | bytes 276484
  125.7 10.5 %copy-start.22 = (bf16[8,2,6,6,64]{4,1,3,2,0:T(2,128)(2,1)S(1)}, bf16[8,2,6,6,64]{4,1,3,2,0:T(2,128)(2,1)}, u32[]{:S(2)}) copy-start(bf16[8,2,6,6,64]{4,1,3,2,0:T(2,128)(2,1)} %param.42) | copy-start | bytes 221188
  133.6 14.3 %all-to-all-start.4 = ((f32[32,16,128]{2,1,0:T(8,128)}), f32[32,16,128]{2,1,0:T(8,128)S(1)}, u32[]{:S(2)}, u32[]{:S(2)}) async-start(f32[32,16,128]{2,1,0:T(8,128)} %get-tuple-element.144), calls=%async_computation.4 | async-start | bytes 524288 | tf_op jit(solution)/shard_map/all_to_all | solution.py:946
  140.0 1.9 collective-permute-start.12
  140.1 6.4 %collective-permute-start.13 = (bf16[192,208]{1,0:T(8,128)(2,1)}, bf16[192,208]{1,0:T(8,128)(2,1)S(1)}, u32[]{:S(2)}, u32[]{:S(2)}) collective-permute-start(bf16[192,208]{1,0:T(8,128)(2,1)} %get-tuple-element.151), channel_id=1, source_target_pairs={{0,2},{1,3},{2,0},{3,1},{4,6},{5,7},{6,4},{7,5},{8,10},{9,11},{10,... | collective-permute-start | bytes 239624 | tf_op jit(solution)/shard_map/ppermute | solution.py:949
  141.8 6.1 %collective-permute-start.14 = (bf16[192,208]{1,0:T(8,128)(2,1)}, bf16[192,208]{1,0:T(8,128)(2,1)S(1)}, u32[]{:S(2)}, u32[]{:S(2)}) collective-permute-start(bf16[192,208]{1,0:T(8,128)(2,1)} %get-tuple-element.152), channel_id=1, source_target_pairs={{0,3},{1,2},{2,1},{3,0},{4,7},{5,6},{6,5},{7,4},{8,11},{9,10},{10,... | collective-permute-start | bytes 239624 | tf_op jit(solution)/shard_map/ppermute | solution.py:949
  173.7 11.9 %all-to-all-start.6 = ((f32[32,8,128]{2,1,0:T(8,128)}), f32[32,8,128]{2,1,0:T(8,128)S(1)}, u32[]{:S(2)}, u32[]{:S(2)}) async-start(f32[32,8,128]{2,1,0:T(8,128)} %get-tuple-element.167), calls=%async_computation.6 | async-start | bytes 262144 | tf_op jit(solution)/shard_map/all_to_all | solution.py:946
  176.3 57.1 %reduce-scatter.2.cloned.1.call-start = ((), (), s32[]{:S(2)}) async-start(), calls=%async_computation.13 | async-start | bytes 4096000 | tf_op jit(solution)/shard_map/reduce_scatter | solution.py:1198
  187.2 20.6 %collective-permute-start.15 = (bf16[192,208]{1,0:T(8,128)(2,1)S(1)}, bf16[192,208]{1,0:T(8,128)(2,1)S(1)}, u32[]{:S(2)}, u32[]{:S(2)}) collective-permute-start(bf16[192,208]{1,0:T(8,128)(2,1)S(1)} %copy-done.61), channel_id=1, source_target_pairs={{0,1},{1,0},{2,3},{3,2},{4,5},{5,4},{6,7},{7,6},{8,9},{9,8},{10,11... | collective-permute-start | bytes 239624 | tf_op jit(solution)/shard_map/ppermute | solution.py:949
  187.3 20.5 %collective-permute-start.16 = (bf16[192,208]{1,0:T(8,128)(2,1)S(1)}, bf16[192,208]{1,0:T(8,128)(2,1)S(1)}, u32[]{:S(2)}, u32[]{:S(2)}) collective-permute-start(bf16[192,208]{1,0:T(8,128)(2,1)S(1)} %copy-done.60), channel_id=1, source_target_pairs={{0,2},{1,3},{2,0},{3,1},{4,6},{5,7},{6,4},{7,5},{8,10},{9,11},{10,... | collective-permute-start | bytes 239624 | tf_op jit(solution)/shard_map/ppermute | solution.py:949
  189.0 18.8 %collective-permute-start.17 = (bf16[192,208]{1,0:T(8,128)(2,1)S(1)}, bf16[192,208]{1,0:T(8,128)(2,1)S(1)}, u32[]{:S(2)}, u32[]{:S(2)}) collective-permute-start(bf16[192,208]{1,0:T(8,128)(2,1)S(1)} %copy-done.59), channel_id=1, source_target_pairs={{0,3},{1,2},{2,1},{3,0},{4,7},{5,6},{6,5},{7,4},{8,11},{9,10},{10,... | collective-permute-start | bytes 239624 | tf_op jit(solution)/shard_map/ppermute | solution.py:949
  198.9 14.2 %all-to-all-start.7 = ((f32[32,8,128]{2,1,0:T(8,128)}), f32[32,8,128]{2,1,0:T(8,128)S(1)}, u32[]{:S(2)}, u32[]{:S(2)}) async-start(f32[32,8,128]{2,1,0:T(8,128)} %get-tuple-element.177), calls=%async_computation.7 | async-start | bytes 262144 | tf_op jit(solution)/shard_map/all_to_all | solution.py:946
  218.6 11.1 %copy-start.27 = (f32[8,128]{1,0:T(8,128)S(1)}, f32[8,128]{1,0:T(8,128)}, u32[]{:S(2)}) copy-start(f32[8,128]{1,0:T(8,128)} %get-tuple-element.168.refs_1_) | copy-start | bytes 12292
  218.6 11.1 %copy-start.1 = (bf16[4,192,208]{2,1,0:T(8,128)(2,1)S(1)}, bf16[4,192,208]{2,1,0:T(8,128)(2,1)}, u32[]{:S(2)}) copy-start(bf16[4,192,208]{2,1,0:T(8,128)(2,1)} %shard_map.413.refs_10_) | copy-start | bytes 958468
  229.6 6.6 %collective-permute-start.18 = (bf16[2,4224,128]{2,1,0:T(8,128)(2,1)}, bf16[2,4224,128]{2,1,0:T(8,128)(2,1)S(1)}, u32[]{:S(2)}, u32[]{:S(2)}) collective-permute-start(bf16[2,4224,128]{2,1,0:T(8,128)(2,1)} %get-tuple-element.190.refs_2_), channel_id=1, source_target_pairs={{0,1},{1,0},{2,3},{3,2},{4,5},{5,4},{6,7},{7,6},{8,9},{9,8},{10,11... | collective-permute-start | bytes 6488072 | tf_op jit(solution)/shard_map/ppermute | solution.py:949
  235.6 24.8 %collective-permute-start.19 = (bf16[4,400,128]{2,1,0:T(8,128)(2,1)}, bf16[4,400,128]{2,1,0:T(8,128)(2,1)}, u32[]{:S(2)}, u32[]{:S(2)}) collective-permute-start(bf16[4,400,128]{2,1,0:T(8,128)(2,1)} %get-tuple-element.191.refs_2_), channel_id=1, source_target_pairs={{0,4},{4,0},{8,12},{12,8},{16,20},{20,16},{24,28},{28,24},{1,5},{5... | collective-permute-start | bytes 1228808 | tf_op jit(solution)/shard_map/ppermute | solution.py:1187
  241.4 27.5 %collective-permute-start.21 = (bf16[1,4224,128]{2,1,0:T(8,128)(2,1)}, bf16[1,4224,128]{2,1,0:T(8,128)(2,1)S(1)}, u32[]{:S(2)}, u32[]{:S(2)}) collective-permute-start(bf16[1,4224,128]{2,1,0:T(8,128)(2,1)} %get-tuple-element.201), channel_id=1, source_target_pairs={{0,2},{1,3},{2,0},{3,1},{4,6},{5,7},{6,4},{7,5},{8,10},{9,11},{10,... | collective-permute-start | bytes 3244040 | tf_op jit(solution)/shard_map/ppermute | solution.py:949
  257.3 18.5 %all-to-all-start.8 = ((f32[32,8,128]{2,1,0:T(8,128)}), f32[32,8,128]{2,1,0:T(8,128)S(1)}, u32[]{:S(2)}, u32[]{:S(2)}) async-start(f32[32,8,128]{2,1,0:T(8,128)} %get-tuple-element.193), calls=%async_computation.9 | async-start | bytes 262144 | tf_op jit(solution)/shard_map/all_to_all | solution.py:946
  262.4 10.3 %collective-permute-start.20 = (bf16[2,400,128]{2,1,0:T(8,128)(2,1)}, bf16[2,400,128]{2,1,0:T(8,128)(2,1)S(1)}, u32[]{:S(2)}, u32[]{:S(2)}) collective-permute-start(bf16[2,400,128]{2,1,0:T(8,128)(2,1)} %get-tuple-element.200), channel_id=1, source_target_pairs={{0,8},{4,12},{8,0},{12,4},{16,24},{20,28},{24,16},{28,20},{1,9},{5... | collective-permute-start | bytes 614408 | tf_op jit(solution)/shard_map/ppermute | solution.py:1187
  275.1 12.9 %collective-permute-start.25 = (bf16[1,400,128]{2,1,0:T(8,128)(2,1)}, bf16[1,400,128]{2,1,0:T(8,128)(2,1)S(1)}, u32[]{:S(2)}, u32[]{:S(2)}) collective-permute-start(bf16[1,400,128]{2,1,0:T(8,128)(2,1)} %get-tuple-element.208), channel_id=1, source_target_pairs={{0,16},{4,20},{8,24},{12,28},{16,0},{20,4},{24,8},{28,12},{1,17},{... | collective-permute-start | bytes 307208 | tf_op jit(solution)/shard_map/ppermute | solution.py:1187
  275.8 33.3 %all-to-all-start.9 = ((bf16[8,528,128]{2,1,0:T(8,128)(2,1)}), bf16[8,528,128]{2,1,0:T(8,128)(2,1)S(1)}, u32[]{:S(2)}, u32[]{:S(2)}) async-start(bf16[8,528,128]{2,1,0:T(8,128)(2,1)} %bitcast.18), calls=%async_computation.10 | async-start | bytes 2162688 | tf_op jit(solution)/shard_map/all_to_all | solution.py:1267
  294.3 1.9 collective-permute-start.26
  299.0 8.0 %collective-permute-start.27 = (bf16[1,768,128]{2,1,0:T(8,128)(2,1)}, bf16[1,768,128]{2,1,0:T(8,128)(2,1)S(1)}, u32[]{:S(2)}, u32[]{:S(2)}) collective-permute-start(bf16[1,768,128]{2,1,0:T(8,128)(2,1)} %get-tuple-element.212), channel_id=1, source_target_pairs={{0,2},{1,3},{2,0},{3,1},{4,6},{5,7},{6,4},{7,5},{8,10},{9,11},{10,... | collective-permute-start | bytes 589832 | tf_op jit(solution)/shard_map/ppermute | solution.py:949
  299.5 18.4 %collective-permute-start.22 = (bf16[132,1152]{1,0:T(8,128)(2,1)S(1)}, bf16[132,1152]{1,0:T(8,128)(2,1)S(1)}, u32[]{:S(2)}, u32[]{:S(2)}) collective-permute-start(bf16[132,1152]{1,0:T(8,128)(2,1)S(1)} %copy-done.38), channel_id=1, source_target_pairs={{0,1},{1,0},{2,3},{3,2},{4,5},{5,4},{6,7},{7,6},{8,9},{9,8},{10,11... | collective-permute-start | bytes 912392 | tf_op jit(solution)/shard_map/ppermute | solution.py:949
  299.6 18.4 %collective-permute-start.23 = (bf16[132,1152]{1,0:T(8,128)(2,1)S(1)}, bf16[132,1152]{1,0:T(8,128)(2,1)S(1)}, u32[]{:S(2)}, u32[]{:S(2)}) collective-permute-start(bf16[132,1152]{1,0:T(8,128)(2,1)S(1)} %copy-done.37), channel_id=1, source_target_pairs={{0,2},{1,3},{2,0},{3,1},{4,6},{5,7},{6,4},{7,5},{8,10},{9,11},{10,... | collective-permute-start | bytes 912392 | tf_op jit(solution)/shard_map/ppermute | solution.py:949
  301.2 17.6 %collective-permute-start.24 = (bf16[132,1152]{1,0:T(8,128)(2,1)S(1)}, bf16[132,1152]{1,0:T(8,128)(2,1)S(1)}, u32[]{:S(2)}, u32[]{:S(2)}) collective-permute-start(bf16[132,1152]{1,0:T(8,128)(2,1)S(1)} %copy-done.36), channel_id=1, source_target_pairs={{0,3},{1,2},{2,1},{3,0},{4,7},{5,6},{6,5},{7,4},{8,11},{9,10},{10,... | collective-permute-start | bytes 912392 | tf_op jit(solution)/shard_map/ppermute | solution.py:949
  301.4 16.4 %collective-permute-start.29 = (bf16[400,128]{1,0:T(8,128)(2,1)S(1)}, bf16[400,128]{1,0:T(8,128)(2,1)S(1)}, u32[]{:S(2)}, u32[]{:S(2)}) collective-permute-start(bf16[400,128]{1,0:T(8,128)(2,1)S(1)} %copy-done.48), channel_id=1, source_target_pairs={{0,16},{4,20},{8,24},{12,28},{16,0},{20,4},{24,8},{28,12},{1,17},{... | collective-permute-start | bytes 307208 | tf_op jit(solution)/shard_map/ppermute | solution.py:1187
  311.8 12.9 %all-to-all-start.10 = ((bf16[8,96,128]{2,1,0:T(8,128)(2,1)}), bf16[8,96,128]{2,1,0:T(8,128)(2,1)S(1)}, u32[]{:S(2)}, u32[]{:S(2)}) async-start(bf16[8,96,128]{2,1,0:T(8,128)(2,1)} %bitcast.89), calls=%async_computation.11 | async-start | bytes 393216 | tf_op jit(solution)/shard_map/all_to_all | solution.py:1286
  315.8 7.2 %collective-permute-start.28 = (bf16[400,128]{1,0:T(8,128)(2,1)S(1)}, bf16[400,128]{1,0:T(8,128)(2,1)S(1)}, u32[]{:S(2)}, u32[]{:S(2)}) collective-permute-start(bf16[400,128]{1,0:T(8,128)(2,1)S(1)} %copy-done.48), channel_id=1, source_target_pairs={{0,8},{4,12},{8,0},{12,4},{16,24},{20,28},{24,16},{28,20},{1,9},{5... | collective-permute-start | bytes 307208 | tf_op jit(solution)/shard_map/ppermute | solution.py:1187
  317.9 10.2 %copy-start.49 = (bf16[400,128]{1,0:T(8,128)(2,1)}, bf16[400,128]{1,0:T(8,128)(2,1)S(1)}, u32[]{:S(2)}) copy-start(bf16[400,128]{1,0:T(8,128)(2,1)S(1)} %collective-permute-done.29.refs_5_) | copy-start | bytes 307204
  317.9 6.5 %collective-permute-start.30 = (bf16[400,128]{1,0:T(8,128)(2,1)S(1)}, bf16[400,128]{1,0:T(8,128)(2,1)S(1)}, u32[]{:S(2)}, u32[]{:S(2)}) collective-permute-start(bf16[400,128]{1,0:T(8,128)(2,1)S(1)} %collective-permute-done.29.refs_5_), channel_id=1, source_target_pairs={{0,8},{4,12},{8,0},{12,4},{16,24},{20,28},{24,16},{28,20},{1,9},{5... | collective-permute-start | bytes 307208 | tf_op jit(solution)/shard_map/ppermute | solution.py:1187
  328.1 6.0 %copy-start.28 = (f32[8,128]{1,0:T(8,128)S(1)}, f32[8,128]{1,0:T(8,128)}, u32[]{:S(2)}) copy-start(f32[8,128]{1,0:T(8,128)} %get-tuple-element.225) | copy-start | bytes 12292
  328.1 10.2 %copy-start.51 = (bf16[400,128]{1,0:T(8,128)(2,1)S(1)}, bf16[400,128]{1,0:T(8,128)(2,1)}, u32[]{:S(2)}) copy-start(bf16[400,128]{1,0:T(8,128)(2,1)} %copy-done.50) | copy-start | bytes 307204
  328.1 12.3 %copy-start.53 = (bf16[400,128]{1,0:T(8,128)(2,1)S(1)}, bf16[400,128]{1,0:T(8,128)(2,1)}, u32[]{:S(2)}) copy-start(bf16[400,128]{1,0:T(8,128)(2,1)} %copy-done.52) | copy-start | bytes 307204
  328.1 36.1 %all-to-all-start.11 = ((bf16[8,624,128]{2,1,0:T(8,128)(2,1)}), bf16[8,624,128]{2,1,0:T(8,128)(2,1)S(1)}, u32[]{:S(2)}, u32[]{:S(2)}) async-start(bf16[8,624,128]{2,1,0:T(8,128)(2,1)} %shard_map.430), calls=%async_computation.12 | async-start | bytes 2555904 | tf_op jit(solution)/shard_map/all_to_all | solution.py:1305
  336.3 11.2 %collective-permute-start.31 = (bf16[400,128]{1,0:T(8,128)(2,1)S(1)}, bf16[400,128]{1,0:T(8,128)(2,1)S(1)}, u32[]{:S(2)}, u32[]{:S(2)}) collective-permute-start(bf16[400,128]{1,0:T(8,128)(2,1)S(1)} %copy-done.48), channel_id=1, source_target_pairs={{0,4},{4,0},{8,12},{12,8},{16,20},{20,16},{24,28},{28,24},{1,5},{5... | collective-permute-start | bytes 307208 | tf_op jit(solution)/shard_map/ppermute | solution.py:1187
  338.3 12.8 %collective-permute-start.32 = (bf16[400,128]{1,0:T(8,128)(2,1)S(1)}, bf16[400,128]{1,0:T(8,128)(2,1)S(1)}, u32[]{:S(2)}, u32[]{:S(2)}) collective-permute-start(bf16[400,128]{1,0:T(8,128)(2,1)S(1)} %copy-done.51), channel_id=1, source_target_pairs={{0,4},{4,0},{8,12},{12,8},{16,20},{20,16},{24,28},{28,24},{1,5},{5... | collective-permute-start | bytes 307208 | tf_op jit(solution)/shard_map/ppermute | solution.py:1187
  338.4 18.4 %collective-permute-start.33 = (bf16[400,128]{1,0:T(8,128)(2,1)}, bf16[400,128]{1,0:T(8,128)(2,1)S(1)}, u32[]{:S(2)}, u32[]{:S(2)}) collective-permute-start(bf16[400,128]{1,0:T(8,128)(2,1)} %copy-done.49), channel_id=1, source_target_pairs={{0,4},{4,0},{8,12},{12,8},{16,20},{20,16},{24,28},{28,24},{1,5},{5... | collective-permute-start | bytes 307208 | tf_op jit(solution)/shard_map/ppermute | solution.py:1187
  340.4 18.0 %collective-permute-start.34 = (bf16[400,128]{1,0:T(8,128)(2,1)S(1)}, bf16[400,128]{1,0:T(8,128)(2,1)S(1)}, u32[]{:S(2)}, u32[]{:S(2)}) collective-permute-start(bf16[400,128]{1,0:T(8,128)(2,1)S(1)} %copy-done.53), channel_id=1, source_target_pairs={{0,4},{4,0},{8,12},{12,8},{16,20},{20,16},{24,28},{28,24},{1,5},{5... | collective-permute-start | bytes 307208 | tf_op jit(solution)/shard_map/ppermute | solution.py:1187
  347.5 10.8 %copy-start.55 = (bf16[400,128]{1,0:T(8,128)(2,1)}, bf16[400,128]{1,0:T(8,128)(2,1)S(1)}, u32[]{:S(2)}) copy-start(bf16[400,128]{1,0:T(8,128)(2,1)S(1)} %collective-permute-done.31.refs_2_) | copy-start | bytes 307204
  351.2 7.1 %copy-start.56 = (bf16[400,128]{1,0:T(8,128)(2,1)}, bf16[400,128]{1,0:T(8,128)(2,1)S(1)}, u32[]{:S(2)}) copy-start(bf16[400,128]{1,0:T(8,128)(2,1)S(1)} %collective-permute-done.32.refs_4_) | copy-start | bytes 307204
  365.2 7.7 %copy-start.11 = (f32[864,32]{1,0:T(8,128)S(1)}, f32[864,32]{1,0:T(8,128)}, u32[]{:S(2)}) copy-start(f32[864,32]{1,0:T(8,128)} %get-tuple-element.224) | copy-start | bytes 331780
  (51 other events, 79.0 us)
Sparse Core Ops, SparseCore 0:
  186.4 41.3 reduce-scatter.1

commit v6 on v5

--- a/solution.py
+++ b/solution.py
@@ -803,7 +803,7 @@
         w_ref[:, pl.ds(first, 4 * WIDE_COLUMNS)] = jnp.concatenate(parts, axis=1)
         return carry
 
-    lax.fori_loop(0, pack.wide // 4, join, 0)
+    lax.fori_loop(0, pack.wide // 4, join, 0, unroll=5)
 
 
 def point_gradients(

time: 388 us -> 387 us (level)
  no operation moved by 1% of the time
where the time goes in v6:
time: 387 us; the launch traced here: 381 us
  Pallas kernels  169 us (44%)
  starting transfers between devices  72.2 us (19%)
  waiting for transfers between devices  64.8 us (17%)
  local copies, waits for them, and re-layouts  38.1 us (10%)
  between operations  14.9 us (4%)
  blocking collectives  13.3 us (3%)
  other arithmetic  8.41 us (2%)
    pallas_call x36, Pallas kernels, call(): pl.pallas_call(body, out_shape=[jax.ShapeDtypeStruct(s, d) for s, d in ou...  169 us
    all_to_all x7, starting transfers between devices, exchange(): return lax.all_to_all(payload, BOTH, 0, 0)  28.2 us
    unnamed x143, local copies, waits for them, and re-layouts  27.3 us
    all_to_all x7, waiting for transfers between devices, exchange(): return lax.all_to_all(payload, BOTH, 0, 0)  23.2 us
    ppermute x10, waiting for transfers between devices, batch_swap(): return lax.ppermute(value, 'batch', [(i, i ^ bit) for i in range(batches)])  19.1 us
    ppermute x25, waiting for transfers between devices, swap(): return lax.ppermute(value, 'ch', [(i, i ^ bit) for i in range(groups)])  16.1 us
    ppermute x25, starting transfers between devices, swap(): return lax.ppermute(value, 'ch', [(i, i ^ bit) for i in range(groups)])  15.1 us
    all_to_all x1, blocking collectives, exchange(): return lax.all_to_all(payload, BOTH, 0, 0)  13.3 us
  transfers between devices with their start and end apart: 47, of which 20 were waited for; matrix products, arithmetic and copies ran while one was open for 6% of the time, Pallas kernels for 36%

profile of v6, /device:TPU:0, one launch (start us, length us, event | category | flops | bytes accessed | tf_op | source)
XLA Modules:
  0.0 380.9 jit_solution(8803044007003319614)
XLA Ops:
  8.6 2.5 shard_map.391
  11.6 2.5 collective-permute-start.1
  14.1 3.5 all-to-all-start
  19.4 4.8 %shard_map.394 = (bf16[2700,128]{1,0:T(8,128)(2,1)}, bf16[2700,128]{1,0:T(8,128)(2,1)}) custom-call(bf16[2,345600]{1,0:T(2,128)(2,1)} %refs_0_.3, bf16[4,132,1152]{2,1,0:T(8,128)(2,1)} %get-tuple-element.124.refs_1_), custom_call_target="tpu_custom_call" | custom-call | flops 5280000000 | bytes 2764800 | tf_op jit(solution)/shard_map/pallas_call | solution.py:72
  24.2 2.9 reshape.136.refs_0_
  27.4 1.9 reshape.138.refs_0_
  30.4 2.3 shard_map.395.refs_0_
  38.2 5.3 %shard_map.392 = (bf16[1152,528]{1,0:T(8,128)(2,1)}, bf16[576,528]{1,0:T(8,128)(2,1)}, f32[4,1152]{1,0:T(4,128)}, f32[1152,192]{1,0:T(8,128)}, f32[32,8,128]{2,1,0:T(8,128)}) custom-call(s32[1]{0:T(128)} %bitcast.refs_0_, bf16[4,132,1152]{2,1,0:T(8,128)(2,1)} %copy-done, bf16[736,128]{1,0:T(8,128)(2,1)} %get-tuple-element.125.refs_2_, ...), custom_call_target="tpu_custom_call" | custom-call | flops 9459999744 | bytes 5517316 | tf_op jit(solution)/shard_map/pallas_call | solution.py:72
  43.5 5.4 %all-to-all-start.1 = ((f32[32,8,128]{2,1,0:T(8,128)}), f32[32,8,128]{2,1,0:T(8,128)S(1)}, u32[]{:S(2)}, u32[]{:S(2)}) async-start(f32[32,8,128]{2,1,0:T(8,128)} %get-tuple-element.126), calls=%async_computation.1 | async-start | bytes 262144 | tf_op jit(solution)/shard_map/all_to_all | solution.py:946
  50.7 2.3 shard_map.398.refs_11_.refs_0_
  53.0 4.3 %all-to-all-done.1.refs_1_.refs_2_ = f32[32,8,128]{2,1,0:T(8,128)S(1)} async-done(((f32[32,8,128]{2,1,0:T(8,128)}), f32[32,8,128]{2,1,0:T(8,128)S(1)}, u32[]{:S(2)}, u32[]{:S(2)}) %all-to-all-start.1) | async-done | bytes 131104 | tf_op jit(solution)/shard_map/all_to_all | solution.py:946
  59.1 5.7 %shard_map.393 = (f32[1152,256]{1,0:T(8,128)}, f32[1152,128]{1,0:T(8,128)}, f32[16,128]{1,0:T(8,128)}) custom-call(bf16[1152,528]{1,0:T(8,128)(2,1)} %get-tuple-element.129.refs_0_.refs_2_.refs_4_, bf16[576,528]{1,0:T(8,128)(2,1)} %get-tuple-element.130.refs_1_.refs_13_, f32[1152,128]{1,0:T(8,128)} %broadcast_in_dim.16.refs_6_.refs_2_.refs_5_.refs_8_.refs_19_.refs_7_.refs_12_), custom_call_target="tpu_custom_call" | custom-call | flops 13200000000 | bytes 4192256 | tf_op jit(solution)/shard_map/pallas_call | solution.py:72
  66.8 17.0 %shard_map.399 = (bf16[1728,1536]{1,0:T(8,128)(2,1)}, bf16[1728,384]{1,0:T(8,128)(2,1)}, f32[1152,320]{1,0:T(8,128)}, f32[1152,128]{1,0:T(8,128)}, bf16[3,4,80,1...) custom-call(s32[1]{0:T(128)} %bitcast.refs_0_, ...), custom_call_target="tpu_custom_call" | custom-call | flops 27499999232 | bytes 17217540 | tf_op jit(solution)/shard_map/pallas_call | solution.py:72
  83.8 5.6 %all-to-all-start.2 = ((f32[32,16,128]{2,1,0:T(8,128)}), f32[32,16,128]{2,1,0:T(8,128)S(1)}, u32[]{:S(2)}, u32[]{:S(2)}) async-start(f32[32,16,128]{2,1,0:T(8,128)} %get-tuple-element.134), calls=%async_computation.2 | async-start | bytes 524288 | tf_op jit(solution)/shard_map/all_to_all | solution.py:946
  92.2 8.0 %all-to-all-done.2.refs_1_ = f32[32,16,128]{2,1,0:T(8,128)S(1)} async-done(((f32[32,16,128]{2,1,0:T(8,128)}), f32[32,16,128]{2,1,0:T(8,128)S(1)}, u32[]{:S(2)}, u32[]{:S(2)}) %all-to-all-start.2) | async-done | bytes 262176 | tf_op jit(solution)/shard_map/all_to_all | solution.py:946
  100.9 8.1 %shard_map.402 = (bf16[192,832]{1,0:T(8,128)(2,1)}, bf16[576,832]{1,0:T(8,128)(2,1)}, f32[192,192]{1,0:T(8,128)}, f32[32,8,128]{2,1,0:T(8,128)}, f32[16,128]{1,0:T(8,128)}) custom-call(s32[1]{0:T(128)} %bitcast.refs_0_, f32[32,16,128]{2,1,0:T(8,128)} %copy-done.14, f32[32,8,128]{2,1,0:T(8,128)} %copy-done.3, ...), custom_call_target="tpu_custom_call" | custom-call | flops 16499999744 | bytes 7641092 | tf_op jit(solution)/shard_map/pallas_call | solution.py:72
  108.9 3.0 all-to-all-start.3
  112.2 7.9 %all-to-all-done.3.refs_1_ = f32[32,8,128]{2,1,0:T(8,128)S(1)} async-done(((f32[32,8,128]{2,1,0:T(8,128)}), f32[32,8,128]{2,1,0:T(8,128)S(1)}, u32[]{:S(2)}, u32[]{:S(2)}) %all-to-all-start.3) | async-done | bytes 131104 | tf_op jit(solution)/shard_map/all_to_all | solution.py:946
  121.9 2.7 shard_map.403
  125.8 7.8 %shard_map.406 = (bf16[384,1536]{1,0:T(8,128)(2,1)}, bf16[384,384]{1,0:T(8,128)(2,1)}, f32[192,320]{1,0:T(8,128)}, f32[192,128]{1,0:T(8,128)}, bf16[3,4,80,1536]...) custom-call(s32[1]{0:T(128)} %bitcast.refs_0_, ...), custom_call_target="tpu_custom_call" | custom-call | flops 9900000256 | bytes 9107460 | tf_op jit(solution)/shard_map/pallas_call | solution.py:72
  133.6 2.6 all-to-all-start.4
  141.9 4.6 %collective-permute-done.13.refs_11_ = bf16[192,208]{1,0:T(8,128)(2,1)S(1)} collective-permute-done((bf16[192,208]{1,0:T(8,128)(2,1)}, bf16[192,208]{1,0:T(8,128)(2,1)S(1)}, u32[]{:S(2)}, u32[]{:S(2)}) %collective-permute-start.13) | collective-permute-done | bytes 79904 | tf_op jit(solution)/shard_map/ppermute | solution.py:949
  148.6 4.1 %shard_map.408 = (bf16[192,208]{1,0:T(8,128)(2,1)}, bf16[192,208]{1,0:T(8,128)(2,1)}, bf16[192,208]{1,0:T(8,128)(2,1)}, bf16[192,208]{1,0:T(8,128)(2,1)}, f32[19...) custom-call(s32[1]{0:T(128)} %bitcast.refs_0_, ...), custom_call_target="tpu_custom_call" | custom-call | flops 4400000000 | bytes 2570244 | tf_op jit(solution)/shard_map/pallas_call | solution.py:72
  152.8 13.3 %all_to_all.60.refs_0_ = f32[32,8,128]{2,1,0:T(8,128)} all-to-all(f32[32,8,128]{2,1,0:T(8,128)} %get-tuple-element.158), channel_id=1, replica_groups=mesh['batch'=8,'ch'=4] {'batch','ch'}, dimensions={0} | all-to-all | bytes 262144 | tf_op jit(solution)/shard_map/all_to_all | solution.py:946
  166.0 2.2 shard_map.409
  168.2 5.5 %shard_map.410 = (f32[192,192]{1,0:T(8,128)}, f32[32,8,128]{2,1,0:T(8,128)}) custom-call(f32[8,128]{1,0:T(8,128)} %get-tuple-element.157.refs_2_.refs_0_.refs_3_, f32[4,1152]{1,0:T(4,128)} %get-tuple-element.127.refs_3_.refs_1_.refs_4_.refs_5_, bf16[192,320]{1,0:T(8,128)(2,1)} %get-tuple-element.162.refs_2_.refs_1_, ...), custom_call_target="tpu_custom_call" | custom-call | flops 6160000000 | bytes 3966976 | tf_op jit(solution)/shard_map/pallas_call | solution.py:72
  173.7 2.6 all-to-all-start.6
  176.3 5.4 %shard_map.411.refs_20_ = bf16[4,3200,128]{2,1,0:T(8,128)(2,1)} custom-call(s32[1]{0:T(128)} %bitcast.refs_0_, bf16[192,320]{1,0:T(8,128)(2,1)} %get-tuple-element.162.refs_2_.refs_1_, bf16[192,128]{1,0:T(8,128)(2,1)} %get-tuple-element.163.refs_3_.refs_2_, bf16[384,1536]{1,0:T(8,128)(2,1)} %get-tuple-element.173.refs_3_, ...), custom_call_target="tpu_custom_call" | custom-call | flops 5500000256 | bytes 4923396 | tf_op jit(solution)/shard_map/pallas_call | solution.py:72
  181.7 3.9 %copy.84.refs_0_ = bf16[4,3200,128]{2,1,0:T(8,128)(2,1)} copy(bf16[4,3200,128]{2,1,0:T(8,128)(2,1)} %shard_map.411.refs_20_) | data formatting | bytes 6553600
  189.1 9.9 %shard_map.412 = (bf16[192,576]{1,0:T(8,128)(2,1)}, f32[1152,256]{1,0:T(8,128)}, f32[1152,320]{1,0:T(8,128)}, f32[1152,128]{1,0:T(8,128)}, f32[1152,128]{1,0:T(8...) custom-call(f32[32,8,128]{2,1,0:T(8,128)} %copy-done.9, f32[8,128]{1,0:T(8,128)} %get-tuple-element.168.refs_1_, ...), custom_call_target="tpu_custom_call" | custom-call | flops 16499999744 | bytes 10844160 | tf_op jit(solution)/shard_map/pallas_call | solution.py:72
  198.9 5.9 %all-to-all-start.7 = ((f32[32,8,128]{2,1,0:T(8,128)}), f32[32,8,128]{2,1,0:T(8,128)S(1)}, u32[]{:S(2)}, u32[]{:S(2)}) async-start(f32[32,8,128]{2,1,0:T(8,128)} %get-tuple-element.177), calls=%async_computation.7 | async-start | bytes 262144 | tf_op jit(solution)/shard_map/all_to_all | solution.py:946
  204.8 2.9 shard_map.414
  210.2 2.9 all-to-all-done.7.refs_0_
  213.8 4.8 %shard_map.415 = (bf16[1152,320]{1,0:T(8,128)(2,1)}, bf16[1152,128]{1,0:T(8,128)(2,1)}, f32[8,128]{1,0:T(8,128)}) custom-call(f32[32,8,128]{2,1,0:T(8,128)} %copy-done.24, f32[16,128]{1,0:T(8,128)} %get-tuple-element.172.refs_14_.refs_1_.refs_3_, f32[8,128]{1,0:T(8,128)} %get-tuple-element.176.refs_2_.refs_0_.refs_4_, ...), custom_call_target="tpu_custom_call" | custom-call | flops 7699999744 | bytes 5916672 | tf_op jit(solution)/shard_map/pallas_call | solution.py:72
  218.6 11.0 %shard_map.416 = (bf16[2,4224,128]{2,1,0:T(8,128)(2,1)}, bf16[2,4224,128]{2,1,0:T(8,128)(2,1)}) custom-call(s32[1]{0:T(128)} %bitcast.refs_0_, bf16[1152,320]{1,0:T(8,128)(2,1)} %get-tuple-element.181.refs_1_.refs_2_, bf16[1152,128]{1,0:T(8,128)(2,1)} %get-tuple-element.182.refs_2_.refs_3_, bf16[1728,1536]{1,0:T(8,128)(2,1)} %get-tuple-element.186.refs_3_, ...), custom_call_target="tpu_custom_call" | custom-call | flops 11000000512 | bytes 13025284 | tf_op jit(solution)/shard_map/pallas_call | solution.py:72
  233.4 2.2 shard_map.418
  237.5 3.9 %shard_map.419 = (bf16[1,4224,128]{2,1,0:T(8,128)(2,1)}, bf16[1,4224,128]{2,1,0:T(8,128)(2,1)}) custom-call(bf16[2,4224,128]{2,1,0:T(8,128)(2,1)} %get-tuple-element.189.refs_0_, bf16[2,4224,128]{2,1,0:T(8,128)(2,1)} %copy-done.29, bf16[4,400,128]{2,1,0:T(8,128)(2,1)} %get-tuple-element.191.refs_2_), custom_call_target="tpu_custom_call" | custom-call | flops 2750000128 | bytes 6488064 | tf_op jit(solution)/shard_map/pallas_call | solution.py:72
  242.1 15.1 %shard_map.420 = (f32[1152,192]{1,0:T(8,128)}, f32[32,8,128]{2,1,0:T(8,128)}) custom-call(f32[8,128]{1,0:T(8,128)} %get-tuple-element.176.refs_2_.refs_0_.refs_4_, f32[4,1152]{1,0:T(4,128)} %get-tuple-element.127.refs_3_.refs_1_.refs_4_.refs_5_, bf16[1152,320]{1,0:T(8,128)(2,1)} %get-tuple-element.181.refs_1_.refs_2_, ...), custom_call_target="tpu_custom_call" | custom-call | flops 17600000000 | bytes 6793216 | tf_op jit(solution)/shard_map/pallas_call | solution.py:72
  257.3 3.1 all-to-all-start.8
  260.4 1.9 shard_map.421
  264.1 4.7 %collective-permute-done.21.refs_1_ = bf16[1,4224,128]{2,1,0:T(8,128)(2,1)S(1)} collective-permute-done((bf16[1,4224,128]{2,1,0:T(8,128)(2,1)}, bf16[1,4224,128]{2,1,0:T(8,128)(2,1)S(1)}, u32[]{:S(2)}, u32[]{:S(2)}) %collective-permute-start.21) | collective-permute-done | bytes 1081376 | tf_op jit(solution)/shard_map/ppermute | solution.py:949
  269.8 2.8 shard_map.422.refs_2_
  275.8 4.5 %all-to-all-start.9 = ((bf16[8,528,128]{2,1,0:T(8,128)(2,1)}), bf16[8,528,128]{2,1,0:T(8,128)(2,1)S(1)}, u32[]{:S(2)}, u32[]{:S(2)}) async-start(bf16[8,528,128]{2,1,0:T(8,128)(2,1)} %bitcast.18), calls=%async_computation.10 | async-start | bytes 2162688 | tf_op jit(solution)/shard_map/all_to_all | solution.py:1267
  280.3 7.7 %shard_map.424 = (bf16[1152,576]{1,0:T(8,128)(2,1)}, bf16[132,1152]{1,0:T(8,128)(2,1)}, bf16[132,1152]{1,0:T(8,128)(2,1)}, bf16[132,1152]{1,0:T(8,128)(2,1)}, bf...) custom-call(s32[1]{0:T(128)} %bitcast.refs_0_, f32[32,8,128]{2,1,0:T(8,128)} %copy-done.23, ...), custom_call_target="tpu_custom_call" | custom-call | flops 9349999616 | bytes 9220100 | tf_op jit(solution)/shard_map/pallas_call | solution.py:72
  290.2 4.1 %shard_map.426 = (bf16[2,768,128]{2,1,0:T(8,128)(2,1)}, bf16[2,768,128]{2,1,0:T(8,128)(2,1)}) custom-call(s32[1]{0:T(128)} %bitcast.refs_0_, bf16[1152,576]{1,0:T(8,128)(2,1)} %get-tuple-element.207.refs_2_.refs_1_, bf16[1152,528]{1,0:T(8,128)(2,1)} %get-tuple-element.129.refs_0_.refs_2_.refs_4_, bf16[400,128]{1,0:T(8,128)(2,1)} %shard_map.425.refs_3_.refs_1_), custom_call_target="tpu_custom_call" | custom-call | flops 4950000128 | bytes 3330052 | tf_op jit(solution)/shard_map/pallas_call | solution.py:72
  294.4 1.8 collective-permute-done.26.refs_1_
  297.0 2.0 shard_map.427
  301.4 2.8 collective-permute-start.29
  304.2 2.7 collective-permute-done.27.refs_1_
  306.9 2.1 all-to-all-done.9.refs_2_.refs_0_
  311.8 4.0 %all-to-all-start.10 = ((bf16[8,96,128]{2,1,0:T(8,128)(2,1)}), bf16[8,96,128]{2,1,0:T(8,128)(2,1)S(1)}, u32[]{:S(2)}, u32[]{:S(2)}) async-start(bf16[8,96,128]{2,1,0:T(8,128)(2,1)} %bitcast.89), calls=%async_computation.11 | async-start | bytes 393216 | tf_op jit(solution)/shard_map/all_to_all | solution.py:1286
  315.8 2.1 collective-permute-start.28
  319.5 3.0 shard_map.429.refs_2_
  325.6 2.5 shard_map.430
  328.1 4.7 %all-to-all-start.11 = ((bf16[8,624,128]{2,1,0:T(8,128)(2,1)}), bf16[8,624,128]{2,1,0:T(8,128)(2,1)S(1)}, u32[]{:S(2)}, u32[]{:S(2)}) async-start(bf16[8,624,128]{2,1,0:T(8,128)(2,1)} %shard_map.430), calls=%async_computation.12 | async-start | bytes 2555904 | tf_op jit(solution)/shard_map/all_to_all | solution.py:1305
  336.3 2.0 collective-permute-start.31
  338.4 2.0 collective-permute-start.33
  341.1 6.4 %collective-permute-done.31.refs_2_ = bf16[400,128]{1,0:T(8,128)(2,1)S(1)} collective-permute-done((bf16[400,128]{1,0:T(8,128)(2,1)S(1)}, bf16[400,128]{1,0:T(8,128)(2,1)S(1)}, u32[]{:S(2)}, u32[]{:S(2)}) %collective-permute-start.31) | collective-permute-done | bytes 102432 | tf_op jit(solution)/shard_map/ppermute | solution.py:1187
  347.5 3.7 collective-permute-done.32.refs_4_
  351.2 5.6 %collective-permute-done.33.refs_6_ = bf16[400,128]{1,0:T(8,128)(2,1)S(1)} collective-permute-done((bf16[400,128]{1,0:T(8,128)(2,1)}, bf16[400,128]{1,0:T(8,128)(2,1)S(1)}, u32[]{:S(2)}, u32[]{:S(2)}) %collective-permute-start.33) | collective-permute-done | bytes 102432 | tf_op jit(solution)/shard_map/ppermute | solution.py:1187
  358.9 2.8 shard_map.431
  361.8 2.4 all-to-all-done.11.refs_0_
  365.2 6.6 %shard_map.432 = (f32[2,345600]{1,0:T(2,128)}, f32[864,32]{1,0:T(8,128)}, f32[64,528]{1,0:T(8,128)}, f32[40,528]{1,0:T(8,128)}, f32[8,528]{1,0:T(8,128)}, /*inde...) custom-call(bf16[8,624,128]{2,1,0:T(8,128)(2,1)} %copy-done.2, ...), custom_call_target="tpu_custom_call" | custom-call | flops 8800000000 | bytes 6319104 | tf_op jit(solution)/shard_map/pallas_call | solution.py:72
  371.9 2.0 pad_maximum_fusion
  (272 shorter events, 69.6 us)
Async XLA Ops:
  11.2 25.3 %collective-permute-start = (bf16[736,128]{1,0:T(8,128)(2,1)}, bf16[736,128]{1,0:T(8,128)(2,1)S(1)}, u32[]{:S(2)}, u32[]{:S(2)}) collective-permute-start(bf16[736,128]{1,0:T(8,128)(2,1)} %get-tuple-element.125.refs_2_), channel_id=1, source_target_pairs={{0,1},{1,0},{2,3},{3,2},{4,5},{5,4},{6,7},{7,6},{8,9},{9,8},{10,11... | collective-permute-start | bytes 565256 | tf_op jit(solution)/shard_map/ppermute | solution.py:949
  11.6 18.3 %collective-permute-start.1 = (bf16[736,128]{1,0:T(8,128)(2,1)}, bf16[736,128]{1,0:T(8,128)(2,1)S(1)}, u32[]{:S(2)}, u32[]{:S(2)}) collective-permute-start(bf16[736,128]{1,0:T(8,128)(2,1)} %get-tuple-element.125.refs_2_), channel_id=1, source_target_pairs={{0,2},{1,3},{2,0},{3,1},{4,6},{5,7},{6,4},{7,5},{8,10},{9,11},{10,... | collective-permute-start | bytes 565256 | tf_op jit(solution)/shard_map/ppermute | solution.py:949
  14.1 20.2 %all-to-all-start = ((bf16[4,132,1152]{2,1,0:T(8,128)(2,1)}), bf16[4,132,1152]{2,1,0:T(8,128)(2,1)S(1)}, u32[]{:S(2)}, u32[]{:S(2)}) async-start(bf16[4,132,1152]{2,1,0:T(8,128)(2,1)} %get-tuple-element.124.refs_1_), calls=%async_computation | async-start | bytes 2506752 | tf_op jit(solution)/shard_map/all_to_all | solution.py:981
  29.9 2.8 collective-permute-start.2
  35.3 30.2 %collective-permute-start.3 = (bf16[3168,128]{1,0:T(8,128)(2,1)}, bf16[3168,128]{1,0:T(8,128)(2,1)S(1)}, u32[]{:S(2)}, u32[]{:S(2)}) collective-permute-start(bf16[3168,128]{1,0:T(8,128)(2,1)} %shard_map.396.refs_7_), channel_id=1, source_target_pairs={{0,1},{1,0},{2,3},{3,2},{4,5},{5,4},{6,7},{7,6},{8,9},{9,8},{10,11... | collective-permute-start | bytes 2433032 | tf_op jit(solution)/shard_map/ppermute | solution.py:949
  35.4 22.0 %collective-permute-start.4 = (bf16[3168,128]{1,0:T(8,128)(2,1)}, bf16[3168,128]{1,0:T(8,128)(2,1)S(1)}, u32[]{:S(2)}, u32[]{:S(2)}) collective-permute-start(bf16[3168,128]{1,0:T(8,128)(2,1)} %shard_map.396.refs_7_), channel_id=1, source_target_pairs={{0,2},{1,3},{2,0},{3,1},{4,6},{5,7},{6,4},{7,5},{8,10},{9,11},{10,... | collective-permute-start | bytes 2433032 | tf_op jit(solution)/shard_map/ppermute | solution.py:949
  43.5 13.8 %all-to-all-start.1 = ((f32[32,8,128]{2,1,0:T(8,128)}), f32[32,8,128]{2,1,0:T(8,128)S(1)}, u32[]{:S(2)}, u32[]{:S(2)}) async-start(f32[32,8,128]{2,1,0:T(8,128)} %get-tuple-element.126), calls=%async_computation.1 | async-start | bytes 262144 | tf_op jit(solution)/shard_map/all_to_all | solution.py:946
  59.0 6.6 %collective-permute-start.5 = (bf16[3168,128]{1,0:T(8,128)(2,1)}, bf16[3168,128]{1,0:T(8,128)(2,1)S(1)}, u32[]{:S(2)}, u32[]{:S(2)}) collective-permute-start(bf16[3168,128]{1,0:T(8,128)(2,1)} %shard_map.397.refs_9_), channel_id=1, source_target_pairs={{0,1},{1,0},{2,3},{3,2},{4,5},{5,4},{6,7},{7,6},{8,9},{9,8},{10,11... | collective-permute-start | bytes 2433032 | tf_op jit(solution)/shard_map/ppermute | solution.py:949
  64.8 25.0 %collective-permute-start.7 = (bf16[1008,128]{1,0:T(8,128)(2,1)}, bf16[1008,128]{1,0:T(8,128)(2,1)S(1)}, u32[]{:S(2)}, u32[]{:S(2)}) collective-permute-start(bf16[1008,128]{1,0:T(8,128)(2,1)} %shard_map.401.refs_11_), channel_id=1, source_target_pairs={{0,2},{1,3},{2,0},{3,1},{4,6},{5,7},{6,4},{7,5},{8,10},{9,11},{10,... | collective-permute-start | bytes 774152 | tf_op jit(solution)/shard_map/ppermute | solution.py:949
  66.8 22.6 %copy-start.16 = (bf16[1008,128]{1,0:T(8,128)(2,1)S(1)}, bf16[1008,128]{1,0:T(8,128)(2,1)}, u32[]{:S(2)}) copy-start(bf16[1008,128]{1,0:T(8,128)(2,1)} %shard_map.401.refs_11_) | copy-start | bytes 774148
  83.8 16.3 %all-to-all-start.2 = ((f32[32,16,128]{2,1,0:T(8,128)}), f32[32,16,128]{2,1,0:T(8,128)S(1)}, u32[]{:S(2)}, u32[]{:S(2)}) async-start(f32[32,16,128]{2,1,0:T(8,128)} %get-tuple-element.134), calls=%async_computation.2 | async-start | bytes 524288 | tf_op jit(solution)/shard_map/all_to_all | solution.py:946
  89.5 2.7 collective-permute-start.6
  89.8 2.4 collective-permute-start.8
  90.5 29.6 %collective-permute-start.10 = (bf16[3168,128]{1,0:T(8,128)(2,1)}, bf16[3168,128]{1,0:T(8,128)(2,1)S(1)}, u32[]{:S(2)}, u32[]{:S(2)}) collective-permute-start(bf16[3168,128]{1,0:T(8,128)(2,1)} %shard_map.404.refs_7_), channel_id=1, source_target_pairs={{0,2},{1,3},{2,0},{3,1},{4,6},{5,7},{6,4},{7,5},{8,10},{9,11},{10,... | collective-permute-start | bytes 2433032 | tf_op jit(solution)/shard_map/ppermute | solution.py:949
  92.2 8.0 %copy-start.42 = (bf16[1008,128]{1,0:T(8,128)(2,1)}, bf16[1008,128]{1,0:T(8,128)(2,1)S(1)}, u32[]{:S(2)}) copy-start(bf16[1008,128]{1,0:T(8,128)(2,1)S(1)} %collective-permute-done.6.refs_12_) | copy-start | bytes 774148
  92.2 8.0 %copy-start.43 = (bf16[1008,128]{1,0:T(8,128)(2,1)}, bf16[1008,128]{1,0:T(8,128)(2,1)S(1)}, u32[]{:S(2)}) copy-start(bf16[1008,128]{1,0:T(8,128)(2,1)S(1)} %collective-permute-done.8.refs_14_) | copy-start | bytes 774148
  100.9 11.1 %copy-start.5 = (bf16[3168,128]{1,0:T(8,128)(2,1)S(1)}, bf16[3168,128]{1,0:T(8,128)(2,1)}, u32[]{:S(2)}) copy-start(bf16[3168,128]{1,0:T(8,128)(2,1)} %shard_map.404.refs_7_) | copy-start | bytes 2433028
  108.9 11.2 %all-to-all-start.3 = ((f32[32,8,128]{2,1,0:T(8,128)}), f32[32,8,128]{2,1,0:T(8,128)S(1)}, u32[]{:S(2)}, u32[]{:S(2)}) async-start(f32[32,8,128]{2,1,0:T(8,128)} %get-tuple-element.139), calls=%async_computation.3 | async-start | bytes 262144 | tf_op jit(solution)/shard_map/all_to_all | solution.py:946
  111.9 12.7 %collective-permute-start.9 = (bf16[3168,128]{1,0:T(8,128)(2,1)S(1)}, bf16[3168,128]{1,0:T(8,128)(2,1)S(1)}, u32[]{:S(2)}, u32[]{:S(2)}) collective-permute-start(bf16[3168,128]{1,0:T(8,128)(2,1)S(1)} %copy-done.5), channel_id=1, source_target_pairs={{0,1},{1,0},{2,3},{3,2},{4,5},{5,4},{6,7},{7,6},{8,9},{9,8},{10,11... | collective-permute-start | bytes 2433032 | tf_op jit(solution)/shard_map/ppermute | solution.py:949
  121.7 2.9 collective-permute-start.11
  125.7 10.4 %copy-start.19 = (bf16[8,2,6,6,32]{4,1,3,2,0:T(2,128)(2,1)S(1)}, bf16[8,2,6,6,32]{4,1,3,2,0:T(2,128)(2,1)}, u32[]{:S(2)}) copy-start(bf16[8,2,6,6,32]{4,1,3,2,0:T(2,128)(2,1)} %param.45) | copy-start | bytes 110596
  125.7 10.5 %copy-start.20 = (bf16[8,2,6,6,32]{4,1,3,2,0:T(2,128)(2,1)S(1)}, bf16[8,2,6,6,32]{4,1,3,2,0:T(2,128)(2,1)}, u32[]{:S(2)}) copy-start(bf16[8,2,6,6,32]{4,1,3,2,0:T(2,128)(2,1)} %param.44) | copy-start | bytes 110596
  125.7 10.5 %copy-start.21 = (bf16[8,2,6,6,80]{4,1,3,2,0:T(2,128)(2,1)S(1)}, bf16[8,2,6,6,80]{4,1,3,2,0:T(2,128)(2,1)}, u32[]{:S(2)}) copy-start(bf16[8,2,6,6,80]{4,1,3,2,0:T(2,128)(2,1)} %param.43) | copy-start | bytes 276484
  125.7 10.5 %copy-start.22 = (bf16[8,2,6,6,64]{4,1,3,2,0:T(2,128)(2,1)S(1)}, bf16[8,2,6,6,64]{4,1,3,2,0:T(2,128)(2,1)}, u32[]{:S(2)}) copy-start(bf16[8,2,6,6,64]{4,1,3,2,0:T(2,128)(2,1)} %param.42) | copy-start | bytes 221188
  133.6 14.3 %all-to-all-start.4 = ((f32[32,16,128]{2,1,0:T(8,128)}), f32[32,16,128]{2,1,0:T(8,128)S(1)}, u32[]{:S(2)}, u32[]{:S(2)}) async-start(f32[32,16,128]{2,1,0:T(8,128)} %get-tuple-element.144), calls=%async_computation.4 | async-start | bytes 524288 | tf_op jit(solution)/shard_map/all_to_all | solution.py:946
  140.0 1.9 collective-permute-start.12
  140.1 6.4 %collective-permute-start.13 = (bf16[192,208]{1,0:T(8,128)(2,1)}, bf16[192,208]{1,0:T(8,128)(2,1)S(1)}, u32[]{:S(2)}, u32[]{:S(2)}) collective-permute-start(bf16[192,208]{1,0:T(8,128)(2,1)} %get-tuple-element.151), channel_id=1, source_target_pairs={{0,2},{1,3},{2,0},{3,1},{4,6},{5,7},{6,4},{7,5},{8,10},{9,11},{10,... | collective-permute-start | bytes 239624 | tf_op jit(solution)/shard_map/ppermute | solution.py:949
  141.8 6.1 %collective-permute-start.14 = (bf16[192,208]{1,0:T(8,128)(2,1)}, bf16[192,208]{1,0:T(8,128)(2,1)S(1)}, u32[]{:S(2)}, u32[]{:S(2)}) collective-permute-start(bf16[192,208]{1,0:T(8,128)(2,1)} %get-tuple-element.152), channel_id=1, source_target_pairs={{0,3},{1,2},{2,1},{3,0},{4,7},{5,6},{6,5},{7,4},{8,11},{9,10},{10,... | collective-permute-start | bytes 239624 | tf_op jit(solution)/shard_map/ppermute | solution.py:949
  173.7 11.9 %all-to-all-start.6 = ((f32[32,8,128]{2,1,0:T(8,128)}), f32[32,8,128]{2,1,0:T(8,128)S(1)}, u32[]{:S(2)}, u32[]{:S(2)}) async-start(f32[32,8,128]{2,1,0:T(8,128)} %get-tuple-element.167), calls=%async_computation.6 | async-start | bytes 262144 | tf_op jit(solution)/shard_map/all_to_all | solution.py:946
  176.3 57.1 %reduce-scatter.2.cloned.1.call-start = ((), (), s32[]{:S(2)}) async-start(), calls=%async_computation.13 | async-start | bytes 4096000 | tf_op jit(solution)/shard_map/reduce_scatter | solution.py:1198
  187.2 20.6 %collective-permute-start.15 = (bf16[192,208]{1,0:T(8,128)(2,1)S(1)}, bf16[192,208]{1,0:T(8,128)(2,1)S(1)}, u32[]{:S(2)}, u32[]{:S(2)}) collective-permute-start(bf16[192,208]{1,0:T(8,128)(2,1)S(1)} %copy-done.61), channel_id=1, source_target_pairs={{0,1},{1,0},{2,3},{3,2},{4,5},{5,4},{6,7},{7,6},{8,9},{9,8},{10,11... | collective-permute-start | bytes 239624 | tf_op jit(solution)/shard_map/ppermute | solution.py:949
  187.3 20.5 %collective-permute-start.16 = (bf16[192,208]{1,0:T(8,128)(2,1)S(1)}, bf16[192,208]{1,0:T(8,128)(2,1)S(1)}, u32[]{:S(2)}, u32[]{:S(2)}) collective-permute-start(bf16[192,208]{1,0:T(8,128)(2,1)S(1)} %copy-done.60), channel_id=1, source_target_pairs={{0,2},{1,3},{2,0},{3,1},{4,6},{5,7},{6,4},{7,5},{8,10},{9,11},{10,... | collective-permute-start | bytes 239624 | tf_op jit(solution)/shard_map/ppermute | solution.py:949
  189.0 18.8 %collective-permute-start.17 = (bf16[192,208]{1,0:T(8,128)(2,1)S(1)}, bf16[192,208]{1,0:T(8,128)(2,1)S(1)}, u32[]{:S(2)}, u32[]{:S(2)}) collective-permute-start(bf16[192,208]{1,0:T(8,128)(2,1)S(1)} %copy-done.59), channel_id=1, source_target_pairs={{0,3},{1,2},{2,1},{3,0},{4,7},{5,6},{6,5},{7,4},{8,11},{9,10},{10,... | collective-permute-start | bytes 239624 | tf_op jit(solution)/shard_map/ppermute | solution.py:949
  198.9 14.2 %all-to-all-start.7 = ((f32[32,8,128]{2,1,0:T(8,128)}), f32[32,8,128]{2,1,0:T(8,128)S(1)}, u32[]{:S(2)}, u32[]{:S(2)}) async-start(f32[32,8,128]{2,1,0:T(8,128)} %get-tuple-element.177), calls=%async_computation.7 | async-start | bytes 262144 | tf_op jit(solution)/shard_map/all_to_all | solution.py:946
  218.6 11.1 %copy-start.27 = (f32[8,128]{1,0:T(8,128)S(1)}, f32[8,128]{1,0:T(8,128)}, u32[]{:S(2)}) copy-start(f32[8,128]{1,0:T(8,128)} %get-tuple-element.168.refs_1_) | copy-start | bytes 12292
  218.6 11.1 %copy-start.1 = (bf16[4,192,208]{2,1,0:T(8,128)(2,1)S(1)}, bf16[4,192,208]{2,1,0:T(8,128)(2,1)}, u32[]{:S(2)}) copy-start(bf16[4,192,208]{2,1,0:T(8,128)(2,1)} %shard_map.413.refs_10_) | copy-start | bytes 958468
  229.6 6.6 %collective-permute-start.18 = (bf16[2,4224,128]{2,1,0:T(8,128)(2,1)}, bf16[2,4224,128]{2,1,0:T(8,128)(2,1)S(1)}, u32[]{:S(2)}, u32[]{:S(2)}) collective-permute-start(bf16[2,4224,128]{2,1,0:T(8,128)(2,1)} %get-tuple-element.190.refs_2_), channel_id=1, source_target_pairs={{0,1},{1,0},{2,3},{3,2},{4,5},{5,4},{6,7},{7,6},{8,9},{9,8},{10,11... | collective-permute-start | bytes 6488072 | tf_op jit(solution)/shard_map/ppermute | solution.py:949
  235.6 24.8 %collective-permute-start.19 = (bf16[4,400,128]{2,1,0:T(8,128)(2,1)}, bf16[4,400,128]{2,1,0:T(8,128)(2,1)}, u32[]{:S(2)}, u32[]{:S(2)}) collective-permute-start(bf16[4,400,128]{2,1,0:T(8,128)(2,1)} %get-tuple-element.191.refs_2_), channel_id=1, source_target_pairs={{0,4},{4,0},{8,12},{12,8},{16,20},{20,16},{24,28},{28,24},{1,5},{5... | collective-permute-start | bytes 1228808 | tf_op jit(solution)/shard_map/ppermute | solution.py:1187
  241.4 27.5 %collective-permute-start.21 = (bf16[1,4224,128]{2,1,0:T(8,128)(2,1)}, bf16[1,4224,128]{2,1,0:T(8,128)(2,1)S(1)}, u32[]{:S(2)}, u32[]{:S(2)}) collective-permute-start(bf16[1,4224,128]{2,1,0:T(8,128)(2,1)} %get-tuple-element.201), channel_id=1, source_target_pairs={{0,2},{1,3},{2,0},{3,1},{4,6},{5,7},{6,4},{7,5},{8,10},{9,11},{10,... | collective-permute-start | bytes 3244040 | tf_op jit(solution)/shard_map/ppermute | solution.py:949
  257.3 18.5 %all-to-all-start.8 = ((f32[32,8,128]{2,1,0:T(8,128)}), f32[32,8,128]{2,1,0:T(8,128)S(1)}, u32[]{:S(2)}, u32[]{:S(2)}) async-start(f32[32,8,128]{2,1,0:T(8,128)} %get-tuple-element.193), calls=%async_computation.9 | async-start | bytes 262144 | tf_op jit(solution)/shard_map/all_to_all | solution.py:946
  262.4 10.3 %collective-permute-start.20 = (bf16[2,400,128]{2,1,0:T(8,128)(2,1)}, bf16[2,400,128]{2,1,0:T(8,128)(2,1)S(1)}, u32[]{:S(2)}, u32[]{:S(2)}) collective-permute-start(bf16[2,400,128]{2,1,0:T(8,128)(2,1)} %get-tuple-element.200), channel_id=1, source_target_pairs={{0,8},{4,12},{8,0},{12,4},{16,24},{20,28},{24,16},{28,20},{1,9},{5... | collective-permute-start | bytes 614408 | tf_op jit(solution)/shard_map/ppermute | solution.py:1187
  275.1 12.9 %collective-permute-start.25 = (bf16[1,400,128]{2,1,0:T(8,128)(2,1)}, bf16[1,400,128]{2,1,0:T(8,128)(2,1)S(1)}, u32[]{:S(2)}, u32[]{:S(2)}) collective-permute-start(bf16[1,400,128]{2,1,0:T(8,128)(2,1)} %get-tuple-element.208), channel_id=1, source_target_pairs={{0,16},{4,20},{8,24},{12,28},{16,0},{20,4},{24,8},{28,12},{1,17},{... | collective-permute-start | bytes 307208 | tf_op jit(solution)/shard_map/ppermute | solution.py:1187
  275.8 33.3 %all-to-all-start.9 = ((bf16[8,528,128]{2,1,0:T(8,128)(2,1)}), bf16[8,528,128]{2,1,0:T(8,128)(2,1)S(1)}, u32[]{:S(2)}, u32[]{:S(2)}) async-start(bf16[8,528,128]{2,1,0:T(8,128)(2,1)} %bitcast.18), calls=%async_computation.10 | async-start | bytes 2162688 | tf_op jit(solution)/shard_map/all_to_all | solution.py:1267
  294.3 1.9 collective-permute-start.26
  299.0 8.0 %collective-permute-start.27 = (bf16[1,768,128]{2,1,0:T(8,128)(2,1)}, bf16[1,768,128]{2,1,0:T(8,128)(2,1)S(1)}, u32[]{:S(2)}, u32[]{:S(2)}) collective-permute-start(bf16[1,768,128]{2,1,0:T(8,128)(2,1)} %get-tuple-element.212), channel_id=1, source_target_pairs={{0,2},{1,3},{2,0},{3,1},{4,6},{5,7},{6,4},{7,5},{8,10},{9,11},{10,... | collective-permute-start | bytes 589832 | tf_op jit(solution)/shard_map/ppermute | solution.py:949
  299.5 18.4 %collective-permute-start.22 = (bf16[132,1152]{1,0:T(8,128)(2,1)S(1)}, bf16[132,1152]{1,0:T(8,128)(2,1)S(1)}, u32[]{:S(2)}, u32[]{:S(2)}) collective-permute-start(bf16[132,1152]{1,0:T(8,128)(2,1)S(1)} %copy-done.38), channel_id=1, source_target_pairs={{0,1},{1,0},{2,3},{3,2},{4,5},{5,4},{6,7},{7,6},{8,9},{9,8},{10,11... | collective-permute-start | bytes 912392 | tf_op jit(solution)/shard_map/ppermute | solution.py:949
  299.6 18.4 %collective-permute-start.23 = (bf16[132,1152]{1,0:T(8,128)(2,1)S(1)}, bf16[132,1152]{1,0:T(8,128)(2,1)S(1)}, u32[]{:S(2)}, u32[]{:S(2)}) collective-permute-start(bf16[132,1152]{1,0:T(8,128)(2,1)S(1)} %copy-done.37), channel_id=1, source_target_pairs={{0,2},{1,3},{2,0},{3,1},{4,6},{5,7},{6,4},{7,5},{8,10},{9,11},{10,... | collective-permute-start | bytes 912392 | tf_op jit(solution)/shard_map/ppermute | solution.py:949
  301.2 17.6 %collective-permute-start.24 = (bf16[132,1152]{1,0:T(8,128)(2,1)S(1)}, bf16[132,1152]{1,0:T(8,128)(2,1)S(1)}, u32[]{:S(2)}, u32[]{:S(2)}) collective-permute-start(bf16[132,1152]{1,0:T(8,128)(2,1)S(1)} %copy-done.36), channel_id=1, source_target_pairs={{0,3},{1,2},{2,1},{3,0},{4,7},{5,6},{6,5},{7,4},{8,11},{9,10},{10,... | collective-permute-start | bytes 912392 | tf_op jit(solution)/shard_map/ppermute | solution.py:949
  301.4 16.4 %collective-permute-start.29 = (bf16[400,128]{1,0:T(8,128)(2,1)S(1)}, bf16[400,128]{1,0:T(8,128)(2,1)S(1)}, u32[]{:S(2)}, u32[]{:S(2)}) collective-permute-start(bf16[400,128]{1,0:T(8,128)(2,1)S(1)} %copy-done.48), channel_id=1, source_target_pairs={{0,16},{4,20},{8,24},{12,28},{16,0},{20,4},{24,8},{28,12},{1,17},{... | collective-permute-start | bytes 307208 | tf_op jit(solution)/shard_map/ppermute | solution.py:1187
  311.8 12.9 %all-to-all-start.10 = ((bf16[8,96,128]{2,1,0:T(8,128)(2,1)}), bf16[8,96,128]{2,1,0:T(8,128)(2,1)S(1)}, u32[]{:S(2)}, u32[]{:S(2)}) async-start(bf16[8,96,128]{2,1,0:T(8,128)(2,1)} %bitcast.89), calls=%async_computation.11 | async-start | bytes 393216 | tf_op jit(solution)/shard_map/all_to_all | solution.py:1286
  315.8 7.2 %collective-permute-start.28 = (bf16[400,128]{1,0:T(8,128)(2,1)S(1)}, bf16[400,128]{1,0:T(8,128)(2,1)S(1)}, u32[]{:S(2)}, u32[]{:S(2)}) collective-permute-start(bf16[400,128]{1,0:T(8,128)(2,1)S(1)} %copy-done.48), channel_id=1, source_target_pairs={{0,8},{4,12},{8,0},{12,4},{16,24},{20,28},{24,16},{28,20},{1,9},{5... | collective-permute-start | bytes 307208 | tf_op jit(solution)/shard_map/ppermute | solution.py:1187
  317.9 10.2 %copy-start.49 = (bf16[400,128]{1,0:T(8,128)(2,1)}, bf16[400,128]{1,0:T(8,128)(2,1)S(1)}, u32[]{:S(2)}) copy-start(bf16[400,128]{1,0:T(8,128)(2,1)S(1)} %collective-permute-done.29.refs_5_) | copy-start | bytes 307204
  317.9 6.5 %collective-permute-start.30 = (bf16[400,128]{1,0:T(8,128)(2,1)S(1)}, bf16[400,128]{1,0:T(8,128)(2,1)S(1)}, u32[]{:S(2)}, u32[]{:S(2)}) collective-permute-start(bf16[400,128]{1,0:T(8,128)(2,1)S(1)} %collective-permute-done.29.refs_5_), channel_id=1, source_target_pairs={{0,8},{4,12},{8,0},{12,4},{16,24},{20,28},{24,16},{28,20},{1,9},{5... | collective-permute-start | bytes 307208 | tf_op jit(solution)/shard_map/ppermute | solution.py:1187
  328.1 6.0 %copy-start.28 = (f32[8,128]{1,0:T(8,128)S(1)}, f32[8,128]{1,0:T(8,128)}, u32[]{:S(2)}) copy-start(f32[8,128]{1,0:T(8,128)} %get-tuple-element.225) | copy-start | bytes 12292
  328.1 10.2 %copy-start.51 = (bf16[400,128]{1,0:T(8,128)(2,1)S(1)}, bf16[400,128]{1,0:T(8,128)(2,1)}, u32[]{:S(2)}) copy-start(bf16[400,128]{1,0:T(8,128)(2,1)} %copy-done.50) | copy-start | bytes 307204
  328.1 12.3 %copy-start.53 = (bf16[400,128]{1,0:T(8,128)(2,1)S(1)}, bf16[400,128]{1,0:T(8,128)(2,1)}, u32[]{:S(2)}) copy-start(bf16[400,128]{1,0:T(8,128)(2,1)} %copy-done.52) | copy-start | bytes 307204
  328.1 36.1 %all-to-all-start.11 = ((bf16[8,624,128]{2,1,0:T(8,128)(2,1)}), bf16[8,624,128]{2,1,0:T(8,128)(2,1)S(1)}, u32[]{:S(2)}, u32[]{:S(2)}) async-start(bf16[8,624,128]{2,1,0:T(8,128)(2,1)} %shard_map.430), calls=%async_computation.12 | async-start | bytes 2555904 | tf_op jit(solution)/shard_map/all_to_all | solution.py:1305
  336.3 11.2 %collective-permute-start.31 = (bf16[400,128]{1,0:T(8,128)(2,1)S(1)}, bf16[400,128]{1,0:T(8,128)(2,1)S(1)}, u32[]{:S(2)}, u32[]{:S(2)}) collective-permute-start(bf16[400,128]{1,0:T(8,128)(2,1)S(1)} %copy-done.48), channel_id=1, source_target_pairs={{0,4},{4,0},{8,12},{12,8},{16,20},{20,16},{24,28},{28,24},{1,5},{5... | collective-permute-start | bytes 307208 | tf_op jit(solution)/shard_map/ppermute | solution.py:1187
  338.3 12.8 %collective-permute-start.32 = (bf16[400,128]{1,0:T(8,128)(2,1)S(1)}, bf16[400,128]{1,0:T(8,128)(2,1)S(1)}, u32[]{:S(2)}, u32[]{:S(2)}) collective-permute-start(bf16[400,128]{1,0:T(8,128)(2,1)S(1)} %copy-done.51), channel_id=1, source_target_pairs={{0,4},{4,0},{8,12},{12,8},{16,20},{20,16},{24,28},{28,24},{1,5},{5... | collective-permute-start | bytes 307208 | tf_op jit(solution)/shard_map/ppermute | solution.py:1187
  338.4 18.4 %collective-permute-start.33 = (bf16[400,128]{1,0:T(8,128)(2,1)}, bf16[400,128]{1,0:T(8,128)(2,1)S(1)}, u32[]{:S(2)}, u32[]{:S(2)}) collective-permute-start(bf16[400,128]{1,0:T(8,128)(2,1)} %copy-done.49), channel_id=1, source_target_pairs={{0,4},{4,0},{8,12},{12,8},{16,20},{20,16},{24,28},{28,24},{1,5},{5... | collective-permute-start | bytes 307208 | tf_op jit(solution)/shard_map/ppermute | solution.py:1187
  340.4 18.0 %collective-permute-start.34 = (bf16[400,128]{1,0:T(8,128)(2,1)S(1)}, bf16[400,128]{1,0:T(8,128)(2,1)S(1)}, u32[]{:S(2)}, u32[]{:S(2)}) collective-permute-start(bf16[400,128]{1,0:T(8,128)(2,1)S(1)} %copy-done.53), channel_id=1, source_target_pairs={{0,4},{4,0},{8,12},{12,8},{16,20},{20,16},{24,28},{28,24},{1,5},{5... | collective-permute-start | bytes 307208 | tf_op jit(solution)/shard_map/ppermute | solution.py:1187
  347.5 10.8 %copy-start.55 = (bf16[400,128]{1,0:T(8,128)(2,1)}, bf16[400,128]{1,0:T(8,128)(2,1)S(1)}, u32[]{:S(2)}) copy-start(bf16[400,128]{1,0:T(8,128)(2,1)S(1)} %collective-permute-done.31.refs_2_) | copy-start | bytes 307204
  351.2 7.1 %copy-start.56 = (bf16[400,128]{1,0:T(8,128)(2,1)}, bf16[400,128]{1,0:T(8,128)(2,1)S(1)}, u32[]{:S(2)}) copy-start(bf16[400,128]{1,0:T(8,128)(2,1)S(1)} %collective-permute-done.32.refs_4_) | copy-start | bytes 307204
  365.2 6.6 %copy-start.11 = (f32[864,32]{1,0:T(8,128)S(1)}, f32[864,32]{1,0:T(8,128)}, u32[]{:S(2)}) copy-start(f32[864,32]{1,0:T(8,128)} %get-tuple-element.224) | copy-start | bytes 331780
  (51 other events, 79.0 us)
Sparse Core Ops, SparseCore 0:
  186.4 41.3 reduce-scatter.1
